TPU v7x, 256 devices: a whole 4x4x8 slice. The times are simulated.
256 devices in a mesh: seq: 128 (over z, x, y_lo, core), dp: 2 (over y_hi).
Axes of the slice: x: 4, y: 4 (y_hi: 2, y_lo: 2; y = y_hi * 2 + y_lo), z: 8, core: 2. Of those that a mesh axis runs over, the one named last changes fastest.
Arguments:
- x_tokens: bfloat16 [2, 32768, 768], P('dp', 'seq'), may hold values from -21 to 21
- cotangent: bfloat16 [2, 32768, 768], P('dp', 'seq'), may hold values from -6 to 6
- w_qkv: bfloat16 [768, 2304], replicated, may hold values from -0.21875 to 0.21875
- w_out: bfloat16 [768, 768], replicated, may hold values from -0.21875 to 0.21875
Outputs:
- sublayer_out: bfloat16 [2, 32768, 768], P('dp', 'seq')
- input_grad: bfloat16 [2, 32768, 768], P('dp', 'seq')
- qkv_grad: float32 [768, 2304], P('seq')
- out_grad: float32 [768, 768], P('seq')
All inputs are finite; a program needn't handle non-finite values.
Results may differ from a plain program's by a relative error of at most 0.019.
The roundings to bfloat16 on the way count: a program that leaves them out, or rounds other values in their place, can miss the bound.
Values may be sent and summed in bfloat16 or wider, within the bound.
No kernel may reach another device: no remote copies, remote signals or barrier semaphores. Data moves between devices by JAX's collectives and lax.ppermute only.
A program may use at most 128 MiB of HBM per device.

v0:
```python
import jax
import jax.numpy as jnp
from jax import lax
from jax.sharding import PartitionSpec as P

DH = 64
NR = 128


half_root = 0.7071067811865476


def from_partner(block, axis, distance):
    count = lax.axis_size(axis)
    route = []
    for low in range(count):
        high = low | 1 << distance
        if high != low and high < count:
            route += [(low, high), (high, low)]
    return lax.ppermute(block, axis, route)


def for_sending(value):

    def short(part):
        return part.astype(jnp.bfloat16) if part.dtype == jnp.float32 else part

    return jax.tree.map(short, value)


def product(form, left, right):
    return jnp.einsum(form, left, right, preferred_element_type=jnp.float32)


def coarsen(level_nodes):
    groups, height, features = level_nodes.shape
    paired = level_nodes.reshape(groups // 2, height, 2, features).astype(jnp.float32)
    return ((paired[:, :, 0] + paired[:, :, 1]) * half_root).astype(jnp.bfloat16)


def coarsen_back(gradients):
    groups, height, features = gradients.shape
    return jnp.repeat(gradients * half_root, 2, axis=1).reshape(groups * 2, height, features)


def mirror(level_nodes):
    halves_shape = (level_nodes.shape[0] // 2, 2) + level_nodes.shape[1:]
    return jnp.flip(level_nodes.reshape(halves_shape), 1).reshape(level_nodes.shape)


def build_tree(keyval, block_rows):
    current = keyval.reshape(keyval.shape[0] // block_rows, block_rows, keyval.shape[1])
    current = coarsen(current)
    layers = [current]
    return layers


def join_pair(current, partner, bit_value):
    lower_first = bit_value == 0
    first_half = jnp.where(lower_first, current, partner)
    second_half = jnp.where(lower_first, partner, current)
    return coarsen(jnp.stack([first_half, second_half]))[0]


def pair_attention(block_rows, queries, exact, inner, remote, upstream_heads):
    tokens = queries.shape[0]
    head_size = queries.shape[-1]
    inverse_root = head_size ** (-0.5)
    pair_span = 2 * block_rows
    grouped_query = queries.reshape(tokens // pair_span, pair_span, 2, head_size)
    exact_key = exact[:, 0].reshape(grouped_query.shape)
    exact_value = exact[:, 1].reshape(grouped_query.shape)
    grouped_back = upstream_heads.reshape(grouped_query.shape)
    pieces = [
        product("gqhd,gkhd->hgqk", grouped_query, exact_key).reshape(2, tokens, pair_span)
        * inverse_root
    ]
    dpieces = [product("gqhd,gkhd->hgqk", grouped_back, exact_value).reshape(2, tokens, pair_span)]
    pieces.append(product("qhd,khd->hqk", queries, remote[:, 0]) * inverse_root)
    dpieces.append(product("qhd,khd->hqk", upstream_heads, remote[:, 1]))
    top = jnp.max(pieces[0], axis=-1, keepdims=True)
    for piece in pieces[1:]:
        top = jnp.maximum(top, jnp.max(piece, axis=-1, keepdims=True))
    shifted = [jnp.exp(piece - top) for piece in pieces]
    total = jnp.sum(shifted[0], axis=-1, keepdims=True)
    for piece in shifted[1:]:
        total = total + jnp.sum(piece, axis=-1, keepdims=True)
    probs = [piece / total for piece in shifted]
    w_parts = [piece.astype(jnp.bfloat16) for piece in probs]
    row_delta = jnp.sum(probs[0] * dpieces[0], axis=-1, keepdims=True)
    for place in range(1, len(probs)):
        row_delta = row_delta + jnp.sum(probs[place] * dpieces[place], axis=-1, keepdims=True)
    s_parts = [
        (probs[place] * (dpieces[place] - row_delta) * inverse_root).astype(jnp.bfloat16)
        for place in range(len(probs))
    ]
    w_first = w_parts[0].reshape(2, tokens // pair_span, pair_span, pair_span)
    s_first = s_parts[0].reshape(w_first.shape)
    attended = product("hgqk,gkhd->gqhd", w_first, exact_value).reshape(tokens, 2, head_size)
    dquery = product("hgqk,gkhd->gqhd", s_first, exact_key).reshape(tokens, 2, head_size)
    dexact = jnp.stack(
        [
            product("hgqk,gqhd->gkhd", s_first, grouped_query).reshape(tokens, 2, head_size),
            product("hgqk,gqhd->gkhd", w_first, grouped_back).reshape(tokens, 2, head_size),
        ],
        axis=1,
    )
    dinner = []
    attended = attended + product("hqk,khd->qhd", w_parts[-1], remote[:, 1])
    dquery = dquery + product("hqk,khd->qhd", s_parts[-1], remote[:, 0])
    dremote = jnp.stack(
        [
            product("hqk,qhd->khd", s_parts[-1], queries),
            product("hqk,qhd->khd", w_parts[-1], upstream_heads),
        ],
        axis=1,
    )
    return (attended, dquery, dexact, tuple(dinner), dremote)


def to_pairs(values_in, head_size):
    leading = values_in.shape[:-1]
    pair_count = values_in.shape[-1] // (4 * head_size)
    reshaped = values_in.reshape(leading + (2, pair_count, 2, head_size))
    return jnp.moveaxis(reshaped, len(leading) + 1, 0)


def from_pairs(values_in):
    moved = jnp.moveaxis(values_in, 0, values_in.ndim - 3)
    return moved.reshape(moved.shape[:-4] + (-1,))


def local_attention(block_rows, head_size, queries, keyval, inner, remote, attended_grad):
    tokens = queries.shape[0]
    pair_query = jnp.moveaxis(queries.reshape(tokens, -1, 2, head_size), 1, 0)
    pair_back = jnp.moveaxis(attended_grad.reshape(tokens, -1, 2, head_size), 1, 0)
    pair_exact = to_pairs(keyval, head_size)
    pair_inner = tuple((to_pairs(mirror(level_nodes), head_size) for level_nodes in inner))
    pair_remote = to_pairs(remote, head_size)

    def one_pair(operands):
        return pair_attention(block_rows, *operands)

    attended, dquery, dexact, dinner, dremote = lax.map(
        one_pair, (pair_query, pair_exact, pair_inner, pair_remote, pair_back)
    )
    attended = jnp.moveaxis(attended, 0, 1).reshape(tokens, -1)
    dquery = jnp.moveaxis(dquery, 0, 1).reshape(tokens, -1)
    dinner = tuple((mirror(from_pairs(gradients)) for gradients in dinner))
    return (attended, dquery, from_pairs(dexact), dinner, from_pairs(dremote))


def tree_backward(summary_grad, dexact):
    current = summary_grad[None]
    return coarsen_back(current).reshape(dexact.shape) + dexact


def shards(x_tokens, cotangent, w_qkv, w_out):
    tokens_in = x_tokens[0]
    upstream = cotangent[0]
    features = tokens_in.shape[1]
    block_rows = NR
    head_size = DH
    seq_count = lax.axis_size("seq")
    axis_depth = seq_count.bit_length() - 1
    position = lax.axis_index("seq")
    projected = jnp.dot(tokens_in, w_qkv, preferred_element_type=jnp.float32).astype(jnp.bfloat16)
    queries = projected[:, :features]
    keyval = projected[:, features:]
    layers = build_tree(keyval, block_rows)
    current = layers[-1][0]
    partners = []
    for tier_index in range(axis_depth):
        partner = from_partner(current, "seq", tier_index)
        partners.append(partner)
        if tier_index + 1 < axis_depth:
            current = join_pair(current, partner, position // 2**tier_index % 2)
    remote = jnp.concatenate(partners, axis=0)
    attended_grad = jnp.dot(upstream, w_out.T, preferred_element_type=jnp.float32).astype(
        jnp.bfloat16
    )
    attended_f, dquery, dexact, dinner, dremote = local_attention(
        block_rows, head_size, queries, keyval, layers[:-1], remote, attended_grad
    )
    attended = attended_f.astype(jnp.bfloat16)
    layer_out = jnp.dot(attended, w_out, preferred_element_type=jnp.float32).astype(jnp.bfloat16)
    remote_grads = dremote.reshape(axis_depth, block_rows, 2 * features)
    carried = None
    for tier_index in reversed(range(axis_depth)):
        outgoing = remote_grads[tier_index]
        kept_half = None
        if carried is not None:
            halves = coarsen_back(carried[None])
            lower_bit = position // 2**tier_index % 2 == 0
            kept_half = jnp.where(lower_bit, halves[0], halves[1])
            outgoing = outgoing + jnp.where(lower_bit, halves[1], halves[0])
        received = from_partner(for_sending(outgoing), "seq", tier_index).astype(outgoing.dtype)
        carried = received if kept_half is None else received + kept_half
    leaf_grads = tree_backward(carried, dexact)
    proj_grads = jnp.concatenate([dquery, leaf_grads], axis=1).astype(jnp.bfloat16)
    input_grad = jnp.dot(proj_grads, w_qkv.T, preferred_element_type=jnp.float32).astype(
        jnp.bfloat16
    )
    rows_att = lax.slice_in_dim(attended, 0, features // seq_count * lax.axis_size("seq"), axis=1)
    shares = lax.psum_scatter(
        jnp.concatenate(
            [
                jnp.dot(tokens_in.T, proj_grads, preferred_element_type=jnp.float32),
                jnp.dot(rows_att.T, upstream, preferred_element_type=jnp.float32),
            ],
            axis=1,
        ),
        "seq",
        scatter_dimension=0,
        tiled=True,
    )
    totals = lax.psum(shares.astype(jnp.bfloat16), "dp").astype(jnp.float32)
    return (layer_out[None], input_grad[None], totals[:, : 3 * features], totals[:, 3 * features :])


def solution(mesh):
    return jax.shard_map(
        shards,
        mesh=mesh,
        in_specs=(P("dp", "seq", None), P("dp", "seq", None), P(), P()),
        out_specs=(P("dp", "seq", None), P("dp", "seq", None), P("seq", None), P("seq", None)),
        check_vma=False,
    )
```

profile of v0, /device:TPU:1, one launch (start us, length us, event | category | flops | bytes accessed | tf_op | source)
XLA Modules:
  0.0 1128.3 jit_solution(18412617449165220696)
XLA Ops:
  7.5 3.0 reshape.405
  10.5 3.2 fusion.91
  14.6 3.2 collective-permute-start
  22.8 3.0 reshape.406
  25.9 3.2 fusion.90
  30.0 10.6 collective-permute-done.1
  43.9 3.0 reshape.407
  47.0 3.2 fusion.89
  51.3 9.7 collective-permute-done.2
  64.2 3.0 reshape.408
  67.3 3.2 fusion.88
  72.4 9.3 collective-permute-done.3
  85.0 3.0 reshape.409
  88.0 3.2 fusion.87
  92.1 7.9 collective-permute-done.4
  103.3 3.0 reshape.410
  106.3 3.2 fusion.86
  112.4 18.8 %collective-permute-done.5 = bf16[128,1536]{1,0:T(8,128)(2,1)} collective-permute-done((bf16[128,1536]{1,0:T(8,128)(2,1)}, bf16[128,1536]{1,0:T(8,128)(2,1)}, u32[]{:S(2)}, u32[]{:S(2)}) %collective-permute-start.5) | collective-permute-done | bytes 393248 | tf_op jit(solution)/shard_map/ppermute | solution.py:20
  134.5 3.0 reshape.411
  137.5 3.2 fusion.85
  141.6 5.0 collective-permute-start.6
  152.6 2.6 convolution_convert_fusion.3
  157.2 6.9 collective-permute-done.6
  165.9 4.6 copy.181
  170.5 71.6 %while.16 = (s32[]{:T(128)}, bf16[6,256,2,64]{1,3,2,0:T(8,128)(2,1)}, bf16[6,256,2,64]{1,3,2,0:T(8,128)(2,1)}, f32[6,256,2,2,64]{1,4,3,0,2:T(8,128)}, f32[6,896,...) while((s32[]{:T(128)}, ...), condition=%wide.region_7.8_spmd, body=%wide.region_0.7_spmd.sunk | while | flops 467433984 | bytes 32839900 | solution.py:144
  245.7 4.6 fusion.84
  250.3 13.8 %collective-permute-done.7 = bf16[128,1536]{0,1:T(8,128)(2,1)S(1)} collective-permute-done((bf16[128,1536]{0,1:T(8,128)(2,1)S(1)}, bf16[128,1536]{0,1:T(8,128)(2,1)S(1)}, u32[]{:S(2)}, u32[]{:S(2)}) %collective-permute-start.7) | collective-permute-done | bytes 393248 | tf_op jit(solution)/shard_map/ppermute | solution.py:20
  269.9 2.6 select_n.270
  281.4 2.6 select_n.272
  286.3 6.9 collective-permute-done.8
  300.2 2.6 select_n.274
  324.8 2.6 select_n.278
  331.9 2.7 collective-permute-start.10
  339.0 2.6 select_n.280
  363.1 2.6 select_n.284
  375.2 2.6 select_n.286
  389.2 2.6 select_n.288
  401.1 2.6 select_n.290
  408.3 3.0 collective-permute-start.13
  412.6 3.1 copy.212
  417.6 3.1 fusion.76
  434.3 2.8 broadcast_in_dim.90
  437.1 3.2 broadcast_in_dim.91
  444.3 4.0 convolution_bitcast_fusion.8
  448.3 8.0 pad_maximum_fusion
  456.3 638.7 %all-reduce.2 = bf16[768,3072]{0,1:T(8,128)(2,1)} all-reduce(f32[768,3072]{0,1:T(8,128)} %pad_maximum_fusion), channel_id=2, replica_groups=mesh['seq'=128,'dp'=2] {'seq'}, use_global_device_ids=true, to_apply=%region_8.9.clone | all-reduce | flops 2359296 | bytes 14155776
  1095.0 2.6 dynamic-slice_convert_fusion
  1097.6 23.2 %psum.7 = bf16[6,3072]{0,1:T(8,128)(2,1)} all-reduce(bf16[6,3072]{0,1:T(8,128)(2,1)} %dynamic-slice_convert_fusion), channel_id=1, replica_groups=mesh['seq'=128,'dp'=2] {'dp'}, use_global_device_ids=true, to_apply=%region_9.10 | all-reduce | flops 18432 | bytes 73728 | tf_op jit(solution)/shard_map/psum | solution.py:217
  (293 shorter events, 260.5 us)
Async XLA Ops:
  0.6 2.0 copy-start
  4.7 1.0 copy-start.6
  14.6 4.9 collective-permute-start
  30.0 10.6 collective-permute-start.1
  51.1 9.9 collective-permute-start.2
  71.4 10.3 collective-permute-start.3
  92.1 7.9 collective-permute-start.4
  110.4 20.7 %collective-permute-start.5 = (bf16[128,1536]{1,0:T(8,128)(2,1)}, bf16[128,1536]{1,0:T(8,128)(2,1)}, u32[]{:S(2)}, u32[]{:S(2)}) collective-permute-start(bf16[128,1536]{1,0:T(8,128)(2,1)} %fusion.74), channel_id=1, source_target_pairs={{0,64},{64,0},{2,66},{66,2},{4,68},{68,4},{6,70},{70,6},{8,72},{72... | collective-permute-start | bytes 1179656 | tf_op jit(solution)/shard_map/ppermute | solution.py:20
  141.6 22.5 %collective-permute-start.6 = (bf16[128,1536]{1,0:T(8,128)(2,1)}, bf16[128,1536]{1,0:T(8,128)(2,1)}, u32[]{:S(2)}, u32[]{:S(2)}) collective-permute-start(bf16[128,1536]{1,0:T(8,128)(2,1)} %fusion.75), channel_id=1, source_target_pairs={{0,128},{128,0},{2,130},{130,2},{4,132},{132,4},{6,134},{134,6},{8... | collective-permute-start | bytes 1179656 | tf_op jit(solution)/shard_map/ppermute | solution.py:20
  170.5 3.2 copy-start.1
  175.0 1.3 copy-start.8
  182.4 3.2 copy-start.1
  186.9 1.3 copy-start.8
  194.3 3.2 copy-start.1
  198.8 1.3 copy-start.8
  206.3 3.2 copy-start.1
  210.8 1.3 copy-start.8
  218.2 3.2 copy-start.1
  222.7 1.3 copy-start.8
  230.1 3.2 copy-start.1
  234.6 1.3 copy-start.8
  243.3 20.8 %collective-permute-start.7 = (bf16[128,1536]{0,1:T(8,128)(2,1)S(1)}, bf16[128,1536]{0,1:T(8,128)(2,1)S(1)}, u32[]{:S(2)}, u32[]{:S(2)}) collective-permute-start(bf16[128,1536]{0,1:T(8,128)(2,1)S(1)} %bitcast.318), channel_id=1, source_target_pairs={{0,128},{128,0},{2,130},{130,2},{4,132},{132,4},{6,134},{134,6},{8... | collective-permute-start | bytes 1179656 | tf_op jit(solution)/shard_map/ppermute | solution.py:20
  277.0 16.2 %collective-permute-start.8 = (bf16[128,1536]{0,1:T(8,128)(2,1)}, bf16[128,1536]{0,1:T(8,128)(2,1)}, u32[]{:S(2)}, u32[]{:S(2)}) collective-permute-start(bf16[128,1536]{0,1:T(8,128)(2,1)} %fusion.63), channel_id=1, source_target_pairs={{0,64},{64,0},{2,66},{66,2},{4,68},{68,4},{6,70},{70,6},{8,72},{72... | collective-permute-start | bytes 1179656 | tf_op jit(solution)/shard_map/ppermute | solution.py:20
  307.3 10.5 collective-permute-start.9
  331.9 12.1 %collective-permute-start.10 = (bf16[128,1536]{0,1:T(8,128)(2,1)}, bf16[128,1536]{0,1:T(8,128)(2,1)}, u32[]{:S(2)}, u32[]{:S(2)}) collective-permute-start(bf16[128,1536]{0,1:T(8,128)(2,1)} %fusion.65), channel_id=1, source_target_pairs={{0,16},{16,0},{2,18},{18,2},{4,20},{20,4},{6,22},{22,6},{8,24},{24... | collective-permute-start | bytes 1179656 | tf_op jit(solution)/shard_map/ppermute | solution.py:20
  358.2 9.8 collective-permute-start.11
  377.8 5.9 copy-start.9
  382.4 11.7 %collective-permute-start.12 = (bf16[128,1536]{0,1:T(8,128)(2,1)}, bf16[128,1536]{0,1:T(8,128)(2,1)}, u32[]{:S(2)}, u32[]{:S(2)}) collective-permute-start(bf16[128,1536]{0,1:T(8,128)(2,1)} %fusion.67), channel_id=1, source_target_pairs={{0,4},{4,0},{2,6},{6,2},{8,12},{12,8},{10,14},{14,10},{16,20},{20,... | collective-permute-start | bytes 1179656 | tf_op jit(solution)/shard_map/ppermute | solution.py:20
  406.0 5.3 copy-start.3
  406.0 5.3 copy-start.5
  408.3 21.5 %collective-permute-start.13 = (bf16[128,1536]{0,1:T(8,128)(2,1)}, bf16[128,1536]{0,1:T(8,128)(2,1)}, u32[]{:S(2)}, u32[]{:S(2)}) collective-permute-start(bf16[128,1536]{0,1:T(8,128)(2,1)} %fusion.68), channel_id=1, source_target_pairs={{0,2},{2,0},{4,6},{6,4},{8,10},{10,8},{12,14},{14,12},{16,18},{18,... | collective-permute-start | bytes 1179656 | tf_op jit(solution)/shard_map/ppermute | solution.py:20
  440.3 2.1 copy-start.4
  442.4 1.9 copy-start.7
  1120.8 2.3 copy-start.2
where the time goes:
time: 1150 us; the launch traced here: 1130 us
  blocking collectives  662 us (58%)
  local copies, waits for them, and re-layouts  213 us (19%)
  other arithmetic  87.2 us (8%)
  waiting for transfers between devices  86.8 us (8%)
  matrix products  55.4 us (5%)
  starting transfers between devices  21.5 us (2%)
    unnamed x1, blocking collectives  639 us
    ppermute x14, waiting for transfers between devices, from_partner(): return lax.ppermute(block, axis, route)  86.8 us
    select_n x18, local copies, waits for them, and re-layouts, shards(): outgoing = outgoing + jnp.where(lower_bit, halves[1], halves[0])  42.2 us
    select_n x18, local copies, waits for them, and re-layouts, shards(): kept_half = jnp.where(lower_bit, halves[0], halves[1])  42.1 us
    dot_general x72, matrix products, product(): return jnp.einsum(form, left, right, preferred_element_type=jnp.float32)  40.5 us
    broadcast_in_dim x14, local copies, waits for them, and re-layouts, coarsen_back(): jnp.repeat(gradients * half_root, 2, axis=1)  32.1 us
    psum x1, blocking collectives, shards(): totals = lax.psum(shares.astype(jnp.bfloat16), 'dp').astype(jnp.float32)  23.2 us
  transfers between devices with their start and end apart: 14, of which 10 were waited for; matrix products, arithmetic and copies ran while one was open for 7% of the time, Pallas kernels for 0%

commit v1 on v0

v1 whole, which is shorter than its diff:
```python
import jax
import jax.numpy as jnp
from jax import lax
from jax.experimental import pallas as pl
from jax.experimental.pallas import tpu as pltpu
from jax.sharding import Mesh, PartitionSpec as P

D = 768
H = 384
TOK = 256
NR = 128
DH = 64
ZN, XN, YN = 8, 4, 2
ZR = 48
SLOT = 112
HALF_ROOT = 0.7071067811865476
LOG2E = 1.4426950408889634
VMEM = 56 * 1024 * 1024
F32 = jnp.float32
BF16 = jnp.bfloat16


def dot(a, b):
    return lax.dot_general(a, b, (((1,), (0,)), ((), ())), preferred_element_type=F32)


def dot_nt(a, b):
    return lax.dot_general(a, b, (((1,), (1,)), ((), ())), preferred_element_type=F32)


def dot_tn(a, b):
    return lax.dot_general(a, b, (((0,), (0,)), ((), ())), preferred_element_type=F32)


def iota(shape, axis):
    return lax.broadcasted_iota(jnp.int32, shape, axis)


def pair_matrix(rows, cols, valid):
    r, k = iota((rows, cols), 0), iota((rows, cols), 1)
    return (((k >> 1) == r) & (r < valid)).astype(BF16)


def coarsen(node, rows=None, valid=None):
    rows = node.shape[0] // 2 if rows is None else rows
    valid = rows if valid is None else valid
    return (dot(pair_matrix(rows, node.shape[0], valid), node) * HALF_ROOT).astype(BF16)


def spread(grad, rows, valid=None):
    r, k = iota((rows, grad.shape[0]), 0), iota((rows, grad.shape[0]), 1)
    hot = (r >> 1) == k
    if valid is not None:
        hot = hot & (r < valid)
    up = lax.dot_general(
        hot.astype(F32), grad, (((1,), (0,)), ((), ())),
        precision=lax.Precision.HIGHEST, preferred_element_type=F32,
    )
    return up * HALF_ROOT


def whole(*shape):
    return pl.BlockSpec(shape, lambda *_: (0,) * len(shape))


def call(body, grid, ins, outs, scratch=()):
    return pl.pallas_call(
        body,
        grid_spec=pltpu.PrefetchScalarGridSpec(
            num_scalar_prefetch=1,
            grid=grid,
            in_specs=ins,
            out_specs=[s for s, _ in outs],
            scratch_shapes=list(scratch),
        ),
        out_shape=[jax.ShapeDtypeStruct(shape, kind) for _, (shape, kind) in outs],
        compiler_params=pltpu.CompilerParams(vmem_limit_bytes=VMEM),
    )


def project_body(pos, x_own, x_oth, ct_own, ct_oth, wq, wk, wv, wo, perm, q_out, kv_out, ag_out, n1_out, n2_out, n3_out, n4_out, zs_out, xt_out):
    c, z = pos[0], pos[1]
    oth = 1 - c

    def both(first, second):
        return ((c, first), (oth, second))

    for e, x in both(x_own, x_oth):
        kv_out[e, 0] = dot(x[...], wk[...]).astype(BF16)
        kv_out[e, 1] = dot(x[...], wv[...]).astype(BF16)
    for p in range(2):
        for e in range(2):
            n1_out[e, p] = coarsen(kv_out[e, p])
            n2_out[p, e * 64 : (e + 1) * 64] = coarsen(n1_out[e, p])
        n3 = coarsen(n2_out[p])
        n4 = coarsen(n3)
        n5 = coarsen(n4)
        n6 = coarsen(n5, 16, 8)
        n7 = coarsen(n6, 16, 4)
        n3_out[p] = n3
        n4_out[p] = n4
        zs_out[z, p] = jnp.zeros_like(n5)
        zs_out[z ^ 1, p] = n5
        for far in (2, 3):
            zs_out[z ^ far, p] = n6
        for far in (4, 5, 6, 7):
            zs_out[z ^ far, p] = n7
    for e, x in both(x_own, x_oth):
        q_out[e] = dot(x[...], wq[...]).astype(BF16)
        xt_out[e] = dot_nt(perm[...], x[...]).astype(BF16)
    for e, ct in both(ct_own, ct_oth):
        ag_out[e] = dot_nt(ct[...], wo[...]).astype(BF16)


def project(pos, x_own, x_oth, ct_own, ct_oth, w_qkv, w_out, perm):
    col = lambda part: pl.BlockSpec((D, H), lambda i, s: (0, 2 * part + s[0]))
    outs = [
        (2, TOK, H), (2, 2, TOK, H), (2, TOK, H), (2, 2, NR, H), (2, NR, H), (2, 64, H), (2, 32, H), (ZN, 2, 16, H), (2, D, TOK),
    ]
    return call(
        project_body,
        (1,),
        [whole(TOK, D)] * 4 + [col(0), col(1), col(2), pl.BlockSpec((H, D), lambda i, s: (s[0], 0)), whole(D, D)],
        [(whole(*shape), (shape, BF16)) for shape in outs],
    )(pos, x_own, x_oth, ct_own, ct_oth, w_qkv, w_qkv, w_qkv, w_out, perm)


def z_source(z, rows_axis, shape):
    i = iota(shape, rows_axis)
    near = 16 * (z ^ 1) + i
    mid = 16 * (z ^ (2 + ((i - 16) >> 3))) + ((i - 16) & 7)
    far = 16 * (z ^ (4 + ((i - 32) >> 2))) + ((i - 32) & 3)
    return jnp.where(i < 16, near, jnp.where(i < 32, mid, far))


def plane_body(pos, zr, n3, n4, out):
    z, j = pos[1], pos[2]
    hot = (iota((ZR, 128), 1) == z_source(z, 0, (ZR, 128))).astype(BF16)
    for p in range(2):
        rows = dot(hot, zr[:, p].reshape(128, H)).astype(BF16)
        for slot in range(8):
            out[slot, p, :ZR] = rows
        blank = jnp.zeros((64, H), BF16)
        for far in (0, 1):
            out[j ^ far, p, ZR:] = blank
        for far in (2, 3):
            out[j ^ far, p, ZR:] = n3[p]
        for far in (4, 5, 6, 7):
            out[j ^ far, p, ZR : ZR + 32] = n4[p]
            out[j ^ far, p, ZR + 32 :] = blank[:32]


def plane_slots(pos, zr, n3, n4):
    return call(
        plane_body,
        (1,),
        [whole(ZN, 2, 16, H), whole(2, 64, H), whole(2, 32, H)],
        [(whole(8, 2, SLOT, H), ((8, 2, SLOT, H), BF16))],
    )(pos, zr, n3, n4)[0]


def attention_body(pos, q, ag, kv, n1, yr, xr, att_out, dq_out, dkv_out, dn1_out, dy_out, dx_out, keys, s_ref, dw_ref, w_ref, ds_ref, drem):
    j = pos[2]
    for p in range(2):
        for e in range(2):
            keys[e, p, :256] = kv[e, p]
            keys[e, p, 256:384] = n1[1 - e, p]
            keys[e, p, 384:512] = yr[p]
            for far in (2, 3):
                start = 512 + 64 * (far - 2)
                keys[e, p, start : start + 64] = xr[j ^ far, p, ZR:]
            for far in (4, 5, 6, 7):
                start = 640 + 32 * (far - 4)
                keys[e, p, start : start + 32] = xr[j ^ far, p, ZR : ZR + 32]
            for slot in range(8):
                start = 768 + ZR * slot
                keys[e, p, start : start + ZR] = xr[slot, p, :ZR]
    lane = iota((TOK, 128), 1)
    for e in range(2):
        att_t, dq_t = [], []
        dk = dv = None
        for h in range(2):
            mine = (lane >> 6) == h
            qh = jnp.where(mine, q[e], jnp.zeros((), BF16))
            ah = jnp.where(mine, ag[e], jnp.zeros((), BF16))
            s_ref[...] = dot_nt(keys[e, 0], qh)
            dw_ref[...] = dot_nt(keys[e, 1], ah)
            top = jnp.max(s_ref[...], axis=0, keepdims=True)
            s_ref[...] = jnp.exp2((s_ref[...] - top) * (LOG2E * DH ** -0.5))
            total = jnp.sum(s_ref[...], axis=0, keepdims=True)
            inverse = 1.0 / total
            delta = jnp.sum(s_ref[...] * dw_ref[...], axis=0, keepdims=True) * inverse
            prob = s_ref[...] * inverse
            w_ref[...] = prob.astype(BF16)
            ds_ref[...] = (prob * (dw_ref[...] - delta) * DH ** -0.5).astype(BF16)
            att_t.append(dot_tn(keys[e, 1], w_ref[...])[64 * h : 64 * h + 64])
            dq_t.append(dot_tn(keys[e, 0], ds_ref[...])[64 * h : 64 * h + 64])
            dkh, dvh = dot(ds_ref[...], qh), dot(w_ref[...], ah)
            dk = dkh if dk is None else dk + dkh
            dv = dvh if dv is None else dv + dvh
        att_out[e] = jnp.concatenate(att_t, axis=0).T.astype(BF16)
        dq_out[e] = jnp.concatenate(dq_t, axis=0).T.astype(BF16)
        for p, grad in ((0, dk), (1, dv)):
            dkv_out[e, p] = grad[:256]
            dn1_out[1 - e, p] = grad[256:384]
            if e == 0:
                drem[p] = grad[384:]
            else:
                drem[p] = drem[p] + grad[384:]
    for p in range(2):
        rows = drem[p].astype(BF16)
        dy_out[p] = rows[:128]
        blank = jnp.zeros((64, 128), BF16)
        for far in (0, 1):
            dx_out[j ^ far, p, ZR:] = blank
        for far in (2, 3):
            start = 128 + 64 * (far - 2)
            dx_out[j ^ far, p, ZR:] = rows[start : start + 64]
        for far in (4, 5, 6, 7):
            start = 256 + 32 * (far - 4)
            dx_out[j ^ far, p, ZR : ZR + 32] = rows[start : start + 32]
            dx_out[j ^ far, p, ZR + 32 :] = blank[:32]
        for slot in range(8):
            start = 384 + ZR * slot
            dx_out[slot, p, :ZR] = rows[start : start + ZR]


def attention(pos, q, ag, kv, n1, yr, xr):
    def cut(*lead):
        return pl.BlockSpec(lead + (128,), lambda i, s: (0,) * len(lead) + (i,))

    outs = [
        ((2, TOK), BF16), ((2, TOK), BF16), ((2, 2, TOK), F32), ((2, 2, NR), F32), ((2, NR), BF16), ((8, 2, SLOT), BF16),
    ]
    n = 1152
    return call(
        attention_body,
        (H // 128,),
        [cut(2, TOK), cut(2, TOK), cut(2, 2, TOK), cut(2, 2, NR), cut(2, NR), cut(8, 2, SLOT)],
        [(cut(*lead), (lead + (H,), kind)) for lead, kind in outs],
        [
            pltpu.VMEM((2, 2, n, 128), BF16), pltpu.VMEM((n, TOK), F32), pltpu.VMEM((n, TOK), F32),
            pltpu.VMEM((n, TOK), BF16), pltpu.VMEM((n, TOK), BF16), pltpu.VMEM((2, 768, 128), F32),
        ],
    )(pos, q, ag, kv, n1, yr, xr)


def output_body(pos, att_own, att_oth, ct_own, ct_oth, w_own, w_oth, p_own, p_oth, out, grad_out):
    c = pos[0]
    out[...] = (dot(att_own[c], w_own[...]) + dot(att_oth[c], w_oth[...])).astype(BF16)
    total = None
    for e, ct in ((c, ct_own), (1 - c, ct_oth)):
        att_t = (dot_nt(p_own[...], att_own[e]) + dot_nt(p_oth[...], att_oth[e])).astype(BF16)
        term = dot(att_t, ct[...])
        total = term if total is None else total + term
    grad_out[...] = total.astype(BF16).reshape(8, 96, H)


def output_side(pos, att_own, att_oth, ct_own, ct_oth, w_out, perm):
    row = lambda flip: pl.BlockSpec((H, D), lambda i, s: (s[0] ^ flip, 0))
    col = lambda flip, rows: pl.BlockSpec((rows, H), lambda i, s: (0, s[0] ^ flip))
    return call(
        output_body,
        (1,),
        [whole(2, TOK, H)] * 2 + [col(0, TOK)] * 2 + [row(0), row(1), col(0, D), col(1, D)],
        [(whole(TOK, D), ((TOK, D), BF16)), (whole(8, 96, H), ((8, 96, H), BF16))],
    )(pos, att_own, att_oth, ct_own, ct_oth, w_out, w_out, perm, perm)


def back_body(pos, xr, out):
    z = pos[1]
    hot = (iota((128, ZR), 0) == z_source(z, 1, (128, ZR))).astype(BF16)
    for p in range(2):
        total = xr[0, p, :ZR].astype(F32)
        for slot in range(1, 8):
            total = total + xr[slot, p, :ZR].astype(F32)
        out[:, p] = dot(hot, total.astype(BF16)).astype(BF16).reshape(8, 16, H)


def back_slots(pos, xr):
    return call(
        back_body,
        (1,),
        [whole(8, 2, SLOT, H)],
        [(whole(ZN, 2, 16, H), ((ZN, 2, 16, H), BF16))],
    )(pos, xr)[0]


def leaf_body(pos, zr, xr, yr, dn1, dkv, dq, xt, pg_out, gqk_out, gv_out):
    z, j = pos[1], pos[2]

    def gather(ref, index, fars, p, lo, hi):
        total = None
        for far in fars:
            term = ref[index ^ far, p, lo:hi].astype(F32)
            total = term if total is None else total + term
        return total

    for p in range(2):
        g7 = gather(zr, z, (4, 5, 6, 7), p, 0, 16)
        g6 = gather(zr, z, (2, 3), p, 0, 16) + spread(g7, 16, 8)
        g5 = gather(zr, z, (1,), p, 0, 16) + spread(g6, 16)
        g4 = gather(xr, j, (4, 5, 6, 7), p, ZR, ZR + 32) + spread(g5, 32)
        g3 = gather(xr, j, (2, 3), p, ZR, ZR + 64) + spread(g4, 64)
        g2 = yr[p].astype(F32) + spread(g3, 128)
        for e in range(2):
            g1 = dn1[e, p] + spread(g2[64 * e : 64 * e + 64], 128)
            leaf = dkv[e, p] + spread(g1, 256)
            pg_out[e, :, H * (1 + p) : H * (2 + p)] = leaf.astype(BF16)
    for e in range(2):
        pg_out[e, :, :H] = dq[e]
    for part, out in ((0, gqk_out.at[0]), (1, gqk_out.at[1]), (2, gv_out)):
        total = dot(xt[0], pg_out[0, :, H * part : H * part + H]) + dot(xt[1], pg_out[1, :, H * part : H * part + H])
        out[...] = total.astype(BF16).reshape(8, 96, H)


def leaf_grads(pos, zr, xr, yr, dn1, dkv, dq, xt):
    return call(
        leaf_body,
        (1,),
        [
            whole(ZN, 2, 16, H), whole(8, 2, SLOT, H), whole(2, NR, H), whole(2, 2, NR, H), whole(2, 2, TOK, H),
            whole(2, TOK, H), whole(2, D, TOK),
        ],
        [
            (whole(2, TOK, 3 * H), ((2, TOK, 3 * H), BF16)),
            (whole(2, 8, 96, H), ((2, 8, 96, H), BF16)),
            (whole(8, 96, H), ((8, 96, H), BF16)),
        ],
    )(pos, zr, xr, yr, dn1, dkv, dq, xt)


def input_body(pos, pg_own, pg_oth, *rest):
    out = rest[-1]
    total = None
    for part in range(3):
        for pg, w in ((pg_own, rest[part]), (pg_oth, rest[3 + part])):
            term = dot_nt(pg[:, H * part : H * part + H], w[...])
            total = term if total is None else total + term
    out[...] = total.astype(BF16)


def input_side(pos, pg_own, pg_oth, w_qkv):
    col = lambda part, flip: pl.BlockSpec((D, H), lambda i, s: (0, 2 * part + (s[0] ^ flip)))
    return call(
        input_body,
        (1,),
        [whole(TOK, 3 * H)] * 2 + [col(part, flip) for flip in (0, 1) for part in range(3)],
        [(whole(TOK, D), ((TOK, D), BF16))],
    )(pos, pg_own, pg_oth, *[w_qkv] * 6)[0]


def swap(value, axis):
    return lax.ppermute(value, axis, [(0, 1), (1, 0)])


def shards(x_tokens, cotangent, w_qkv, w_out):
    x_own, ct_own = x_tokens[0], cotangent[0]
    c, z = lax.axis_index("c"), lax.axis_index("z")
    j = 2 * lax.axis_index("x") + lax.axis_index("y")
    pos = jnp.stack([c, z, j]).astype(jnp.int32)
    x_oth, ct_oth = swap(x_own, "c"), swap(ct_own, "c")
    f = jnp.arange(D, dtype=jnp.int32)
    source = 96 * (f // 12 % 8) + 12 * (f // 96) + f % 12
    perm = (source[:, None] == f[None, :]).astype(BF16)

    q, kv, ag, n1, n2, n3, n4, zs, xt = project(pos, x_own, x_oth, ct_own, ct_oth, w_qkv, w_out, perm)
    yr = swap(n2, "y")
    zr = lax.all_to_all(zs, "z", 0, 0)
    xs = plane_slots(pos, zr, n3, n4)
    xr = lax.all_to_all(xs, ("x", "y"), 0, 0)
    att, dq, dkv, dn1, dy, dx = attention(pos, q, ag, kv, n1, yr, xr)

    att_oth = swap(att, "c")
    dy_r = swap(dy, "y")
    dx_r = lax.all_to_all(dx, ("x", "y"), 0, 0)
    dz = back_slots(pos, dx_r)
    dz_r = lax.all_to_all(dz, "z", 0, 0)
    layer_out, g_out = output_side(pos, att, att_oth, ct_own, ct_oth, w_out, perm)
    pg, g_qk, g_v = leaf_grads(pos, dz_r, dx_r, dy_r, dn1, dkv, dq, xt)
    pg_own = lax.dynamic_index_in_dim(pg, c, 0, keepdims=False)
    pg_oth = swap(lax.dynamic_index_in_dim(pg, 1 - c, 0, keepdims=False), "c")
    input_grad = input_side(pos, pg_own, pg_oth, w_qkv)

    first = jnp.concatenate([g_qk[0], g_out], axis=-1)
    second = jnp.concatenate([g_qk[1], g_v], axis=-1)
    terms = jnp.stack([first, second], axis=1).reshape(16, 96, D)
    terms = lax.all_to_all(terms, ("x", "y", "dp"), 0, 0)
    terms = jnp.sum(terms.astype(F32), axis=0).astype(BF16).reshape(ZN, 12, D)
    terms = lax.all_to_all(terms, "z", 0, 0)
    mine = jnp.sum(terms.astype(F32), axis=0).astype(BF16)
    other = swap(mine, "dp")
    low = lax.axis_index("dp") == 0
    rows = jnp.concatenate([jnp.where(low, mine, other), jnp.where(low, other, mine)], axis=1)
    keep = lax.dynamic_slice_in_dim(rows, 6 * c, 6, 0)
    got = swap(lax.dynamic_slice_in_dim(rows, 6 - 6 * c, 6, 0), "c")
    left, right = jnp.where(c == 0, keep, got), jnp.where(c == 0, got, keep)
    part = lambda k: [left[:, H * k : H * k + H], right[:, H * k : H * k + H]]
    qkv_grad = jnp.concatenate(part(0) + part(2) + part(3), axis=1).astype(F32)
    out_grad = jnp.concatenate(part(1), axis=1).astype(F32)
    return (layer_out[None], input_grad[None], qkv_grad, out_grad)


def solution(mesh):
    split = Mesh(mesh.devices.reshape(ZN, XN, YN, 2, 2), ("z", "x", "y", "c", "dp"))
    seq = ("z", "x", "y", "c")
    return jax.shard_map(
        shards,
        mesh=split,
        in_specs=(P("dp", seq, None), P("dp", seq, None), P(), P()),
        out_specs=(P("dp", seq, None), P("dp", seq, None), P(seq, None), P(seq, None)),
        check_vma=False,
    )
```

time: 1150 us -> 212 us (0.18); the launches traced: 1130 us -> 211 us
  blocking collectives: 662 us -> 16 us
  local copies, waits for them, and re-layouts: 213 us -> 12.5 us
  other arithmetic: 87.2 us -> 4.82 us
  Pallas kernels: 0 us -> 55.8 us
  matrix products: 55.4 us -> 0 us
  starting transfers between devices: 21.5 us -> 47.6 us
  waiting for transfers between devices: 86.8 us -> 73.5 us
    unnamed x1 -> x0, blocking collectives: 639 us -> none
    select_n x36 -> x0, local copies, waits for them, and re-layouts: 84.3 us -> none  [the longest x18 42.2 us: shards(): outgoing = outgoing + jnp.where(lower_bit, halves[1], halves[0])]
    ppermute x14 -> x8, waiting for transfers between devices: 86.8 us -> 20.5 us  [swap(): return lax.ppermute(value, axis, [(0, 1), (1, 0)])]
    pallas_call x0 -> x7, Pallas kernels: none -> 55.8 us  [the longest x1 20.2 us: attention(): call(attention_body, (H // 128,), [cut(2, TOK), cut(2, TOK), cut(2, 2, TO...]
    dot_general x78 -> x0, matrix products: 55.4 us -> none  [the longest x72 40.5 us: product(): return jnp.einsum(form, left, right, preferred_element_type=jnp.float32)]
    all_to_all x0 -> x5, waiting for transfers between devices: none -> 53 us  [the longest x1 31.3 us: shards(): terms = lax.all_to_all(terms, ('x', 'y', 'dp'), 0, 0)]
    slice x14 -> x2, local copies, waits for them, and re-layouts: 37.5 us -> 0.02 us  [shards(): part = lambda k: [left[:, H * k:H * k + H], right[:, H * k:H * k + H]]]
    broadcast_in_dim x14 -> x0, local copies, waits for them, and re-layouts: 32.1 us -> none  [coarsen_back(): jnp.repeat(gradients * half_root, 2, axis=1)]
  transfers between devices with their start and end apart: 14 -> 13, of which waited for: 10 -> 6; matrix products, arithmetic and copies ran while one was open for 7% -> 1% of each run, Pallas kernels for 0% -> 7%
where the time goes in v1:
time: 212 us; the launch traced here: 211 us
  waiting for transfers between devices  73.5 us (35%)
  Pallas kernels  55.8 us (26%)
  starting transfers between devices  47.6 us (22%)
  blocking collectives  16 us (8%)
  local copies, waits for them, and re-layouts  12.5 us (6%)
  other arithmetic  4.82 us (2%)
    all_to_all x1, waiting for transfers between devices, shards(): terms = lax.all_to_all(terms, ('x', 'y', 'dp'), 0, 0)  31.3 us
    ppermute x8, starting transfers between devices, swap(): return lax.ppermute(value, axis, [(0, 1), (1, 0)])  23.7 us
    ppermute x8, waiting for transfers between devices, swap(): return lax.ppermute(value, axis, [(0, 1), (1, 0)])  20.5 us
    pallas_call x1, Pallas kernels, attention(): call(attention_body, (H // 128,), [cut(2, TOK), cut(2, TOK), cut(2, 2, TO...  20.2 us
    all_to_all x1, waiting for transfers between devices, shards(): dx_r = lax.all_to_all(dx, ('x', 'y'), 0, 0)  19.6 us
    all_to_all x1, blocking collectives, shards(): zr = lax.all_to_all(zs, 'z', 0, 0)  16 us
    pallas_call x1, Pallas kernels, leaf_grads(): call(leaf_body, (1,), [whole(ZN, 2, 16, H), whole(8, 2, SLOT, H), whole(2...  9.83 us
    pallas_call x1, Pallas kernels, project(): call(project_body, (1,), [whole(TOK, D)] * 4 + [col(0), col(1), col(2), p...  8.68 us
  transfers between devices with their start and end apart: 13, of which 6 were waited for; matrix products, arithmetic and copies ran while one was open for 1% of the time, Pallas kernels for 7%

profile of v1, /device:TPU:1, one launch (start us, length us, event | category | flops | bytes accessed | tf_op | source)
XLA Modules:
  0.0 211.1 jit_solution(503388905899925592)
XLA Ops:
  0.6 3.3 %collective-permute-start.1 = (bf16[256,768]{1,0:T(8,128)(2,1)}, bf16[256,768]{1,0:T(8,128)(2,1)S(1)}, u32[]{:S(2)}, u32[]{:S(2)}) collective-permute-start(bf16[256,768]{1,0:T(8,128)(2,1)} %bitcast.21), channel_id=1, source_target_pairs={{0,2},{2,0},{1,3},{3,1},{4,6},{6,4},{5,7},{7,5},{8,10},{10,8},{9,1... | collective-permute-start | bytes 1179656 | tf_op jit(solution)/shard_map/ppermute | solution.py:354
  4.0 0.1 collective-permute-start
  4.1 0.6 pad_add_fusion.pos
  4.7 1.3 fusion.perm.p_own.p_oth
  6.1 0.8 copy-done.2
  6.8 0.7 copy-done.10
  7.6 8.7 %shard_map.75 = (bf16[2,256,384]{2,1,0:T(8,128)(2,1)}, bf16[2,2,256,384]{3,2,1,0:T(8,128)(2,1)}, bf16[2,256,384]{2,1,0:T(8,128)(2,1)}, bf16[2,2,128,384]{3,2,1,0...) custom-call(s32[3]{0:T(128)} %pad_add_fusion.pos, ...), custom_call_target="tpu_custom_call" | custom-call | tf_op jit(solution)/shard_map/pallas_call | solution.py:120
  16.3 16.0 %all_to_all.30.zr = bf16[8,2,16,384]{3,2,1,0:T(8,128)(2,1)} all-to-all(bf16[8,2,16,384]{3,2,1,0:T(8,128)(2,1)} %get-tuple-element.29), channel_id=1, replica_groups=mesh['z'=8,'x'=4,'y'=2,'c'=2,'dp'=2] {'z'}, dimensions={0} | all-to-all | bytes 393216 | tf_op jit(solution)/shard_map/all_to_all | solution.py:369
  32.2 3.0 %shard_map.76 = bf16[8,2,112,384]{3,2,1,0:T(8,128)(2,1)} custom-call(s32[3]{0:T(128)} %pad_add_fusion.pos, bf16[8,2,16,384]{3,2,1,0:T(8,128)(2,1)} %all_to_all.30.zr, bf16[2,64,384]{2,1,0:T(8,128)(2,1)} %get-tuple-element.30.n3, bf16[2,32,384]{2,1,0:T(8,128)(2,1)} %get-tuple-element.31.n4), custom_call_target="tpu_custom_call" | custom-call | tf_op jit(solution)/shard_map/pallas_call | solution.py:154
  35.2 5.1 %all-to-all-start.1 = ((bf16[8,2,112,384]{3,2,1,0:T(8,128)(2,1)}), bf16[8,2,112,384]{3,2,1,0:T(8,128)(2,1)S(1)}, u32[]{:S(2)}, u32[]{:S(2)}) async-start(bf16[8,2,112,384]{3,2,1,0:T(8,128)(2,1)} %shard_map.76), calls=%async_computation.1 | async-start | bytes 2752512 | tf_op jit(solution)/shard_map/all_to_all | solution.py:371
  40.4 1.5 collective-permute-start.2
  41.8 17.8 %collective-permute-done.2.yr = bf16[2,128,384]{2,1,0:T(8,128)(2,1)S(1)} collective-permute-done((bf16[2,128,384]{2,1,0:T(8,128)(2,1)S(1)}, bf16[2,128,384]{2,1,0:T(8,128)(2,1)S(1)}, u32[]{:S(2)}, u32[]{:S(2)}) %collective-permute-start.2) | collective-permute-done | bytes 196640 | tf_op jit(solution)/shard_map/ppermute | solution.py:354
  59.6 0.7 copy-done.12
  60.3 0.5 copy-done.1
  60.8 20.2 %shard_map.77 = (bf16[2,256,384]{2,1,0:T(8,128)(2,1)}, bf16[2,256,384]{2,1,0:T(8,128)(2,1)}, f32[2,2,256,384]{3,2,1,0:T(8,128)}, f32[2,2,128,384]{3,2,1,0:T(8,12...) custom-call(s32[3]{0:T(128)} %pad_add_fusion.pos, bf16[2,256,384]{2,1,0:T(8,128)(2,1)} %get-tuple-element.24.q, ...), custom_call_target="tpu_custom_call" | custom-call | tf_op jit(solution)/shard_map/pallas_call | solution.py:236
  81.0 6.6 %all-to-all-start.2 = ((bf16[8,2,112,384]{3,2,1,0:T(8,128)(2,1)}), bf16[8,2,112,384]{3,2,1,0:T(8,128)(2,1)S(1)}, u32[]{:S(2)}, u32[]{:S(2)}) async-start(bf16[8,2,112,384]{3,2,1,0:T(8,128)(2,1)} %get-tuple-element.34), calls=%async_computation.2 | async-start | bytes 2752512 | tf_op jit(solution)/shard_map/all_to_all | solution.py:376
  87.7 0.9 collective-permute-start.3
  88.5 19.6 %all-to-all-done.2.xr = bf16[8,2,112,384]{3,2,1,0:T(8,128)(2,1)S(1)} async-done(((bf16[8,2,112,384]{3,2,1,0:T(8,128)(2,1)}), bf16[8,2,112,384]{3,2,1,0:T(8,128)(2,1)S(1)}, u32[]{:S(2)}, u32[]{:S(2)}) %all-to-all-start.2) | async-done | bytes 1376288 | tf_op jit(solution)/shard_map/all_to_all | solution.py:376
  108.2 1.1 copy-done
  109.3 3.0 %shard_map.79 = bf16[8,2,16,384]{3,2,1,0:T(8,128)(2,1)} custom-call(s32[3]{0:T(128)} %pad_add_fusion.pos, bf16[8,2,112,384]{3,2,1,0:T(8,128)(2,1)} %copy-done), custom_call_target="tpu_custom_call" | custom-call | tf_op jit(solution)/shard_map/pallas_call | solution.py:281
  112.2 3.6 %all-to-all-start.3 = ((bf16[8,2,16,384]{3,2,1,0:T(8,128)(2,1)}), bf16[8,2,16,384]{3,2,1,0:T(8,128)(2,1)S(1)}, u32[]{:S(2)}, u32[]{:S(2)}) async-start(bf16[8,2,16,384]{3,2,1,0:T(8,128)(2,1)} %shard_map.79), calls=%async_computation.3 | async-start | bytes 393216 | tf_op jit(solution)/shard_map/all_to_all | solution.py:378
  115.8 0.1 collective-permute-start.4
  115.9 0.7 copy-done.9
  116.7 6.0 %shard_map.78 = (bf16[256,768]{1,0:T(8,128)(2,1)}, bf16[8,96,384]{2,1,0:T(8,128)(2,1)}) custom-call(s32[3]{0:T(128)} %pad_add_fusion.pos, bf16[2,256,384]{2,1,0:T(8,128)(2,1)} %get-tuple-element.32.att_own, bf16[2,256,384]{2,1,0:T(8,128)(2,1)} %copy-done.9, bf16[256,768]{1,0:T(8,128)(2,1)} %bitcast.23, bf16[256,768]{1,0:T(8,128)(2,1)} %copy-done.2, ...), custom_call_target="tpu_custom_call" | custom-call | tf_op jit(solution)/shard_map/pallas_call | solution.py:262
  122.7 1.3 all-to-all-done.3.zr
  124.0 0.7 copy-done.4
  124.6 9.8 %shard_map.80 = (bf16[2,256,1152]{2,1,0:T(8,128)(2,1)}, bf16[2,8,96,384]{3,2,1,0:T(8,128)(2,1)}, bf16[8,96,384]{2,1,0:T(8,128)(2,1)}) custom-call(s32[3]{0:T(128)} %pad_add_fusion.pos, bf16[8,2,16,384]{3,2,1,0:T(8,128)(2,1)} %copy-done.4, bf16[8,2,112,384]{3,2,1,0:T(8,128)(2,1)} %copy-done, bf16[2,128,384]{2,1,0:T(8,128)(2,1)} %copy-done.11, ...), custom_call_target="tpu_custom_call" | custom-call | tf_op jit(solution)/shard_map/pallas_call | solution.py:318
  134.5 1.4 slice_bitcast_fusion.1
  135.9 0.1 maximum_bitcast_fusion
  136.0 0.9 copy-done.7
  137.0 0.1 maximum_bitcast_fusion.1
  137.1 0.2 pad_maximum_fusion
  137.3 1.6 copy.8
  138.9 5.2 %all-to-all-start.4 = ((bf16[16,96,768]{2,1,0:T(8,128)(2,1)}), bf16[16,96,768]{2,1,0:T(8,128)(2,1)S(1)}, u32[]{:S(2)}, u32[]{:S(2)}) async-start(bf16[16,96,768]{2,1,0:T(8,128)(2,1)} %bitcast.20), calls=%async_computation.4 | async-start | bytes 4718592 | tf_op jit(solution)/shard_map/all_to_all | solution.py:388
  144.1 31.3 %all-to-all-done.4 = bf16[16,96,768]{2,1,0:T(8,128)(2,1)S(1)} async-done(((bf16[16,96,768]{2,1,0:T(8,128)(2,1)}), bf16[16,96,768]{2,1,0:T(8,128)(2,1)S(1)}, u32[]{:S(2)}, u32[]{:S(2)}) %all-to-all-start.4) | async-done | bytes 2359328 | tf_op jit(solution)/shard_map/all_to_all | solution.py:388
  175.4 1.0 reduce_sum.24
  176.4 1.6 reshape.55
  178.0 3.4 %all-to-all-start.5 = ((bf16[8,12,768]{2,1,0:T(8,128)(2,1)}), bf16[8,12,768]{2,1,0:T(8,128)(2,1)S(1)}, u32[]{:S(2)}, u32[]{:S(2)}) async-start(bf16[8,12,768]{2,1,0:T(8,128)(2,1)} %reshape.55), calls=%async_computation.5 | async-start | bytes 393216 | tf_op jit(solution)/shard_map/all_to_all | solution.py:390
  181.4 0.9 dynamic-slice_bitcast_fusion
  182.4 6.9 %collective-permute-start.5 = (bf16[256,1152]{1,0:T(8,128)(2,1)S(1)}, bf16[256,1152]{1,0:T(8,128)(2,1)S(1)}, u32[]{:S(2)}, u32[]{:S(2)}) collective-permute-start(bf16[256,1152]{1,0:T(8,128)(2,1)S(1)} %get-tuple-element.46), channel_id=1, source_target_pairs={{0,2},{2,0},{1,3},{3,1},{4,6},{6,4},{5,7},{7,5},{8,10},{10,8},{9,1... | collective-permute-start | bytes 1769480 | tf_op jit(solution)/shard_map/ppermute | solution.py:354
  189.3 0.7 all-to-all-done.5
  190.0 1.9 collective-permute-start.6
  191.9 2.7 %collective-permute-done.6 = bf16[12,768]{1,0:T(8,128)(2,1)S(1)} collective-permute-done((bf16[12,768]{1,0:T(8,128)(2,1)S(1)}, bf16[12,768]{1,0:T(8,128)(2,1)S(1)}, u32[]{:S(2)}, u32[]{:S(2)}) %collective-permute-start.6) | collective-permute-done | bytes 18464 | tf_op jit(solution)/shard_map/ppermute | solution.py:354
  194.7 9.1 %collective-permute-start.7 = (bf16[6,1536]{1,0:T(8,128)(2,1)S(1)}, bf16[6,1536]{1,0:T(8,128)(2,1)S(1)}, u32[]{:S(2)}, u32[]{:S(2)}) collective-permute-start(bf16[6,1536]{1,0:T(8,128)(2,1)S(1)} %fusion.1), channel_id=1, source_target_pairs={{0,2},{2,0},{1,3},{3,1},{4,6},{6,4},{5,7},{7,5},{8,10},{10,8},{9,1... | collective-permute-start | bytes 55304 | tf_op jit(solution)/shard_map/ppermute | solution.py:354
  203.7 0.9 copy-done.5
  204.6 5.1 %shard_map.81 = bf16[256,768]{1,0:T(8,128)(2,1)} custom-call(s32[3]{0:T(128)} %pad_add_fusion.pos, bf16[256,1152]{1,0:T(8,128)(2,1)} %get-tuple-element.47.pg_own, bf16[256,1152]{1,0:T(8,128)(2,1)} %copy-done.5, bf16[768,2304]{1,0:T(8,128)(2,1)} %rest_5_.1, bf16[768,2304]{1,0:T(8,128)(2,1)} %rest_5_.1, bf16[768,2304]{1,0:T(8,128)(2,1)} %rest_5_.1, ...), custom_call_target="tpu_custom_call" | custom-call | tf_op jit(solution)/shard_map/pallas_call | solution.py:345
  209.9 0.6 convert_element_type.18
  210.5 0.6 maximum_convert_fusion
  (39 shorter events, 0.3 us)
Async XLA Ops:
  0.6 5.4 %collective-permute-start.1 = (bf16[256,768]{1,0:T(8,128)(2,1)}, bf16[256,768]{1,0:T(8,128)(2,1)S(1)}, u32[]{:S(2)}, u32[]{:S(2)}) collective-permute-start(bf16[256,768]{1,0:T(8,128)(2,1)} %bitcast.21), channel_id=1, source_target_pairs={{0,2},{2,0},{1,3},{3,1},{4,6},{6,4},{5,7},{7,5},{8,10},{10,8},{9,1... | collective-permute-start | bytes 1179656 | tf_op jit(solution)/shard_map/ppermute | solution.py:354
  4.0 2.1 %collective-permute-start = (bf16[256,768]{1,0:T(8,128)(2,1)}, bf16[256,768]{1,0:T(8,128)(2,1)S(1)}, u32[]{:S(2)}, u32[]{:S(2)}) collective-permute-start(bf16[256,768]{1,0:T(8,128)(2,1)} %bitcast.24), channel_id=1, source_target_pairs={{0,2},{2,0},{1,3},{3,1},{4,6},{6,4},{5,7},{7,5},{8,10},{10,8},{9,1... | collective-permute-start | bytes 1179656 | tf_op jit(solution)/shard_map/ppermute | solution.py:354
  6.0 0.8 copy-start.2
  6.8 0.7 copy-start.10
  35.2 5.1 %copy-start.14 = (bf16[2,128,384]{2,1,0:T(8,128)(2,1)S(1)}, bf16[2,128,384]{2,1,0:T(8,128)(2,1)}, u32[]{:S(2)}) copy-start(bf16[2,128,384]{2,1,0:T(8,128)(2,1)} %get-tuple-element.28) | copy-start | bytes 589828
  35.2 24.4 %all-to-all-start.1 = ((bf16[8,2,112,384]{3,2,1,0:T(8,128)(2,1)}), bf16[8,2,112,384]{3,2,1,0:T(8,128)(2,1)S(1)}, u32[]{:S(2)}, u32[]{:S(2)}) async-start(bf16[8,2,112,384]{3,2,1,0:T(8,128)(2,1)} %shard_map.76), calls=%async_computation.1 | async-start | bytes 2752512 | tf_op jit(solution)/shard_map/all_to_all | solution.py:371
  40.4 19.3 %collective-permute-start.2 = (bf16[2,128,384]{2,1,0:T(8,128)(2,1)S(1)}, bf16[2,128,384]{2,1,0:T(8,128)(2,1)S(1)}, u32[]{:S(2)}, u32[]{:S(2)}) collective-permute-start(bf16[2,128,384]{2,1,0:T(8,128)(2,1)S(1)} %copy-done.14), channel_id=1, source_target_pairs={{0,4},{4,0},{1,5},{5,1},{2,6},{6,2},{3,7},{7,3},{8,12},{12,8},{9,1... | collective-permute-start | bytes 589832 | tf_op jit(solution)/shard_map/ppermute | solution.py:354
  59.6 0.7 copy-start.12
  59.6 1.2 copy-start.1
  81.0 6.6 %copy-start.8 = (bf16[2,256,384]{2,1,0:T(8,128)(2,1)S(1)}, bf16[2,256,384]{2,1,0:T(8,128)(2,1)}, u32[]{:S(2)}) copy-start(bf16[2,256,384]{2,1,0:T(8,128)(2,1)} %get-tuple-element.32.att_own) | copy-start | bytes 1179652
  81.0 27.1 %all-to-all-start.2 = ((bf16[8,2,112,384]{3,2,1,0:T(8,128)(2,1)}), bf16[8,2,112,384]{3,2,1,0:T(8,128)(2,1)S(1)}, u32[]{:S(2)}, u32[]{:S(2)}) async-start(bf16[8,2,112,384]{3,2,1,0:T(8,128)(2,1)} %get-tuple-element.34), calls=%async_computation.2 | async-start | bytes 2752512 | tf_op jit(solution)/shard_map/all_to_all | solution.py:376
  87.7 28.2 %copy-start.13 = (bf16[2,128,384]{2,1,0:T(8,128)(2,1)S(1)}, bf16[2,128,384]{2,1,0:T(8,128)(2,1)}, u32[]{:S(2)}) copy-start(bf16[2,128,384]{2,1,0:T(8,128)(2,1)} %get-tuple-element.35) | copy-start | bytes 589828
  87.7 28.3 %collective-permute-start.3 = (bf16[2,256,384]{2,1,0:T(8,128)(2,1)S(1)}, bf16[2,256,384]{2,1,0:T(8,128)(2,1)S(1)}, u32[]{:S(2)}, u32[]{:S(2)}) collective-permute-start(bf16[2,256,384]{2,1,0:T(8,128)(2,1)S(1)} %copy-done.8), channel_id=1, source_target_pairs={{0,2},{2,0},{1,3},{3,1},{4,6},{6,4},{5,7},{7,5},{8,10},{10,8},{9,1... | collective-permute-start | bytes 1179656 | tf_op jit(solution)/shard_map/ppermute | solution.py:354
  108.2 1.1 copy-start
  112.2 11.7 %all-to-all-start.3 = ((bf16[8,2,16,384]{3,2,1,0:T(8,128)(2,1)}), bf16[8,2,16,384]{3,2,1,0:T(8,128)(2,1)S(1)}, u32[]{:S(2)}, u32[]{:S(2)}) async-start(bf16[8,2,16,384]{3,2,1,0:T(8,128)(2,1)} %shard_map.79), calls=%async_computation.3 | async-start | bytes 393216 | tf_op jit(solution)/shard_map/all_to_all | solution.py:378
  115.8 6.8 %collective-permute-start.4 = (bf16[2,128,384]{2,1,0:T(8,128)(2,1)S(1)}, bf16[2,128,384]{2,1,0:T(8,128)(2,1)S(1)}, u32[]{:S(2)}, u32[]{:S(2)}) collective-permute-start(bf16[2,128,384]{2,1,0:T(8,128)(2,1)S(1)} %copy-done.13), channel_id=1, source_target_pairs={{0,4},{4,0},{1,5},{5,1},{2,6},{6,2},{3,7},{7,3},{8,12},{12,8},{9,1... | collective-permute-start | bytes 589832 | tf_op jit(solution)/shard_map/ppermute | solution.py:354
  115.9 0.7 copy-start.9
  122.7 1.3 copy-start.11
  124.0 0.7 copy-start.4
  134.5 1.4 copy-start.6
  135.9 1.1 copy-start.7
  138.9 36.5 %all-to-all-start.4 = ((bf16[16,96,768]{2,1,0:T(8,128)(2,1)}), bf16[16,96,768]{2,1,0:T(8,128)(2,1)S(1)}, u32[]{:S(2)}, u32[]{:S(2)}) async-start(bf16[16,96,768]{2,1,0:T(8,128)(2,1)} %bitcast.20), calls=%async_computation.4 | async-start | bytes 4718592 | tf_op jit(solution)/shard_map/all_to_all | solution.py:388
  144.1 37.3 %copy-start.3 = (bf16[2,256,1152]{2,1,0:T(8,128)(2,1)S(1)}, bf16[2,256,1152]{2,1,0:T(8,128)(2,1)}, u32[]{:S(2)}) copy-start(bf16[2,256,1152]{2,1,0:T(8,128)(2,1)} %get-tuple-element.40) | copy-start | bytes 3538948
  178.0 11.9 %all-to-all-start.5 = ((bf16[8,12,768]{2,1,0:T(8,128)(2,1)}), bf16[8,12,768]{2,1,0:T(8,128)(2,1)S(1)}, u32[]{:S(2)}, u32[]{:S(2)}) async-start(bf16[8,12,768]{2,1,0:T(8,128)(2,1)} %reshape.55), calls=%async_computation.5 | async-start | bytes 393216 | tf_op jit(solution)/shard_map/all_to_all | solution.py:390
  182.4 21.4 %collective-permute-start.5 = (bf16[256,1152]{1,0:T(8,128)(2,1)S(1)}, bf16[256,1152]{1,0:T(8,128)(2,1)S(1)}, u32[]{:S(2)}, u32[]{:S(2)}) collective-permute-start(bf16[256,1152]{1,0:T(8,128)(2,1)S(1)} %get-tuple-element.46), channel_id=1, source_target_pairs={{0,2},{2,0},{1,3},{3,1},{4,6},{6,4},{5,7},{7,5},{8,10},{10,8},{9,1... | collective-permute-start | bytes 1769480 | tf_op jit(solution)/shard_map/ppermute | solution.py:354
  190.0 4.6 %collective-permute-start.6 = (bf16[12,768]{1,0:T(8,128)(2,1)S(1)}, bf16[12,768]{1,0:T(8,128)(2,1)S(1)}, u32[]{:S(2)}, u32[]{:S(2)}) collective-permute-start(bf16[12,768]{1,0:T(8,128)(2,1)S(1)} %reduce_sum.25), channel_id=1, source_target_pairs={{0,1},{1,0},{2,3},{3,2},{4,5},{5,4},{6,7},{7,6},{8,9},{9,8},{10,11... | collective-permute-start | bytes 55304 | tf_op jit(solution)/shard_map/ppermute | solution.py:354
  194.7 15.1 %collective-permute-start.7 = (bf16[6,1536]{1,0:T(8,128)(2,1)S(1)}, bf16[6,1536]{1,0:T(8,128)(2,1)S(1)}, u32[]{:S(2)}, u32[]{:S(2)}) collective-permute-start(bf16[6,1536]{1,0:T(8,128)(2,1)S(1)} %fusion.1), channel_id=1, source_target_pairs={{0,2},{2,0},{1,3},{3,1},{4,6},{6,4},{5,7},{7,5},{8,10},{10,8},{9,1... | collective-permute-start | bytes 55304 | tf_op jit(solution)/shard_map/ppermute | solution.py:354
  203.7 0.9 copy-start.5

commit v2 on v1

v2 whole, which is shorter than its diff:
```python
import jax
import jax.numpy as jnp
from jax import lax
from jax.experimental import pallas as pl
from jax.experimental.pallas import tpu as pltpu
from jax.sharding import Mesh, PartitionSpec as P

D = 768
H = 384
TOK = 256
NR = 128
DH = 64
ZN, XN, YN = 8, 4, 2
ZR = 48
HALF_ROOT = 0.7071067811865476
LOG2E = 1.4426950408889634
VMEM = 56 * 1024 * 1024
F32 = jnp.float32
BF16 = jnp.bfloat16


def dot(a, b):
    return lax.dot_general(a, b, (((1,), (0,)), ((), ())), preferred_element_type=F32)


def dot_nt(a, b):
    return lax.dot_general(a, b, (((1,), (1,)), ((), ())), preferred_element_type=F32)


def dot_tn(a, b):
    return lax.dot_general(a, b, (((0,), (0,)), ((), ())), preferred_element_type=F32)


def iota(shape, axis):
    return lax.broadcasted_iota(jnp.int32, shape, axis)


def pair_matrix(rows, cols, valid):
    r, k = iota((rows, cols), 0), iota((rows, cols), 1)
    return (((k >> 1) == r) & (r < valid)).astype(BF16)


def coarsen(node, rows=None, valid=None):
    rows = node.shape[0] // 2 if rows is None else rows
    valid = rows if valid is None else valid
    return (dot(pair_matrix(rows, node.shape[0], valid), node) * HALF_ROOT).astype(BF16)


def spread(grad, rows, valid=None):
    height = grad.shape[0]
    r, k = iota((rows, 2 * height), 0), iota((rows, 2 * height), 1)
    hot = (r >> 1) == (k & (height - 1))
    if valid is not None:
        hot = hot & (r < valid)
    high = grad.astype(BF16)
    low = (grad - high.astype(F32)).astype(BF16)
    return dot(hot.astype(BF16), jnp.concatenate([high, low], axis=0)) * HALF_ROOT


def whole(*shape):
    return pl.BlockSpec(shape, lambda *_: (0,) * len(shape))


def call(body, grid, ins, outs, scratch=()):
    return pl.pallas_call(
        body,
        grid_spec=pltpu.PrefetchScalarGridSpec(
            num_scalar_prefetch=1,
            grid=grid,
            in_specs=ins,
            out_specs=[s for s, _ in outs],
            scratch_shapes=list(scratch),
        ),
        out_shape=[jax.ShapeDtypeStruct(shape, kind) for _, (shape, kind) in outs],
        compiler_params=pltpu.CompilerParams(vmem_limit_bytes=VMEM),
    )


def tree_body(pos, x_own, x_oth, wk, wv, kv_out, n1_out, n2_out, zs_out):
    c, z = pos[0], pos[1]
    for e, x in ((c, x_own), (1 - c, x_oth)):
        kv_out[e, 0] = dot(x[...], wk[...]).astype(BF16)
        kv_out[e, 1] = dot(x[...], wv[...]).astype(BF16)
    blank = jnp.zeros((16, H), BF16)
    for p in range(2):
        for e in range(2):
            n1_out[e, p] = coarsen(kv_out[e, p])
            n2_out[p, e * 64 : (e + 1) * 64] = coarsen(n1_out[e, p])
        n5 = coarsen(coarsen(coarsen(n2_out[p])))
        n6 = coarsen(n5, 16, 8)
        n7 = coarsen(n6, 16, 4)
        zs_out[z, p] = blank
        zs_out[z ^ 1, p] = n5
        for far in (2, 3):
            zs_out[z ^ far, p] = n6
        for far in (4, 5, 6, 7):
            zs_out[z ^ far, p] = n7


def tree(pos, x_own, x_oth, w_qkv):
    col = lambda part: pl.BlockSpec((D, H), lambda i, s: (0, 2 * part + s[0]))
    outs = [(2, 2, TOK, H), (2, 2, NR, H), (2, NR, H), (ZN, 2, 16, H)]
    return call(
        tree_body,
        (1,),
        [whole(TOK, D)] * 2 + [col(1), col(2)],
        [(whole(*shape), (shape, BF16)) for shape in outs],
    )(pos, x_own, x_oth, w_qkv, w_qkv)


def project_body(pos, x_own, x_oth, ct_own, ct_oth, wq, wo, perm, q_out, ag_out, xt_out):
    c = pos[0]
    for e, x, ct in ((c, x_own, ct_own), (1 - c, x_oth, ct_oth)):
        q_out[e] = dot(x[...], wq[...]).astype(BF16)
        ag_out[e] = dot_nt(ct[...], wo[...]).astype(BF16)
        xt_out[e] = dot_nt(perm[...], x[...]).astype(BF16)


def project(pos, x_own, x_oth, ct_own, ct_oth, w_qkv, w_out, perm):
    outs = [(2, TOK, H), (2, TOK, H), (2, D, TOK)]
    return call(
        project_body,
        (1,),
        [whole(TOK, D)] * 4
        + [pl.BlockSpec((D, H), lambda i, s: (0, s[0])), pl.BlockSpec((H, D), lambda i, s: (s[0], 0)), whole(D, D)],
        [(whole(*shape), (shape, BF16)) for shape in outs],
    )(pos, x_own, x_oth, ct_own, ct_oth, w_qkv, w_out, perm)


def pair_body(pos, own, oth, near_out, far_out):
    y = pos[2] & 1
    for p in range(2):
        for half, n2 in ((y, own), (1 - y, oth)):
            near_out[half, p] = coarsen(n2[p])
            far_out[half, p] = coarsen(near_out[half, p])


def pair_nodes(pos, own, oth):
    outs = [(2, 2, 64, H), (2, 2, 32, H)]
    return call(
        pair_body, (1,), [whole(2, NR, H)] * 2, [(whole(*shape), (shape, BF16)) for shape in outs]
    )(pos, own, oth)


def pair_back_body(pos, near, far_a, far_b, dy, keep_out, send_out):
    y = pos[2] & 1
    for p in range(2):
        for half, out in ((y, None), (1 - y, send_out)):
            grad = near[half, p].astype(F32) + spread(far_a[half, p].astype(F32) + far_b[half, p].astype(F32), 64)
            if out is None:
                keep_out[p] = grad
            else:
                out[p] = (dy[p].astype(F32) + spread(grad, NR)).astype(BF16)


def pair_back(pos, near, far_a, far_b, dy):
    return call(
        pair_back_body,
        (1,),
        [whole(2, 2, 64, H), whole(2, 2, 32, H), whole(2, 2, 32, H), whole(2, NR, H)],
        [(whole(2, 64, H), ((2, 64, H), F32)), (whole(2, NR, H), ((2, NR, H), BF16))],
    )(pos, near, far_a, far_b, dy)


def z_source(z, rows_axis, shape):
    i = iota(shape, rows_axis)
    near = 16 * (z ^ 1) + i
    mid = 16 * (z ^ (2 + ((i - 16) >> 3))) + ((i - 16) & 7)
    far = 16 * (z ^ (4 + ((i - 32) >> 2))) + ((i - 32) & 3)
    return jnp.where(i < 16, near, jnp.where(i < 32, mid, far))


def plane_body(pos, zr, out):
    hot = (iota((ZR, 128), 1) == z_source(pos[1], 0, (ZR, 128))).astype(BF16)
    for p in range(2):
        rows = dot(hot, zr[:, p].reshape(128, H)).astype(BF16)
        for slot in range(8):
            out[slot, p] = rows


def plane_slots(pos, zr):
    return call(
        plane_body,
        (1,),
        [whole(ZN, 2, 16, H)],
        [(whole(8, 2, ZR, H), ((8, 2, ZR, H), BF16))],
    )(pos, zr)[0]


def attention_body(pos, q, ag, kv, n1, yr, near, far_a, far_b, xr, att_out, dq_out, dkv_out, dn1_out, dy_out, dnear_out, dfar_a_out, dfar_b_out, dx_out, keys, s_ref, dw_ref, w_ref, ds_ref, drem):
    for p in range(2):
        for e in range(2):
            keys[e, p, :256] = kv[e, p]
            keys[e, p, 256:384] = n1[1 - e, p]
            keys[e, p, 384:512] = yr[p]
            for half in range(2):
                start = 512 + 64 * half
                keys[e, p, start : start + 64] = near[half, p]
                start = 640 + 32 * half
                keys[e, p, start : start + 32] = far_a[half, p]
                start = 704 + 32 * half
                keys[e, p, start : start + 32] = far_b[half, p]
            for slot in range(8):
                start = 768 + ZR * slot
                keys[e, p, start : start + ZR] = xr[slot, p]
    lane = iota((TOK, 128), 1)
    for e in range(2):
        att_t, dq_t = [], []
        dk = dv = None
        for h in range(2):
            mine = (lane >> 6) == h
            qh = jnp.where(mine, q[e], jnp.zeros((), BF16))
            ah = jnp.where(mine, ag[e], jnp.zeros((), BF16))
            s_ref[...] = dot_nt(keys[e, 0], qh)
            dw_ref[...] = dot_nt(keys[e, 1], ah)
            top = jnp.max(s_ref[...], axis=0, keepdims=True)
            s_ref[...] = jnp.exp2((s_ref[...] - top) * (LOG2E * DH ** -0.5))
            total = jnp.sum(s_ref[...], axis=0, keepdims=True)
            inverse = 1.0 / total
            delta = jnp.sum(s_ref[...] * dw_ref[...], axis=0, keepdims=True) * inverse
            prob = s_ref[...] * inverse
            w_ref[...] = prob.astype(BF16)
            ds_ref[...] = (prob * (dw_ref[...] - delta) * DH ** -0.5).astype(BF16)
            att_t.append(dot_tn(keys[e, 1], w_ref[...])[64 * h : 64 * h + 64])
            dq_t.append(dot_tn(keys[e, 0], ds_ref[...])[64 * h : 64 * h + 64])
            dkh, dvh = dot(ds_ref[...], qh), dot(w_ref[...], ah)
            dk = dkh if dk is None else dk + dkh
            dv = dvh if dv is None else dv + dvh
        att_out[e] = jnp.concatenate(att_t, axis=0).T.astype(BF16)
        dq_out[e] = jnp.concatenate(dq_t, axis=0).T.astype(BF16)
        for p, grad in ((0, dk), (1, dv)):
            dkv_out[e, p] = grad[:256]
            dn1_out[1 - e, p] = grad[256:384]
            if e == 0:
                drem[p] = grad[384:]
            else:
                drem[p] = drem[p] + grad[384:]
    for p in range(2):
        rows = drem[p].astype(BF16)
        dy_out[p] = rows[:128]
        for half in range(2):
            start = 128 + 64 * half
            dnear_out[half, p] = rows[start : start + 64]
            start = 256 + 32 * half
            dfar_a_out[half, p] = rows[start : start + 32]
            start = 320 + 32 * half
            dfar_b_out[half, p] = rows[start : start + 32]
        for slot in range(8):
            start = 384 + ZR * slot
            dx_out[slot, p] = rows[start : start + ZR]


def attention(pos, q, ag, kv, n1, yr, near, far_a, far_b, xr):
    def cut(*lead):
        return pl.BlockSpec(lead + (128,), lambda i, s: (0,) * len(lead) + (i,))

    outs = [
        ((2, TOK), BF16), ((2, TOK), BF16), ((2, 2, TOK), F32), ((2, 2, NR), F32), ((2, NR), BF16),
        ((2, 2, 64), BF16), ((2, 2, 32), BF16), ((2, 2, 32), BF16), ((8, 2, ZR), BF16),
    ]
    n = 1152
    return call(
        attention_body,
        (H // 128,),
        [cut(2, TOK), cut(2, TOK), cut(2, 2, TOK), cut(2, 2, NR), cut(2, NR), cut(2, 2, 64), cut(2, 2, 32), cut(2, 2, 32), cut(8, 2, ZR)],
        [(cut(*lead), (lead + (H,), kind)) for lead, kind in outs],
        [
            pltpu.VMEM((2, 2, n, 128), BF16), pltpu.VMEM((n, TOK), F32), pltpu.VMEM((n, TOK), F32),
            pltpu.VMEM((n, TOK), BF16), pltpu.VMEM((n, TOK), BF16), pltpu.VMEM((2, 768, 128), F32),
        ],
    )(pos, q, ag, kv, n1, yr, near, far_a, far_b, xr)


def output_body(pos, att_own, att_oth, ct_own, ct_oth, dq, xt, w_own, w_oth, p_own, p_oth, out, grad_out):
    c = pos[0]
    total = dot(xt[0], dq[0]) + dot(xt[1], dq[1])
    grad_out[:, 0] = total.astype(BF16).reshape(8, 96, H)
    total = None
    for e, ct in ((c, ct_own), (1 - c, ct_oth)):
        att_t = (dot_nt(p_own[...], att_own[e]) + dot_nt(p_oth[...], att_oth[e])).astype(BF16)
        term = dot(att_t, ct[...])
        total = term if total is None else total + term
    grad_out[:, 1] = total.astype(BF16).reshape(8, 96, H)
    out[...] = (dot(att_own[c], w_own[...]) + dot(att_oth[c], w_oth[...])).astype(BF16)


def output_side(pos, att_own, att_oth, ct_own, ct_oth, dq, xt, w_out, perm):
    row = lambda flip: pl.BlockSpec((H, D), lambda i, s: (s[0] ^ flip, 0))
    col = lambda flip, rows: pl.BlockSpec((rows, H), lambda i, s: (0, s[0] ^ flip))
    return call(
        output_body,
        (1,),
        [whole(2, TOK, H)] * 2 + [col(0, TOK)] * 2 + [whole(2, TOK, H), whole(2, D, TOK)] + [row(0), row(1), col(0, D), col(1, D)],
        [(whole(TOK, D), ((TOK, D), BF16)), (whole(8, 2, 96, H), ((8, 2, 96, H), BF16))],
    )(pos, att_own, att_oth, ct_own, ct_oth, dq, xt, w_out, w_out, perm, perm)


def back_body(pos, xr, out):
    hot = (iota((128, ZR), 0) == z_source(pos[1], 1, (128, ZR))).astype(BF16)
    for p in range(2):
        total = xr[0, p].astype(F32)
        for slot in range(1, 8):
            total = total + xr[slot, p].astype(F32)
        out[:, p] = dot(hot, total.astype(BF16)).astype(BF16).reshape(8, 16, H)


def back_slots(pos, xr):
    return call(
        back_body,
        (1,),
        [whole(8, 2, ZR, H)],
        [(whole(ZN, 2, 16, H), ((ZN, 2, 16, H), BF16))],
    )(pos, xr)[0]


def leaf_body(pos, zr, keep, yr, dn1, dkv, dq, xt, pg_out, grad_out):
    z = pos[1]

    def gather(ref, index, fars, p, rows):
        total = None
        for far in fars:
            term = ref[index ^ far, p, :rows].astype(F32)
            total = term if total is None else total + term
        return total

    for p in range(2):
        g7 = gather(zr, z, (4, 5, 6, 7), p, 16)
        g6 = gather(zr, z, (2, 3), p, 16) + spread(g7, 16, 8)
        g5 = gather(zr, z, (1,), p, 16) + spread(g6, 16)
        g3 = keep[p] + spread(spread(g5, 32), 64)
        g2 = yr[p].astype(F32) + spread(g3, 128)
        for e in range(2):
            g1 = dn1[e, p] + spread(g2[64 * e : 64 * e + 64], 128)
            leaf = dkv[e, p] + spread(g1, 256)
            pg_out[e, :, H * (1 + p) : H * (2 + p)] = leaf.astype(BF16)
        cols = slice(H * (1 + p), H * (2 + p))
        total = dot(xt[0], pg_out[0, :, cols]) + dot(xt[1], pg_out[1, :, cols])
        grad_out[:, p] = total.astype(BF16).reshape(8, 96, H)
    for e in range(2):
        pg_out[e, :, :H] = dq[e]


def leaf_grads(pos, zr, keep, yr, dn1, dkv, dq, xt):
    return call(
        leaf_body,
        (1,),
        [
            whole(ZN, 2, 16, H), whole(2, 64, H), whole(2, NR, H), whole(2, 2, NR, H), whole(2, 2, TOK, H),
            whole(2, TOK, H), whole(2, D, TOK),
        ],
        [
            (whole(2, TOK, 3 * H), ((2, TOK, 3 * H), BF16)),
            (whole(8, 2, 96, H), ((8, 2, 96, H), BF16)),
        ],
    )(pos, zr, keep, yr, dn1, dkv, dq, xt)


def input_body(pos, pg_own, pg_oth, *rest):
    out = rest[-1]
    total = None
    for part in range(3):
        for pg, w in ((pg_own, rest[part]), (pg_oth, rest[3 + part])):
            term = dot_nt(pg[:, H * part : H * part + H], w[...])
            total = term if total is None else total + term
    out[...] = total.astype(BF16)


def input_side(pos, pg_own, pg_oth, w_qkv):
    col = lambda part, flip: pl.BlockSpec((D, H), lambda i, s: (0, 2 * part + (s[0] ^ flip)))
    return call(
        input_body,
        (1,),
        [whole(TOK, 3 * H)] * 2 + [col(part, flip) for flip in (0, 1) for part in range(3)],
        [(whole(TOK, D), ((TOK, D), BF16))],
    )(pos, pg_own, pg_oth, *[w_qkv] * 6)[0]


def total_of(ref):
    total = ref[0].astype(F32)
    for slot in range(1, ref.shape[0]):
        total = total + ref[slot].astype(F32)
    return total


def middle_body(pos, first, second, out):
    i, k = iota((256, 96), 0), iota((256, 96), 1)
    row, half = i & 7, (i >> 3) & 1
    hit = (k == 6 * (i >> 4) + row) & (row < 6)
    rows = dot((hit & (half == 0)).astype(BF16), first[...])
    rows = rows + dot((hit & (half == 1)).astype(BF16), total_of(second).astype(BF16))
    rows = rows.astype(BF16).reshape(ZN, 2, 16, H)
    for copy in range(2):
        out[:, :, copy] = rows


def middle_sum(pos, first, second):
    shape = (ZN, 2, 2, 16, H)
    return call(middle_body, (1,), [whole(96, H), whole(16, 96, H)], [(whole(*shape), (shape, BF16))])(pos, first, second)[0]


def last_body(pos, terms, qkv_out, out_out):
    for core in range(2):
        for dp in range(2):
            total = terms[0, core, dp].astype(F32)
            for z in range(1, ZN):
                total = total + terms[z, core, dp].astype(F32)
            if dp == 0:
                qkv_out[:, H * core : H * core + H] = total[:6]
            else:
                out_out[:, H * core : H * core + H] = total[:6]
            start = D * (1 + dp) + H * core
            qkv_out[:, start : start + H] = total[8:14]


def last_sum(pos, terms):
    return call(
        last_body,
        (1,),
        [whole(ZN, 2, 2, 16, H)],
        [(whole(6, 3 * D), ((6, 3 * D), F32)), (whole(6, D), ((6, D), F32))],
    )(pos, terms)


def swap(value, axis):
    return lax.ppermute(value, axis, [(0, 1), (1, 0)])


def along_x(value, far):
    return lax.ppermute(value, "x", [(i, i ^ far) for i in range(XN)])


def shards(x_tokens, cotangent, w_qkv, w_out):
    x_own, ct_own = x_tokens[0], cotangent[0]
    c, z = lax.axis_index("c"), lax.axis_index("z")
    j = 2 * lax.axis_index("x") + lax.axis_index("y")
    pos = jnp.stack([c, z, j]).astype(jnp.int32)
    x_oth, ct_oth = swap(x_own, "c"), swap(ct_own, "c")
    f = jnp.arange(D, dtype=jnp.int32)
    source = 96 * (f // 12 % 8) + 12 * (f // 96) + f % 12
    perm = (source[:, None] == f[None, :]).astype(BF16)

    kv, n1, n2, zs = tree(pos, x_own, x_oth, w_qkv)
    zr = lax.all_to_all(zs, "z", 0, 0)
    yr = swap(n2, "y")
    near, far = pair_nodes(pos, n2, yr)
    near, far_a, far_b = along_x(near, 1), along_x(far, 2), along_x(far, 3)
    q, ag, xt = project(pos, x_own, x_oth, ct_own, ct_oth, w_qkv, w_out, perm)
    zr, q, ag, xt, near, far_a, far_b = lax.optimization_barrier((zr, q, ag, xt, near, far_a, far_b))
    xr = lax.all_to_all(plane_slots(pos, zr), ("x", "y"), 0, 0)
    att, dq, dkv, dn1, dy, dnear, dfar_a, dfar_b, dx = attention(pos, q, ag, kv, n1, yr, near, far_a, far_b, xr)

    dx_r = lax.all_to_all(dx, ("x", "y"), 0, 0)
    att_oth = swap(att, "c")
    keep, dy = pair_back(pos, along_x(dnear, 1), along_x(dfar_a, 2), along_x(dfar_b, 3), dy)
    dy_r = swap(dy, "y")
    layer_out, terms = output_side(pos, att, att_oth, ct_own, ct_oth, dq, xt, w_out, perm)
    first = lax.psum_scatter(terms.reshape(XN, 4, 96, H), "x", scatter_dimension=0)
    first = lax.psum_scatter(first, ("y", "dp"), scatter_dimension=0)
    dz_r = lax.all_to_all(back_slots(pos, dx_r), "z", 0, 0)
    pg, terms = leaf_grads(pos, dz_r, keep, dy_r, dn1, dkv, dq, xt)
    second = lax.all_to_all(terms.reshape(16, 96, H), ("x", "y", "dp"), 0, 0)
    pg_own = lax.dynamic_index_in_dim(pg, c, 0, keepdims=False)
    pg_oth = swap(lax.dynamic_index_in_dim(pg, 1 - c, 0, keepdims=False), "c")
    input_grad = input_side(pos, pg_own, pg_oth, w_qkv)
    second, input_grad = lax.optimization_barrier((second, input_grad))
    terms = middle_sum(pos, first, second).reshape(32, 16, H)
    terms = lax.all_to_all(terms, ("z", "c", "dp"), 0, 0)
    qkv_grad, out_grad = last_sum(pos, terms.reshape(ZN, 2, 2, 16, H))
    return (layer_out[None], input_grad[None], qkv_grad, out_grad)


def solution(mesh):
    split = Mesh(mesh.devices.reshape(ZN, XN, YN, 2, 2), ("z", "x", "y", "c", "dp"))
    seq = ("z", "x", "y", "c")
    return jax.shard_map(
        shards,
        mesh=split,
        in_specs=(P("dp", seq, None), P("dp", seq, None), P(), P()),
        out_specs=(P("dp", seq, None), P("dp", seq, None), P(seq, None), P(seq, None)),
        check_vma=False,
    )
```

time: 212 us -> 213 us (level)
  waiting for transfers between devices: 73.5 us -> 38.1 us
  blocking collectives: 16 us -> 37.6 us
  between operations: 0.84 us -> 14.2 us
  Pallas kernels: 55.8 us -> 67.2 us
  local copies, waits for them, and re-layouts: 12.5 us -> 7.74 us
  other arithmetic: 4.82 us -> 1.96 us
  starting transfers between devices: 47.6 us -> 45 us
    all_to_all x4 -> x3, waiting for transfers between devices: 33.3 us -> 0.01 us  [the longest x1 0.01 us: shards(): dz_r = lax.all_to_all(back_slots(pos, dx_r), 'z', 0, 0)]
    all_to_all x1 -> x2, blocking collectives: 16 us -> 37.6 us  [the longest x1 24.3 us: shards(): terms = lax.all_to_all(terms, ('z', 'c', 'dp'), 0, 0)]
    reduce_scatter x0 -> x2, waiting for transfers between devices: none -> 18.1 us  [the longest x1 18.1 us: shards(): first = lax.psum_scatter(first, ('y', 'dp'), scatter_dimension=0)]
    ppermute x8 -> x6, waiting for transfers between devices: 20.5 us -> 7.56 us  [swap(): return lax.ppermute(value, axis, [(0, 1), (1, 0)])]
    pallas_call x5 -> x10, Pallas kernels: 30.5 us -> 41.8 us  [the longest x1 7.71 us: leaf_grads(): call(leaf_body, (1,), [whole(ZN, 2, 16, H), whole(2, 64, H), whole(2, NR,...]
    all_to_all x1, waiting for transfers between devices: 19.6 us -> 8.48 us  [shards(): dx_r = lax.all_to_all(dx, ('x', 'y'), 0, 0)]
    ppermute x8 -> x6, starting transfers between devices: 23.7 us -> 13.9 us  [swap(): return lax.ppermute(value, axis, [(0, 1), (1, 0)])]
    ppermute x0 -> x6, starting transfers between devices: none -> 7.47 us  [along_x(): return lax.ppermute(value, 'x', [(i, i ^ far) for i in range(XN)])]
  transfers between devices with their start and end apart: 13 -> 18, of which waited for: 6 -> 8; matrix products, arithmetic and copies ran while one was open for 1% -> 1% of each run, Pallas kernels for 7% -> 13%
where the time goes in v2:
time: 213 us; the launch traced here: 212 us
  Pallas kernels  67.2 us (32%)
  starting transfers between devices  45 us (21%)
  waiting for transfers between devices  38.1 us (18%)
  blocking collectives  37.6 us (18%)
  between operations  14.2 us (7%)
  local copies, waits for them, and re-layouts  7.74 us (4%)
    all_to_all x1, blocking collectives, shards(): terms = lax.all_to_all(terms, ('z', 'c', 'dp'), 0, 0)  24.3 us
    pallas_call x1, Pallas kernels, attention(): call(attention_body, (H // 128,), [cut(2, TOK), cut(2, TOK), cut(2, 2, TO...  20.2 us
    reduce_scatter x1, waiting for transfers between devices, shards(): first = lax.psum_scatter(first, ('y', 'dp'), scatter_dimension=0)  18.1 us
    ppermute x6, starting transfers between devices, swap(): return lax.ppermute(value, axis, [(0, 1), (1, 0)])  13.9 us
    all_to_all x1, blocking collectives, shards(): xr = lax.all_to_all(plane_slots(pos, zr), ('x', 'y'), 0, 0)  13.3 us
    all_to_all x1, waiting for transfers between devices, shards(): dx_r = lax.all_to_all(dx, ('x', 'y'), 0, 0)  8.48 us
    all_to_all x1, starting transfers between devices, shards(): zr = lax.all_to_all(zs, 'z', 0, 0)  7.94 us
    pallas_call x1, Pallas kernels, leaf_grads(): call(leaf_body, (1,), [whole(ZN, 2, 16, H), whole(2, 64, H), whole(2, NR,...  7.71 us
  transfers between devices with their start and end apart: 18, of which 8 were waited for; matrix products, arithmetic and copies ran while one was open for 1% of the time, Pallas kernels for 13%

profile of v2, /device:TPU:1, one launch (start us, length us, event | category | flops | bytes accessed | tf_op | source)
XLA Modules:
  0.0 211.8 jit_solution(7199795128123929714)
XLA Ops:
  7.2 3.3 %collective-permute-start = (bf16[256,768]{1,0:T(8,128)(2,1)}, bf16[256,768]{1,0:T(8,128)(2,1)S(1)}, u32[]{:S(2)}, u32[]{:S(2)}) collective-permute-start(bf16[256,768]{1,0:T(8,128)(2,1)} %bitcast.17), channel_id=1, source_target_pairs={{0,2},{2,0},{1,3},{3,1},{4,6},{6,4},{5,7},{7,5},{8,10},{10,8},{9,1... | collective-permute-start | bytes 1179656 | tf_op jit(solution)/shard_map/ppermute | solution.py:425
  10.5 0.7 pad_add_fusion.pos
  11.2 0.9 collective-permute-done.x_oth
  12.1 0.7 copy-done.2
  12.8 6.0 %shard_map.75 = (bf16[2,2,256,384]{3,2,1,0:T(8,128)(2,1)}, bf16[2,2,128,384]{3,2,1,0:T(8,128)(2,1)}, bf16[2,128,384]{2,1,0:T(8,128)(2,1)}, bf16[8,2,16,384]{3,2,1,0:T(8,128)(2,1)}) custom-call(s32[3]{0:T(128)} %pad_add_fusion.pos, bf16[256,768]{1,0:T(8,128)(2,1)} %bitcast.18, bf16[256,768]{1,0:T(8,128)(2,1)} %copy-done.2, bf16[768,2304]{1,0:T(8,128)(2,1)} %rest_5_.1, ...), custom_call_target="tpu_custom_call" | custom-call | tf_op jit(solution)/shard_map/pallas_call | solution.py:103
  18.8 0.5 collective-permute-start.1
  19.2 7.9 %all-to-all-start = ((bf16[8,2,16,384]{3,2,1,0:T(8,128)(2,1)}), bf16[8,2,16,384]{3,2,1,0:T(8,128)(2,1)S(1)}, u32[]{:S(2)}, u32[]{:S(2)}) async-start(bf16[8,2,16,384]{3,2,1,0:T(8,128)(2,1)} %get-tuple-element.39), calls=%async_computation | async-start | bytes 393216 | tf_op jit(solution)/shard_map/all_to_all | solution.py:443
  27.2 0.7 copy-done.8
  27.9 3.0 %shard_map.77 = (bf16[2,2,64,384]{3,2,1,0:T(8,128)(2,1)}, bf16[2,2,32,384]{3,2,1,0:T(8,128)(2,1)}) custom-call(s32[3]{0:T(128)} %pad_add_fusion.pos, bf16[2,128,384]{2,1,0:T(8,128)(2,1)} %get-tuple-element.43.own, bf16[2,128,384]{2,1,0:T(8,128)(2,1)} %copy-done.8), custom_call_target="tpu_custom_call" | custom-call | tf_op jit(solution)/shard_map/pallas_call | solution.py:140
  31.0 2.7 %collective-permute-start.4 = (bf16[2,2,32,384]{3,2,1,0:T(8,128)(2,1)}, bf16[2,2,32,384]{3,2,1,0:T(8,128)(2,1)S(1)}, u32[]{:S(2)}, u32[]{:S(2)}) collective-permute-start(bf16[2,2,32,384]{3,2,1,0:T(8,128)(2,1)} %get-tuple-element.45), channel_id=1, source_target_pairs={{0,16},{8,24},{16,0},{24,8},{1,17},{9,25},{17,1},{25,9},{2,18},{10... | collective-permute-start | bytes 294920 | tf_op jit(solution)/shard_map/ppermute | solution.py:429
  33.7 0.9 collective-permute-start.5
  34.6 1.3 fusion.perm.p_own.p_oth
  35.9 0.7 copy-done.4
  36.6 5.3 %shard_map.76 = (bf16[2,256,384]{2,1,0:T(8,128)(2,1)}, bf16[2,256,384]{2,1,0:T(8,128)(2,1)}, bf16[2,768,256]{2,1,0:T(8,128)(2,1)}) custom-call(s32[3]{0:T(128)} %pad_add_fusion.pos, bf16[256,768]{1,0:T(8,128)(2,1)} %bitcast.19, bf16[256,768]{1,0:T(8,128)(2,1)} %copy-done.2, bf16[256,768]{1,0:T(8,128)(2,1)} %bitcast.22, bf16[256,768]{1,0:T(8,128)(2,1)} %copy-done.4, ...), custom_call_target="tpu_custom_call" | custom-call | tf_op jit(solution)/shard_map/pallas_call | solution.py:121
  41.9 0.7 copy-done.7
  42.6 2.6 %shard_map.78 = bf16[8,2,48,384]{3,2,1,0:T(8,128)(2,1)} custom-call(s32[3]{0:T(128)} %pad_add_fusion.pos, bf16[8,2,16,384]{3,2,1,0:T(8,128)(2,1)} %copy-done.7), custom_call_target="tpu_custom_call" | custom-call | tf_op jit(solution)/shard_map/pallas_call | solution.py:182
  45.2 13.3 %all_to_all.30.xr = bf16[8,2,48,384]{3,2,1,0:T(8,128)(2,1)} all-to-all(bf16[8,2,48,384]{3,2,1,0:T(8,128)(2,1)} %shard_map.78), channel_id=1, replica_groups=mesh['z'=8,'x'=4,'y'=2,'c'=2,'dp'=2] {'x','y'}, dimensions={0} | all-to-all | bytes 1179648 | tf_op jit(solution)/shard_map/all_to_all | solution.py:449
  58.6 20.2 %shard_map.79 = (bf16[2,256,384]{2,1,0:T(8,128)(2,1)}, bf16[2,256,384]{2,1,0:T(8,128)(2,1)}, f32[2,2,256,384]{3,2,1,0:T(8,128)}, f32[2,2,128,384]{3,2,1,0:T(8,12...) custom-call(s32[3]{0:T(128)} %pad_add_fusion.pos, ...), custom_call_target="tpu_custom_call" | custom-call | tf_op jit(solution)/shard_map/pallas_call | solution.py:262
  78.8 2.9 %collective-permute-start.6 = (bf16[2,256,384]{2,1,0:T(8,128)(2,1)}, bf16[2,256,384]{2,1,0:T(8,128)(2,1)S(1)}, u32[]{:S(2)}, u32[]{:S(2)}) collective-permute-start(bf16[2,256,384]{2,1,0:T(8,128)(2,1)} %get-tuple-element.54.att_own), channel_id=1, source_target_pairs={{0,2},{2,0},{1,3},{3,1},{4,6},{6,4},{5,7},{7,5},{8,10},{10,8},{9,1... | collective-permute-start | bytes 1179656 | tf_op jit(solution)/shard_map/ppermute | solution.py:425
  81.7 1.6 collective-permute-done.6.att_oth
  83.3 0.8 copy-done.10
  84.0 6.1 %shard_map.80 = (bf16[256,768]{1,0:T(8,128)(2,1)}, bf16[8,2,96,384]{3,2,1,0:T(8,128)(2,1)}) custom-call(s32[3]{0:T(128)} %pad_add_fusion.pos, bf16[2,256,384]{2,1,0:T(8,128)(2,1)} %get-tuple-element.54.att_own, bf16[2,256,384]{2,1,0:T(8,128)(2,1)} %copy-done.10, bf16[256,768]{1,0:T(8,128)(2,1)} %bitcast.23, bf16[256,768]{1,0:T(8,128)(2,1)} %copy-done.4, ...), custom_call_target="tpu_custom_call" | custom-call | tf_op jit(solution)/shard_map/pallas_call | solution.py:290
  90.2 3.7 %all-to-all-start.2 = ((bf16[8,2,48,384]{3,2,1,0:T(8,128)(2,1)}), bf16[8,2,48,384]{3,2,1,0:T(8,128)(2,1)S(1)}, u32[]{:S(2)}, u32[]{:S(2)}) async-start(bf16[8,2,48,384]{3,2,1,0:T(8,128)(2,1)} %get-tuple-element.58), calls=%async_computation.2 | async-start | bytes 1179648 | tf_op jit(solution)/shard_map/all_to_all | solution.py:452
  93.9 1.4 collective-permute-start.7
  95.3 8.5 %all-to-all-done.2.xr = bf16[8,2,48,384]{3,2,1,0:T(8,128)(2,1)S(1)} async-done(((bf16[8,2,48,384]{3,2,1,0:T(8,128)(2,1)}), bf16[8,2,48,384]{3,2,1,0:T(8,128)(2,1)S(1)}, u32[]{:S(2)}, u32[]{:S(2)}) %all-to-all-start.2) | async-done | bytes 589856 | tf_op jit(solution)/shard_map/all_to_all | solution.py:452
  103.8 0.8 copy-done.1
  104.6 2.6 %shard_map.81 = bf16[8,2,16,384]{3,2,1,0:T(8,128)(2,1)} custom-call(s32[3]{0:T(128)} %pad_add_fusion.pos, bf16[8,2,48,384]{3,2,1,0:T(8,128)(2,1)} %copy-done.1), custom_call_target="tpu_custom_call" | custom-call | tf_op jit(solution)/shard_map/pallas_call | solution.py:308
  107.2 6.6 %all-to-all-start.3 = ((bf16[8,2,16,384]{3,2,1,0:T(8,128)(2,1)}), bf16[8,2,16,384]{3,2,1,0:T(8,128)(2,1)S(1)}, u32[]{:S(2)}, u32[]{:S(2)}) async-start(bf16[8,2,16,384]{3,2,1,0:T(8,128)(2,1)} %shard_map.81), calls=%async_computation.3 | async-start | bytes 393216 | tf_op jit(solution)/shard_map/all_to_all | solution.py:459
  113.8 1.3 collective-permute-start.8
  115.1 1.2 collective-permute-start.9
  116.3 2.8 %collective-permute-done.8.far_a = bf16[2,2,32,384]{3,2,1,0:T(8,128)(2,1)S(1)} collective-permute-done((bf16[2,2,32,384]{3,2,1,0:T(8,128)(2,1)S(1)}, bf16[2,2,32,384]{3,2,1,0:T(8,128)(2,1)S(1)}, u32[]{:S(2)}, u32[]{:S(2)}) %collective-permute-start.8) | collective-permute-done | bytes 98336 | tf_op jit(solution)/shard_map/ppermute | solution.py:429
  119.2 1.0 collective-permute-done.9.far_b
  120.2 0.6 copy-done.15
  121.0 3.0 %shard_map.82 = (f32[2,64,384]{2,1,0:T(8,128)}, bf16[2,128,384]{2,1,0:T(8,128)(2,1)}) custom-call(s32[3]{0:T(128)} %pad_add_fusion.pos, bf16[2,2,64,384]{3,2,1,0:T(8,128)(2,1)} %copy-done.12, bf16[2,2,32,384]{3,2,1,0:T(8,128)(2,1)} %copy-done.14, bf16[2,2,32,384]{3,2,1,0:T(8,128)(2,1)} %copy-done.15, bf16[2,128,384]{2,1,0:T(8,128)(2,1)} %get-tuple-element.62.dy), custom_call_target="tpu_custom_call" | custom-call | tf_op jit(solution)/shard_map/pallas_call | solution.py:157
  123.9 1.2 collective-permute-start.10
  125.1 3.5 %collective-permute-done.10.yr = bf16[2,128,384]{2,1,0:T(8,128)(2,1)S(1)} collective-permute-done((bf16[2,128,384]{2,1,0:T(8,128)(2,1)}, bf16[2,128,384]{2,1,0:T(8,128)(2,1)S(1)}, u32[]{:S(2)}, u32[]{:S(2)}) %collective-permute-start.10) | collective-permute-done | bytes 196640 | tf_op jit(solution)/shard_map/ppermute | solution.py:425
  128.7 0.7 copy-done.11
  129.4 7.7 %shard_map.83 = (bf16[2,256,1152]{2,1,0:T(8,128)(2,1)}, bf16[8,2,96,384]{3,2,1,0:T(8,128)(2,1)}) custom-call(s32[3]{0:T(128)} %pad_add_fusion.pos, bf16[8,2,16,384]{3,2,1,0:T(8,128)(2,1)} %copy-done.6, f32[2,64,384]{2,1,0:T(8,128)} %get-tuple-element.63.keep, bf16[2,128,384]{2,1,0:T(8,128)(2,1)} %copy-done.11, f32[2,2,128,384]{3,2,1,0:T(8,128)} %get-tuple-element.65.dn1, ...), custom_call_target="tpu_custom_call" | custom-call | tf_op jit(solution)/shard_map/pallas_call | solution.py:344
  137.1 5.3 %all-to-all-start.4 = ((bf16[16,96,384]{2,1,0:T(8,128)(2,1)}), bf16[16,96,384]{2,1,0:T(8,128)(2,1)S(1)}, u32[]{:S(2)}, u32[]{:S(2)}) async-start(bf16[16,96,384]{2,1,0:T(8,128)(2,1)} %bitcast.26), calls=%async_computation.4 | async-start | bytes 2359296 | tf_op jit(solution)/shard_map/all_to_all | solution.py:461
  142.4 0.9 dynamic-slice_bitcast_fusion
  143.4 6.0 %collective-permute-start.11 = (bf16[256,1152]{1,0:T(8,128)(2,1)S(1)}, bf16[256,1152]{1,0:T(8,128)(2,1)S(1)}, u32[]{:S(2)}, u32[]{:S(2)}) collective-permute-start(bf16[256,1152]{1,0:T(8,128)(2,1)S(1)} %get-tuple-element.74), channel_id=1, source_target_pairs={{0,2},{2,0},{1,3},{3,1},{4,6},{6,4},{5,7},{7,5},{8,10},{10,8},{9,1... | collective-permute-start | bytes 1769480 | tf_op jit(solution)/shard_map/ppermute | solution.py:425
  149.4 1.6 collective-permute-done.11.pg_oth
  151.0 0.8 copy-done.9
  151.8 5.1 %shard_map.84 = bf16[256,768]{1,0:T(8,128)(2,1)} custom-call(s32[3]{0:T(128)} %pad_add_fusion.pos, bf16[256,1152]{1,0:T(8,128)(2,1)} %get-tuple-element.75.pg_own, bf16[256,1152]{1,0:T(8,128)(2,1)} %copy-done.9, bf16[768,2304]{1,0:T(8,128)(2,1)} %rest_5_.1, bf16[768,2304]{1,0:T(8,128)(2,1)} %rest_5_.1, bf16[768,2304]{1,0:T(8,128)(2,1)} %rest_5_.1, ...), custom_call_target="tpu_custom_call" | custom-call | tf_op jit(solution)/shard_map/pallas_call | solution.py:370
  157.0 18.1 %reduce-scatter.5.cloned.1.call-done = bf16[1,96,384]{2,1,0:T(8,128)(2,1)} async-done(((bf16[4,96,384]{2,1,0:T(8,128)(2,1)}), bf16[1,96,384]{2,1,0:T(8,128)(2,1)}) %reduce-scatter.5.cloned.1.call-update) | async-done | bytes 73744 | tf_op jit(solution)/shard_map/reduce_scatter | solution.py:458
  175.1 3.2 %shard_map.85 = bf16[8,2,2,16,384]{4,3,2,1,0:T(8,128)(2,1)} custom-call(s32[3]{0:T(128)} %pad_add_fusion.pos, bf16[96,384]{1,0:T(8,128)(2,1)} %bitcast.29, bf16[16,96,384]{2,1,0:T(8,128)(2,1)} %copy-done), custom_call_target="tpu_custom_call" | custom-call | tf_op jit(solution)/shard_map/pallas_call | solution.py:398
  178.3 24.3 %all_to_all.31 = bf16[32,16,384]{2,1,0:T(8,128)(2,1)} all-to-all(bf16[32,16,384]{2,1,0:T(8,128)(2,1)} %bitcast.21), channel_id=1, replica_groups=mesh['z'=8,'x'=4,'y'=2,'c'=2,'dp'=2] {'z','c','dp'}, dimensions={0} | all-to-all | bytes 786432 | tf_op jit(solution)/shard_map/all_to_all | solution.py:467
  202.6 2.3 %shard_map.86 = (f32[6,2304]{1,0:T(8,128)}, f32[6,768]{1,0:T(8,128)}) custom-call(s32[3]{0:T(128)} %pad_add_fusion.pos, bf16[8,2,2,16,384]{4,3,2,1,0:T(8,128)(2,1)} %bitcast.20), custom_call_target="tpu_custom_call" | custom-call | tf_op jit(solution)/shard_map/pallas_call | solution.py:416
  (50 shorter events, 0.4 us)
Async XLA Ops:
  7.2 4.9 %collective-permute-start = (bf16[256,768]{1,0:T(8,128)(2,1)}, bf16[256,768]{1,0:T(8,128)(2,1)S(1)}, u32[]{:S(2)}, u32[]{:S(2)}) collective-permute-start(bf16[256,768]{1,0:T(8,128)(2,1)} %bitcast.17), channel_id=1, source_target_pairs={{0,2},{2,0},{1,3},{3,1},{4,6},{6,4},{5,7},{7,5},{8,10},{10,8},{9,1... | collective-permute-start | bytes 1179656 | tf_op jit(solution)/shard_map/ppermute | solution.py:425
  11.2 7.6 %copy-start.3 = (bf16[1,256,768]{2,1,0:T(8,128)(2,1)S(1)}, bf16[1,256,768]{2,1,0:T(8,128)(2,1)}, u32[]{:S(2)}) copy-start(bf16[1,256,768]{2,1,0:T(8,128)(2,1)} %param.5) | copy-start | bytes 1179652
  12.1 0.7 copy-start.2
  18.8 8.5 %collective-permute-start.2 = (bf16[2,128,384]{2,1,0:T(8,128)(2,1)}, bf16[2,128,384]{2,1,0:T(8,128)(2,1)S(1)}, u32[]{:S(2)}, u32[]{:S(2)}) collective-permute-start(bf16[2,128,384]{2,1,0:T(8,128)(2,1)} %get-tuple-element.43.own), channel_id=1, source_target_pairs={{0,4},{4,0},{1,5},{5,1},{2,6},{6,2},{3,7},{7,3},{8,12},{12,8},{9,1... | collective-permute-start | bytes 589832 | tf_op jit(solution)/shard_map/ppermute | solution.py:425
  18.8 17.1 %collective-permute-start.1 = (bf16[256,768]{1,0:T(8,128)(2,1)S(1)}, bf16[256,768]{1,0:T(8,128)(2,1)S(1)}, u32[]{:S(2)}, u32[]{:S(2)}) collective-permute-start(bf16[256,768]{1,0:T(8,128)(2,1)S(1)} %bitcast.24), channel_id=1, source_target_pairs={{0,2},{2,0},{1,3},{3,1},{4,6},{6,4},{5,7},{7,5},{8,10},{10,8},{9,1... | collective-permute-start | bytes 1179656 | tf_op jit(solution)/shard_map/ppermute | solution.py:425
  19.2 22.7 %all-to-all-start = ((bf16[8,2,16,384]{3,2,1,0:T(8,128)(2,1)}), bf16[8,2,16,384]{3,2,1,0:T(8,128)(2,1)S(1)}, u32[]{:S(2)}, u32[]{:S(2)}) async-start(bf16[8,2,16,384]{3,2,1,0:T(8,128)(2,1)} %get-tuple-element.39), calls=%async_computation | async-start | bytes 393216 | tf_op jit(solution)/shard_map/all_to_all | solution.py:443
  27.2 122.2 %reduce-scatter.3.cloned.1.call-start = ((), (), s32[]{:S(2)}) async-start(), calls=%async_computation.8 | async-start | bytes 1474560 | tf_op jit(solution)/shard_map/reduce_scatter | solution.py:457
  27.2 0.7 copy-start.8
  31.0 10.9 %collective-permute-start.4 = (bf16[2,2,32,384]{3,2,1,0:T(8,128)(2,1)}, bf16[2,2,32,384]{3,2,1,0:T(8,128)(2,1)S(1)}, u32[]{:S(2)}, u32[]{:S(2)}) collective-permute-start(bf16[2,2,32,384]{3,2,1,0:T(8,128)(2,1)} %get-tuple-element.45), channel_id=1, source_target_pairs={{0,16},{8,24},{16,0},{24,8},{1,17},{9,25},{17,1},{25,9},{2,18},{10... | collective-permute-start | bytes 294920 | tf_op jit(solution)/shard_map/ppermute | solution.py:429
  33.7 8.2 %collective-permute-start.5 = (bf16[2,2,32,384]{3,2,1,0:T(8,128)(2,1)}, bf16[2,2,32,384]{3,2,1,0:T(8,128)(2,1)S(1)}, u32[]{:S(2)}, u32[]{:S(2)}) collective-permute-start(bf16[2,2,32,384]{3,2,1,0:T(8,128)(2,1)} %get-tuple-element.45), channel_id=1, source_target_pairs={{0,24},{8,16},{16,8},{24,0},{1,25},{9,17},{17,9},{25,1},{2,26},{10... | collective-permute-start | bytes 294920 | tf_op jit(solution)/shard_map/ppermute | solution.py:429
  34.6 7.4 %collective-permute-start.3 = (bf16[2,2,64,384]{3,2,1,0:T(8,128)(2,1)}, bf16[2,2,64,384]{3,2,1,0:T(8,128)(2,1)S(1)}, u32[]{:S(2)}, u32[]{:S(2)}) collective-permute-start(bf16[2,2,64,384]{3,2,1,0:T(8,128)(2,1)} %get-tuple-element.44), channel_id=1, source_target_pairs={{0,8},{8,0},{16,24},{24,16},{1,9},{9,1},{17,25},{25,17},{2,10},{10... | collective-permute-start | bytes 589832 | tf_op jit(solution)/shard_map/ppermute | solution.py:429
  35.9 0.8 copy-start.4
  41.9 16.7 %copy-start.16 = (bf16[2,2,32,384]{3,2,1,0:T(8,128)(2,1)}, bf16[2,2,32,384]{3,2,1,0:T(8,128)(2,1)S(1)}, u32[]{:S(2)}) copy-start(bf16[2,2,32,384]{3,2,1,0:T(8,128)(2,1)S(1)} %collective-permute-done.4.far_a) | copy-start | bytes 294916
  41.9 16.7 %copy-start.17 = (bf16[2,2,32,384]{3,2,1,0:T(8,128)(2,1)}, bf16[2,2,32,384]{3,2,1,0:T(8,128)(2,1)S(1)}, u32[]{:S(2)}) copy-start(bf16[2,2,32,384]{3,2,1,0:T(8,128)(2,1)S(1)} %collective-permute-done.5.far_b) | copy-start | bytes 294916
  41.9 0.7 copy-start.7
  41.9 16.6 %copy-start.13 = (bf16[2,2,64,384]{3,2,1,0:T(8,128)(2,1)}, bf16[2,2,64,384]{3,2,1,0:T(8,128)(2,1)S(1)}, u32[]{:S(2)}) copy-start(bf16[2,2,64,384]{3,2,1,0:T(8,128)(2,1)S(1)} %collective-permute-done.3.near) | copy-start | bytes 589828
  78.8 4.5 %collective-permute-start.6 = (bf16[2,256,384]{2,1,0:T(8,128)(2,1)}, bf16[2,256,384]{2,1,0:T(8,128)(2,1)S(1)}, u32[]{:S(2)}, u32[]{:S(2)}) collective-permute-start(bf16[2,256,384]{2,1,0:T(8,128)(2,1)} %get-tuple-element.54.att_own), channel_id=1, source_target_pairs={{0,2},{2,0},{1,3},{3,1},{4,6},{6,4},{5,7},{7,5},{8,10},{10,8},{9,1... | collective-permute-start | bytes 1179656 | tf_op jit(solution)/shard_map/ppermute | solution.py:425
  83.3 0.8 copy-start.10
  90.2 3.7 %copy-start.18 = (bf16[2,2,64,384]{3,2,1,0:T(8,128)(2,1)S(1)}, bf16[2,2,64,384]{3,2,1,0:T(8,128)(2,1)}, u32[]{:S(2)}) copy-start(bf16[2,2,64,384]{3,2,1,0:T(8,128)(2,1)} %get-tuple-element.59) | copy-start | bytes 589828
  90.2 23.6 %copy-start.20 = (bf16[2,2,32,384]{3,2,1,0:T(8,128)(2,1)S(1)}, bf16[2,2,32,384]{3,2,1,0:T(8,128)(2,1)}, u32[]{:S(2)}) copy-start(bf16[2,2,32,384]{3,2,1,0:T(8,128)(2,1)} %get-tuple-element.60) | copy-start | bytes 294916
  90.2 24.9 %copy-start.19 = (bf16[2,2,32,384]{3,2,1,0:T(8,128)(2,1)S(1)}, bf16[2,2,32,384]{3,2,1,0:T(8,128)(2,1)}, u32[]{:S(2)}) copy-start(bf16[2,2,32,384]{3,2,1,0:T(8,128)(2,1)} %get-tuple-element.61) | copy-start | bytes 294916
  90.2 13.5 %all-to-all-start.2 = ((bf16[8,2,48,384]{3,2,1,0:T(8,128)(2,1)}), bf16[8,2,48,384]{3,2,1,0:T(8,128)(2,1)S(1)}, u32[]{:S(2)}, u32[]{:S(2)}) async-start(bf16[8,2,48,384]{3,2,1,0:T(8,128)(2,1)} %get-tuple-element.58), calls=%async_computation.2 | async-start | bytes 1179648 | tf_op jit(solution)/shard_map/all_to_all | solution.py:452
  93.9 26.3 %collective-permute-start.7 = (bf16[2,2,64,384]{3,2,1,0:T(8,128)(2,1)S(1)}, bf16[2,2,64,384]{3,2,1,0:T(8,128)(2,1)S(1)}, u32[]{:S(2)}, u32[]{:S(2)}) collective-permute-start(bf16[2,2,64,384]{3,2,1,0:T(8,128)(2,1)S(1)} %copy-done.18), channel_id=1, source_target_pairs={{0,8},{8,0},{16,24},{24,16},{1,9},{9,1},{17,25},{25,17},{2,10},{10... | collective-permute-start | bytes 589832 | tf_op jit(solution)/shard_map/ppermute | solution.py:429
  103.8 0.8 copy-start.1
  107.2 21.4 %all-to-all-start.3 = ((bf16[8,2,16,384]{3,2,1,0:T(8,128)(2,1)}), bf16[8,2,16,384]{3,2,1,0:T(8,128)(2,1)S(1)}, u32[]{:S(2)}, u32[]{:S(2)}) async-start(bf16[8,2,16,384]{3,2,1,0:T(8,128)(2,1)} %shard_map.81), calls=%async_computation.3 | async-start | bytes 393216 | tf_op jit(solution)/shard_map/all_to_all | solution.py:459
  113.8 5.3 %collective-permute-start.8 = (bf16[2,2,32,384]{3,2,1,0:T(8,128)(2,1)S(1)}, bf16[2,2,32,384]{3,2,1,0:T(8,128)(2,1)S(1)}, u32[]{:S(2)}, u32[]{:S(2)}) collective-permute-start(bf16[2,2,32,384]{3,2,1,0:T(8,128)(2,1)S(1)} %copy-done.20), channel_id=1, source_target_pairs={{0,16},{8,24},{16,0},{24,8},{1,17},{9,25},{17,1},{25,9},{2,18},{10... | collective-permute-start | bytes 294920 | tf_op jit(solution)/shard_map/ppermute | solution.py:429
  115.1 5.1 %collective-permute-start.9 = (bf16[2,2,32,384]{3,2,1,0:T(8,128)(2,1)S(1)}, bf16[2,2,32,384]{3,2,1,0:T(8,128)(2,1)S(1)}, u32[]{:S(2)}, u32[]{:S(2)}) collective-permute-start(bf16[2,2,32,384]{3,2,1,0:T(8,128)(2,1)S(1)} %copy-done.19), channel_id=1, source_target_pairs={{0,24},{8,16},{16,8},{24,0},{1,25},{9,17},{17,9},{25,1},{2,26},{10... | collective-permute-start | bytes 294920 | tf_op jit(solution)/shard_map/ppermute | solution.py:429
  119.2 1.0 copy-start.14
  120.2 0.6 copy-start.15
  120.2 0.8 copy-start.12
  123.9 4.7 %collective-permute-start.10 = (bf16[2,128,384]{2,1,0:T(8,128)(2,1)}, bf16[2,128,384]{2,1,0:T(8,128)(2,1)S(1)}, u32[]{:S(2)}, u32[]{:S(2)}) collective-permute-start(bf16[2,128,384]{2,1,0:T(8,128)(2,1)} %get-tuple-element.64), channel_id=1, source_target_pairs={{0,4},{4,0},{1,5},{5,1},{2,6},{6,2},{3,7},{7,3},{8,12},{12,8},{9,1... | collective-permute-start | bytes 589832 | tf_op jit(solution)/shard_map/ppermute | solution.py:425
  128.6 0.7 copy-start.11
  128.7 0.7 copy-start.6
  137.1 5.3 %copy-start.5 = (bf16[2,256,1152]{2,1,0:T(8,128)(2,1)S(1)}, bf16[2,256,1152]{2,1,0:T(8,128)(2,1)}, u32[]{:S(2)}) copy-start(bf16[2,256,1152]{2,1,0:T(8,128)(2,1)} %get-tuple-element.68) | copy-start | bytes 3538948
  137.1 19.9 %all-to-all-start.4 = ((bf16[16,96,384]{2,1,0:T(8,128)(2,1)}), bf16[16,96,384]{2,1,0:T(8,128)(2,1)S(1)}, u32[]{:S(2)}, u32[]{:S(2)}) async-start(bf16[16,96,384]{2,1,0:T(8,128)(2,1)} %bitcast.26), calls=%async_computation.4 | async-start | bytes 2359296 | tf_op jit(solution)/shard_map/all_to_all | solution.py:461
  142.4 32.8 %reduce-scatter.5.cloned.1.call-start = ((), (), s32[]{:S(2)}) async-start(), calls=%async_computation.9 | async-start | bytes 368640 | tf_op jit(solution)/shard_map/reduce_scatter | solution.py:458
  143.4 7.6 %collective-permute-start.11 = (bf16[256,1152]{1,0:T(8,128)(2,1)S(1)}, bf16[256,1152]{1,0:T(8,128)(2,1)S(1)}, u32[]{:S(2)}, u32[]{:S(2)}) collective-permute-start(bf16[256,1152]{1,0:T(8,128)(2,1)S(1)} %get-tuple-element.74), channel_id=1, source_target_pairs={{0,2},{2,0},{1,3},{3,1},{4,6},{6,4},{5,7},{7,5},{8,10},{10,8},{9,1... | collective-permute-start | bytes 1769480 | tf_op jit(solution)/shard_map/ppermute | solution.py:425
  151.0 0.8 copy-start.9
  157.0 18.1 %copy-start = (bf16[16,96,384]{2,1,0:T(8,128)(2,1)}, bf16[16,96,384]{2,1,0:T(8,128)(2,1)S(1)}, u32[]{:S(2)}) copy-start(bf16[16,96,384]{2,1,0:T(8,128)(2,1)S(1)} %all-to-all-done.4.second) | copy-start | bytes 3538948
Sparse Core Ops, SparseCore 0:
  90.3 28.0 reduce-scatter.2
  149.5 25.5 reduce-scatter.4

commit v3 on v2

--- a/solution.py
+++ b/solution.py
@@ -1,5 +1,6 @@
 import jax
 import jax.numpy as jnp
+import numpy as np
 from jax import lax
 from jax.experimental import pallas as pl
 from jax.experimental.pallas import tpu as pltpu
@@ -81,20 +82,30 @@
     for e, x in ((c, x_own), (1 - c, x_oth)):
         kv_out[e, 0] = dot(x[...], wk[...]).astype(BF16)
         kv_out[e, 1] = dot(x[...], wv[...]).astype(BF16)
-    blank = jnp.zeros((16, H), BF16)
-    for p in range(2):
-        for e in range(2):
-            n1_out[e, p] = coarsen(kv_out[e, p])
-            n2_out[p, e * 64 : (e + 1) * 64] = coarsen(n1_out[e, p])
-        n5 = coarsen(coarsen(coarsen(n2_out[p])))
-        n6 = coarsen(n5, 16, 8)
-        n7 = coarsen(n6, 16, 4)
-        zs_out[z, p] = blank
-        zs_out[z ^ 1, p] = n5
-        for far in (2, 3):
-            zs_out[z ^ far, p] = n6
-        for far in (4, 5, 6, 7):
-            zs_out[z ^ far, p] = n7
+
+    def store(ref, *index):
+        def put(node):
+            for p in range(2):
+                ref[index + (p,)] = node[:, H * p : H * p + H]
+
+        return put
+
+    halves = []
+    for e in range(2):
+        n1 = coarsen(jnp.concatenate([kv_out[e, 0], kv_out[e, 1]], axis=1))
+        store(n1_out, e)(n1)
+        halves.append(coarsen(n1))
+    n2 = jnp.concatenate(halves, axis=0)
+    store(n2_out)(n2)
+    n5 = coarsen(coarsen(coarsen(n2)))
+    n6 = coarsen(n5, 16, 8)
+    n7 = coarsen(n6, 16, 4)
+    store(zs_out, z)(jnp.zeros_like(n5))
+    store(zs_out, z ^ 1)(n5)
+    for far in (2, 3):
+        store(zs_out, z ^ far)(n6)
+    for far in (4, 5, 6, 7):
+        store(zs_out, z ^ far)(n7)
 
 
 def tree(pos, x_own, x_oth, w_qkv):
@@ -172,10 +183,11 @@
 
 def plane_body(pos, zr, out):
     hot = (iota((ZR, 128), 1) == z_source(pos[1], 0, (ZR, 128))).astype(BF16)
-    for p in range(2):
-        rows = dot(hot, zr[:, p].reshape(128, H)).astype(BF16)
-        for slot in range(8):
-            out[slot, p] = rows
+    both = jnp.concatenate([zr[:, p].reshape(128, H) for p in range(2)], axis=1)
+    rows = dot(hot, both).astype(BF16)
+    for slot in range(8):
+        for p in range(2):
+            out[slot, p] = rows[:, H * p : H * p + H]
 
 
 def plane_slots(pos, zr):
@@ -271,28 +283,53 @@
     )(pos, q, ag, kv, n1, yr, near, far_a, far_b, xr)
 
 
-def output_body(pos, att_own, att_oth, ct_own, ct_oth, dq, xt, w_own, w_oth, p_own, p_oth, out, grad_out):
-    c = pos[0]
+def output_body(pos, att_own, att_oth, ct_own, ct_oth, dq, xt, w_own, w_oth, p_own, p_oth, out, *rest):
+    c, x = pos[0], pos[2] >> 1
+    slots = rest[-1]
     total = dot(xt[0], dq[0]) + dot(xt[1], dq[1])
-    grad_out[:, 0] = total.astype(BF16).reshape(8, 96, H)
+    slots[:, :, 0] = total.astype(BF16).reshape(XN, YN, 96, H)
     total = None
     for e, ct in ((c, ct_own), (1 - c, ct_oth)):
         att_t = (dot_nt(p_own[...], att_own[e]) + dot_nt(p_oth[...], att_oth[e])).astype(BF16)
         term = dot(att_t, ct[...])
         total = term if total is None else total + term
-    grad_out[:, 1] = total.astype(BF16).reshape(8, 96, H)
+    slots[:, :, 1] = total.astype(BF16).reshape(XN, YN, 96, H)
+    for far in range(XN):
+        rest[far][...] = slots[x ^ far]
     out[...] = (dot(att_own[c], w_own[...]) + dot(att_oth[c], w_oth[...])).astype(BF16)
 
 
 def output_side(pos, att_own, att_oth, ct_own, ct_oth, dq, xt, w_out, perm):
     row = lambda flip: pl.BlockSpec((H, D), lambda i, s: (s[0] ^ flip, 0))
     col = lambda flip, rows: pl.BlockSpec((rows, H), lambda i, s: (0, s[0] ^ flip))
+    slot = (YN, 2, 96, H)
     return call(
         output_body,
         (1,),
         [whole(2, TOK, H)] * 2 + [col(0, TOK)] * 2 + [whole(2, TOK, H), whole(2, D, TOK)] + [row(0), row(1), col(0, D), col(1, D)],
-        [(whole(TOK, D), ((TOK, D), BF16)), (whole(8, 2, 96, H), ((8, 2, 96, H), BF16))],
+        [(whole(TOK, D), ((TOK, D), BF16))] + [(whole(*slot), (slot, BF16))] * XN,
+        [pltpu.VMEM((XN,) + slot, BF16)],
     )(pos, att_own, att_oth, ct_own, ct_oth, dq, xt, w_out, w_out, perm, perm)
+
+
+def x_sum_body(pos, t0, t1, t2, t3, *rest):
+    y, dp = pos[2] & 1, pos[3]
+    slots = rest[-1]
+    total = (t0[...].astype(F32) + t1[...].astype(F32)) + (t2[...].astype(F32) + t3[...].astype(F32))
+    slots[...] = total.astype(BF16)
+    for far in range(4):
+        rest[far][...] = slots[y ^ (far >> 1), dp ^ (far & 1)]
+
+
+def x_sum(pos, *terms):
+    shape = (YN, 2, 96, H)
+    return call(
+        x_sum_body,
+        (1,),
+        [whole(*shape)] * 4,
+        [(whole(96, H), ((96, H), BF16))] * 4,
+        [pltpu.VMEM(shape, BF16)],
+    )(pos, *terms)
 
 
 def back_body(pos, xr, out):
@@ -313,46 +350,64 @@
     )(pos, xr)[0]
 
 
-def leaf_body(pos, zr, keep, yr, dn1, dkv, dq, xt, pg_out, grad_out):
-    z = pos[1]
-
-    def gather(ref, index, fars, p, rows):
+def base_body(pos, dkv, dn1, yr, keep, out):
+    def hot(rows, width, shift, start):
+        r, k = iota((rows, width), 0), iota((rows, width), 1)
+        return (((r >> shift) + start) == (k & (NR - 1 if width > NR else width - 1))).astype(BF16)
+
+    def split(grad):
+        high = grad.astype(BF16)
+        return high, (grad - high.astype(F32)).astype(BF16)
+
+    for p in range(2):
+        keep_high, keep_low = split(keep[p])
+        for e in range(2):
+            total = dkv[e, p] + dot(hot(TOK, 2 * NR, 1, 0), jnp.concatenate(split(dn1[e, p]), axis=0)) * HALF_ROOT
+            total = total + dot(hot(TOK, NR, 2, 64 * e), yr[p]) * 0.5
+            up = hot(TOK, 64, 3, 32 * e)
+            out[e, p] = total + (dot(up, keep_high) + dot(up, keep_low)) * (0.5 * HALF_ROOT)
+
+
+def base_grads(pos, dkv, dn1, yr, keep):
+    shape = (2, 2, TOK, H)
+    return call(
+        base_body,
+        (1,),
+        [whole(*shape), whole(2, 2, NR, H), whole(2, NR, H), whole(2, 64, H)],
+        [(whole(*shape), (shape, F32))],
+    )(pos, dkv, dn1, yr, keep)[0]
+
+
+def leaf_body(pos, zr, base, dq, xt, pg_out, grad_out):
+    t, k = iota((2 * TOK, 128), 0), iota((2 * TOK, 128), 1)
+    far, row = (k >> 4) ^ pos[1], k & 15
+    odd = jnp.where((far == 1) & (row == t >> 5), 0.25, jnp.where((far >= 4) & (row == t >> 7), 0.125, 0.0)).astype(BF16)
+    even = jnp.where(((far >> 1) == 1) & (row == t >> 6), 0.125, 0.0).astype(BF16)
+    both = jnp.concatenate([zr[:, p].reshape(128, H) for p in range(2)], axis=1)
+    up = dot(odd, both) * HALF_ROOT + dot(even, both)
+    for p in range(2):
+        cols = slice(H * (1 + p), H * (2 + p))
         total = None
-        for far in fars:
-            term = ref[index ^ far, p, :rows].astype(F32)
+        for e in range(2):
+            leaf = (base[e, p] + up[TOK * e : TOK * e + TOK, H * p : H * p + H]).astype(BF16)
+            pg_out[e, :, cols] = leaf
+            term = dot(xt[e], leaf)
             total = term if total is None else total + term
-        return total
-
-    for p in range(2):
-        g7 = gather(zr, z, (4, 5, 6, 7), p, 16)
-        g6 = gather(zr, z, (2, 3), p, 16) + spread(g7, 16, 8)
-        g5 = gather(zr, z, (1,), p, 16) + spread(g6, 16)
-        g3 = keep[p] + spread(spread(g5, 32), 64)
-        g2 = yr[p].astype(F32) + spread(g3, 128)
-        for e in range(2):
-            g1 = dn1[e, p] + spread(g2[64 * e : 64 * e + 64], 128)
-            leaf = dkv[e, p] + spread(g1, 256)
-            pg_out[e, :, H * (1 + p) : H * (2 + p)] = leaf.astype(BF16)
-        cols = slice(H * (1 + p), H * (2 + p))
-        total = dot(xt[0], pg_out[0, :, cols]) + dot(xt[1], pg_out[1, :, cols])
         grad_out[:, p] = total.astype(BF16).reshape(8, 96, H)
     for e in range(2):
         pg_out[e, :, :H] = dq[e]
 
 
-def leaf_grads(pos, zr, keep, yr, dn1, dkv, dq, xt):
+def leaf_grads(pos, zr, base, dq, xt):
     return call(
         leaf_body,
         (1,),
-        [
-            whole(ZN, 2, 16, H), whole(2, 64, H), whole(2, NR, H), whole(2, 2, NR, H), whole(2, 2, TOK, H),
-            whole(2, TOK, H), whole(2, D, TOK),
-        ],
+        [whole(ZN, 2, 16, H), whole(2, 2, TOK, H), whole(2, TOK, H), whole(2, D, TOK)],
         [
             (whole(2, TOK, 3 * H), ((2, TOK, 3 * H), BF16)),
             (whole(8, 2, 96, H), ((8, 2, 96, H), BF16)),
         ],
-    )(pos, zr, keep, yr, dn1, dkv, dq, xt)
+    )(pos, zr, base, dq, xt)
 
 
 def input_body(pos, pg_own, pg_oth, *rest):
@@ -375,97 +430,123 @@
     )(pos, pg_own, pg_oth, *[w_qkv] * 6)[0]
 
 
-def total_of(ref):
-    total = ref[0].astype(F32)
-    for slot in range(1, ref.shape[0]):
-        total = total + ref[slot].astype(F32)
+def total_of(refs):
+    total = refs[0].astype(F32)
+    for ref in refs[1:]:
+        total = total + ref.astype(F32)
     return total
 
 
-def middle_body(pos, first, second, out):
+def middle_body(pos, f0, f1, f2, f3, second, out):
+    first = total_of([f0[...], f1[...], f2[...], f3[...]]).astype(BF16)
     i, k = iota((256, 96), 0), iota((256, 96), 1)
     row, half = i & 7, (i >> 3) & 1
     hit = (k == 6 * (i >> 4) + row) & (row < 6)
-    rows = dot((hit & (half == 0)).astype(BF16), first[...])
-    rows = rows + dot((hit & (half == 1)).astype(BF16), total_of(second).astype(BF16))
-    rows = rows.astype(BF16).reshape(ZN, 2, 16, H)
-    for copy in range(2):
-        out[:, :, copy] = rows
-
-
-def middle_sum(pos, first, second):
-    shape = (ZN, 2, 2, 16, H)
-    return call(middle_body, (1,), [whole(96, H), whole(16, 96, H)], [(whole(*shape), (shape, BF16))])(pos, first, second)[0]
-
-
-def last_body(pos, terms, qkv_out, out_out):
+    rows = dot((hit & (half == 0)).astype(BF16), first)
+    rows = rows + dot((hit & (half == 1)).astype(BF16), total_of([second[slot] for slot in range(16)]).astype(BF16))
+    out[...] = rows.astype(BF16).reshape(ZN, 2, 16, H)
+
+
+def middle_sum(pos, firsts, second):
+    shape = (ZN, 2, 16, H)
+    return call(
+        middle_body, (1,), [whole(96, H)] * 4 + [whole(16, 96, H)], [(whole(*shape), (shape, BF16))]
+    )(pos, *firsts, second)[0]
+
+
+def z_sum_body(pos, terms, own_out, oth_out):
+    for core, out in ((pos[0], own_out), (1 - pos[0], oth_out)):
+        out[...] = total_of([terms[z, core] for z in range(ZN)]).astype(BF16)
+
+
+def z_sum(pos, terms):
+    return call(
+        z_sum_body,
+        (1,),
+        [whole(ZN, 2, 16, H)],
+        [(whole(16, H), ((16, H), BF16))] * 2,
+    )(pos, terms)
+
+
+def last_body(pos, own, from_dp, from_core, from_both, qkv_out, out_out, parts):
+    core, dp = pos[0], pos[3]
+    parts[core, dp] = own[...]
+    parts[core, 1 - dp] = from_dp[...]
+    parts[1 - core, dp] = from_core[...]
+    parts[1 - core, 1 - dp] = from_both[...]
     for core in range(2):
-        for dp in range(2):
-            total = terms[0, core, dp].astype(F32)
-            for z in range(1, ZN):
-                total = total + terms[z, core, dp].astype(F32)
-            if dp == 0:
-                qkv_out[:, H * core : H * core + H] = total[:6]
-            else:
-                out_out[:, H * core : H * core + H] = total[:6]
-            start = D * (1 + dp) + H * core
-            qkv_out[:, start : start + H] = total[8:14]
-
-
-def last_sum(pos, terms):
+        low, high = parts[core, 0].astype(F32), parts[core, 1].astype(F32)
+        cols = lambda part: slice(D * part + H * core, D * part + H * core + H)
+        qkv_out[:, cols(0)] = low[:6]
+        qkv_out[:, cols(1)] = low[8:14]
+        qkv_out[:, cols(2)] = high[8:14]
+        out_out[:, cols(0)] = high[:6]
+
+
+def last_rows(pos, *parts):
     return call(
         last_body,
         (1,),
-        [whole(ZN, 2, 2, 16, H)],
+        [whole(16, H)] * 4,
         [(whole(6, 3 * D), ((6, 3 * D), F32)), (whole(6, D), ((6, D), F32))],
-    )(pos, terms)
+        [pltpu.VMEM((2, 2, 16, H), BF16)],
+    )(pos, *parts)
 
 
 def swap(value, axis):
     return lax.ppermute(value, axis, [(0, 1), (1, 0)])
 
 
-def along_x(value, far):
-    return lax.ppermute(value, "x", [(i, i ^ far) for i in range(XN)])
+def along(value, axes, far, count=4):
+    return lax.ppermute(value, axes, [(i, i ^ far) for i in range(count)])
+
+
+def row_order():
+    f = np.arange(D)
+    source = 96 * (f // 12 % 8) + 12 * (f // 96) + f % 12
+    return jnp.asarray(source[:, None] == f[None, :], BF16)
 
 
 def shards(x_tokens, cotangent, w_qkv, w_out):
     x_own, ct_own = x_tokens[0], cotangent[0]
-    c, z = lax.axis_index("c"), lax.axis_index("z")
+    c, z, dp = lax.axis_index("c"), lax.axis_index("z"), lax.axis_index("dp")
     j = 2 * lax.axis_index("x") + lax.axis_index("y")
-    pos = jnp.stack([c, z, j]).astype(jnp.int32)
+    pos = jnp.stack([c, z, j, dp]).astype(jnp.int32)
     x_oth, ct_oth = swap(x_own, "c"), swap(ct_own, "c")
-    f = jnp.arange(D, dtype=jnp.int32)
-    source = 96 * (f // 12 % 8) + 12 * (f // 96) + f % 12
-    perm = (source[:, None] == f[None, :]).astype(BF16)
+    perm = row_order()
 
     kv, n1, n2, zs = tree(pos, x_own, x_oth, w_qkv)
     zr = lax.all_to_all(zs, "z", 0, 0)
     yr = swap(n2, "y")
     near, far = pair_nodes(pos, n2, yr)
-    near, far_a, far_b = along_x(near, 1), along_x(far, 2), along_x(far, 3)
+    near, far_a, far_b = along(near, "x", 1), along(far, "x", 2), along(far, "x", 3)
+    zr, near, far_a, far_b, ct_oth = lax.optimization_barrier((zr, near, far_a, far_b, ct_oth))
+    xr = lax.all_to_all(plane_slots(pos, zr), ("x", "y"), 0, 0)
     q, ag, xt = project(pos, x_own, x_oth, ct_own, ct_oth, w_qkv, w_out, perm)
-    zr, q, ag, xt, near, far_a, far_b = lax.optimization_barrier((zr, q, ag, xt, near, far_a, far_b))
-    xr = lax.all_to_all(plane_slots(pos, zr), ("x", "y"), 0, 0)
     att, dq, dkv, dn1, dy, dnear, dfar_a, dfar_b, dx = attention(pos, q, ag, kv, n1, yr, near, far_a, far_b, xr)
 
     dx_r = lax.all_to_all(dx, ("x", "y"), 0, 0)
     att_oth = swap(att, "c")
-    keep, dy = pair_back(pos, along_x(dnear, 1), along_x(dfar_a, 2), along_x(dfar_b, 3), dy)
-    dy_r = swap(dy, "y")
-    layer_out, terms = output_side(pos, att, att_oth, ct_own, ct_oth, dq, xt, w_out, perm)
-    first = lax.psum_scatter(terms.reshape(XN, 4, 96, H), "x", scatter_dimension=0)
-    first = lax.psum_scatter(first, ("y", "dp"), scatter_dimension=0)
+    back = (along(dnear, "x", 1), along(dfar_a, "x", 2), along(dfar_b, "x", 3))
+    layer_out, *terms = output_side(pos, att, att_oth, ct_own, ct_oth, dq, xt, w_out, perm)
+    dx_r, back, terms = lax.optimization_barrier((dx_r, back, terms))
     dz_r = lax.all_to_all(back_slots(pos, dx_r), "z", 0, 0)
-    pg, terms = leaf_grads(pos, dz_r, keep, dy_r, dn1, dkv, dq, xt)
+    firsts = terms[:1] + [along(terms[far], "x", far) for far in (1, 2, 3)]
+    keep, dy = pair_back(pos, *back, dy)
+    base = base_grads(pos, dkv, dn1, swap(dy, "y"), keep)
+    dz_r, base, firsts = lax.optimization_barrier((dz_r, base, firsts))
+    pg, terms = leaf_grads(pos, dz_r, base, dq, xt)
     second = lax.all_to_all(terms.reshape(16, 96, H), ("x", "y", "dp"), 0, 0)
+    firsts = list(x_sum(pos, *firsts))
+    firsts = firsts[:1] + [along(firsts[far], ("y", "dp"), far) for far in (1, 2, 3)]
     pg_own = lax.dynamic_index_in_dim(pg, c, 0, keepdims=False)
     pg_oth = swap(lax.dynamic_index_in_dim(pg, 1 - c, 0, keepdims=False), "c")
     input_grad = input_side(pos, pg_own, pg_oth, w_qkv)
-    second, input_grad = lax.optimization_barrier((second, input_grad))
-    terms = middle_sum(pos, first, second).reshape(32, 16, H)
-    terms = lax.all_to_all(terms, ("z", "c", "dp"), 0, 0)
-    qkv_grad, out_grad = last_sum(pos, terms.reshape(ZN, 2, 2, 16, H))
+    second, input_grad, firsts = lax.optimization_barrier((second, input_grad, firsts))
+    terms = lax.all_to_all(middle_sum(pos, firsts, second), "z", 0, 0)
+    own, oth = z_sum(pos, terms)
+    pair = ("c", "dp")
+    qkv_grad, out_grad = last_rows(pos, own, along(own, pair, 1), along(oth, pair, 2), along(oth, pair, 3))
     return (layer_out[None], input_grad[None], qkv_grad, out_grad)
 
 

time: 213 us -> 185 us (0.87)
  blocking collectives: 37.6 us -> 15.3 us
  starting transfers between devices: 45 us -> 61.4 us
  waiting for transfers between devices: 38.1 us -> 22.9 us
  between operations: 14.2 us -> 0.89 us
  Pallas kernels: 67.2 us -> 73.5 us
    all_to_all x2 -> x1, blocking collectives: 37.6 us -> 15.3 us  [shards(): terms = lax.all_to_all(middle_sum(pos, firsts, second), 'z', 0, 0)]
    reduce_scatter x2 -> x0, waiting for transfers between devices: 18.1 us -> none  [the longest x1 18.1 us: shards(): first = lax.psum_scatter(first, ('y', 'dp'), scatter_dimension=0)]
    ppermute x6 -> x15, starting transfers between devices: 7.47 us -> 22.1 us  [along(): return lax.ppermute(value, axes, [(i, i ^ far) for i in range(count)])]
    ppermute x6 -> x15, waiting for transfers between devices: 3.85 us -> 15.6 us  [along(): return lax.ppermute(value, axes, [(i, i ^ far) for i in range(count)])]
    all_to_all x1, waiting for transfers between devices: 8.48 us -> 0.01 us  [shards(): dx_r = lax.all_to_all(dx, ('x', 'y'), 0, 0)]
    pallas_call x3 -> x6, Pallas kernels: 13.2 us -> 20.3 us  [the longest x1 5.38 us: leaf_grads(): call(leaf_body, (1,), [whole(ZN, 2, 16, H), whole(2, 2, TOK, H), whole(2,...]
    all_to_all x0 -> x1, starting transfers between devices: none -> 3.72 us  [shards(): xr = lax.all_to_all(plane_slots(pos, zr), ('x', 'y'), 0, 0)]
    ppermute x6, waiting for transfers between devices: 7.56 us -> 5.24 us  [swap(): return lax.ppermute(value, axis, [(0, 1), (1, 0)])]
  transfers between devices with their start and end apart: 18 -> 26, of which waited for: 8 -> 11; matrix products, arithmetic and copies ran while one was open for 1% -> 1% of each run, Pallas kernels for 13% -> 19%
where the time goes in v3:
time: 185 us; the launch traced here: 184 us
  Pallas kernels  73.5 us (40%)
  starting transfers between devices  61.4 us (33%)
  waiting for transfers between devices  22.9 us (12%)
  blocking collectives  15.3 us (8%)
  local copies, waits for them, and re-layouts  9.41 us (5%)
    ppermute x15, starting transfers between devices, along(): return lax.ppermute(value, axes, [(i, i ^ far) for i in range(count)])  22.1 us
    pallas_call x1, Pallas kernels, attention(): call(attention_body, (H // 128,), [cut(2, TOK), cut(2, TOK), cut(2, 2, TO...  20.3 us
    ppermute x15, waiting for transfers between devices, along(): return lax.ppermute(value, axes, [(i, i ^ far) for i in range(count)])  15.6 us
    all_to_all x1, blocking collectives, shards(): terms = lax.all_to_all(middle_sum(pos, firsts, second), 'z', 0, 0)  15.3 us
    ppermute x6, starting transfers between devices, swap(): return lax.ppermute(value, axis, [(0, 1), (1, 0)])  12 us
    unnamed x68, local copies, waits for them, and re-layouts  8.51 us
    all_to_all x1, starting transfers between devices, shards(): zr = lax.all_to_all(zs, 'z', 0, 0)  7.74 us
    all_to_all x1, starting transfers between devices, shards(): dz_r = lax.all_to_all(back_slots(pos, dx_r), 'z', 0, 0)  6.75 us
  transfers between devices with their start and end apart: 26, of which 11 were waited for; matrix products, arithmetic and copies ran while one was open for 1% of the time, Pallas kernels for 19%

profile of v3, /device:TPU:1, one launch (start us, length us, event | category | flops | bytes accessed | tf_op | source)
XLA Modules:
  0.0 184.0 jit_solution(15231356969189706925)
XLA Ops:
  0.6 3.3 %collective-permute-start = (bf16[256,768]{1,0:T(8,128)(2,1)}, bf16[256,768]{1,0:T(8,128)(2,1)S(1)}, u32[]{:S(2)}, u32[]{:S(2)}) collective-permute-start(bf16[256,768]{1,0:T(8,128)(2,1)} %bitcast.13), channel_id=1, source_target_pairs={{0,2},{2,0},{1,3},{3,1},{4,6},{6,4},{5,7},{7,5},{8,10},{10,8},{9,1... | collective-permute-start | bytes 1179656 | tf_op jit(solution)/shard_map/ppermute | solution.py:497
  4.7 0.8 collective-permute-done.x_oth
  5.5 0.7 copy-done.3
  6.3 5.0 %shard_map.84 = (bf16[2,2,256,384]{3,2,1,0:T(8,128)(2,1)}, bf16[2,2,128,384]{3,2,1,0:T(8,128)(2,1)}, bf16[2,128,384]{2,1,0:T(8,128)(2,1)}, bf16[8,2,16,384]{3,2,1,0:T(8,128)(2,1)}) custom-call(s32[4]{0:T(128)} %pad_add_fusion.pos, bf16[256,768]{1,0:T(8,128)(2,1)} %bitcast.14, bf16[256,768]{1,0:T(8,128)(2,1)} %copy-done.3, bf16[768,2304]{1,0:T(8,128)(2,1)} %rest_5_.1, ...), custom_call_target="tpu_custom_call" | custom-call | tf_op jit(solution)/shard_map/pallas_call | solution.py:114
  11.3 7.7 %all-to-all-start = ((bf16[8,2,16,384]{3,2,1,0:T(8,128)(2,1)}), bf16[8,2,16,384]{3,2,1,0:T(8,128)(2,1)S(1)}, u32[]{:S(2)}, u32[]{:S(2)}) async-start(bf16[8,2,16,384]{3,2,1,0:T(8,128)(2,1)} %get-tuple-element.64), calls=%async_computation | async-start | bytes 393216 | tf_op jit(solution)/shard_map/all_to_all | solution.py:519
  19.7 3.1 %shard_map.85 = (bf16[2,2,64,384]{3,2,1,0:T(8,128)(2,1)}, bf16[2,2,32,384]{3,2,1,0:T(8,128)(2,1)}) custom-call(s32[4]{0:T(128)} %pad_add_fusion.pos, bf16[2,128,384]{2,1,0:T(8,128)(2,1)} %get-tuple-element.65.own, bf16[2,128,384]{2,1,0:T(8,128)(2,1)} %copy-done.8), custom_call_target="tpu_custom_call" | custom-call | tf_op jit(solution)/shard_map/pallas_call | solution.py:151
  22.7 1.2 collective-permute-start.2
  24.0 2.4 %collective-permute-start.3 = (bf16[2,2,32,384]{3,2,1,0:T(8,128)(2,1)}, bf16[2,2,32,384]{3,2,1,0:T(8,128)(2,1)S(1)}, u32[]{:S(2)}, u32[]{:S(2)}) collective-permute-start(bf16[2,2,32,384]{3,2,1,0:T(8,128)(2,1)} %get-tuple-element.67), channel_id=1, source_target_pairs={{0,16},{8,24},{16,0},{24,8},{1,17},{9,25},{17,1},{25,9},{2,18},{10... | collective-permute-start | bytes 294920 | tf_op jit(solution)/shard_map/ppermute | solution.py:501
  26.6 5.8 %collective-permute-done.3.far_a = bf16[2,2,32,384]{3,2,1,0:T(8,128)(2,1)S(1)} collective-permute-done((bf16[2,2,32,384]{3,2,1,0:T(8,128)(2,1)}, bf16[2,2,32,384]{3,2,1,0:T(8,128)(2,1)S(1)}, u32[]{:S(2)}, u32[]{:S(2)}) %collective-permute-start.3) | collective-permute-done | bytes 98336 | tf_op jit(solution)/shard_map/ppermute | solution.py:501
  32.5 0.7 copy-done.7
  33.2 2.6 %shard_map.87 = bf16[8,2,48,384]{3,2,1,0:T(8,128)(2,1)} custom-call(s32[4]{0:T(128)} %pad_add_fusion.pos, bf16[8,2,16,384]{3,2,1,0:T(8,128)(2,1)} %copy-done.7), custom_call_target="tpu_custom_call" | custom-call | tf_op jit(solution)/shard_map/pallas_call | solution.py:194
  35.8 3.7 %all-to-all-start.1 = ((bf16[8,2,48,384]{3,2,1,0:T(8,128)(2,1)}), bf16[8,2,48,384]{3,2,1,0:T(8,128)(2,1)S(1)}, u32[]{:S(2)}, u32[]{:S(2)}) async-start(bf16[8,2,48,384]{3,2,1,0:T(8,128)(2,1)} %shard_map.87), calls=%async_computation.1 | async-start | bytes 1179648 | tf_op jit(solution)/shard_map/all_to_all | solution.py:524
  39.5 5.3 %shard_map.86 = (bf16[2,256,384]{2,1,0:T(8,128)(2,1)}, bf16[2,256,384]{2,1,0:T(8,128)(2,1)}, bf16[2,768,256]{2,1,0:T(8,128)(2,1)}) custom-call(s32[4]{0:T(128)} %pad_add_fusion.pos, bf16[256,768]{1,0:T(8,128)(2,1)} %bitcast.15, bf16[256,768]{1,0:T(8,128)(2,1)} %copy-done.3, bf16[256,768]{1,0:T(8,128)(2,1)} %bitcast.17, bf16[256,768]{1,0:T(8,128)(2,1)} %copy-done.4, ...), custom_call_target="tpu_custom_call" | custom-call | tf_op jit(solution)/shard_map/pallas_call | solution.py:132
  44.8 2.0 %all-to-all-done.1.xr = bf16[8,2,48,384]{3,2,1,0:T(8,128)(2,1)S(1)} async-done(((bf16[8,2,48,384]{3,2,1,0:T(8,128)(2,1)}), bf16[8,2,48,384]{3,2,1,0:T(8,128)(2,1)S(1)}, u32[]{:S(2)}, u32[]{:S(2)}) %all-to-all-start.1) | async-done | bytes 589856 | tf_op jit(solution)/shard_map/all_to_all | solution.py:524
  46.8 0.8 copy-done.2
  47.7 20.3 %shard_map.88 = (bf16[2,256,384]{2,1,0:T(8,128)(2,1)}, bf16[2,256,384]{2,1,0:T(8,128)(2,1)}, f32[2,2,256,384]{3,2,1,0:T(8,128)}, f32[2,2,128,384]{3,2,1,0:T(8,12...) custom-call(s32[4]{0:T(128)} %pad_add_fusion.pos, ...), custom_call_target="tpu_custom_call" | custom-call | tf_op jit(solution)/shard_map/pallas_call | solution.py:274
  68.0 3.7 %all-to-all-start.2 = ((bf16[8,2,48,384]{3,2,1,0:T(8,128)(2,1)}), bf16[8,2,48,384]{3,2,1,0:T(8,128)(2,1)S(1)}, u32[]{:S(2)}, u32[]{:S(2)}) async-start(bf16[8,2,48,384]{3,2,1,0:T(8,128)(2,1)} %get-tuple-element.81), calls=%async_computation.2 | async-start | bytes 1179648 | tf_op jit(solution)/shard_map/all_to_all | solution.py:528
  71.7 3.8 %collective-permute-start.6 = (bf16[2,256,384]{2,1,0:T(8,128)(2,1)S(1)}, bf16[2,256,384]{2,1,0:T(8,128)(2,1)S(1)}, u32[]{:S(2)}, u32[]{:S(2)}) collective-permute-start(bf16[2,256,384]{2,1,0:T(8,128)(2,1)S(1)} %copy-done.10), channel_id=1, source_target_pairs={{0,2},{2,0},{1,3},{3,1},{4,6},{6,4},{5,7},{7,5},{8,10},{10,8},{9,1... | collective-permute-start | bytes 1179656 | tf_op jit(solution)/shard_map/ppermute | solution.py:497
  75.5 1.6 collective-permute-start.7
  77.1 2.4 %collective-permute-start.8 = (bf16[2,2,32,384]{3,2,1,0:T(8,128)(2,1)S(1)}, bf16[2,2,32,384]{3,2,1,0:T(8,128)(2,1)S(1)}, u32[]{:S(2)}, u32[]{:S(2)}) collective-permute-start(bf16[2,2,32,384]{3,2,1,0:T(8,128)(2,1)S(1)} %copy-done.33), channel_id=1, source_target_pairs={{0,16},{8,24},{16,0},{24,8},{1,17},{9,25},{17,1},{25,9},{2,18},{10... | collective-permute-start | bytes 294920 | tf_op jit(solution)/shard_map/ppermute | solution.py:501
  79.6 0.7 copy-done.11
  80.3 6.2 %shard_map.89 = (bf16[256,768]{1,0:T(8,128)(2,1)}, bf16[2,2,96,384]{3,2,1,0:T(8,128)(2,1)}, bf16[2,2,96,384]{3,2,1,0:T(8,128)(2,1)}, bf16[2,2,96,384]{3,2,1,0:T(8,128)(2,1)}, bf16[2,2,96,384]{3,2,1,0:T(8,128)(2,1)}) custom-call(s32[4]{0:T(128)} %pad_add_fusion.pos, bf16[2,256,384]{2,1,0:T(8,128)(2,1)} %get-tuple-element.77.att_own, ...), custom_call_target="tpu_custom_call" | custom-call | tf_op jit(solution)/shard_map/pallas_call | solution.py:306
  87.4 0.8 copy-done.1
  88.2 2.6 %shard_map.90 = bf16[8,2,16,384]{3,2,1,0:T(8,128)(2,1)} custom-call(s32[4]{0:T(128)} %pad_add_fusion.pos, bf16[8,2,48,384]{3,2,1,0:T(8,128)(2,1)} %copy-done.1), custom_call_target="tpu_custom_call" | custom-call | tf_op jit(solution)/shard_map/pallas_call | solution.py:345
  90.9 6.8 %all-to-all-start.3 = ((bf16[8,2,16,384]{3,2,1,0:T(8,128)(2,1)}), bf16[8,2,16,384]{3,2,1,0:T(8,128)(2,1)S(1)}, u32[]{:S(2)}, u32[]{:S(2)}) async-start(bf16[8,2,16,384]{3,2,1,0:T(8,128)(2,1)} %shard_map.90), calls=%async_computation.3 | async-start | bytes 393216 | tf_op jit(solution)/shard_map/all_to_all | solution.py:533
  98.0 3.0 %collective-permute-start.12 = (bf16[2,2,96,384]{3,2,1,0:T(8,128)(2,1)S(1)}, bf16[2,2,96,384]{3,2,1,0:T(8,128)(2,1)S(1)}, u32[]{:S(2)}, u32[]{:S(2)}) collective-permute-start(bf16[2,2,96,384]{3,2,1,0:T(8,128)(2,1)S(1)} %copy-done.29), channel_id=1, source_target_pairs={{0,16},{8,24},{16,0},{24,8},{1,17},{9,25},{17,1},{25,9},{2,18},{10... | collective-permute-start | bytes 884744 | tf_op jit(solution)/shard_map/ppermute | solution.py:501
  101.0 0.8 collective-permute-start.13
  101.8 3.0 %shard_map.91 = (f32[2,64,384]{2,1,0:T(8,128)}, bf16[2,128,384]{2,1,0:T(8,128)(2,1)}) custom-call(s32[4]{0:T(128)} %pad_add_fusion.pos, bf16[2,2,64,384]{3,2,1,0:T(8,128)(2,1)} %copy-done.16, bf16[2,2,32,384]{3,2,1,0:T(8,128)(2,1)} %copy-done.18, bf16[2,2,32,384]{3,2,1,0:T(8,128)(2,1)} %copy-done.19, bf16[2,128,384]{2,1,0:T(8,128)(2,1)} %get-tuple-element.95.dy), custom_call_target="tpu_custom_call" | custom-call | tf_op jit(solution)/shard_map/pallas_call | solution.py:168
  105.4 4.4 %collective-permute-done.10.yr = bf16[2,128,384]{2,1,0:T(8,128)(2,1)S(1)} collective-permute-done((bf16[2,128,384]{2,1,0:T(8,128)(2,1)}, bf16[2,128,384]{2,1,0:T(8,128)(2,1)S(1)}, u32[]{:S(2)}, u32[]{:S(2)}) %collective-permute-start.10) | collective-permute-done | bytes 196640 | tf_op jit(solution)/shard_map/ppermute | solution.py:497
  110.5 4.6 %shard_map.92.base = f32[2,2,256,384]{3,2,1,0:T(8,128)} custom-call(s32[4]{0:T(128)} %pad_add_fusion.pos, f32[2,2,256,384]{3,2,1,0:T(8,128)} %get-tuple-element.90.dkv, f32[2,2,128,384]{3,2,1,0:T(8,128)} %get-tuple-element.91.dn1, bf16[2,128,384]{2,1,0:T(8,128)(2,1)} %copy-done.15, f32[2,64,384]{2,1,0:T(8,128)} %get-tuple-element.97.keep), custom_call_target="tpu_custom_call" | custom-call | tf_op jit(solution)/shard_map/pallas_call | solution.py:373
  115.4 0.7 copy-done.6
  116.1 5.4 %shard_map.93 = (bf16[2,256,1152]{2,1,0:T(8,128)(2,1)}, bf16[8,2,96,384]{3,2,1,0:T(8,128)(2,1)}) custom-call(s32[4]{0:T(128)} %pad_add_fusion.pos, bf16[8,2,16,384]{3,2,1,0:T(8,128)(2,1)} %copy-done.6, f32[2,2,256,384]{3,2,1,0:T(8,128)} %shard_map.92.base, bf16[2,256,384]{2,1,0:T(8,128)(2,1)} %get-tuple-element.78.dq, bf16[2,768,256]{2,1,0:T(8,128)(2,1)} %get-tuple-element.79.xt), custom_call_target="tpu_custom_call" | custom-call | tf_op jit(solution)/shard_map/pallas_call | solution.py:402
  121.5 5.5 %all-to-all-start.4 = ((bf16[16,96,384]{2,1,0:T(8,128)(2,1)}), bf16[16,96,384]{2,1,0:T(8,128)(2,1)S(1)}, u32[]{:S(2)}, u32[]{:S(2)}) async-start(bf16[16,96,384]{2,1,0:T(8,128)(2,1)} %bitcast.19), calls=%async_computation.4 | async-start | bytes 2359296 | tf_op jit(solution)/shard_map/all_to_all | solution.py:539
  127.0 0.9 dynamic-slice_bitcast_fusion
  127.9 4.1 %collective-permute-start.14 = (bf16[256,1152]{1,0:T(8,128)(2,1)S(1)}, bf16[256,1152]{1,0:T(8,128)(2,1)S(1)}, u32[]{:S(2)}, u32[]{:S(2)}) collective-permute-start(bf16[256,1152]{1,0:T(8,128)(2,1)S(1)} %get-tuple-element.124), channel_id=1, source_target_pairs={{0,2},{2,0},{1,3},{3,1},{4,6},{6,4},{5,7},{7,5},{8,10},{10,8},{9,1... | collective-permute-start | bytes 1769480 | tf_op jit(solution)/shard_map/ppermute | solution.py:497
  132.0 2.8 %shard_map.95 = (bf16[96,384]{1,0:T(8,128)(2,1)}, bf16[96,384]{1,0:T(8,128)(2,1)}, bf16[96,384]{1,0:T(8,128)(2,1)}, bf16[96,384]{1,0:T(8,128)(2,1)}) custom-call(s32[4]{0:T(128)} %pad_add_fusion.pos, bf16[2,2,96,384]{3,2,1,0:T(8,128)(2,1)} %get-tuple-element.106.t0, bf16[2,2,96,384]{3,2,1,0:T(8,128)(2,1)} %copy-done.12, bf16[2,2,96,384]{3,2,1,0:T(8,128)(2,1)} %copy-done.13, ...), custom_call_target="tpu_custom_call" | custom-call | tf_op jit(solution)/shard_map/pallas_call | solution.py:326
  134.9 3.1 %collective-permute-start.15 = (bf16[96,384]{1,0:T(8,128)(2,1)}, bf16[96,384]{1,0:T(8,128)(2,1)S(1)}, u32[]{:S(2)}, u32[]{:S(2)}) collective-permute-start(bf16[96,384]{1,0:T(8,128)(2,1)} %get-tuple-element.111), channel_id=1, source_target_pairs={{0,1},{1,0},{4,5},{5,4},{2,3},{3,2},{6,7},{7,6},{8,9},{9,8},{12,13... | collective-permute-start | bytes 221192 | tf_op jit(solution)/shard_map/ppermute | solution.py:501
  138.9 0.8 copy-done.9
  139.7 5.1 %shard_map.94 = bf16[256,768]{1,0:T(8,128)(2,1)} custom-call(s32[4]{0:T(128)} %pad_add_fusion.pos, bf16[256,1152]{1,0:T(8,128)(2,1)} %get-tuple-element.125.pg_own, bf16[256,1152]{1,0:T(8,128)(2,1)} %copy-done.9, bf16[768,2304]{1,0:T(8,128)(2,1)} %rest_5_.1, bf16[768,2304]{1,0:T(8,128)(2,1)} %rest_5_.1, bf16[768,2304]{1,0:T(8,128)(2,1)} %rest_5_.1, ...), custom_call_target="tpu_custom_call" | custom-call | tf_op jit(solution)/shard_map/pallas_call | solution.py:425
  144.9 3.1 %collective-permute-done.15.f1 = bf16[96,384]{1,0:T(8,128)(2,1)S(1)} collective-permute-done((bf16[96,384]{1,0:T(8,128)(2,1)}, bf16[96,384]{1,0:T(8,128)(2,1)S(1)}, u32[]{:S(2)}, u32[]{:S(2)}) %collective-permute-start.15) | collective-permute-done | bytes 73760 | tf_op jit(solution)/shard_map/ppermute | solution.py:501
  148.0 1.2 collective-permute-done.16.f2
  150.3 3.2 %shard_map.96 = bf16[8,2,16,384]{3,2,1,0:T(8,128)(2,1)} custom-call(s32[4]{0:T(128)} %pad_add_fusion.pos, bf16[96,384]{1,0:T(8,128)(2,1)} %get-tuple-element.115.f0, bf16[96,384]{1,0:T(8,128)(2,1)} %copy-done.22, bf16[96,384]{1,0:T(8,128)(2,1)} %copy-done.23, bf16[96,384]{1,0:T(8,128)(2,1)} %copy-done.24, bf16[16,96,384]{2,1,0:T(8,128)(2,1)} %copy-done), custom_call_target="tpu_custom_call" | custom-call | tf_op jit(solution)/shard_map/pallas_call | solution.py:452
  153.5 15.3 %all_to_all.30.terms = bf16[8,2,16,384]{3,2,1,0:T(8,128)(2,1)} all-to-all(bf16[8,2,16,384]{3,2,1,0:T(8,128)(2,1)} %shard_map.96), channel_id=1, replica_groups=mesh['z'=8,'x'=4,'y'=2,'c'=2,'dp'=2] {'z'}, dimensions={0} | all-to-all | bytes 393216 | tf_op jit(solution)/shard_map/all_to_all | solution.py:546
  168.7 2.2 %shard_map.97 = (bf16[16,384]{1,0:T(8,128)(2,1)}, bf16[16,384]{1,0:T(8,128)(2,1)}) custom-call(s32[4]{0:T(128)} %pad_add_fusion.pos, bf16[8,2,16,384]{3,2,1,0:T(8,128)(2,1)} %all_to_all.30.terms), custom_call_target="tpu_custom_call" | custom-call | tf_op jit(solution)/shard_map/pallas_call | solution.py:463
  171.0 2.5 %collective-permute-start.18 = (bf16[16,384]{1,0:T(8,128)(2,1)}, bf16[16,384]{1,0:T(8,128)(2,1)S(1)}, u32[]{:S(2)}, u32[]{:S(2)}) collective-permute-start(bf16[16,384]{1,0:T(8,128)(2,1)} %get-tuple-element.120.own), channel_id=1, source_target_pairs={{0,1},{1,0},{2,3},{3,2},{4,5},{5,4},{6,7},{7,6},{8,9},{9,8},{10,11... | collective-permute-start | bytes 36872 | tf_op jit(solution)/shard_map/ppermute | solution.py:501
  173.5 3.1 %collective-permute-start.19 = (bf16[16,384]{1,0:T(8,128)(2,1)}, bf16[16,384]{1,0:T(8,128)(2,1)S(1)}, u32[]{:S(2)}, u32[]{:S(2)}) collective-permute-start(bf16[16,384]{1,0:T(8,128)(2,1)} %get-tuple-element.121), channel_id=1, source_target_pairs={{0,2},{1,3},{2,0},{3,1},{4,6},{5,7},{6,4},{7,5},{8,10},{9,11},{10,... | collective-permute-start | bytes 36872 | tf_op jit(solution)/shard_map/ppermute | solution.py:501
  177.6 3.8 %collective-permute-done.20.from_both = bf16[16,384]{1,0:T(8,128)(2,1)S(1)} collective-permute-done((bf16[16,384]{1,0:T(8,128)(2,1)}, bf16[16,384]{1,0:T(8,128)(2,1)S(1)}, u32[]{:S(2)}, u32[]{:S(2)}) %collective-permute-start.20) | collective-permute-done | bytes 12320 | tf_op jit(solution)/shard_map/ppermute | solution.py:501
  182.0 2.1 %shard_map.98 = (f32[6,2304]{1,0:T(8,128)}, f32[6,768]{1,0:T(8,128)}) custom-call(s32[4]{0:T(128)} %pad_add_fusion.pos, bf16[16,384]{1,0:T(8,128)(2,1)} %get-tuple-element.120.own, bf16[16,384]{1,0:T(8,128)(2,1)} %copy-done.25, bf16[16,384]{1,0:T(8,128)(2,1)} %copy-done.26, bf16[16,384]{1,0:T(8,128)(2,1)} %copy-done.27), custom_call_target="tpu_custom_call" | custom-call | tf_op jit(solution)/shard_map/pallas_call | solution.py:487
  (90 shorter events, 8.1 us)
Async XLA Ops:
  0.6 4.9 %collective-permute-start = (bf16[256,768]{1,0:T(8,128)(2,1)}, bf16[256,768]{1,0:T(8,128)(2,1)S(1)}, u32[]{:S(2)}, u32[]{:S(2)}) collective-permute-start(bf16[256,768]{1,0:T(8,128)(2,1)} %bitcast.13), channel_id=1, source_target_pairs={{0,2},{2,0},{1,3},{3,1},{4,6},{6,4},{5,7},{7,5},{8,10},{10,8},{9,1... | collective-permute-start | bytes 1179656 | tf_op jit(solution)/shard_map/ppermute | solution.py:497
  4.0 22.7 %collective-permute-start.5 = (bf16[256,768]{1,0:T(8,128)(2,1)}, bf16[256,768]{1,0:T(8,128)(2,1)S(1)}, u32[]{:S(2)}, u32[]{:S(2)}) collective-permute-start(bf16[256,768]{1,0:T(8,128)(2,1)} %bitcast.16), channel_id=1, source_target_pairs={{0,2},{2,0},{1,3},{3,1},{4,6},{6,4},{5,7},{7,5},{8,10},{10,8},{9,1... | collective-permute-start | bytes 1179656 | tf_op jit(solution)/shard_map/ppermute | solution.py:497
  11.3 7.8 %collective-permute-start.1 = (bf16[2,128,384]{2,1,0:T(8,128)(2,1)}, bf16[2,128,384]{2,1,0:T(8,128)(2,1)S(1)}, u32[]{:S(2)}, u32[]{:S(2)}) collective-permute-start(bf16[2,128,384]{2,1,0:T(8,128)(2,1)} %get-tuple-element.65.own), channel_id=1, source_target_pairs={{0,4},{4,0},{1,5},{5,1},{2,6},{6,2},{3,7},{7,3},{8,12},{12,8},{9,1... | collective-permute-start | bytes 589832 | tf_op jit(solution)/shard_map/ppermute | solution.py:497
  11.3 21.2 %all-to-all-start = ((bf16[8,2,16,384]{3,2,1,0:T(8,128)(2,1)}), bf16[8,2,16,384]{3,2,1,0:T(8,128)(2,1)S(1)}, u32[]{:S(2)}, u32[]{:S(2)}) async-start(bf16[8,2,16,384]{3,2,1,0:T(8,128)(2,1)} %get-tuple-element.64), calls=%async_computation | async-start | bytes 393216 | tf_op jit(solution)/shard_map/all_to_all | solution.py:519
  22.7 9.7 %collective-permute-start.2 = (bf16[2,2,64,384]{3,2,1,0:T(8,128)(2,1)}, bf16[2,2,64,384]{3,2,1,0:T(8,128)(2,1)S(1)}, u32[]{:S(2)}, u32[]{:S(2)}) collective-permute-start(bf16[2,2,64,384]{3,2,1,0:T(8,128)(2,1)} %get-tuple-element.66), channel_id=1, source_target_pairs={{0,8},{8,0},{16,24},{24,16},{1,9},{9,1},{17,25},{25,17},{2,10},{10... | collective-permute-start | bytes 589832 | tf_op jit(solution)/shard_map/ppermute | solution.py:501
  24.0 8.5 %collective-permute-start.3 = (bf16[2,2,32,384]{3,2,1,0:T(8,128)(2,1)}, bf16[2,2,32,384]{3,2,1,0:T(8,128)(2,1)S(1)}, u32[]{:S(2)}, u32[]{:S(2)}) collective-permute-start(bf16[2,2,32,384]{3,2,1,0:T(8,128)(2,1)} %get-tuple-element.67), channel_id=1, source_target_pairs={{0,16},{8,24},{16,0},{24,8},{1,17},{9,25},{17,1},{25,9},{2,18},{10... | collective-permute-start | bytes 294920 | tf_op jit(solution)/shard_map/ppermute | solution.py:501
  26.4 6.0 %collective-permute-start.4 = (bf16[2,2,32,384]{3,2,1,0:T(8,128)(2,1)}, bf16[2,2,32,384]{3,2,1,0:T(8,128)(2,1)S(1)}, u32[]{:S(2)}, u32[]{:S(2)}) collective-permute-start(bf16[2,2,32,384]{3,2,1,0:T(8,128)(2,1)} %get-tuple-element.67), channel_id=1, source_target_pairs={{0,24},{8,16},{16,8},{24,0},{1,25},{9,17},{17,9},{25,1},{2,26},{10... | collective-permute-start | bytes 294920 | tf_op jit(solution)/shard_map/ppermute | solution.py:501
  26.6 12.9 %copy-start.4 = (bf16[256,768]{1,0:T(8,128)(2,1)}, bf16[256,768]{1,0:T(8,128)(2,1)S(1)}, u32[]{:S(2)}) copy-start(bf16[256,768]{1,0:T(8,128)(2,1)S(1)} %collective-permute-done.5.ct_oth) | copy-start | bytes 1179652
  32.4 12.4 %copy-start.20 = (bf16[2,2,32,384]{3,2,1,0:T(8,128)(2,1)}, bf16[2,2,32,384]{3,2,1,0:T(8,128)(2,1)S(1)}, u32[]{:S(2)}) copy-start(bf16[2,2,32,384]{3,2,1,0:T(8,128)(2,1)S(1)} %collective-permute-done.3.far_a) | copy-start | bytes 294916
  32.4 12.4 %copy-start.21 = (bf16[2,2,32,384]{3,2,1,0:T(8,128)(2,1)}, bf16[2,2,32,384]{3,2,1,0:T(8,128)(2,1)S(1)}, u32[]{:S(2)}) copy-start(bf16[2,2,32,384]{3,2,1,0:T(8,128)(2,1)S(1)} %collective-permute-done.4.far_b) | copy-start | bytes 294916
  33.2 11.6 %copy-start.17 = (bf16[2,2,64,384]{3,2,1,0:T(8,128)(2,1)}, bf16[2,2,64,384]{3,2,1,0:T(8,128)(2,1)S(1)}, u32[]{:S(2)}) copy-start(bf16[2,2,64,384]{3,2,1,0:T(8,128)(2,1)S(1)} %collective-permute-done.2.near) | copy-start | bytes 589828
  35.8 11.0 %all-to-all-start.1 = ((bf16[8,2,48,384]{3,2,1,0:T(8,128)(2,1)}), bf16[8,2,48,384]{3,2,1,0:T(8,128)(2,1)S(1)}, u32[]{:S(2)}, u32[]{:S(2)}) async-start(bf16[8,2,48,384]{3,2,1,0:T(8,128)(2,1)} %shard_map.87), calls=%async_computation.1 | async-start | bytes 1179648 | tf_op jit(solution)/shard_map/all_to_all | solution.py:524
  67.9 3.7 %copy-start.10 = (bf16[2,256,384]{2,1,0:T(8,128)(2,1)S(1)}, bf16[2,256,384]{2,1,0:T(8,128)(2,1)}, u32[]{:S(2)}) copy-start(bf16[2,256,384]{2,1,0:T(8,128)(2,1)} %get-tuple-element.77.att_own) | copy-start | bytes 1179652
  68.0 7.6 %copy-start.31 = (bf16[2,2,64,384]{3,2,1,0:T(8,128)(2,1)S(1)}, bf16[2,2,64,384]{3,2,1,0:T(8,128)(2,1)}, u32[]{:S(2)}) copy-start(bf16[2,2,64,384]{3,2,1,0:T(8,128)(2,1)} %get-tuple-element.82) | copy-start | bytes 589828
  68.0 9.1 %copy-start.33 = (bf16[2,2,32,384]{3,2,1,0:T(8,128)(2,1)S(1)}, bf16[2,2,32,384]{3,2,1,0:T(8,128)(2,1)}, u32[]{:S(2)}) copy-start(bf16[2,2,32,384]{3,2,1,0:T(8,128)(2,1)} %get-tuple-element.83) | copy-start | bytes 294916
  68.0 11.5 %copy-start.32 = (bf16[2,2,32,384]{3,2,1,0:T(8,128)(2,1)S(1)}, bf16[2,2,32,384]{3,2,1,0:T(8,128)(2,1)}, u32[]{:S(2)}) copy-start(bf16[2,2,32,384]{3,2,1,0:T(8,128)(2,1)} %get-tuple-element.84) | copy-start | bytes 294916
  68.0 19.4 %all-to-all-start.2 = ((bf16[8,2,48,384]{3,2,1,0:T(8,128)(2,1)}), bf16[8,2,48,384]{3,2,1,0:T(8,128)(2,1)S(1)}, u32[]{:S(2)}, u32[]{:S(2)}) async-start(bf16[8,2,48,384]{3,2,1,0:T(8,128)(2,1)} %get-tuple-element.81), calls=%async_computation.2 | async-start | bytes 1179648 | tf_op jit(solution)/shard_map/all_to_all | solution.py:528
  71.7 7.9 %collective-permute-start.6 = (bf16[2,256,384]{2,1,0:T(8,128)(2,1)S(1)}, bf16[2,256,384]{2,1,0:T(8,128)(2,1)S(1)}, u32[]{:S(2)}, u32[]{:S(2)}) collective-permute-start(bf16[2,256,384]{2,1,0:T(8,128)(2,1)S(1)} %copy-done.10), channel_id=1, source_target_pairs={{0,2},{2,0},{1,3},{3,1},{4,6},{6,4},{5,7},{7,5},{8,10},{10,8},{9,1... | collective-permute-start | bytes 1179656 | tf_op jit(solution)/shard_map/ppermute | solution.py:497
  75.5 11.8 %collective-permute-start.7 = (bf16[2,2,64,384]{3,2,1,0:T(8,128)(2,1)S(1)}, bf16[2,2,64,384]{3,2,1,0:T(8,128)(2,1)S(1)}, u32[]{:S(2)}, u32[]{:S(2)}) collective-permute-start(bf16[2,2,64,384]{3,2,1,0:T(8,128)(2,1)S(1)} %copy-done.31), channel_id=1, source_target_pairs={{0,8},{8,0},{16,24},{24,16},{1,9},{9,1},{17,25},{25,17},{2,10},{10... | collective-permute-start | bytes 589832 | tf_op jit(solution)/shard_map/ppermute | solution.py:501
  77.1 9.7 %collective-permute-start.8 = (bf16[2,2,32,384]{3,2,1,0:T(8,128)(2,1)S(1)}, bf16[2,2,32,384]{3,2,1,0:T(8,128)(2,1)S(1)}, u32[]{:S(2)}, u32[]{:S(2)}) collective-permute-start(bf16[2,2,32,384]{3,2,1,0:T(8,128)(2,1)S(1)} %copy-done.33), channel_id=1, source_target_pairs={{0,16},{8,24},{16,0},{24,8},{1,17},{9,25},{17,1},{25,9},{2,18},{10... | collective-permute-start | bytes 294920 | tf_op jit(solution)/shard_map/ppermute | solution.py:501
  79.5 7.8 %collective-permute-start.9 = (bf16[2,2,32,384]{3,2,1,0:T(8,128)(2,1)S(1)}, bf16[2,2,32,384]{3,2,1,0:T(8,128)(2,1)S(1)}, u32[]{:S(2)}, u32[]{:S(2)}) collective-permute-start(bf16[2,2,32,384]{3,2,1,0:T(8,128)(2,1)S(1)} %copy-done.32), channel_id=1, source_target_pairs={{0,24},{8,16},{16,8},{24,0},{1,25},{9,17},{17,9},{25,1},{2,26},{10... | collective-permute-start | bytes 294920 | tf_op jit(solution)/shard_map/ppermute | solution.py:501
  86.5 11.1 %copy-start.30 = (bf16[2,2,96,384]{3,2,1,0:T(8,128)(2,1)S(1)}, bf16[2,2,96,384]{3,2,1,0:T(8,128)(2,1)}, u32[]{:S(2)}) copy-start(bf16[2,2,96,384]{3,2,1,0:T(8,128)(2,1)} %get-tuple-element.99) | copy-start | bytes 884740
  86.5 11.4 %copy-start.29 = (bf16[2,2,96,384]{3,2,1,0:T(8,128)(2,1)S(1)}, bf16[2,2,96,384]{3,2,1,0:T(8,128)(2,1)}, u32[]{:S(2)}) copy-start(bf16[2,2,96,384]{3,2,1,0:T(8,128)(2,1)} %get-tuple-element.100) | copy-start | bytes 884740
  86.5 14.4 %copy-start.28 = (bf16[2,2,96,384]{3,2,1,0:T(8,128)(2,1)S(1)}, bf16[2,2,96,384]{3,2,1,0:T(8,128)(2,1)}, u32[]{:S(2)}) copy-start(bf16[2,2,96,384]{3,2,1,0:T(8,128)(2,1)} %get-tuple-element.101) | copy-start | bytes 884740
  86.8 15.0 %copy-start.18 = (bf16[2,2,32,384]{3,2,1,0:T(8,128)(2,1)}, bf16[2,2,32,384]{3,2,1,0:T(8,128)(2,1)S(1)}, u32[]{:S(2)}) copy-start(bf16[2,2,32,384]{3,2,1,0:T(8,128)(2,1)S(1)} %collective-permute-done.8.far_a) | copy-start | bytes 294916
  87.4 14.5 %copy-start.19 = (bf16[2,2,32,384]{3,2,1,0:T(8,128)(2,1)}, bf16[2,2,32,384]{3,2,1,0:T(8,128)(2,1)S(1)}, u32[]{:S(2)}) copy-start(bf16[2,2,32,384]{3,2,1,0:T(8,128)(2,1)S(1)} %collective-permute-done.9.far_b) | copy-start | bytes 294916
  87.4 14.5 %copy-start.16 = (bf16[2,2,64,384]{3,2,1,0:T(8,128)(2,1)}, bf16[2,2,64,384]{3,2,1,0:T(8,128)(2,1)S(1)}, u32[]{:S(2)}) copy-start(bf16[2,2,64,384]{3,2,1,0:T(8,128)(2,1)S(1)} %collective-permute-done.7.near) | copy-start | bytes 589828
  90.9 24.5 %all-to-all-start.3 = ((bf16[8,2,16,384]{3,2,1,0:T(8,128)(2,1)}), bf16[8,2,16,384]{3,2,1,0:T(8,128)(2,1)S(1)}, u32[]{:S(2)}, u32[]{:S(2)}) async-start(bf16[8,2,16,384]{3,2,1,0:T(8,128)(2,1)} %shard_map.90), calls=%async_computation.3 | async-start | bytes 393216 | tf_op jit(solution)/shard_map/all_to_all | solution.py:533
  97.6 17.5 %collective-permute-start.11 = (bf16[2,2,96,384]{3,2,1,0:T(8,128)(2,1)S(1)}, bf16[2,2,96,384]{3,2,1,0:T(8,128)(2,1)S(1)}, u32[]{:S(2)}, u32[]{:S(2)}) collective-permute-start(bf16[2,2,96,384]{3,2,1,0:T(8,128)(2,1)S(1)} %copy-done.30), channel_id=1, source_target_pairs={{0,8},{8,0},{16,24},{24,16},{1,9},{9,1},{17,25},{25,17},{2,10},{10... | collective-permute-start | bytes 884744 | tf_op jit(solution)/shard_map/ppermute | solution.py:501
  98.0 17.1 %collective-permute-start.12 = (bf16[2,2,96,384]{3,2,1,0:T(8,128)(2,1)S(1)}, bf16[2,2,96,384]{3,2,1,0:T(8,128)(2,1)S(1)}, u32[]{:S(2)}, u32[]{:S(2)}) collective-permute-start(bf16[2,2,96,384]{3,2,1,0:T(8,128)(2,1)S(1)} %copy-done.29), channel_id=1, source_target_pairs={{0,16},{8,24},{16,0},{24,8},{1,17},{9,25},{17,1},{25,9},{2,18},{10... | collective-permute-start | bytes 884744 | tf_op jit(solution)/shard_map/ppermute | solution.py:501
  101.0 14.4 %collective-permute-start.13 = (bf16[2,2,96,384]{3,2,1,0:T(8,128)(2,1)S(1)}, bf16[2,2,96,384]{3,2,1,0:T(8,128)(2,1)S(1)}, u32[]{:S(2)}, u32[]{:S(2)}) collective-permute-start(bf16[2,2,96,384]{3,2,1,0:T(8,128)(2,1)S(1)} %copy-done.28), channel_id=1, source_target_pairs={{0,24},{8,16},{16,8},{24,0},{1,25},{9,17},{17,9},{25,1},{2,26},{10... | collective-permute-start | bytes 884744 | tf_op jit(solution)/shard_map/ppermute | solution.py:501
  104.8 5.0 %collective-permute-start.10 = (bf16[2,128,384]{2,1,0:T(8,128)(2,1)}, bf16[2,128,384]{2,1,0:T(8,128)(2,1)S(1)}, u32[]{:S(2)}, u32[]{:S(2)}) collective-permute-start(bf16[2,128,384]{2,1,0:T(8,128)(2,1)} %get-tuple-element.96), channel_id=1, source_target_pairs={{0,4},{4,0},{1,5},{5,1},{2,6},{6,2},{3,7},{7,3},{8,12},{12,8},{9,1... | collective-permute-start | bytes 589832 | tf_op jit(solution)/shard_map/ppermute | solution.py:497
  115.1 12.8 %copy-start.12 = (bf16[2,2,96,384]{3,2,1,0:T(8,128)(2,1)}, bf16[2,2,96,384]{3,2,1,0:T(8,128)(2,1)S(1)}, u32[]{:S(2)}) copy-start(bf16[2,2,96,384]{3,2,1,0:T(8,128)(2,1)S(1)} %collective-permute-done.11.t1) | copy-start | bytes 884740
  115.1 12.8 %copy-start.13 = (bf16[2,2,96,384]{3,2,1,0:T(8,128)(2,1)}, bf16[2,2,96,384]{3,2,1,0:T(8,128)(2,1)S(1)}, u32[]{:S(2)}) copy-start(bf16[2,2,96,384]{3,2,1,0:T(8,128)(2,1)S(1)} %collective-permute-done.12.t2) | copy-start | bytes 884740
  115.4 12.5 %copy-start.14 = (bf16[2,2,96,384]{3,2,1,0:T(8,128)(2,1)}, bf16[2,2,96,384]{3,2,1,0:T(8,128)(2,1)S(1)}, u32[]{:S(2)}) copy-start(bf16[2,2,96,384]{3,2,1,0:T(8,128)(2,1)S(1)} %collective-permute-done.13.t3) | copy-start | bytes 884740
  121.5 5.5 %copy-start.5 = (bf16[2,256,1152]{2,1,0:T(8,128)(2,1)S(1)}, bf16[2,256,1152]{2,1,0:T(8,128)(2,1)}, u32[]{:S(2)}) copy-start(bf16[2,256,1152]{2,1,0:T(8,128)(2,1)} %get-tuple-element.105) | copy-start | bytes 3538948
  121.5 27.7 %all-to-all-start.4 = ((bf16[16,96,384]{2,1,0:T(8,128)(2,1)}), bf16[16,96,384]{2,1,0:T(8,128)(2,1)S(1)}, u32[]{:S(2)}, u32[]{:S(2)}) async-start(bf16[16,96,384]{2,1,0:T(8,128)(2,1)} %bitcast.19), calls=%async_computation.4 | async-start | bytes 2359296 | tf_op jit(solution)/shard_map/all_to_all | solution.py:539
  127.9 11.0 %collective-permute-start.14 = (bf16[256,1152]{1,0:T(8,128)(2,1)S(1)}, bf16[256,1152]{1,0:T(8,128)(2,1)S(1)}, u32[]{:S(2)}, u32[]{:S(2)}) collective-permute-start(bf16[256,1152]{1,0:T(8,128)(2,1)S(1)} %get-tuple-element.124), channel_id=1, source_target_pairs={{0,2},{2,0},{1,3},{3,1},{4,6},{6,4},{5,7},{7,5},{8,10},{10,8},{9,1... | collective-permute-start | bytes 1769480 | tf_op jit(solution)/shard_map/ppermute | solution.py:497
  134.9 13.1 %collective-permute-start.15 = (bf16[96,384]{1,0:T(8,128)(2,1)}, bf16[96,384]{1,0:T(8,128)(2,1)S(1)}, u32[]{:S(2)}, u32[]{:S(2)}) collective-permute-start(bf16[96,384]{1,0:T(8,128)(2,1)} %get-tuple-element.111), channel_id=1, source_target_pairs={{0,1},{1,0},{4,5},{5,4},{2,3},{3,2},{6,7},{7,6},{8,9},{9,8},{12,13... | collective-permute-start | bytes 221192 | tf_op jit(solution)/shard_map/ppermute | solution.py:501
  138.0 11.1 %collective-permute-start.16 = (bf16[96,384]{1,0:T(8,128)(2,1)}, bf16[96,384]{1,0:T(8,128)(2,1)S(1)}, u32[]{:S(2)}, u32[]{:S(2)}) collective-permute-start(bf16[96,384]{1,0:T(8,128)(2,1)} %get-tuple-element.112), channel_id=1, source_target_pairs={{0,4},{1,5},{4,0},{5,1},{2,6},{3,7},{6,2},{7,3},{8,12},{9,13},{12,... | collective-permute-start | bytes 221192 | tf_op jit(solution)/shard_map/ppermute | solution.py:501
  138.3 10.9 %collective-permute-start.17 = (bf16[96,384]{1,0:T(8,128)(2,1)}, bf16[96,384]{1,0:T(8,128)(2,1)S(1)}, u32[]{:S(2)}, u32[]{:S(2)}) collective-permute-start(bf16[96,384]{1,0:T(8,128)(2,1)} %get-tuple-element.113), channel_id=1, source_target_pairs={{0,5},{1,4},{4,1},{5,0},{2,7},{3,6},{6,3},{7,2},{8,13},{9,12},{12,... | collective-permute-start | bytes 221192 | tf_op jit(solution)/shard_map/ppermute | solution.py:501
  148.0 1.2 copy-start.22
  149.2 1.1 copy-start
  171.0 6.0 %collective-permute-start.18 = (bf16[16,384]{1,0:T(8,128)(2,1)}, bf16[16,384]{1,0:T(8,128)(2,1)S(1)}, u32[]{:S(2)}, u32[]{:S(2)}) collective-permute-start(bf16[16,384]{1,0:T(8,128)(2,1)} %get-tuple-element.120.own), channel_id=1, source_target_pairs={{0,1},{1,0},{2,3},{3,2},{4,5},{5,4},{6,7},{7,6},{8,9},{9,8},{10,11... | collective-permute-start | bytes 36872 | tf_op jit(solution)/shard_map/ppermute | solution.py:501
  173.5 4.1 %collective-permute-start.19 = (bf16[16,384]{1,0:T(8,128)(2,1)}, bf16[16,384]{1,0:T(8,128)(2,1)S(1)}, u32[]{:S(2)}, u32[]{:S(2)}) collective-permute-start(bf16[16,384]{1,0:T(8,128)(2,1)} %get-tuple-element.121), channel_id=1, source_target_pairs={{0,2},{1,3},{2,0},{3,1},{4,6},{5,7},{6,4},{7,5},{8,10},{9,11},{10,... | collective-permute-start | bytes 36872 | tf_op jit(solution)/shard_map/ppermute | solution.py:501
  176.5 4.8 %collective-permute-start.20 = (bf16[16,384]{1,0:T(8,128)(2,1)}, bf16[16,384]{1,0:T(8,128)(2,1)S(1)}, u32[]{:S(2)}, u32[]{:S(2)}) collective-permute-start(bf16[16,384]{1,0:T(8,128)(2,1)} %get-tuple-element.121), channel_id=1, source_target_pairs={{0,3},{1,2},{2,1},{3,0},{4,7},{5,6},{6,5},{7,4},{8,11},{9,10},{10,... | collective-permute-start | bytes 36872 | tf_op jit(solution)/shard_map/ppermute | solution.py:501
  177.0 4.4 %copy-start.25 = (bf16[16,384]{1,0:T(8,128)(2,1)}, bf16[16,384]{1,0:T(8,128)(2,1)S(1)}, u32[]{:S(2)}) copy-start(bf16[16,384]{1,0:T(8,128)(2,1)S(1)} %collective-permute-done.18.from_dp) | copy-start | bytes 36868
  177.6 3.8 %copy-start.26 = (bf16[16,384]{1,0:T(8,128)(2,1)}, bf16[16,384]{1,0:T(8,128)(2,1)S(1)}, u32[]{:S(2)}) copy-start(bf16[16,384]{1,0:T(8,128)(2,1)S(1)} %collective-permute-done.19.from_core) | copy-start | bytes 36868
  (12 other events, 8.7 us)

commit v4 on v3

--- a/solution.py
+++ b/solution.py
@@ -199,7 +199,7 @@
     )(pos, zr)[0]
 
 
-def attention_body(pos, q, ag, kv, n1, yr, near, far_a, far_b, xr, att_out, dq_out, dkv_out, dn1_out, dy_out, dnear_out, dfar_a_out, dfar_b_out, dx_out, keys, s_ref, dw_ref, w_ref, ds_ref, drem):
+def attention_body(pos, q, ag, kv, n1, yr, near, far_a, far_b, xr, att_out, dq_out, dkv_out, dn1_out, dy_out, dnear_out, dfar_a_out, dfar_b_out, dx_out, keys, keys_t, s_ref, dw_ref, w_ref, ds_ref, drem):
     for p in range(2):
         for e in range(2):
             keys[e, p, :256] = kv[e, p]
@@ -215,29 +215,46 @@
             for slot in range(8):
                 start = 768 + ZR * slot
                 keys[e, p, start : start + ZR] = xr[slot, p]
+    for p in range(2):
+        for e in range(2):
+            keys_t[e, p] = keys[e, p].T
     lane = iota((TOK, 128), 1)
-    for e in range(2):
-        att_t, dq_t = [], []
-        dk = dv = None
-        for h in range(2):
-            mine = (lane >> 6) == h
-            qh = jnp.where(mine, q[e], jnp.zeros((), BF16))
-            ah = jnp.where(mine, ag[e], jnp.zeros((), BF16))
-            s_ref[...] = dot_nt(keys[e, 0], qh)
-            dw_ref[...] = dot_nt(keys[e, 1], ah)
-            top = jnp.max(s_ref[...], axis=0, keepdims=True)
-            s_ref[...] = jnp.exp2((s_ref[...] - top) * (LOG2E * DH ** -0.5))
-            total = jnp.sum(s_ref[...], axis=0, keepdims=True)
-            inverse = 1.0 / total
-            delta = jnp.sum(s_ref[...] * dw_ref[...], axis=0, keepdims=True) * inverse
-            prob = s_ref[...] * inverse
-            w_ref[...] = prob.astype(BF16)
-            ds_ref[...] = (prob * (dw_ref[...] - delta) * DH ** -0.5).astype(BF16)
-            att_t.append(dot_tn(keys[e, 1], w_ref[...])[64 * h : 64 * h + 64])
-            dq_t.append(dot_tn(keys[e, 0], ds_ref[...])[64 * h : 64 * h + 64])
-            dkh, dvh = dot(ds_ref[...], qh), dot(w_ref[...], ah)
-            dk = dkh if dk is None else dk + dkh
-            dv = dvh if dv is None else dv + dvh
+    steps = [(e, h) for e in range(2) for h in range(2)]
+    masked = {}
+
+    def scores(step):
+        e, h = steps[step]
+        mine = (lane >> 6) == h
+        qh = jnp.where(mine, q[e], jnp.zeros((), BF16))
+        ah = jnp.where(mine, ag[e], jnp.zeros((), BF16))
+        masked[step] = (qh, ah)
+        s_ref[step % 2] = dot_nt(keys[e, 0], qh)
+        dw_ref[step % 2] = dot_nt(keys[e, 1], ah)
+
+    scores(0)
+    for step, (e, h) in enumerate(steps):
+        if step + 1 < len(steps):
+            scores(step + 1)
+        if h == 0:
+            att_t, dq_t = [], []
+            dk = dv = None
+        s, dw, b = s_ref.at[step % 2], dw_ref.at[step % 2], step % 2
+        qh, ah = masked[step]
+        top = jnp.max(s[...], axis=0, keepdims=True)
+        un = jnp.exp2((s[...] - top) * (LOG2E * DH ** -0.5))
+        s[...] = un
+        inverse = 1.0 / jnp.sum(un, axis=0, keepdims=True)
+        delta = jnp.sum(un * dw[...], axis=0, keepdims=True) * inverse
+        prob = s[...] * inverse
+        w_ref[b] = prob.astype(BF16)
+        ds_ref[b] = (prob * ((dw[...] - delta) * DH ** -0.5)).astype(BF16)
+        att_t.append(dot(keys_t[e, 1, 64 * h : 64 * h + 64], w_ref[b]))
+        dq_t.append(dot(keys_t[e, 0, 64 * h : 64 * h + 64], ds_ref[b]))
+        dkh, dvh = dot(ds_ref[b], qh), dot(w_ref[b], ah)
+        dk = dkh if dk is None else dk + dkh
+        dv = dvh if dv is None else dv + dvh
+        if h == 0:
+            continue
         att_out[e] = jnp.concatenate(att_t, axis=0).T.astype(BF16)
         dq_out[e] = jnp.concatenate(dq_t, axis=0).T.astype(BF16)
         for p, grad in ((0, dk), (1, dv)):
@@ -277,13 +294,28 @@
         [cut(2, TOK), cut(2, TOK), cut(2, 2, TOK), cut(2, 2, NR), cut(2, NR), cut(2, 2, 64), cut(2, 2, 32), cut(2, 2, 32), cut(8, 2, ZR)],
         [(cut(*lead), (lead + (H,), kind)) for lead, kind in outs],
         [
-            pltpu.VMEM((2, 2, n, 128), BF16), pltpu.VMEM((n, TOK), F32), pltpu.VMEM((n, TOK), F32),
-            pltpu.VMEM((n, TOK), BF16), pltpu.VMEM((n, TOK), BF16), pltpu.VMEM((2, 768, 128), F32),
+            pltpu.VMEM((2, 2, n, 128), BF16), pltpu.VMEM((2, 2, 128, n), BF16), pltpu.VMEM((2, n, TOK), F32), pltpu.VMEM((2, n, TOK), F32),
+            pltpu.VMEM((2, n, TOK), BF16), pltpu.VMEM((2, n, TOK), BF16), pltpu.VMEM((2, 768, 128), F32),
         ],
     )(pos, q, ag, kv, n1, yr, near, far_a, far_b, xr)
 
 
-def output_body(pos, att_own, att_oth, ct_own, ct_oth, dq, xt, w_own, w_oth, p_own, p_oth, out, *rest):
+def output_body(pos, att_own, att_oth, w_own, w_oth, out):
+    c = pos[0]
+    out[...] = (dot(att_own[c], w_own[...]) + dot(att_oth[c], w_oth[...])).astype(BF16)
+
+
+def output_side(pos, att_own, att_oth, w_out):
+    row = lambda flip: pl.BlockSpec((H, D), lambda i, s: (s[0] ^ flip, 0))
+    return call(
+        output_body,
+        (1,),
+        [whole(2, TOK, H)] * 2 + [row(0), row(1)],
+        [(whole(TOK, D), ((TOK, D), BF16))],
+    )(pos, att_own, att_oth, w_out, w_out)[0]
+
+
+def terms_body(pos, att_own, att_oth, ct_own, ct_oth, dq, xt, p_own, p_oth, *rest):
     c, x = pos[0], pos[2] >> 1
     slots = rest[-1]
     total = dot(xt[0], dq[0]) + dot(xt[1], dq[1])
@@ -296,20 +328,18 @@
     slots[:, :, 1] = total.astype(BF16).reshape(XN, YN, 96, H)
     for far in range(XN):
         rest[far][...] = slots[x ^ far]
-    out[...] = (dot(att_own[c], w_own[...]) + dot(att_oth[c], w_oth[...])).astype(BF16)
-
-
-def output_side(pos, att_own, att_oth, ct_own, ct_oth, dq, xt, w_out, perm):
-    row = lambda flip: pl.BlockSpec((H, D), lambda i, s: (s[0] ^ flip, 0))
+
+
+def output_terms(pos, att_own, att_oth, ct_own, ct_oth, dq, xt, perm):
     col = lambda flip, rows: pl.BlockSpec((rows, H), lambda i, s: (0, s[0] ^ flip))
     slot = (YN, 2, 96, H)
     return call(
-        output_body,
-        (1,),
-        [whole(2, TOK, H)] * 2 + [col(0, TOK)] * 2 + [whole(2, TOK, H), whole(2, D, TOK)] + [row(0), row(1), col(0, D), col(1, D)],
-        [(whole(TOK, D), ((TOK, D), BF16))] + [(whole(*slot), (slot, BF16))] * XN,
+        terms_body,
+        (1,),
+        [whole(2, TOK, H)] * 2 + [col(0, TOK)] * 2 + [whole(2, TOK, H), whole(2, D, TOK), col(0, D), col(1, D)],
+        [(whole(*slot), (slot, BF16))] * XN,
         [pltpu.VMEM((XN,) + slot, BF16)],
-    )(pos, att_own, att_oth, ct_own, ct_oth, dq, xt, w_out, w_out, perm, perm)
+    )(pos, att_own, att_oth, ct_own, ct_oth, dq, xt, perm, perm)
 
 
 def x_sum_body(pos, t0, t1, t2, t3, *rest):
@@ -350,64 +380,50 @@
     )(pos, xr)[0]
 
 
-def base_body(pos, dkv, dn1, yr, keep, out):
-    def hot(rows, width, shift, start):
-        r, k = iota((rows, width), 0), iota((rows, width), 1)
-        return (((r >> shift) + start) == (k & (NR - 1 if width > NR else width - 1))).astype(BF16)
-
+def leaf_body(pos, zr, dkv, dn1, yr, keep, dq, xt, pg_out, grad_out):
     def split(grad):
         high = grad.astype(BF16)
-        return high, (grad - high.astype(F32)).astype(BF16)
-
-    for p in range(2):
-        keep_high, keep_low = split(keep[p])
-        for e in range(2):
-            total = dkv[e, p] + dot(hot(TOK, 2 * NR, 1, 0), jnp.concatenate(split(dn1[e, p]), axis=0)) * HALF_ROOT
-            total = total + dot(hot(TOK, NR, 2, 64 * e), yr[p]) * 0.5
-            up = hot(TOK, 64, 3, 32 * e)
-            out[e, p] = total + (dot(up, keep_high) + dot(up, keep_low)) * (0.5 * HALF_ROOT)
-
-
-def base_grads(pos, dkv, dn1, yr, keep):
-    shape = (2, 2, TOK, H)
-    return call(
-        base_body,
-        (1,),
-        [whole(*shape), whole(2, 2, NR, H), whole(2, NR, H), whole(2, 64, H)],
-        [(whole(*shape), (shape, F32))],
-    )(pos, dkv, dn1, yr, keep)[0]
-
-
-def leaf_body(pos, zr, base, dq, xt, pg_out, grad_out):
-    t, k = iota((2 * TOK, 128), 0), iota((2 * TOK, 128), 1)
-    far, row = (k >> 4) ^ pos[1], k & 15
-    odd = jnp.where((far == 1) & (row == t >> 5), 0.25, jnp.where((far >= 4) & (row == t >> 7), 0.125, 0.0)).astype(BF16)
-    even = jnp.where(((far >> 1) == 1) & (row == t >> 6), 0.125, 0.0).astype(BF16)
-    both = jnp.concatenate([zr[:, p].reshape(128, H) for p in range(2)], axis=1)
-    up = dot(odd, both) * HALF_ROOT + dot(even, both)
+        return [high, (grad - high.astype(F32)).astype(BF16)]
+
+    def hot(hit, scale):
+        return jnp.where(hit, scale, 0.0).astype(BF16)
+
+    def wide(ref):
+        return jnp.concatenate([ref[0], ref[1]], axis=1)
+
+    zs = jnp.concatenate([zr[:, p].reshape(128, H) for p in range(2)], axis=1)
+    near = split(wide(keep))
+    for e in range(2):
+        t, k = iota((TOK, 128), 0), iota((TOK, 128), 1)
+        far, row, chip = (k >> 4) ^ pos[1], k & 15, t + TOK * e
+        first = hot(t >> 1 == k, 1.0)
+        third = hot(chip >> 3 == k & 63, 0.5)
+        odd = hot((far == 1) & (row == chip >> 5), 0.25) + hot((far >= 4) & (row == chip >> 7), 0.125)
+        even = [hot(chip >> 2 == k, 0.5), hot((far >> 1 == 1) & (row == chip >> 6), 0.125)]
+        up = dot(jnp.concatenate([first, first, third, odd], axis=1), jnp.concatenate(split(wide(dn1.at[e])) + near + [zs], axis=0))
+        up = up * HALF_ROOT + dot(jnp.concatenate(even, axis=1), jnp.concatenate([wide(yr), zs], axis=0))
+        for p in range(2):
+            pg_out[e, :, H * (1 + p) : H * (2 + p)] = (dkv[e, p] + up[:, H * p : H * p + H]).astype(BF16)
+        pg_out[e, :, :H] = dq[e]
     for p in range(2):
         cols = slice(H * (1 + p), H * (2 + p))
-        total = None
-        for e in range(2):
-            leaf = (base[e, p] + up[TOK * e : TOK * e + TOK, H * p : H * p + H]).astype(BF16)
-            pg_out[e, :, cols] = leaf
-            term = dot(xt[e], leaf)
-            total = term if total is None else total + term
+        total = dot(xt[0], pg_out[0, :, cols]) + dot(xt[1], pg_out[1, :, cols])
         grad_out[:, p] = total.astype(BF16).reshape(8, 96, H)
-    for e in range(2):
-        pg_out[e, :, :H] = dq[e]
-
-
-def leaf_grads(pos, zr, base, dq, xt):
+
+
+def leaf_grads(pos, zr, dkv, dn1, yr, keep, dq, xt):
     return call(
         leaf_body,
         (1,),
-        [whole(ZN, 2, 16, H), whole(2, 2, TOK, H), whole(2, TOK, H), whole(2, D, TOK)],
+        [
+            whole(ZN, 2, 16, H), whole(2, 2, TOK, H), whole(2, 2, NR, H), whole(2, NR, H), whole(2, 64, H),
+            whole(2, TOK, H), whole(2, D, TOK),
+        ],
         [
             (whole(2, TOK, 3 * H), ((2, TOK, 3 * H), BF16)),
             (whole(8, 2, 96, H), ((8, 2, 96, H), BF16)),
         ],
-    )(pos, zr, base, dq, xt)
+    )(pos, zr, dkv, dn1, yr, keep, dq, xt)
 
 
 def input_body(pos, pg_own, pg_oth, *rest):
@@ -519,8 +535,8 @@
     zr = lax.all_to_all(zs, "z", 0, 0)
     yr = swap(n2, "y")
     near, far = pair_nodes(pos, n2, yr)
+    zr, near, far, ct_oth = lax.optimization_barrier((zr, near, far, ct_oth))
     near, far_a, far_b = along(near, "x", 1), along(far, "x", 2), along(far, "x", 3)
-    zr, near, far_a, far_b, ct_oth = lax.optimization_barrier((zr, near, far_a, far_b, ct_oth))
     xr = lax.all_to_all(plane_slots(pos, zr), ("x", "y"), 0, 0)
     q, ag, xt = project(pos, x_own, x_oth, ct_own, ct_oth, w_qkv, w_out, perm)
     att, dq, dkv, dn1, dy, dnear, dfar_a, dfar_b, dx = attention(pos, q, ag, kv, n1, yr, near, far_a, far_b, xr)
@@ -528,22 +544,24 @@
     dx_r = lax.all_to_all(dx, ("x", "y"), 0, 0)
     att_oth = swap(att, "c")
     back = (along(dnear, "x", 1), along(dfar_a, "x", 2), along(dfar_b, "x", 3))
-    layer_out, *terms = output_side(pos, att, att_oth, ct_own, ct_oth, dq, xt, w_out, perm)
-    dx_r, back, terms = lax.optimization_barrier((dx_r, back, terms))
+    first, *firsts = output_terms(pos, att, att_oth, ct_own, ct_oth, dq, xt, perm)
+    dx_r, back, first = lax.optimization_barrier((dx_r, back, first))
     dz_r = lax.all_to_all(back_slots(pos, dx_r), "z", 0, 0)
-    firsts = terms[:1] + [along(terms[far], "x", far) for far in (1, 2, 3)]
+    firsts = x_sum(pos, first, *[along(firsts[far - 1], "x", far) for far in (1, 2, 3)])
     keep, dy = pair_back(pos, *back, dy)
-    base = base_grads(pos, dkv, dn1, swap(dy, "y"), keep)
-    dz_r, base, firsts = lax.optimization_barrier((dz_r, base, firsts))
-    pg, terms = leaf_grads(pos, dz_r, base, dq, xt)
+    dz_r, firsts = lax.optimization_barrier((dz_r, firsts))
+    pg, terms = leaf_grads(pos, dz_r, dkv, dn1, swap(dy, "y"), keep, dq, xt)
     second = lax.all_to_all(terms.reshape(16, 96, H), ("x", "y", "dp"), 0, 0)
-    firsts = list(x_sum(pos, *firsts))
-    firsts = firsts[:1] + [along(firsts[far], ("y", "dp"), far) for far in (1, 2, 3)]
+    firsts = list(firsts[:1]) + [along(firsts[far], ("y", "dp"), far) for far in (1, 2, 3)]
     pg_own = lax.dynamic_index_in_dim(pg, c, 0, keepdims=False)
     pg_oth = swap(lax.dynamic_index_in_dim(pg, 1 - c, 0, keepdims=False), "c")
     input_grad = input_side(pos, pg_own, pg_oth, w_qkv)
     second, input_grad, firsts = lax.optimization_barrier((second, input_grad, firsts))
-    terms = lax.all_to_all(middle_sum(pos, firsts, second), "z", 0, 0)
+    terms = middle_sum(pos, firsts, second)
+    terms, att, att_oth = lax.optimization_barrier((terms, att, att_oth))
+    terms = lax.all_to_all(terms, "z", 0, 0)
+    layer_out = output_side(pos, att, att_oth, w_out)
+    terms, layer_out = lax.optimization_barrier((terms, layer_out))
     own, oth = z_sum(pos, terms)
     pair = ("c", "dp")
     qkv_grad, out_grad = last_rows(pos, own, along(own, pair, 1), along(oth, pair, 2), along(oth, pair, 3))

time: 185 us -> 188 us (1.016)
  waiting for transfers between devices: 22.9 us -> 38.5 us
  blocking collectives: 15.3 us -> 0 us
  starting transfers between devices: 61.4 us -> 66.2 us
  Pallas kernels: 73.5 us -> 69.8 us
    all_to_all x1 -> x0, blocking collectives: 15.3 us -> none  [shards(): terms = lax.all_to_all(middle_sum(pos, firsts, second), 'z', 0, 0)]
    ppermute x15, waiting for transfers between devices: 15.6 us -> 27 us  [along(): return lax.ppermute(value, axes, [(i, i ^ far) for i in range(count)])]
    all_to_all x0 -> x1, starting transfers between devices: none -> 6.56 us  [shards(): terms = lax.all_to_all(terms, 'z', 0, 0)]
    all_to_all x0 -> x1, waiting for transfers between devices: none -> 5.96 us  [shards(): terms = lax.all_to_all(terms, 'z', 0, 0)]
    pallas_call x1, Pallas kernels: 20.3 us -> 17.9 us  [attention(): call(attention_body, (H // 128,), [cut(2, TOK), cut(2, TOK), cut(2, 2, TO...]
    all_to_all x1, waiting for transfers between devices: 2.01 us -> 0.01 us  [shards(): xr = lax.all_to_all(plane_slots(pos, zr), ('x', 'y'), 0, 0)]
    unnamed x68 -> x80, local copies, waits for them, and re-layouts: 8.51 us -> 10 us
  transfers between devices with their start and end apart: 26 -> 27, of which waited for: 11 -> 12; matrix products, arithmetic and copies ran while one was open for 1% -> 1% of each run, Pallas kernels for 19% -> 18%
where the time goes in v4:
time: 188 us; the launch traced here: 187 us
  Pallas kernels  69.8 us (37%)
  starting transfers between devices  66.2 us (35%)
  waiting for transfers between devices  38.5 us (20%)
  local copies, waits for them, and re-layouts  11 us (6%)
    ppermute x15, waiting for transfers between devices, along(): return lax.ppermute(value, axes, [(i, i ^ far) for i in range(count)])  27 us
    ppermute x15, starting transfers between devices, along(): return lax.ppermute(value, axes, [(i, i ^ far) for i in range(count)])  21 us
    pallas_call x1, Pallas kernels, attention(): call(attention_body, (H // 128,), [cut(2, TOK), cut(2, TOK), cut(2, 2, TO...  17.9 us
    ppermute x6, starting transfers between devices, swap(): return lax.ppermute(value, axis, [(0, 1), (1, 0)])  11.6 us
    unnamed x80, local copies, waits for them, and re-layouts  10 us
    all_to_all x1, starting transfers between devices, shards(): terms = lax.all_to_all(terms, 'z', 0, 0)  6.56 us
    all_to_all x1, starting transfers between devices, shards(): zr = lax.all_to_all(zs, 'z', 0, 0)  6.45 us
    all_to_all x1, starting transfers between devices, shards(): dz_r = lax.all_to_all(back_slots(pos, dx_r), 'z', 0, 0)  6.36 us
  transfers between devices with their start and end apart: 27, of which 12 were waited for; matrix products, arithmetic and copies ran while one was open for 1% of the time, Pallas kernels for 18%

profile of v4, /device:TPU:1, one launch (start us, length us, event | category | flops | bytes accessed | tf_op | source)
XLA Modules:
  0.0 187.0 jit_solution(7293406124073326241)
XLA Ops:
  0.6 3.3 %collective-permute-start = (bf16[256,768]{1,0:T(8,128)(2,1)}, bf16[256,768]{1,0:T(8,128)(2,1)S(1)}, u32[]{:S(2)}, u32[]{:S(2)}) collective-permute-start(bf16[256,768]{1,0:T(8,128)(2,1)} %bitcast.13), channel_id=1, source_target_pairs={{0,2},{2,0},{1,3},{3,1},{4,6},{6,4},{5,7},{7,5},{8,10},{10,8},{9,1... | collective-permute-start | bytes 1179656 | tf_op jit(solution)/shard_map/ppermute | solution.py:513
  4.6 0.9 collective-permute-done.x_oth
  6.3 5.0 %shard_map.84 = (bf16[2,2,256,384]{3,2,1,0:T(8,128)(2,1)}, bf16[2,2,128,384]{3,2,1,0:T(8,128)(2,1)}, bf16[2,128,384]{2,1,0:T(8,128)(2,1)}, bf16[8,2,16,384]{3,2,1,0:T(8,128)(2,1)}) custom-call(s32[4]{0:T(128)} %pad_add_fusion.pos, bf16[256,768]{1,0:T(8,128)(2,1)} %bitcast.14, bf16[256,768]{1,0:T(8,128)(2,1)} %copy-done.3, bf16[768,2304]{1,0:T(8,128)(2,1)} %rest_5_.1, ...), custom_call_target="tpu_custom_call" | custom-call | tf_op jit(solution)/shard_map/pallas_call | solution.py:114
  11.3 6.5 %all-to-all-start = ((bf16[8,2,16,384]{3,2,1,0:T(8,128)(2,1)}), bf16[8,2,16,384]{3,2,1,0:T(8,128)(2,1)S(1)}, u32[]{:S(2)}, u32[]{:S(2)}) async-start(bf16[8,2,16,384]{3,2,1,0:T(8,128)(2,1)} %get-tuple-element.63), calls=%async_computation | async-start | bytes 393216 | tf_op jit(solution)/shard_map/all_to_all | solution.py:535
  17.7 1.3 collective-permute-start.1
  19.0 4.7 %collective-permute-done.1.oth.yr = bf16[2,128,384]{2,1,0:T(8,128)(2,1)S(1)} collective-permute-done((bf16[2,128,384]{2,1,0:T(8,128)(2,1)}, bf16[2,128,384]{2,1,0:T(8,128)(2,1)S(1)}, u32[]{:S(2)}, u32[]{:S(2)}) %collective-permute-start.1) | collective-permute-done | bytes 196640 | tf_op jit(solution)/shard_map/ppermute | solution.py:513
  24.4 3.0 %shard_map.85 = (bf16[2,2,64,384]{3,2,1,0:T(8,128)(2,1)}, bf16[2,2,32,384]{3,2,1,0:T(8,128)(2,1)}) custom-call(s32[4]{0:T(128)} %pad_add_fusion.pos, bf16[2,128,384]{2,1,0:T(8,128)(2,1)} %get-tuple-element.64.own, bf16[2,128,384]{2,1,0:T(8,128)(2,1)} %copy-done.11), custom_call_target="tpu_custom_call" | custom-call | tf_op jit(solution)/shard_map/pallas_call | solution.py:151
  28.2 2.6 %shard_map.87 = bf16[8,2,48,384]{3,2,1,0:T(8,128)(2,1)} custom-call(s32[4]{0:T(128)} %pad_add_fusion.pos, bf16[8,2,16,384]{3,2,1,0:T(8,128)(2,1)} %copy-done.10), custom_call_target="tpu_custom_call" | custom-call | tf_op jit(solution)/shard_map/pallas_call | solution.py:194
  30.8 5.0 %all-to-all-start.1 = ((bf16[8,2,48,384]{3,2,1,0:T(8,128)(2,1)}), bf16[8,2,48,384]{3,2,1,0:T(8,128)(2,1)S(1)}, u32[]{:S(2)}, u32[]{:S(2)}) async-start(bf16[8,2,48,384]{3,2,1,0:T(8,128)(2,1)} %shard_map.87), calls=%async_computation.1 | async-start | bytes 1179648 | tf_op jit(solution)/shard_map/all_to_all | solution.py:540
  35.9 1.5 collective-permute-start.3
  37.3 2.4 %collective-permute-start.4 = (bf16[2,2,32,384]{3,2,1,0:T(8,128)(2,1)S(1)}, bf16[2,2,32,384]{3,2,1,0:T(8,128)(2,1)S(1)}, u32[]{:S(2)}, u32[]{:S(2)}) collective-permute-start(bf16[2,2,32,384]{3,2,1,0:T(8,128)(2,1)S(1)} %copy-done.36), channel_id=1, source_target_pairs={{0,16},{8,24},{16,0},{24,8},{1,17},{9,25},{17,1},{25,9},{2,18},{10... | collective-permute-start | bytes 294920 | tf_op jit(solution)/shard_map/ppermute | solution.py:517
  39.8 5.3 %shard_map.86 = (bf16[2,256,384]{2,1,0:T(8,128)(2,1)}, bf16[2,256,384]{2,1,0:T(8,128)(2,1)}, bf16[2,768,256]{2,1,0:T(8,128)(2,1)}) custom-call(s32[4]{0:T(128)} %pad_add_fusion.pos, bf16[256,768]{1,0:T(8,128)(2,1)} %bitcast.15, bf16[256,768]{1,0:T(8,128)(2,1)} %copy-done.3, bf16[256,768]{1,0:T(8,128)(2,1)} %bitcast.17, bf16[256,768]{1,0:T(8,128)(2,1)} %copy-done.6, ...), custom_call_target="tpu_custom_call" | custom-call | tf_op jit(solution)/shard_map/pallas_call | solution.py:132
  45.1 5.1 %collective-permute-done.4.far_a = bf16[2,2,32,384]{3,2,1,0:T(8,128)(2,1)S(1)} collective-permute-done((bf16[2,2,32,384]{3,2,1,0:T(8,128)(2,1)S(1)}, bf16[2,2,32,384]{3,2,1,0:T(8,128)(2,1)S(1)}, u32[]{:S(2)}, u32[]{:S(2)}) %collective-permute-start.4) | collective-permute-done | bytes 98336 | tf_op jit(solution)/shard_map/ppermute | solution.py:517
  51.2 17.9 %shard_map.88 = (bf16[2,256,384]{2,1,0:T(8,128)(2,1)}, bf16[2,256,384]{2,1,0:T(8,128)(2,1)}, f32[2,2,256,384]{3,2,1,0:T(8,128)}, f32[2,2,128,384]{3,2,1,0:T(8,12...) custom-call(s32[4]{0:T(128)} %pad_add_fusion.pos, ...), custom_call_target="tpu_custom_call" | custom-call | tf_op jit(solution)/shard_map/pallas_call | solution.py:291
  69.2 3.7 %all-to-all-start.2 = ((bf16[8,2,48,384]{3,2,1,0:T(8,128)(2,1)}), bf16[8,2,48,384]{3,2,1,0:T(8,128)(2,1)S(1)}, u32[]{:S(2)}, u32[]{:S(2)}) async-start(bf16[8,2,48,384]{3,2,1,0:T(8,128)(2,1)} %get-tuple-element.75), calls=%async_computation.2 | async-start | bytes 1179648 | tf_op jit(solution)/shard_map/all_to_all | solution.py:544
  72.9 3.4 %collective-permute-start.9 = (bf16[2,256,384]{2,1,0:T(8,128)(2,1)S(1)}, bf16[2,256,384]{2,1,0:T(8,128)(2,1)S(1)}, u32[]{:S(2)}, u32[]{:S(2)}) collective-permute-start(bf16[2,256,384]{2,1,0:T(8,128)(2,1)S(1)} %copy-done.4), channel_id=1, source_target_pairs={{0,2},{2,0},{1,3},{3,1},{4,6},{6,4},{5,7},{7,5},{8,10},{10,8},{9,1... | collective-permute-start | bytes 1179656 | tf_op jit(solution)/shard_map/ppermute | solution.py:513
  76.2 1.4 collective-permute-start.6
  77.6 2.4 %collective-permute-start.7 = (bf16[2,2,32,384]{3,2,1,0:T(8,128)(2,1)S(1)}, bf16[2,2,32,384]{3,2,1,0:T(8,128)(2,1)S(1)}, u32[]{:S(2)}, u32[]{:S(2)}) collective-permute-start(bf16[2,2,32,384]{3,2,1,0:T(8,128)(2,1)S(1)} %copy-done.35), channel_id=1, source_target_pairs={{0,16},{8,24},{16,0},{24,8},{1,17},{9,25},{17,1},{25,9},{2,18},{10... | collective-permute-start | bytes 294920 | tf_op jit(solution)/shard_map/ppermute | solution.py:517
  80.9 5.5 %shard_map.89 = (bf16[2,2,96,384]{3,2,1,0:T(8,128)(2,1)}, bf16[2,2,96,384]{3,2,1,0:T(8,128)(2,1)}, bf16[2,2,96,384]{3,2,1,0:T(8,128)(2,1)}, bf16[2,2,96,384]{3,2,1,0:T(8,128)(2,1)}) custom-call(s32[4]{0:T(128)} %pad_add_fusion.pos, bf16[2,256,384]{2,1,0:T(8,128)(2,1)} %get-tuple-element.113.att_own, bf16[2,256,384]{2,1,0:T(8,128)(2,1)} %copy-done.5, ...), custom_call_target="tpu_custom_call" | custom-call | tf_op jit(solution)/shard_map/pallas_call | solution.py:336
  86.4 0.9 collective-permute-done.7.far_a
  87.9 0.9 copy-done.1
  88.8 2.6 %shard_map.90 = bf16[8,2,16,384]{3,2,1,0:T(8,128)(2,1)} custom-call(s32[4]{0:T(128)} %pad_add_fusion.pos, bf16[8,2,48,384]{3,2,1,0:T(8,128)(2,1)} %copy-done.1), custom_call_target="tpu_custom_call" | custom-call | tf_op jit(solution)/shard_map/pallas_call | solution.py:375
  91.4 6.4 %all-to-all-start.3 = ((bf16[8,2,16,384]{3,2,1,0:T(8,128)(2,1)}), bf16[8,2,16,384]{3,2,1,0:T(8,128)(2,1)S(1)}, u32[]{:S(2)}, u32[]{:S(2)}) async-start(bf16[8,2,16,384]{3,2,1,0:T(8,128)(2,1)} %shard_map.90), calls=%async_computation.3 | async-start | bytes 393216 | tf_op jit(solution)/shard_map/all_to_all | solution.py:549
  97.9 2.2 %collective-permute-start.11 = (bf16[2,2,96,384]{3,2,1,0:T(8,128)(2,1)S(1)}, bf16[2,2,96,384]{3,2,1,0:T(8,128)(2,1)S(1)}, u32[]{:S(2)}, u32[]{:S(2)}) collective-permute-start(bf16[2,2,96,384]{3,2,1,0:T(8,128)(2,1)S(1)} %copy-done.30), channel_id=1, source_target_pairs={{0,16},{8,24},{16,0},{24,8},{1,17},{9,25},{17,1},{25,9},{2,18},{10... | collective-permute-start | bytes 884744 | tf_op jit(solution)/shard_map/ppermute | solution.py:517
  100.1 1.6 collective-permute-start.12
  101.8 3.0 %shard_map.92 = (f32[2,64,384]{2,1,0:T(8,128)}, bf16[2,128,384]{2,1,0:T(8,128)(2,1)}) custom-call(s32[4]{0:T(128)} %pad_add_fusion.pos, bf16[2,2,64,384]{3,2,1,0:T(8,128)(2,1)} %copy-done.17, bf16[2,2,32,384]{3,2,1,0:T(8,128)(2,1)} %copy-done.19, bf16[2,2,32,384]{3,2,1,0:T(8,128)(2,1)} %copy-done.20, bf16[2,128,384]{2,1,0:T(8,128)(2,1)} %get-tuple-element.98.dy), custom_call_target="tpu_custom_call" | custom-call | tf_op jit(solution)/shard_map/pallas_call | solution.py:168
  105.4 5.1 %collective-permute-done.11.t2 = bf16[2,2,96,384]{3,2,1,0:T(8,128)(2,1)S(1)} collective-permute-done((bf16[2,2,96,384]{3,2,1,0:T(8,128)(2,1)S(1)}, bf16[2,2,96,384]{3,2,1,0:T(8,128)(2,1)S(1)}, u32[]{:S(2)}, u32[]{:S(2)}) %collective-permute-start.11) | collective-permute-done | bytes 294944 | tf_op jit(solution)/shard_map/ppermute | solution.py:517
  110.5 4.0 %collective-permute-done.12.t3 = bf16[2,2,96,384]{3,2,1,0:T(8,128)(2,1)S(1)} collective-permute-done((bf16[2,2,96,384]{3,2,1,0:T(8,128)(2,1)S(1)}, bf16[2,2,96,384]{3,2,1,0:T(8,128)(2,1)S(1)}, u32[]{:S(2)}, u32[]{:S(2)}) %collective-permute-start.12) | collective-permute-done | bytes 294944 | tf_op jit(solution)/shard_map/ppermute | solution.py:517
  115.3 2.8 %shard_map.91 = (bf16[96,384]{1,0:T(8,128)(2,1)}, bf16[96,384]{1,0:T(8,128)(2,1)}, bf16[96,384]{1,0:T(8,128)(2,1)}, bf16[96,384]{1,0:T(8,128)(2,1)}) custom-call(s32[4]{0:T(128)} %pad_add_fusion.pos, bf16[2,2,96,384]{3,2,1,0:T(8,128)(2,1)} %get-tuple-element.84.t0, bf16[2,2,96,384]{3,2,1,0:T(8,128)(2,1)} %copy-done.13, bf16[2,2,96,384]{3,2,1,0:T(8,128)(2,1)} %copy-done.14, ...), custom_call_target="tpu_custom_call" | custom-call | tf_op jit(solution)/shard_map/pallas_call | solution.py:356
  118.9 6.0 %shard_map.93 = (bf16[2,256,1152]{2,1,0:T(8,128)(2,1)}, bf16[8,2,96,384]{3,2,1,0:T(8,128)(2,1)}) custom-call(s32[4]{0:T(128)} %pad_add_fusion.pos, bf16[8,2,16,384]{3,2,1,0:T(8,128)(2,1)} %copy-done.8, f32[2,2,256,384]{3,2,1,0:T(8,128)} %get-tuple-element.93.dkv, f32[2,2,128,384]{3,2,1,0:T(8,128)} %get-tuple-element.94.dn1, bf16[2,128,384]{2,1,0:T(8,128)(2,1)} %copy-done.16, ...), custom_call_target="tpu_custom_call" | custom-call | tf_op jit(solution)/shard_map/pallas_call | solution.py:415
  124.8 5.5 %all-to-all-start.4 = ((bf16[16,96,384]{2,1,0:T(8,128)(2,1)}), bf16[16,96,384]{2,1,0:T(8,128)(2,1)S(1)}, u32[]{:S(2)}, u32[]{:S(2)}) async-start(bf16[16,96,384]{2,1,0:T(8,128)(2,1)} %bitcast.19), calls=%async_computation.4 | async-start | bytes 2359296 | tf_op jit(solution)/shard_map/all_to_all | solution.py:554
  130.3 0.9 dynamic-slice_bitcast_fusion
  131.3 2.8 %collective-permute-start.14 = (bf16[256,1152]{1,0:T(8,128)(2,1)S(1)}, bf16[256,1152]{1,0:T(8,128)(2,1)S(1)}, u32[]{:S(2)}, u32[]{:S(2)}) collective-permute-start(bf16[256,1152]{1,0:T(8,128)(2,1)S(1)} %get-tuple-element.122), channel_id=1, source_target_pairs={{0,2},{2,0},{1,3},{3,1},{4,6},{6,4},{5,7},{7,5},{8,10},{10,8},{9,1... | collective-permute-start | bytes 1769480 | tf_op jit(solution)/shard_map/ppermute | solution.py:513
  134.1 3.1 %collective-permute-start.15 = (bf16[96,384]{1,0:T(8,128)(2,1)S(1)}, bf16[96,384]{1,0:T(8,128)(2,1)S(1)}, u32[]{:S(2)}, u32[]{:S(2)}) collective-permute-start(bf16[96,384]{1,0:T(8,128)(2,1)S(1)} %copy-done.39), channel_id=1, source_target_pairs={{0,1},{1,0},{4,5},{5,4},{2,3},{3,2},{6,7},{7,6},{8,9},{9,8},{12,13... | collective-permute-start | bytes 221192 | tf_op jit(solution)/shard_map/ppermute | solution.py:517
  139.0 5.1 %shard_map.94 = bf16[256,768]{1,0:T(8,128)(2,1)} custom-call(s32[4]{0:T(128)} %pad_add_fusion.pos, bf16[256,1152]{1,0:T(8,128)(2,1)} %get-tuple-element.123.pg_own, bf16[256,1152]{1,0:T(8,128)(2,1)} %copy-done.12, bf16[768,2304]{1,0:T(8,128)(2,1)} %rest_5_.1, bf16[768,2304]{1,0:T(8,128)(2,1)} %rest_5_.1, bf16[768,2304]{1,0:T(8,128)(2,1)} %rest_5_.1, ...), custom_call_target="tpu_custom_call" | custom-call | tf_op jit(solution)/shard_map/pallas_call | solution.py:441
  144.2 5.7 %collective-permute-done.15.f1 = bf16[96,384]{1,0:T(8,128)(2,1)S(1)} collective-permute-done((bf16[96,384]{1,0:T(8,128)(2,1)S(1)}, bf16[96,384]{1,0:T(8,128)(2,1)S(1)}, u32[]{:S(2)}, u32[]{:S(2)}) %collective-permute-start.15) | collective-permute-done | bytes 73760 | tf_op jit(solution)/shard_map/ppermute | solution.py:517
  149.9 1.7 collective-permute-done.16.f2
  151.6 0.9 collective-permute-done.17.f3
  153.2 1.0 copy-done
  154.2 3.2 %shard_map.95 = bf16[8,2,16,384]{3,2,1,0:T(8,128)(2,1)} custom-call(s32[4]{0:T(128)} %pad_add_fusion.pos, bf16[96,384]{1,0:T(8,128)(2,1)} %get-tuple-element.107.f0, bf16[96,384]{1,0:T(8,128)(2,1)} %copy-done.23, bf16[96,384]{1,0:T(8,128)(2,1)} %copy-done.24, bf16[96,384]{1,0:T(8,128)(2,1)} %copy-done.25, bf16[16,96,384]{2,1,0:T(8,128)(2,1)} %copy-done), custom_call_target="tpu_custom_call" | custom-call | tf_op jit(solution)/shard_map/pallas_call | solution.py:468
  157.4 6.6 %all-to-all-start.5 = ((bf16[8,2,16,384]{3,2,1,0:T(8,128)(2,1)}), bf16[8,2,16,384]{3,2,1,0:T(8,128)(2,1)S(1)}, u32[]{:S(2)}, u32[]{:S(2)}) async-start(bf16[8,2,16,384]{3,2,1,0:T(8,128)(2,1)} %shard_map.95), calls=%async_computation.5 | async-start | bytes 393216 | tf_op jit(solution)/shard_map/all_to_all | solution.py:562
  163.9 3.5 %shard_map.96 = bf16[256,768]{1,0:T(8,128)(2,1)} custom-call(s32[4]{0:T(128)} %pad_add_fusion.pos, bf16[2,256,384]{2,1,0:T(8,128)(2,1)} %get-tuple-element.113.att_own, bf16[2,256,384]{2,1,0:T(8,128)(2,1)} %copy-done.5, bf16[768,768]{1,0:T(8,128)(2,1)} %w_oth.1, bf16[768,768]{1,0:T(8,128)(2,1)} %w_oth.1), custom_call_target="tpu_custom_call" | custom-call | tf_op jit(solution)/shard_map/pallas_call | solution.py:310
  167.4 6.0 %all-to-all-done.5.terms = bf16[8,2,16,384]{3,2,1,0:T(8,128)(2,1)S(1)} async-done(((bf16[8,2,16,384]{3,2,1,0:T(8,128)(2,1)}), bf16[8,2,16,384]{3,2,1,0:T(8,128)(2,1)S(1)}, u32[]{:S(2)}, u32[]{:S(2)}) %all-to-all-start.5) | async-done | bytes 196640 | tf_op jit(solution)/shard_map/all_to_all | solution.py:562
  174.0 2.2 %shard_map.97 = (bf16[16,384]{1,0:T(8,128)(2,1)}, bf16[16,384]{1,0:T(8,128)(2,1)}) custom-call(s32[4]{0:T(128)} %pad_add_fusion.pos, bf16[8,2,16,384]{3,2,1,0:T(8,128)(2,1)} %copy-done.9), custom_call_target="tpu_custom_call" | custom-call | tf_op jit(solution)/shard_map/pallas_call | solution.py:479
  176.3 3.2 %collective-permute-start.19 = (bf16[16,384]{1,0:T(8,128)(2,1)}, bf16[16,384]{1,0:T(8,128)(2,1)S(1)}, u32[]{:S(2)}, u32[]{:S(2)}) collective-permute-start(bf16[16,384]{1,0:T(8,128)(2,1)} %get-tuple-element.119), channel_id=1, source_target_pairs={{0,2},{1,3},{2,0},{3,1},{4,6},{5,7},{6,4},{7,5},{8,10},{9,11},{10,... | collective-permute-start | bytes 36872 | tf_op jit(solution)/shard_map/ppermute | solution.py:517
  179.5 2.0 %collective-permute-start.20 = (bf16[16,384]{1,0:T(8,128)(2,1)}, bf16[16,384]{1,0:T(8,128)(2,1)S(1)}, u32[]{:S(2)}, u32[]{:S(2)}) collective-permute-start(bf16[16,384]{1,0:T(8,128)(2,1)} %get-tuple-element.119), channel_id=1, source_target_pairs={{0,3},{1,2},{2,1},{3,0},{4,7},{5,6},{6,5},{7,4},{8,11},{9,10},{10,... | collective-permute-start | bytes 36872 | tf_op jit(solution)/shard_map/ppermute | solution.py:517
  181.4 2.9 %collective-permute-done.20.from_both = bf16[16,384]{1,0:T(8,128)(2,1)S(1)} collective-permute-done((bf16[16,384]{1,0:T(8,128)(2,1)}, bf16[16,384]{1,0:T(8,128)(2,1)S(1)}, u32[]{:S(2)}, u32[]{:S(2)}) %collective-permute-start.20) | collective-permute-done | bytes 12320 | tf_op jit(solution)/shard_map/ppermute | solution.py:517
  184.9 2.1 %shard_map.98 = (f32[6,2304]{1,0:T(8,128)}, f32[6,768]{1,0:T(8,128)}) custom-call(s32[4]{0:T(128)} %pad_add_fusion.pos, bf16[16,384]{1,0:T(8,128)(2,1)} %get-tuple-element.118.own, bf16[16,384]{1,0:T(8,128)(2,1)} %copy-done.26, bf16[16,384]{1,0:T(8,128)(2,1)} %copy-done.27, bf16[16,384]{1,0:T(8,128)(2,1)} %copy-done.28), custom_call_target="tpu_custom_call" | custom-call | tf_op jit(solution)/shard_map/pallas_call | solution.py:503
  (103 shorter events, 11.3 us)
Async XLA Ops:
  0.6 4.9 %collective-permute-start = (bf16[256,768]{1,0:T(8,128)(2,1)}, bf16[256,768]{1,0:T(8,128)(2,1)S(1)}, u32[]{:S(2)}, u32[]{:S(2)}) collective-permute-start(bf16[256,768]{1,0:T(8,128)(2,1)} %bitcast.13), channel_id=1, source_target_pairs={{0,2},{2,0},{1,3},{3,1},{4,6},{6,4},{5,7},{7,5},{8,10},{10,8},{9,1... | collective-permute-start | bytes 1179656 | tf_op jit(solution)/shard_map/ppermute | solution.py:513
  4.0 23.5 %collective-permute-start.2 = (bf16[256,768]{1,0:T(8,128)(2,1)}, bf16[256,768]{1,0:T(8,128)(2,1)S(1)}, u32[]{:S(2)}, u32[]{:S(2)}) collective-permute-start(bf16[256,768]{1,0:T(8,128)(2,1)} %bitcast.16), channel_id=1, source_target_pairs={{0,2},{2,0},{1,3},{3,1},{4,6},{6,4},{5,7},{7,5},{8,10},{10,8},{9,1... | collective-permute-start | bytes 1179656 | tf_op jit(solution)/shard_map/ppermute | solution.py:513
  11.3 16.3 %all-to-all-start = ((bf16[8,2,16,384]{3,2,1,0:T(8,128)(2,1)}), bf16[8,2,16,384]{3,2,1,0:T(8,128)(2,1)S(1)}, u32[]{:S(2)}, u32[]{:S(2)}) async-start(bf16[8,2,16,384]{3,2,1,0:T(8,128)(2,1)} %get-tuple-element.63), calls=%async_computation | async-start | bytes 393216 | tf_op jit(solution)/shard_map/all_to_all | solution.py:535
  17.7 6.0 %collective-permute-start.1 = (bf16[2,128,384]{2,1,0:T(8,128)(2,1)}, bf16[2,128,384]{2,1,0:T(8,128)(2,1)S(1)}, u32[]{:S(2)}, u32[]{:S(2)}) collective-permute-start(bf16[2,128,384]{2,1,0:T(8,128)(2,1)} %get-tuple-element.64.own), channel_id=1, source_target_pairs={{0,4},{4,0},{1,5},{5,1},{2,6},{6,2},{3,7},{7,3},{8,12},{12,8},{9,1... | collective-permute-start | bytes 589832 | tf_op jit(solution)/shard_map/ppermute | solution.py:513
  27.5 8.4 %copy-start.33 = (bf16[2,2,64,384]{3,2,1,0:T(8,128)(2,1)S(1)}, bf16[2,2,64,384]{3,2,1,0:T(8,128)(2,1)}, u32[]{:S(2)}) copy-start(bf16[2,2,64,384]{3,2,1,0:T(8,128)(2,1)} %get-tuple-element.72) | copy-start | bytes 589828
  27.5 9.8 %copy-start.36 = (bf16[2,2,32,384]{3,2,1,0:T(8,128)(2,1)S(1)}, bf16[2,2,32,384]{3,2,1,0:T(8,128)(2,1)}, u32[]{:S(2)}) copy-start(bf16[2,2,32,384]{3,2,1,0:T(8,128)(2,1)} %get-tuple-element.73) | copy-start | bytes 294916
  27.5 12.3 %copy-start.6 = (bf16[256,768]{1,0:T(8,128)(2,1)}, bf16[256,768]{1,0:T(8,128)(2,1)S(1)}, u32[]{:S(2)}) copy-start(bf16[256,768]{1,0:T(8,128)(2,1)S(1)} %collective-permute-done.2.ct_oth) | copy-start | bytes 1179652
  30.8 19.4 %all-to-all-start.1 = ((bf16[8,2,48,384]{3,2,1,0:T(8,128)(2,1)}), bf16[8,2,48,384]{3,2,1,0:T(8,128)(2,1)S(1)}, u32[]{:S(2)}, u32[]{:S(2)}) async-start(bf16[8,2,48,384]{3,2,1,0:T(8,128)(2,1)} %shard_map.87), calls=%async_computation.1 | async-start | bytes 1179648 | tf_op jit(solution)/shard_map/all_to_all | solution.py:540
  35.9 14.3 %collective-permute-start.3 = (bf16[2,2,64,384]{3,2,1,0:T(8,128)(2,1)S(1)}, bf16[2,2,64,384]{3,2,1,0:T(8,128)(2,1)S(1)}, u32[]{:S(2)}, u32[]{:S(2)}) collective-permute-start(bf16[2,2,64,384]{3,2,1,0:T(8,128)(2,1)S(1)} %copy-done.33), channel_id=1, source_target_pairs={{0,8},{8,0},{16,24},{24,16},{1,9},{9,1},{17,25},{25,17},{2,10},{10... | collective-permute-start | bytes 589832 | tf_op jit(solution)/shard_map/ppermute | solution.py:517
  37.3 12.9 %collective-permute-start.4 = (bf16[2,2,32,384]{3,2,1,0:T(8,128)(2,1)S(1)}, bf16[2,2,32,384]{3,2,1,0:T(8,128)(2,1)S(1)}, u32[]{:S(2)}, u32[]{:S(2)}) collective-permute-start(bf16[2,2,32,384]{3,2,1,0:T(8,128)(2,1)S(1)} %copy-done.36), channel_id=1, source_target_pairs={{0,16},{8,24},{16,0},{24,8},{1,17},{9,25},{17,1},{25,9},{2,18},{10... | collective-permute-start | bytes 294920 | tf_op jit(solution)/shard_map/ppermute | solution.py:517
  39.7 10.5 %collective-permute-start.5 = (bf16[2,2,32,384]{3,2,1,0:T(8,128)(2,1)S(1)}, bf16[2,2,32,384]{3,2,1,0:T(8,128)(2,1)S(1)}, u32[]{:S(2)}, u32[]{:S(2)}) collective-permute-start(bf16[2,2,32,384]{3,2,1,0:T(8,128)(2,1)S(1)} %copy-done.36), channel_id=1, source_target_pairs={{0,24},{8,16},{16,8},{24,0},{1,25},{9,17},{17,9},{25,1},{2,26},{10... | collective-permute-start | bytes 294920 | tf_op jit(solution)/shard_map/ppermute | solution.py:517
  69.1 3.7 %copy-start.4 = (bf16[2,256,384]{2,1,0:T(8,128)(2,1)S(1)}, bf16[2,256,384]{2,1,0:T(8,128)(2,1)}, u32[]{:S(2)}) copy-start(bf16[2,256,384]{2,1,0:T(8,128)(2,1)} %get-tuple-element.113.att_own) | copy-start | bytes 1179652
  69.1 7.1 %copy-start.32 = (bf16[2,2,64,384]{3,2,1,0:T(8,128)(2,1)S(1)}, bf16[2,2,64,384]{3,2,1,0:T(8,128)(2,1)}, u32[]{:S(2)}) copy-start(bf16[2,2,64,384]{3,2,1,0:T(8,128)(2,1)} %get-tuple-element.76) | copy-start | bytes 589828
  69.1 8.5 %copy-start.35 = (bf16[2,2,32,384]{3,2,1,0:T(8,128)(2,1)S(1)}, bf16[2,2,32,384]{3,2,1,0:T(8,128)(2,1)}, u32[]{:S(2)}) copy-start(bf16[2,2,32,384]{3,2,1,0:T(8,128)(2,1)} %get-tuple-element.77) | copy-start | bytes 294916
  69.1 10.9 %copy-start.34 = (bf16[2,2,32,384]{3,2,1,0:T(8,128)(2,1)S(1)}, bf16[2,2,32,384]{3,2,1,0:T(8,128)(2,1)}, u32[]{:S(2)}) copy-start(bf16[2,2,32,384]{3,2,1,0:T(8,128)(2,1)} %get-tuple-element.78) | copy-start | bytes 294916
  69.2 18.7 %all-to-all-start.2 = ((bf16[8,2,48,384]{3,2,1,0:T(8,128)(2,1)}), bf16[8,2,48,384]{3,2,1,0:T(8,128)(2,1)S(1)}, u32[]{:S(2)}, u32[]{:S(2)}) async-start(bf16[8,2,48,384]{3,2,1,0:T(8,128)(2,1)} %get-tuple-element.75), calls=%async_computation.2 | async-start | bytes 1179648 | tf_op jit(solution)/shard_map/all_to_all | solution.py:544
  72.9 7.3 %collective-permute-start.9 = (bf16[2,256,384]{2,1,0:T(8,128)(2,1)S(1)}, bf16[2,256,384]{2,1,0:T(8,128)(2,1)S(1)}, u32[]{:S(2)}, u32[]{:S(2)}) collective-permute-start(bf16[2,256,384]{2,1,0:T(8,128)(2,1)S(1)} %copy-done.4), channel_id=1, source_target_pairs={{0,2},{2,0},{1,3},{3,1},{4,6},{6,4},{5,7},{7,5},{8,10},{10,8},{9,1... | collective-permute-start | bytes 1179656 | tf_op jit(solution)/shard_map/ppermute | solution.py:513
  76.2 11.6 %collective-permute-start.6 = (bf16[2,2,64,384]{3,2,1,0:T(8,128)(2,1)S(1)}, bf16[2,2,64,384]{3,2,1,0:T(8,128)(2,1)S(1)}, u32[]{:S(2)}, u32[]{:S(2)}) collective-permute-start(bf16[2,2,64,384]{3,2,1,0:T(8,128)(2,1)S(1)} %copy-done.32), channel_id=1, source_target_pairs={{0,8},{8,0},{16,24},{24,16},{1,9},{9,1},{17,25},{25,17},{2,10},{10... | collective-permute-start | bytes 589832 | tf_op jit(solution)/shard_map/ppermute | solution.py:517
  77.6 9.7 %collective-permute-start.7 = (bf16[2,2,32,384]{3,2,1,0:T(8,128)(2,1)S(1)}, bf16[2,2,32,384]{3,2,1,0:T(8,128)(2,1)S(1)}, u32[]{:S(2)}, u32[]{:S(2)}) collective-permute-start(bf16[2,2,32,384]{3,2,1,0:T(8,128)(2,1)S(1)} %copy-done.35), channel_id=1, source_target_pairs={{0,16},{8,24},{16,0},{24,8},{1,17},{9,25},{17,1},{25,9},{2,18},{10... | collective-permute-start | bytes 294920 | tf_op jit(solution)/shard_map/ppermute | solution.py:517
  80.1 7.8 %collective-permute-start.8 = (bf16[2,2,32,384]{3,2,1,0:T(8,128)(2,1)S(1)}, bf16[2,2,32,384]{3,2,1,0:T(8,128)(2,1)S(1)}, u32[]{:S(2)}, u32[]{:S(2)}) collective-permute-start(bf16[2,2,32,384]{3,2,1,0:T(8,128)(2,1)S(1)} %copy-done.34), channel_id=1, source_target_pairs={{0,24},{8,16},{16,8},{24,0},{1,25},{9,17},{17,9},{25,1},{2,26},{10... | collective-permute-start | bytes 294920 | tf_op jit(solution)/shard_map/ppermute | solution.py:517
  86.4 11.4 %copy-start.31 = (bf16[2,2,96,384]{3,2,1,0:T(8,128)(2,1)S(1)}, bf16[2,2,96,384]{3,2,1,0:T(8,128)(2,1)}, u32[]{:S(2)}) copy-start(bf16[2,2,96,384]{3,2,1,0:T(8,128)(2,1)} %get-tuple-element.85) | copy-start | bytes 884740
  86.4 11.5 %copy-start.30 = (bf16[2,2,96,384]{3,2,1,0:T(8,128)(2,1)S(1)}, bf16[2,2,96,384]{3,2,1,0:T(8,128)(2,1)}, u32[]{:S(2)}) copy-start(bf16[2,2,96,384]{3,2,1,0:T(8,128)(2,1)} %get-tuple-element.86) | copy-start | bytes 884740
  86.4 13.8 %copy-start.29 = (bf16[2,2,96,384]{3,2,1,0:T(8,128)(2,1)S(1)}, bf16[2,2,96,384]{3,2,1,0:T(8,128)(2,1)}, u32[]{:S(2)}) copy-start(bf16[2,2,96,384]{3,2,1,0:T(8,128)(2,1)} %get-tuple-element.87) | copy-start | bytes 884740
  87.3 14.4 %copy-start.19 = (bf16[2,2,32,384]{3,2,1,0:T(8,128)(2,1)}, bf16[2,2,32,384]{3,2,1,0:T(8,128)(2,1)S(1)}, u32[]{:S(2)}) copy-start(bf16[2,2,32,384]{3,2,1,0:T(8,128)(2,1)S(1)} %collective-permute-done.7.far_a) | copy-start | bytes 294916
  87.9 13.9 %copy-start.20 = (bf16[2,2,32,384]{3,2,1,0:T(8,128)(2,1)}, bf16[2,2,32,384]{3,2,1,0:T(8,128)(2,1)S(1)}, u32[]{:S(2)}) copy-start(bf16[2,2,32,384]{3,2,1,0:T(8,128)(2,1)S(1)} %collective-permute-done.8.far_b) | copy-start | bytes 294916
  87.9 13.9 %copy-start.17 = (bf16[2,2,64,384]{3,2,1,0:T(8,128)(2,1)}, bf16[2,2,64,384]{3,2,1,0:T(8,128)(2,1)S(1)}, u32[]{:S(2)}) copy-start(bf16[2,2,64,384]{3,2,1,0:T(8,128)(2,1)S(1)} %collective-permute-done.6.near) | copy-start | bytes 589828
  91.4 26.7 %all-to-all-start.3 = ((bf16[8,2,16,384]{3,2,1,0:T(8,128)(2,1)}), bf16[8,2,16,384]{3,2,1,0:T(8,128)(2,1)S(1)}, u32[]{:S(2)}, u32[]{:S(2)}) async-start(bf16[8,2,16,384]{3,2,1,0:T(8,128)(2,1)} %shard_map.90), calls=%async_computation.3 | async-start | bytes 393216 | tf_op jit(solution)/shard_map/all_to_all | solution.py:549
  97.8 7.6 %collective-permute-start.10 = (bf16[2,2,96,384]{3,2,1,0:T(8,128)(2,1)S(1)}, bf16[2,2,96,384]{3,2,1,0:T(8,128)(2,1)S(1)}, u32[]{:S(2)}, u32[]{:S(2)}) collective-permute-start(bf16[2,2,96,384]{3,2,1,0:T(8,128)(2,1)S(1)} %copy-done.31), channel_id=1, source_target_pairs={{0,8},{8,0},{16,24},{24,16},{1,9},{9,1},{17,25},{25,17},{2,10},{10... | collective-permute-start | bytes 884744 | tf_op jit(solution)/shard_map/ppermute | solution.py:517
  97.9 12.6 %collective-permute-start.11 = (bf16[2,2,96,384]{3,2,1,0:T(8,128)(2,1)S(1)}, bf16[2,2,96,384]{3,2,1,0:T(8,128)(2,1)S(1)}, u32[]{:S(2)}, u32[]{:S(2)}) collective-permute-start(bf16[2,2,96,384]{3,2,1,0:T(8,128)(2,1)S(1)} %copy-done.30), channel_id=1, source_target_pairs={{0,16},{8,24},{16,0},{24,8},{1,17},{9,25},{17,1},{25,9},{2,18},{10... | collective-permute-start | bytes 884744 | tf_op jit(solution)/shard_map/ppermute | solution.py:517
  100.1 14.4 %collective-permute-start.12 = (bf16[2,2,96,384]{3,2,1,0:T(8,128)(2,1)S(1)}, bf16[2,2,96,384]{3,2,1,0:T(8,128)(2,1)S(1)}, u32[]{:S(2)}, u32[]{:S(2)}) collective-permute-start(bf16[2,2,96,384]{3,2,1,0:T(8,128)(2,1)S(1)} %copy-done.29), channel_id=1, source_target_pairs={{0,24},{8,16},{16,8},{24,0},{1,25},{9,17},{17,9},{25,1},{2,26},{10... | collective-permute-start | bytes 884744 | tf_op jit(solution)/shard_map/ppermute | solution.py:517
  104.7 13.4 %collective-permute-start.13 = (bf16[2,128,384]{2,1,0:T(8,128)(2,1)}, bf16[2,128,384]{2,1,0:T(8,128)(2,1)S(1)}, u32[]{:S(2)}, u32[]{:S(2)}) collective-permute-start(bf16[2,128,384]{2,1,0:T(8,128)(2,1)} %get-tuple-element.99), channel_id=1, source_target_pairs={{0,4},{4,0},{1,5},{5,1},{2,6},{6,2},{3,7},{7,3},{8,12},{12,8},{9,1... | collective-permute-start | bytes 589832 | tf_op jit(solution)/shard_map/ppermute | solution.py:513
  105.4 9.2 %copy-start.13 = (bf16[2,2,96,384]{3,2,1,0:T(8,128)(2,1)}, bf16[2,2,96,384]{3,2,1,0:T(8,128)(2,1)S(1)}, u32[]{:S(2)}) copy-start(bf16[2,2,96,384]{3,2,1,0:T(8,128)(2,1)S(1)} %collective-permute-done.10.t1) | copy-start | bytes 884740
  110.5 4.0 %copy-start.14 = (bf16[2,2,96,384]{3,2,1,0:T(8,128)(2,1)}, bf16[2,2,96,384]{3,2,1,0:T(8,128)(2,1)S(1)}, u32[]{:S(2)}) copy-start(bf16[2,2,96,384]{3,2,1,0:T(8,128)(2,1)S(1)} %collective-permute-done.11.t2) | copy-start | bytes 884740
  124.8 5.5 %copy-start.7 = (bf16[2,256,1152]{2,1,0:T(8,128)(2,1)S(1)}, bf16[2,256,1152]{2,1,0:T(8,128)(2,1)}, u32[]{:S(2)}) copy-start(bf16[2,256,1152]{2,1,0:T(8,128)(2,1)} %get-tuple-element.102) | copy-start | bytes 3538948
  124.8 27.7 %all-to-all-start.4 = ((bf16[16,96,384]{2,1,0:T(8,128)(2,1)}), bf16[16,96,384]{2,1,0:T(8,128)(2,1)S(1)}, u32[]{:S(2)}, u32[]{:S(2)}) async-start(bf16[16,96,384]{2,1,0:T(8,128)(2,1)} %bitcast.19), calls=%async_computation.4 | async-start | bytes 2359296 | tf_op jit(solution)/shard_map/all_to_all | solution.py:554
  130.3 3.8 %copy-start.39 = (bf16[96,384]{1,0:T(8,128)(2,1)S(1)}, bf16[96,384]{1,0:T(8,128)(2,1)}, u32[]{:S(2)}) copy-start(bf16[96,384]{1,0:T(8,128)(2,1)} %get-tuple-element.104) | copy-start | bytes 221188
  130.3 6.9 %copy-start.38 = (bf16[96,384]{1,0:T(8,128)(2,1)S(1)}, bf16[96,384]{1,0:T(8,128)(2,1)}, u32[]{:S(2)}) copy-start(bf16[96,384]{1,0:T(8,128)(2,1)} %get-tuple-element.105) | copy-start | bytes 221188
  130.3 7.2 %copy-start.37 = (bf16[96,384]{1,0:T(8,128)(2,1)S(1)}, bf16[96,384]{1,0:T(8,128)(2,1)}, u32[]{:S(2)}) copy-start(bf16[96,384]{1,0:T(8,128)(2,1)} %get-tuple-element.106) | copy-start | bytes 221188
  131.3 6.9 %collective-permute-start.14 = (bf16[256,1152]{1,0:T(8,128)(2,1)S(1)}, bf16[256,1152]{1,0:T(8,128)(2,1)S(1)}, u32[]{:S(2)}, u32[]{:S(2)}) collective-permute-start(bf16[256,1152]{1,0:T(8,128)(2,1)S(1)} %get-tuple-element.122), channel_id=1, source_target_pairs={{0,2},{2,0},{1,3},{3,1},{4,6},{6,4},{5,7},{7,5},{8,10},{10,8},{9,1... | collective-permute-start | bytes 1769480 | tf_op jit(solution)/shard_map/ppermute | solution.py:513
  134.1 15.8 %collective-permute-start.15 = (bf16[96,384]{1,0:T(8,128)(2,1)S(1)}, bf16[96,384]{1,0:T(8,128)(2,1)S(1)}, u32[]{:S(2)}, u32[]{:S(2)}) collective-permute-start(bf16[96,384]{1,0:T(8,128)(2,1)S(1)} %copy-done.39), channel_id=1, source_target_pairs={{0,1},{1,0},{4,5},{5,4},{2,3},{3,2},{6,7},{7,6},{8,9},{9,8},{12,13... | collective-permute-start | bytes 221192 | tf_op jit(solution)/shard_map/ppermute | solution.py:517
  137.2 14.4 %collective-permute-start.16 = (bf16[96,384]{1,0:T(8,128)(2,1)S(1)}, bf16[96,384]{1,0:T(8,128)(2,1)S(1)}, u32[]{:S(2)}, u32[]{:S(2)}) collective-permute-start(bf16[96,384]{1,0:T(8,128)(2,1)S(1)} %copy-done.38), channel_id=1, source_target_pairs={{0,4},{1,5},{4,0},{5,1},{2,6},{3,7},{6,2},{7,3},{8,12},{9,13},{12,... | collective-permute-start | bytes 221192 | tf_op jit(solution)/shard_map/ppermute | solution.py:517
  137.5 15.0 %collective-permute-start.17 = (bf16[96,384]{1,0:T(8,128)(2,1)S(1)}, bf16[96,384]{1,0:T(8,128)(2,1)S(1)}, u32[]{:S(2)}, u32[]{:S(2)}) collective-permute-start(bf16[96,384]{1,0:T(8,128)(2,1)S(1)} %copy-done.37), channel_id=1, source_target_pairs={{0,5},{1,4},{4,1},{5,0},{2,7},{3,6},{6,3},{7,2},{8,13},{9,12},{12,... | collective-permute-start | bytes 221192 | tf_op jit(solution)/shard_map/ppermute | solution.py:517
  157.4 16.0 %all-to-all-start.5 = ((bf16[8,2,16,384]{3,2,1,0:T(8,128)(2,1)}), bf16[8,2,16,384]{3,2,1,0:T(8,128)(2,1)S(1)}, u32[]{:S(2)}, u32[]{:S(2)}) async-start(bf16[8,2,16,384]{3,2,1,0:T(8,128)(2,1)} %shard_map.95), calls=%async_computation.5 | async-start | bytes 393216 | tf_op jit(solution)/shard_map/all_to_all | solution.py:562
  176.2 5.2 %collective-permute-start.18 = (bf16[16,384]{1,0:T(8,128)(2,1)}, bf16[16,384]{1,0:T(8,128)(2,1)S(1)}, u32[]{:S(2)}, u32[]{:S(2)}) collective-permute-start(bf16[16,384]{1,0:T(8,128)(2,1)} %get-tuple-element.118.own), channel_id=1, source_target_pairs={{0,1},{1,0},{2,3},{3,2},{4,5},{5,4},{6,7},{7,6},{8,9},{9,8},{10,11... | collective-permute-start | bytes 36872 | tf_op jit(solution)/shard_map/ppermute | solution.py:517
  176.3 5.2 %collective-permute-start.19 = (bf16[16,384]{1,0:T(8,128)(2,1)}, bf16[16,384]{1,0:T(8,128)(2,1)S(1)}, u32[]{:S(2)}, u32[]{:S(2)}) collective-permute-start(bf16[16,384]{1,0:T(8,128)(2,1)} %get-tuple-element.119), channel_id=1, source_target_pairs={{0,2},{1,3},{2,0},{3,1},{4,6},{5,7},{6,4},{7,5},{8,10},{9,11},{10,... | collective-permute-start | bytes 36872 | tf_op jit(solution)/shard_map/ppermute | solution.py:517
  179.5 4.8 %collective-permute-start.20 = (bf16[16,384]{1,0:T(8,128)(2,1)}, bf16[16,384]{1,0:T(8,128)(2,1)S(1)}, u32[]{:S(2)}, u32[]{:S(2)}) collective-permute-start(bf16[16,384]{1,0:T(8,128)(2,1)} %get-tuple-element.119), channel_id=1, source_target_pairs={{0,3},{1,2},{2,1},{3,0},{4,7},{5,6},{6,5},{7,4},{8,11},{9,10},{10,... | collective-permute-start | bytes 36872 | tf_op jit(solution)/shard_map/ppermute | solution.py:517
  181.4 2.9 %copy-start.26 = (bf16[16,384]{1,0:T(8,128)(2,1)}, bf16[16,384]{1,0:T(8,128)(2,1)S(1)}, u32[]{:S(2)}) copy-start(bf16[16,384]{1,0:T(8,128)(2,1)S(1)} %collective-permute-done.18.from_dp) | copy-start | bytes 36868
  181.4 2.9 %copy-start.27 = (bf16[16,384]{1,0:T(8,128)(2,1)}, bf16[16,384]{1,0:T(8,128)(2,1)S(1)}, u32[]{:S(2)}) copy-start(bf16[16,384]{1,0:T(8,128)(2,1)S(1)} %collective-permute-done.19.from_core) | copy-start | bytes 36868
  (19 other events, 16.3 us)

commit v5 on v4

--- a/solution.py
+++ b/solution.py
@@ -47,22 +47,11 @@
     return (dot(pair_matrix(rows, node.shape[0], valid), node) * HALF_ROOT).astype(BF16)
 
 
-def spread(grad, rows, valid=None):
-    height = grad.shape[0]
-    r, k = iota((rows, 2 * height), 0), iota((rows, 2 * height), 1)
-    hot = (r >> 1) == (k & (height - 1))
-    if valid is not None:
-        hot = hot & (r < valid)
-    high = grad.astype(BF16)
-    low = (grad - high.astype(F32)).astype(BF16)
-    return dot(hot.astype(BF16), jnp.concatenate([high, low], axis=0)) * HALF_ROOT
-
-
 def whole(*shape):
     return pl.BlockSpec(shape, lambda *_: (0,) * len(shape))
 
 
-def call(body, grid, ins, outs, scratch=()):
+def call(body, grid, ins, outs, scratch=(), aliases={}):
     return pl.pallas_call(
         body,
         grid_spec=pltpu.PrefetchScalarGridSpec(
@@ -73,11 +62,12 @@
             scratch_shapes=list(scratch),
         ),
         out_shape=[jax.ShapeDtypeStruct(shape, kind) for _, (shape, kind) in outs],
+        input_output_aliases=dict(aliases),
         compiler_params=pltpu.CompilerParams(vmem_limit_bytes=VMEM),
     )
 
 
-def tree_body(pos, x_own, x_oth, wk, wv, kv_out, n1_out, n2_out, zs_out):
+def tree_body(pos, x_own, x_oth, wk, wv, kv_out, n1_out, n2_out, n3_out, n4_out, zs_out):
     c, z = pos[0], pos[1]
     for e, x in ((c, x_own), (1 - c, x_oth)):
         kv_out[e, 0] = dot(x[...], wk[...]).astype(BF16)
@@ -97,7 +87,11 @@
         halves.append(coarsen(n1))
     n2 = jnp.concatenate(halves, axis=0)
     store(n2_out)(n2)
-    n5 = coarsen(coarsen(coarsen(n2)))
+    n3 = coarsen(n2)
+    store(n3_out)(n3)
+    n4 = coarsen(n3)
+    store(n4_out)(n4)
+    n5 = coarsen(n4)
     n6 = coarsen(n5, 16, 8)
     n7 = coarsen(n6, 16, 4)
     store(zs_out, z)(jnp.zeros_like(n5))
@@ -110,7 +104,7 @@
 
 def tree(pos, x_own, x_oth, w_qkv):
     col = lambda part: pl.BlockSpec((D, H), lambda i, s: (0, 2 * part + s[0]))
-    outs = [(2, 2, TOK, H), (2, 2, NR, H), (2, NR, H), (ZN, 2, 16, H)]
+    outs = [(2, 2, TOK, H), (2, 2, NR, H), (2, NR, H), (2, 64, H), (2, 32, H), (ZN, 2, 16, H)]
     return call(
         tree_body,
         (1,),
@@ -136,41 +130,6 @@
         + [pl.BlockSpec((D, H), lambda i, s: (0, s[0])), pl.BlockSpec((H, D), lambda i, s: (s[0], 0)), whole(D, D)],
         [(whole(*shape), (shape, BF16)) for shape in outs],
     )(pos, x_own, x_oth, ct_own, ct_oth, w_qkv, w_out, perm)
-
-
-def pair_body(pos, own, oth, near_out, far_out):
-    y = pos[2] & 1
-    for p in range(2):
-        for half, n2 in ((y, own), (1 - y, oth)):
-            near_out[half, p] = coarsen(n2[p])
-            far_out[half, p] = coarsen(near_out[half, p])
-
-
-def pair_nodes(pos, own, oth):
-    outs = [(2, 2, 64, H), (2, 2, 32, H)]
-    return call(
-        pair_body, (1,), [whole(2, NR, H)] * 2, [(whole(*shape), (shape, BF16)) for shape in outs]
-    )(pos, own, oth)
-
-
-def pair_back_body(pos, near, far_a, far_b, dy, keep_out, send_out):
-    y = pos[2] & 1
-    for p in range(2):
-        for half, out in ((y, None), (1 - y, send_out)):
-            grad = near[half, p].astype(F32) + spread(far_a[half, p].astype(F32) + far_b[half, p].astype(F32), 64)
-            if out is None:
-                keep_out[p] = grad
-            else:
-                out[p] = (dy[p].astype(F32) + spread(grad, NR)).astype(BF16)
-
-
-def pair_back(pos, near, far_a, far_b, dy):
-    return call(
-        pair_back_body,
-        (1,),
-        [whole(2, 2, 64, H), whole(2, 2, 32, H), whole(2, 2, 32, H), whole(2, NR, H)],
-        [(whole(2, 64, H), ((2, 64, H), F32)), (whole(2, NR, H), ((2, NR, H), BF16))],
-    )(pos, near, far_a, far_b, dy)
 
 
 def z_source(z, rows_axis, shape):
@@ -199,19 +158,14 @@
     )(pos, zr)[0]
 
 
-def attention_body(pos, q, ag, kv, n1, yr, near, far_a, far_b, xr, att_out, dq_out, dkv_out, dn1_out, dy_out, dnear_out, dfar_a_out, dfar_b_out, dx_out, keys, keys_t, s_ref, dw_ref, w_ref, ds_ref, drem):
+def attention_body(pos, q, ag, kv, n1, yr, wr, wy, xr, att_out, dq_out, dkv_out, dn1_out, dy_out, dw_out, dx_out, keys, keys_t, s_ref, dw_ref, w_ref, ds_ref, drem):
     for p in range(2):
         for e in range(2):
             keys[e, p, :256] = kv[e, p]
             keys[e, p, 256:384] = n1[1 - e, p]
             keys[e, p, 384:512] = yr[p]
-            for half in range(2):
-                start = 512 + 64 * half
-                keys[e, p, start : start + 64] = near[half, p]
-                start = 640 + 32 * half
-                keys[e, p, start : start + 32] = far_a[half, p]
-                start = 704 + 32 * half
-                keys[e, p, start : start + 32] = far_b[half, p]
+            keys[e, p, 512:640] = wr[p]
+            keys[e, p, 640:768] = wy[p]
             for slot in range(8):
                 start = 768 + ZR * slot
                 keys[e, p, start : start + ZR] = xr[slot, p]
@@ -266,38 +220,33 @@
                 drem[p] = drem[p] + grad[384:]
     for p in range(2):
         rows = drem[p].astype(BF16)
-        dy_out[p] = rows[:128]
-        for half in range(2):
-            start = 128 + 64 * half
-            dnear_out[half, p] = rows[start : start + 64]
-            start = 256 + 32 * half
-            dfar_a_out[half, p] = rows[start : start + 32]
-            start = 320 + 32 * half
-            dfar_b_out[half, p] = rows[start : start + 32]
+        dy_out[p, :NR] = rows[:128]
+        dy_out[p, NR:] = rows[256:384]
+        dw_out[p] = drem[p, 128:256]
         for slot in range(8):
             start = 384 + ZR * slot
             dx_out[slot, p] = rows[start : start + ZR]
 
 
-def attention(pos, q, ag, kv, n1, yr, near, far_a, far_b, xr):
+def attention(pos, q, ag, kv, n1, yr, wr, wy, xr):
     def cut(*lead):
         return pl.BlockSpec(lead + (128,), lambda i, s: (0,) * len(lead) + (i,))
 
     outs = [
-        ((2, TOK), BF16), ((2, TOK), BF16), ((2, 2, TOK), F32), ((2, 2, NR), F32), ((2, NR), BF16),
-        ((2, 2, 64), BF16), ((2, 2, 32), BF16), ((2, 2, 32), BF16), ((8, 2, ZR), BF16),
+        ((2, TOK), BF16), ((2, TOK), BF16), ((2, 2, TOK), F32), ((2, 2, NR), F32), ((2, 2 * NR), BF16),
+        ((2, NR), F32), ((8, 2, ZR), BF16),
     ]
     n = 1152
     return call(
         attention_body,
         (H // 128,),
-        [cut(2, TOK), cut(2, TOK), cut(2, 2, TOK), cut(2, 2, NR), cut(2, NR), cut(2, 2, 64), cut(2, 2, 32), cut(2, 2, 32), cut(8, 2, ZR)],
+        [cut(2, TOK), cut(2, TOK), cut(2, 2, TOK), cut(2, 2, NR), cut(2, NR), cut(2, NR), cut(2, NR), cut(8, 2, ZR)],
         [(cut(*lead), (lead + (H,), kind)) for lead, kind in outs],
         [
             pltpu.VMEM((2, 2, n, 128), BF16), pltpu.VMEM((2, 2, 128, n), BF16), pltpu.VMEM((2, n, TOK), F32), pltpu.VMEM((2, n, TOK), F32),
             pltpu.VMEM((2, n, TOK), BF16), pltpu.VMEM((2, n, TOK), BF16), pltpu.VMEM((2, 768, 128), F32),
         ],
-    )(pos, q, ag, kv, n1, yr, near, far_a, far_b, xr)
+    )(pos, q, ag, kv, n1, yr, wr, wy, xr)
 
 
 def output_body(pos, att_own, att_oth, w_own, w_oth, out):
@@ -315,51 +264,33 @@
     )(pos, att_own, att_oth, w_out, w_out)[0]
 
 
-def terms_body(pos, att_own, att_oth, ct_own, ct_oth, dq, xt, p_own, p_oth, *rest):
-    c, x = pos[0], pos[2] >> 1
-    slots = rest[-1]
+def terms_body(pos, att_own, att_oth, ct_own, ct_oth, dq, xt, p_own, p_oth, out):
+    c = pos[0]
     total = dot(xt[0], dq[0]) + dot(xt[1], dq[1])
-    slots[:, :, 0] = total.astype(BF16).reshape(XN, YN, 96, H)
+    out[:, 0, 0] = total.astype(BF16).reshape(8, 96, H)
     total = None
     for e, ct in ((c, ct_own), (1 - c, ct_oth)):
         att_t = (dot_nt(p_own[...], att_own[e]) + dot_nt(p_oth[...], att_oth[e])).astype(BF16)
         term = dot(att_t, ct[...])
         total = term if total is None else total + term
-    slots[:, :, 1] = total.astype(BF16).reshape(XN, YN, 96, H)
-    for far in range(XN):
-        rest[far][...] = slots[x ^ far]
+    out[:, 1, 0] = total.astype(BF16).reshape(8, 96, H)
+
+
+TERMS = (8, 2, 2, 96, H)
+
+
+def terms_half(index):
+    return pl.BlockSpec((8, 2, 1, 96, H), lambda i, s: (0, 0, index, 0, 0))
 
 
 def output_terms(pos, att_own, att_oth, ct_own, ct_oth, dq, xt, perm):
     col = lambda flip, rows: pl.BlockSpec((rows, H), lambda i, s: (0, s[0] ^ flip))
-    slot = (YN, 2, 96, H)
     return call(
         terms_body,
         (1,),
         [whole(2, TOK, H)] * 2 + [col(0, TOK)] * 2 + [whole(2, TOK, H), whole(2, D, TOK), col(0, D), col(1, D)],
-        [(whole(*slot), (slot, BF16))] * XN,
-        [pltpu.VMEM((XN,) + slot, BF16)],
-    )(pos, att_own, att_oth, ct_own, ct_oth, dq, xt, perm, perm)
-
-
-def x_sum_body(pos, t0, t1, t2, t3, *rest):
-    y, dp = pos[2] & 1, pos[3]
-    slots = rest[-1]
-    total = (t0[...].astype(F32) + t1[...].astype(F32)) + (t2[...].astype(F32) + t3[...].astype(F32))
-    slots[...] = total.astype(BF16)
-    for far in range(4):
-        rest[far][...] = slots[y ^ (far >> 1), dp ^ (far & 1)]
-
-
-def x_sum(pos, *terms):
-    shape = (YN, 2, 96, H)
-    return call(
-        x_sum_body,
-        (1,),
-        [whole(*shape)] * 4,
-        [(whole(96, H), ((96, H), BF16))] * 4,
-        [pltpu.VMEM(shape, BF16)],
-    )(pos, *terms)
+        [(terms_half(0), (TERMS, BF16))],
+    )(pos, att_own, att_oth, ct_own, ct_oth, dq, xt, perm, perm)[0]
 
 
 def back_body(pos, xr, out):
@@ -380,7 +311,26 @@
     )(pos, xr)[0]
 
 
-def leaf_body(pos, zr, dkv, dn1, yr, keep, dq, xt, pg_out, grad_out):
+def hand_back_body(pos, dw, dy, *outs):
+    start = 0
+    for out in outs:
+        rows = out.shape[1]
+        for p in range(2):
+            total = dw[p, start : start + rows] + dy[p, NR + start : NR + start + rows].astype(F32)
+            out[p] = total.astype(BF16)
+        start += rows
+
+
+def hand_back(pos, dw, dy):
+    return call(
+        hand_back_body,
+        (1,),
+        [whole(2, NR, H), whole(2, 2 * NR, H)],
+        [(whole(2, rows, H), ((2, rows, H), BF16)) for rows in (64, 32, 32)],
+    )(pos, dw, dy)
+
+
+def leaf_body(pos, zr, dkv, dn1, dy, g3, g4_a, g4_b, dq, xt, _, pg_out, grad_out):
     def split(grad):
         high = grad.astype(BF16)
         return [high, (grad - high.astype(F32)).astype(BF16)]
@@ -392,38 +342,39 @@
         return jnp.concatenate([ref[0], ref[1]], axis=1)
 
     zs = jnp.concatenate([zr[:, p].reshape(128, H) for p in range(2)], axis=1)
-    near = split(wide(keep))
+    ws = jnp.concatenate([wide(g3), wide(g4_a), wide(g4_b)], axis=0)
+    ys = jnp.concatenate([dy[p, :NR] for p in range(2)], axis=1)
     for e in range(2):
         t, k = iota((TOK, 128), 0), iota((TOK, 128), 1)
         far, row, chip = (k >> 4) ^ pos[1], k & 15, t + TOK * e
         first = hot(t >> 1 == k, 1.0)
-        third = hot(chip >> 3 == k & 63, 0.5)
+        third = hot(chip >> 3 == k, 0.5)
         odd = hot((far == 1) & (row == chip >> 5), 0.25) + hot((far >= 4) & (row == chip >> 7), 0.125)
-        even = [hot(chip >> 2 == k, 0.5), hot((far >> 1 == 1) & (row == chip >> 6), 0.125)]
-        up = dot(jnp.concatenate([first, first, third, odd], axis=1), jnp.concatenate(split(wide(dn1.at[e])) + near + [zs], axis=0))
-        up = up * HALF_ROOT + dot(jnp.concatenate(even, axis=1), jnp.concatenate([wide(yr), zs], axis=0))
+        second = hot(chip >> 2 == k, 0.5)
+        fourth = hot((k >= 64) & (chip >> 4 == k & 31), 0.25)
+        even = hot((far >> 1 == 1) & (row == chip >> 6), 0.125)
+        up = dot(jnp.concatenate([first, first, third, odd], axis=1), jnp.concatenate(split(wide(dn1.at[e])) + [ws, zs], axis=0))
+        up = up * HALF_ROOT + dot(jnp.concatenate([second, fourth, even], axis=1), jnp.concatenate([ys, ws, zs], axis=0))
         for p in range(2):
             pg_out[e, :, H * (1 + p) : H * (2 + p)] = (dkv[e, p] + up[:, H * p : H * p + H]).astype(BF16)
         pg_out[e, :, :H] = dq[e]
     for p in range(2):
         cols = slice(H * (1 + p), H * (2 + p))
         total = dot(xt[0], pg_out[0, :, cols]) + dot(xt[1], pg_out[1, :, cols])
-        grad_out[:, p] = total.astype(BF16).reshape(8, 96, H)
-
-
-def leaf_grads(pos, zr, dkv, dn1, yr, keep, dq, xt):
+        grad_out[:, p, 0] = total.astype(BF16).reshape(8, 96, H)
+
+
+def leaf_grads(pos, zr, dkv, dn1, dy, g3, g4_a, g4_b, dq, xt, terms):
     return call(
         leaf_body,
         (1,),
         [
-            whole(ZN, 2, 16, H), whole(2, 2, TOK, H), whole(2, 2, NR, H), whole(2, NR, H), whole(2, 64, H),
-            whole(2, TOK, H), whole(2, D, TOK),
+            whole(ZN, 2, 16, H), whole(2, 2, TOK, H), whole(2, 2, NR, H), whole(2, 2 * NR, H), whole(2, 64, H), whole(2, 32, H),
+            whole(2, 32, H), whole(2, TOK, H), whole(2, D, TOK), pl.BlockSpec(memory_space=pl.ANY),
         ],
-        [
-            (whole(2, TOK, 3 * H), ((2, TOK, 3 * H), BF16)),
-            (whole(8, 2, 96, H), ((8, 2, 96, H), BF16)),
-        ],
-    )(pos, zr, dkv, dn1, yr, keep, dq, xt)
+        [(whole(2, TOK, 3 * H), ((2, TOK, 3 * H), BF16)), (terms_half(1), (TERMS, BF16))],
+        aliases={10: 1},
+    )(pos, zr, dkv, dn1, dy, g3, g4_a, g4_b, dq, xt, terms)
 
 
 def input_body(pos, pg_own, pg_oth, *rest):
@@ -453,21 +404,21 @@
     return total
 
 
-def middle_body(pos, f0, f1, f2, f3, second, out):
-    first = total_of([f0[...], f1[...], f2[...], f3[...]]).astype(BF16)
+def middle_body(pos, terms, out):
     i, k = iota((256, 96), 0), iota((256, 96), 1)
     row, half = i & 7, (i >> 3) & 1
     hit = (k == 6 * (i >> 4) + row) & (row < 6)
-    rows = dot((hit & (half == 0)).astype(BF16), first)
-    rows = rows + dot((hit & (half == 1)).astype(BF16), total_of([second[slot] for slot in range(16)]).astype(BF16))
+    rows = None
+    for group in range(2):
+        total = total_of([terms[slot, group] for slot in range(16)]).astype(BF16)
+        part = dot((hit & (half == group)).astype(BF16), total)
+        rows = part if rows is None else rows + part
     out[...] = rows.astype(BF16).reshape(ZN, 2, 16, H)
 
 
-def middle_sum(pos, firsts, second):
+def middle_sum(pos, terms):
     shape = (ZN, 2, 16, H)
-    return call(
-        middle_body, (1,), [whole(96, H)] * 4 + [whole(16, 96, H)], [(whole(*shape), (shape, BF16))]
-    )(pos, *firsts, second)[0]
+    return call(middle_body, (1,), [whole(16, 2, 96, H)], [(whole(*shape), (shape, BF16))])(pos, terms)[0]
 
 
 def z_sum_body(pos, terms, own_out, oth_out):
@@ -531,37 +482,33 @@
     x_oth, ct_oth = swap(x_own, "c"), swap(ct_own, "c")
     perm = row_order()
 
-    kv, n1, n2, zs = tree(pos, x_own, x_oth, w_qkv)
+    kv, n1, n2, n3, n4, zs = tree(pos, x_own, x_oth, w_qkv)
+    yr = swap(n2, "y")
+    wr = jnp.concatenate([along(n3, "x", 1), along(n4, "x", 2), along(n4, "x", 3)], axis=1)
+    wy = swap(wr, "y")
     zr = lax.all_to_all(zs, "z", 0, 0)
-    yr = swap(n2, "y")
-    near, far = pair_nodes(pos, n2, yr)
-    zr, near, far, ct_oth = lax.optimization_barrier((zr, near, far, ct_oth))
-    near, far_a, far_b = along(near, "x", 1), along(far, "x", 2), along(far, "x", 3)
+    zr, yr, wy, ct_oth = lax.optimization_barrier((zr, yr, wy, ct_oth))
     xr = lax.all_to_all(plane_slots(pos, zr), ("x", "y"), 0, 0)
     q, ag, xt = project(pos, x_own, x_oth, ct_own, ct_oth, w_qkv, w_out, perm)
-    att, dq, dkv, dn1, dy, dnear, dfar_a, dfar_b, dx = attention(pos, q, ag, kv, n1, yr, near, far_a, far_b, xr)
+    att, dq, dkv, dn1, dy, dw, dx = attention(pos, q, ag, kv, n1, yr, wr, wy, xr)
 
     dx_r = lax.all_to_all(dx, ("x", "y"), 0, 0)
     att_oth = swap(att, "c")
-    back = (along(dnear, "x", 1), along(dfar_a, "x", 2), along(dfar_b, "x", 3))
-    first, *firsts = output_terms(pos, att, att_oth, ct_own, ct_oth, dq, xt, perm)
-    dx_r, back, first = lax.optimization_barrier((dx_r, back, first))
+    dy = swap(dy, "y")
+    terms = output_terms(pos, att, att_oth, ct_own, ct_oth, dq, xt, perm)
+    dx_r, terms, dy = lax.optimization_barrier((dx_r, terms, dy))
     dz_r = lax.all_to_all(back_slots(pos, dx_r), "z", 0, 0)
-    firsts = x_sum(pos, first, *[along(firsts[far - 1], "x", far) for far in (1, 2, 3)])
-    keep, dy = pair_back(pos, *back, dy)
-    dz_r, firsts = lax.optimization_barrier((dz_r, firsts))
-    pg, terms = leaf_grads(pos, dz_r, dkv, dn1, swap(dy, "y"), keep, dq, xt)
-    second = lax.all_to_all(terms.reshape(16, 96, H), ("x", "y", "dp"), 0, 0)
-    firsts = list(firsts[:1]) + [along(firsts[far], ("y", "dp"), far) for far in (1, 2, 3)]
+    g3, g4_a, g4_b = hand_back(pos, dw, dy)
+    g3, g4_a, g4_b = along(g3, "x", 1), along(g4_a, "x", 2), along(g4_b, "x", 3)
+    dz_r, g3, g4_a, g4_b = lax.optimization_barrier((dz_r, g3, g4_a, g4_b))
+    pg, terms = leaf_grads(pos, dz_r, dkv, dn1, dy, g3, g4_a, g4_b, dq, xt, terms)
+    terms = lax.all_to_all(terms.reshape(16, 2, 96, H), ("x", "y", "dp"), 0, 0)
     pg_own = lax.dynamic_index_in_dim(pg, c, 0, keepdims=False)
     pg_oth = swap(lax.dynamic_index_in_dim(pg, 1 - c, 0, keepdims=False), "c")
     input_grad = input_side(pos, pg_own, pg_oth, w_qkv)
-    second, input_grad, firsts = lax.optimization_barrier((second, input_grad, firsts))
-    terms = middle_sum(pos, firsts, second)
-    terms, att, att_oth = lax.optimization_barrier((terms, att, att_oth))
-    terms = lax.all_to_all(terms, "z", 0, 0)
     layer_out = output_side(pos, att, att_oth, w_out)
-    terms, layer_out = lax.optimization_barrier((terms, layer_out))
+    terms, input_grad, layer_out = lax.optimization_barrier((terms, input_grad, layer_out))
+    terms = lax.all_to_all(middle_sum(pos, terms), "z", 0, 0)
     own, oth = z_sum(pos, terms)
     pair = ("c", "dp")
     qkv_grad, out_grad = last_rows(pos, own, along(own, pair, 1), along(oth, pair, 2), along(oth, pair, 3))

time: 188 us -> 188 us (level)
  blocking collectives: 0 us -> 14.3 us
  starting transfers between devices: 66.2 us -> 60.2 us
  Pallas kernels: 69.8 us -> 63.9 us
  local copies, waits for them, and re-layouts: 11 us -> 8.47 us
    ppermute x15 -> x9, waiting for transfers between devices: 27 us -> 5.84 us  [along(): return lax.ppermute(value, axes, [(i, i ^ far) for i in range(count)])]
    all_to_all x0 -> x1, blocking collectives: none -> 14.3 us  [shards(): terms = lax.all_to_all(middle_sum(pos, terms), 'z', 0, 0)]
    all_to_all x2 -> x1, waiting for transfers between devices: 5.96 us -> 14.6 us  [shards(): terms = lax.all_to_all(terms.reshape(16, 2, 96, H), ('x', 'y', 'dp'), 0, 0)]
    all_to_all x2 -> x1, starting transfers between devices: 12 us -> 4.89 us  [shards(): terms = lax.all_to_all(terms.reshape(16, 2, 96, H), ('x', 'y', 'dp'), 0, 0)]
    ppermute x6 -> x7, waiting for transfers between devices: 5.6 us -> 12.5 us  [swap(): return lax.ppermute(value, axis, [(0, 1), (1, 0)])]
    pallas_call x4 -> x2, Pallas kernels: 12 us -> 6.01 us  [the longest x1 3.54 us: middle_sum(): call(middle_body, (1,), [whole(16, 2, 96, H)], [(whole(*shape), (shape, B...]
    all_to_all x1, waiting for transfers between devices: 0.01 us -> 3.21 us  [shards(): zr = lax.all_to_all(zs, 'z', 0, 0)]
    unnamed x80 -> x44, local copies, waits for them, and re-layouts: 10 us -> 7.53 us
  transfers between devices with their start and end apart: 27 -> 21, of which waited for: 12 -> 9; matrix products, arithmetic and copies ran while one was open for 1% -> 1% of each run, Pallas kernels for 18% -> 12%
where the time goes in v5:
time: 188 us; the launch traced here: 187 us
  Pallas kernels  63.9 us (34%)
  starting transfers between devices  60.2 us (32%)
  waiting for transfers between devices  38.4 us (20%)
  blocking collectives  14.3 us (8%)
  local copies, waits for them, and re-layouts  8.47 us (5%)
    ppermute x9, starting transfers between devices, along(): return lax.ppermute(value, axes, [(i, i ^ far) for i in range(count)])  23 us
    pallas_call x1, Pallas kernels, attention(): call(attention_body, (H // 128,), [cut(2, TOK), cut(2, TOK), cut(2, 2, TO...  17.8 us
    all_to_all x1, waiting for transfers between devices, shards(): terms = lax.all_to_all(terms.reshape(16, 2, 96, H), ('x', 'y', 'dp'), 0, 0)  14.6 us
    all_to_all x1, blocking collectives, shards(): terms = lax.all_to_all(middle_sum(pos, terms), 'z', 0, 0)  14.3 us
    ppermute x7, starting transfers between devices, swap(): return lax.ppermute(value, axis, [(0, 1), (1, 0)])  13.3 us
    ppermute x7, waiting for transfers between devices, swap(): return lax.ppermute(value, axis, [(0, 1), (1, 0)])  12.5 us
    all_to_all x1, starting transfers between devices, shards(): zr = lax.all_to_all(zs, 'z', 0, 0)  7.75 us
    unnamed x44, local copies, waits for them, and re-layouts  7.53 us
  transfers between devices with their start and end apart: 21, of which 9 were waited for; matrix products, arithmetic and copies ran while one was open for 1% of the time, Pallas kernels for 12%

profile of v5, /device:TPU:1, one launch (start us, length us, event | category | flops | bytes accessed | tf_op | source)
XLA Modules:
  0.0 186.7 jit_solution(4942250816214781643)
XLA Ops:
  0.6 3.3 %collective-permute-start = (bf16[256,768]{1,0:T(8,128)(2,1)}, bf16[256,768]{1,0:T(8,128)(2,1)S(1)}, u32[]{:S(2)}, u32[]{:S(2)}) collective-permute-start(bf16[256,768]{1,0:T(8,128)(2,1)} %bitcast.14), channel_id=1, source_target_pairs={{0,2},{2,0},{1,3},{3,1},{4,6},{6,4},{5,7},{7,5},{8,10},{10,8},{9,1... | collective-permute-start | bytes 1179656 | tf_op jit(solution)/shard_map/ppermute | solution.py:464
  4.6 0.9 collective-permute-done.x_oth
  5.5 0.7 copy-done.3
  6.3 5.0 %shard_map.84 = (bf16[2,2,256,384]{3,2,1,0:T(8,128)(2,1)}, bf16[2,2,128,384]{3,2,1,0:T(8,128)(2,1)}, bf16[2,128,384]{2,1,0:T(8,128)(2,1)}, bf16[2,64,384]{2,1,0:...) custom-call(s32[4]{0:T(128)} %pad_add_fusion.pos, bf16[256,768]{1,0:T(8,128)(2,1)} %bitcast.15, ...), custom_call_target="tpu_custom_call" | custom-call | tf_op jit(solution)/shard_map/pallas_call | solution.py:108
  11.7 2.1 %collective-permute-start.3 = (bf16[2,32,384]{2,1,0:T(8,128)(2,1)}, bf16[2,32,384]{2,1,0:T(8,128)(2,1)S(1)}, u32[]{:S(2)}, u32[]{:S(2)}) collective-permute-start(bf16[2,32,384]{2,1,0:T(8,128)(2,1)} %get-tuple-element.46), channel_id=1, source_target_pairs={{0,16},{8,24},{16,0},{24,8},{1,17},{9,25},{17,1},{25,9},{2,18},{10... | collective-permute-start | bytes 147464 | tf_op jit(solution)/shard_map/ppermute | solution.py:468
  13.9 1.9 %collective-permute-start.4 = (bf16[2,32,384]{2,1,0:T(8,128)(2,1)}, bf16[2,32,384]{2,1,0:T(8,128)(2,1)S(1)}, u32[]{:S(2)}, u32[]{:S(2)}) collective-permute-start(bf16[2,32,384]{2,1,0:T(8,128)(2,1)} %get-tuple-element.46), channel_id=1, source_target_pairs={{0,24},{8,16},{16,8},{24,0},{1,25},{9,17},{17,9},{25,1},{2,26},{10... | collective-permute-start | bytes 147464 | tf_op jit(solution)/shard_map/ppermute | solution.py:468
  15.8 7.7 %all-to-all-start = ((bf16[8,2,16,384]{3,2,1,0:T(8,128)(2,1)}), bf16[8,2,16,384]{3,2,1,0:T(8,128)(2,1)S(1)}, u32[]{:S(2)}, u32[]{:S(2)}) async-start(bf16[8,2,16,384]{3,2,1,0:T(8,128)(2,1)} %get-tuple-element.43), calls=%async_computation | async-start | bytes 393216 | tf_op jit(solution)/shard_map/all_to_all | solution.py:489
  23.9 5.1 %collective-permute-done.5.wy = bf16[2,128,384]{2,1,0:T(8,128)(2,1)S(1)} collective-permute-done((bf16[2,128,384]{2,1,0:T(8,128)(2,1)S(1)}, bf16[2,128,384]{2,1,0:T(8,128)(2,1)S(1)}, u32[]{:S(2)}, u32[]{:S(2)}) %collective-permute-start.5) | collective-permute-done | bytes 196640 | tf_op jit(solution)/shard_map/ppermute | solution.py:464
  29.0 3.2 %all-to-all-done.zr = bf16[8,2,16,384]{3,2,1,0:T(8,128)(2,1)S(1)} async-done(((bf16[8,2,16,384]{3,2,1,0:T(8,128)(2,1)}), bf16[8,2,16,384]{3,2,1,0:T(8,128)(2,1)S(1)}, u32[]{:S(2)}, u32[]{:S(2)}) %all-to-all-start) | async-done | bytes 196640 | tf_op jit(solution)/shard_map/all_to_all | solution.py:489
  32.2 0.7 copy-done.9
  32.9 2.6 %shard_map.86 = bf16[8,2,48,384]{3,2,1,0:T(8,128)(2,1)} custom-call(s32[4]{0:T(128)} %pad_add_fusion.pos, bf16[8,2,16,384]{3,2,1,0:T(8,128)(2,1)} %copy-done.9), custom_call_target="tpu_custom_call" | custom-call | tf_op jit(solution)/shard_map/pallas_call | solution.py:153
  35.5 3.8 %all-to-all-start.1 = ((bf16[8,2,48,384]{3,2,1,0:T(8,128)(2,1)}), bf16[8,2,48,384]{3,2,1,0:T(8,128)(2,1)S(1)}, u32[]{:S(2)}, u32[]{:S(2)}) async-start(bf16[8,2,48,384]{3,2,1,0:T(8,128)(2,1)} %shard_map.86), calls=%async_computation.1 | async-start | bytes 1179648 | tf_op jit(solution)/shard_map/all_to_all | solution.py:491
  39.2 5.3 %shard_map.85 = (bf16[2,256,384]{2,1,0:T(8,128)(2,1)}, bf16[2,256,384]{2,1,0:T(8,128)(2,1)}, bf16[2,768,256]{2,1,0:T(8,128)(2,1)}) custom-call(s32[4]{0:T(128)} %pad_add_fusion.pos, bf16[256,768]{1,0:T(8,128)(2,1)} %bitcast.16, bf16[256,768]{1,0:T(8,128)(2,1)} %copy-done.3, bf16[256,768]{1,0:T(8,128)(2,1)} %bitcast.17, bf16[256,768]{1,0:T(8,128)(2,1)} %copy-done.7, ...), custom_call_target="tpu_custom_call" | custom-call | tf_op jit(solution)/shard_map/pallas_call | solution.py:126
  44.5 2.3 %all-to-all-done.1.xr = bf16[8,2,48,384]{3,2,1,0:T(8,128)(2,1)S(1)} async-done(((bf16[8,2,48,384]{3,2,1,0:T(8,128)(2,1)}), bf16[8,2,48,384]{3,2,1,0:T(8,128)(2,1)S(1)}, u32[]{:S(2)}, u32[]{:S(2)}) %all-to-all-start.1) | async-done | bytes 589856 | tf_op jit(solution)/shard_map/all_to_all | solution.py:491
  46.8 0.9 copy-done.2
  47.7 17.8 %shard_map.87 = (bf16[2,256,384]{2,1,0:T(8,128)(2,1)}, bf16[2,256,384]{2,1,0:T(8,128)(2,1)}, f32[2,2,256,384]{3,2,1,0:T(8,128)}, f32[2,2,128,384]{3,2,1,0:T(8,12...) custom-call(s32[4]{0:T(128)} %pad_add_fusion.pos, ...), custom_call_target="tpu_custom_call" | custom-call | tf_op jit(solution)/shard_map/pallas_call | solution.py:240
  65.5 3.5 %all-to-all-start.2 = ((bf16[8,2,48,384]{3,2,1,0:T(8,128)(2,1)}), bf16[8,2,48,384]{3,2,1,0:T(8,128)(2,1)S(1)}, u32[]{:S(2)}, u32[]{:S(2)}) async-start(bf16[8,2,48,384]{3,2,1,0:T(8,128)(2,1)} %get-tuple-element.55), calls=%async_computation.2 | async-start | bytes 1179648 | tf_op jit(solution)/shard_map/all_to_all | solution.py:495
  69.0 4.2 %collective-permute-start.7 = (bf16[2,256,384]{2,1,0:T(8,128)(2,1)}, bf16[2,256,384]{2,1,0:T(8,128)(2,1)S(1)}, u32[]{:S(2)}, u32[]{:S(2)}) collective-permute-start(bf16[2,256,384]{2,1,0:T(8,128)(2,1)} %get-tuple-element.56.att_own), channel_id=1, source_target_pairs={{0,2},{2,0},{1,3},{3,1},{4,6},{6,4},{5,7},{7,5},{8,10},{10,8},{9,1... | collective-permute-start | bytes 1179656 | tf_op jit(solution)/shard_map/ppermute | solution.py:464
  73.2 1.6 collective-permute-start.8
  74.8 0.8 copy-done.5
  75.5 5.5 %shard_map.88._ = bf16[8,2,2,96,384]{4,3,2,1,0:T(8,128)(2,1)} custom-call(s32[4]{0:T(128)} %pad_add_fusion.pos, bf16[2,256,384]{2,1,0:T(8,128)(2,1)} %get-tuple-element.56.att_own, bf16[2,256,384]{2,1,0:T(8,128)(2,1)} %copy-done.5, bf16[256,768]{1,0:T(8,128)(2,1)} %bitcast.18, bf16[256,768]{1,0:T(8,128)(2,1)} %copy-done.7, ...), custom_call_target="tpu_custom_call" | custom-call | tf_op jit(solution)/shard_map/pallas_call | solution.py:288
  81.0 6.5 %collective-permute-done.8.dy = bf16[2,256,384]{2,1,0:T(8,128)(2,1)S(1)} collective-permute-done((bf16[2,256,384]{2,1,0:T(8,128)(2,1)}, bf16[2,256,384]{2,1,0:T(8,128)(2,1)S(1)}, u32[]{:S(2)}, u32[]{:S(2)}) %collective-permute-start.8) | collective-permute-done | bytes 393248 | tf_op jit(solution)/shard_map/ppermute | solution.py:464
  87.5 0.9 copy-done.1
  88.4 2.6 %shard_map.89 = bf16[8,2,16,384]{3,2,1,0:T(8,128)(2,1)} custom-call(s32[4]{0:T(128)} %pad_add_fusion.pos, bf16[8,2,48,384]{3,2,1,0:T(8,128)(2,1)} %copy-done.1), custom_call_target="tpu_custom_call" | custom-call | tf_op jit(solution)/shard_map/pallas_call | solution.py:306
  91.0 4.0 %all-to-all-start.3 = ((bf16[8,2,16,384]{3,2,1,0:T(8,128)(2,1)}), bf16[8,2,16,384]{3,2,1,0:T(8,128)(2,1)S(1)}, u32[]{:S(2)}, u32[]{:S(2)}) async-start(bf16[8,2,16,384]{3,2,1,0:T(8,128)(2,1)} %shard_map.89), calls=%async_computation.3 | async-start | bytes 393216 | tf_op jit(solution)/shard_map/all_to_all | solution.py:500
  95.0 2.5 %shard_map.90 = (bf16[2,64,384]{2,1,0:T(8,128)(2,1)}, bf16[2,32,384]{2,1,0:T(8,128)(2,1)}, bf16[2,32,384]{2,1,0:T(8,128)(2,1)}) custom-call(s32[4]{0:T(128)} %pad_add_fusion.pos, f32[2,128,384]{2,1,0:T(8,128)} %get-tuple-element.61.dw, bf16[2,256,384]{2,1,0:T(8,128)(2,1)} %copy-done.4), custom_call_target="tpu_custom_call" | custom-call | tf_op jit(solution)/shard_map/pallas_call | solution.py:325
  97.4 1.2 collective-permute-start.9
  98.6 1.7 collective-permute-start.10
  100.3 1.0 collective-permute-start.11
  101.3 2.1 %collective-permute-done.10.g4_a = bf16[2,32,384]{2,1,0:T(8,128)(2,1)S(1)} collective-permute-done((bf16[2,32,384]{2,1,0:T(8,128)(2,1)}, bf16[2,32,384]{2,1,0:T(8,128)(2,1)S(1)}, u32[]{:S(2)}, u32[]{:S(2)}) %collective-permute-start.10) | collective-permute-done | bytes 49184 | tf_op jit(solution)/shard_map/ppermute | solution.py:468
  103.4 1.6 collective-permute-done.11.g4_b
  105.7 6.2 %shard_map.91 = (bf16[2,256,1152]{2,1,0:T(8,128)(2,1)}, bf16[8,2,2,96,384]{4,3,2,1,0:T(8,128)(2,1)}) custom-call(s32[4]{0:T(128)} %pad_add_fusion.pos, bf16[8,2,16,384]{3,2,1,0:T(8,128)(2,1)} %copy-done.10, f32[2,2,256,384]{3,2,1,0:T(8,128)} %get-tuple-element.67.dkv, f32[2,2,128,384]{3,2,1,0:T(8,128)} %get-tuple-element.68.dn1, ...), custom_call_target="tpu_custom_call", output_to_operand_aliasing={{1}: (10, {})} | custom-call | tf_op jit(solution)/shard_map/pallas_call | solution.py:368
  112.0 4.9 %all-to-all-start.4 = ((bf16[16,2,96,384]{3,2,1,0:T(8,128)(2,1)}), bf16[16,2,96,384]{3,2,1,0:T(8,128)(2,1)S(1)}, u32[]{:S(2)}, u32[]{:S(2)}) async-start(bf16[16,2,96,384]{3,2,1,0:T(8,128)(2,1)} %bitcast.13), calls=%async_computation.4 | async-start | bytes 4718592 | tf_op jit(solution)/shard_map/all_to_all | solution.py:505
  116.9 0.9 dynamic-slice_bitcast_fusion
  117.8 3.5 %collective-permute-start.12 = (bf16[256,1152]{1,0:T(8,128)(2,1)S(1)}, bf16[256,1152]{1,0:T(8,128)(2,1)S(1)}, u32[]{:S(2)}, u32[]{:S(2)}) collective-permute-start(bf16[256,1152]{1,0:T(8,128)(2,1)S(1)} %get-tuple-element.82), channel_id=1, source_target_pairs={{0,2},{2,0},{1,3},{3,1},{4,6},{6,4},{5,7},{7,5},{8,10},{10,8},{9,1... | collective-permute-start | bytes 1769480 | tf_op jit(solution)/shard_map/ppermute | solution.py:464
  121.3 3.5 %shard_map.93 = bf16[256,768]{1,0:T(8,128)(2,1)} custom-call(s32[4]{0:T(128)} %pad_add_fusion.pos, bf16[2,256,384]{2,1,0:T(8,128)(2,1)} %get-tuple-element.56.att_own, bf16[2,256,384]{2,1,0:T(8,128)(2,1)} %copy-done.5, bf16[768,768]{1,0:T(8,128)(2,1)} %w_oth.1, bf16[768,768]{1,0:T(8,128)(2,1)} %w_oth.1), custom_call_target="tpu_custom_call" | custom-call | tf_op jit(solution)/shard_map/pallas_call | solution.py:259
  124.7 0.8 copy-done.11
  125.5 5.1 %shard_map.92 = bf16[256,768]{1,0:T(8,128)(2,1)} custom-call(s32[4]{0:T(128)} %pad_add_fusion.pos, bf16[256,1152]{1,0:T(8,128)(2,1)} %get-tuple-element.83.pg_own, bf16[256,1152]{1,0:T(8,128)(2,1)} %copy-done.11, bf16[768,2304]{1,0:T(8,128)(2,1)} %rest_5_.1, bf16[768,2304]{1,0:T(8,128)(2,1)} %rest_5_.1, bf16[768,2304]{1,0:T(8,128)(2,1)} %rest_5_.1, ...), custom_call_target="tpu_custom_call" | custom-call | tf_op jit(solution)/shard_map/pallas_call | solution.py:392
  130.7 14.6 %all-to-all-done.4.terms = bf16[16,2,96,384]{3,2,1,0:T(8,128)(2,1)S(1)} async-done(((bf16[16,2,96,384]{3,2,1,0:T(8,128)(2,1)}), bf16[16,2,96,384]{3,2,1,0:T(8,128)(2,1)S(1)}, u32[]{:S(2)}, u32[]{:S(2)}) %all-to-all-start.4) | async-done | bytes 2359328 | tf_op jit(solution)/shard_map/all_to_all | solution.py:505
  145.3 1.4 copy-done
  146.7 3.5 %shard_map.94 = bf16[8,2,16,384]{3,2,1,0:T(8,128)(2,1)} custom-call(s32[4]{0:T(128)} %pad_add_fusion.pos, bf16[16,2,96,384]{3,2,1,0:T(8,128)(2,1)} %copy-done), custom_call_target="tpu_custom_call" | custom-call | tf_op jit(solution)/shard_map/pallas_call | solution.py:421
  150.2 14.3 %all_to_all.30.terms = bf16[8,2,16,384]{3,2,1,0:T(8,128)(2,1)} all-to-all(bf16[8,2,16,384]{3,2,1,0:T(8,128)(2,1)} %shard_map.94), channel_id=1, replica_groups=mesh['z'=8,'x'=4,'y'=2,'c'=2,'dp'=2] {'z'}, dimensions={0} | all-to-all | bytes 393216 | tf_op jit(solution)/shard_map/all_to_all | solution.py:511
  164.5 2.2 %shard_map.95 = (bf16[16,384]{1,0:T(8,128)(2,1)}, bf16[16,384]{1,0:T(8,128)(2,1)}) custom-call(s32[4]{0:T(128)} %pad_add_fusion.pos, bf16[8,2,16,384]{3,2,1,0:T(8,128)(2,1)} %all_to_all.30.terms), custom_call_target="tpu_custom_call" | custom-call | tf_op jit(solution)/shard_map/pallas_call | solution.py:430
  166.8 1.5 collective-permute-start.13
  168.2 11.0 %collective-permute-start.14 = (bf16[16,384]{1,0:T(8,128)(2,1)}, bf16[16,384]{1,0:T(8,128)(2,1)S(1)}, u32[]{:S(2)}, u32[]{:S(2)}) collective-permute-start(bf16[16,384]{1,0:T(8,128)(2,1)} %get-tuple-element.79), channel_id=1, source_target_pairs={{0,2},{1,3},{2,0},{3,1},{4,6},{5,7},{6,4},{7,5},{8,10},{9,11},{10,... | collective-permute-start | bytes 36872 | tf_op jit(solution)/shard_map/ppermute | solution.py:468
  179.2 2.6 %collective-permute-start.15 = (bf16[16,384]{1,0:T(8,128)(2,1)}, bf16[16,384]{1,0:T(8,128)(2,1)S(1)}, u32[]{:S(2)}, u32[]{:S(2)}) collective-permute-start(bf16[16,384]{1,0:T(8,128)(2,1)} %get-tuple-element.79), channel_id=1, source_target_pairs={{0,3},{1,2},{2,1},{3,0},{4,7},{5,6},{6,5},{7,4},{8,11},{9,10},{10,... | collective-permute-start | bytes 36872 | tf_op jit(solution)/shard_map/ppermute | solution.py:468
  181.9 2.2 %collective-permute-done.15.from_both = bf16[16,384]{1,0:T(8,128)(2,1)S(1)} collective-permute-done((bf16[16,384]{1,0:T(8,128)(2,1)}, bf16[16,384]{1,0:T(8,128)(2,1)S(1)}, u32[]{:S(2)}, u32[]{:S(2)}) %collective-permute-start.15) | collective-permute-done | bytes 12320 | tf_op jit(solution)/shard_map/ppermute | solution.py:468
  184.7 2.1 %shard_map.96 = (f32[6,2304]{1,0:T(8,128)}, f32[6,768]{1,0:T(8,128)}) custom-call(s32[4]{0:T(128)} %pad_add_fusion.pos, bf16[16,384]{1,0:T(8,128)(2,1)} %get-tuple-element.78.own, bf16[16,384]{1,0:T(8,128)(2,1)} %copy-done.18, bf16[16,384]{1,0:T(8,128)(2,1)} %copy-done.19, bf16[16,384]{1,0:T(8,128)(2,1)} %copy-done.20), custom_call_target="tpu_custom_call" | custom-call | tf_op jit(solution)/shard_map/pallas_call | solution.py:454
  (55 shorter events, 2.8 us)
Async XLA Ops:
  0.6 4.9 %collective-permute-start = (bf16[256,768]{1,0:T(8,128)(2,1)}, bf16[256,768]{1,0:T(8,128)(2,1)S(1)}, u32[]{:S(2)}, u32[]{:S(2)}) collective-permute-start(bf16[256,768]{1,0:T(8,128)(2,1)} %bitcast.14), channel_id=1, source_target_pairs={{0,2},{2,0},{1,3},{3,1},{4,6},{6,4},{5,7},{7,5},{8,10},{10,8},{9,1... | collective-permute-start | bytes 1179656 | tf_op jit(solution)/shard_map/ppermute | solution.py:464
  4.6 6.7 %copy-start.6 = (bf16[1,256,768]{2,1,0:T(8,128)(2,1)S(1)}, bf16[1,256,768]{2,1,0:T(8,128)(2,1)}, u32[]{:S(2)}) copy-start(bf16[1,256,768]{2,1,0:T(8,128)(2,1)} %param.6) | copy-start | bytes 1179652
  5.5 0.7 copy-start.3
  11.3 12.3 %collective-permute-start.2 = (bf16[2,64,384]{2,1,0:T(8,128)(2,1)}, bf16[2,64,384]{2,1,0:T(8,128)(2,1)S(1)}, u32[]{:S(2)}, u32[]{:S(2)}) collective-permute-start(bf16[2,64,384]{2,1,0:T(8,128)(2,1)} %get-tuple-element.45), channel_id=1, source_target_pairs={{0,8},{8,0},{16,24},{24,16},{1,9},{9,1},{17,25},{25,17},{2,10},{10... | collective-permute-start | bytes 294920 | tf_op jit(solution)/shard_map/ppermute | solution.py:468
  11.3 12.6 %collective-permute-start.6 = (bf16[256,768]{1,0:T(8,128)(2,1)S(1)}, bf16[256,768]{1,0:T(8,128)(2,1)S(1)}, u32[]{:S(2)}, u32[]{:S(2)}) collective-permute-start(bf16[256,768]{1,0:T(8,128)(2,1)S(1)} %bitcast.19), channel_id=1, source_target_pairs={{0,2},{2,0},{1,3},{3,1},{4,6},{6,4},{5,7},{7,5},{8,10},{10,8},{9,1... | collective-permute-start | bytes 1179656 | tf_op jit(solution)/shard_map/ppermute | solution.py:464
  11.7 11.8 %collective-permute-start.3 = (bf16[2,32,384]{2,1,0:T(8,128)(2,1)}, bf16[2,32,384]{2,1,0:T(8,128)(2,1)S(1)}, u32[]{:S(2)}, u32[]{:S(2)}) collective-permute-start(bf16[2,32,384]{2,1,0:T(8,128)(2,1)} %get-tuple-element.46), channel_id=1, source_target_pairs={{0,16},{8,24},{16,0},{24,8},{1,17},{9,25},{17,1},{25,9},{2,18},{10... | collective-permute-start | bytes 147464 | tf_op jit(solution)/shard_map/ppermute | solution.py:468
  13.9 9.7 %collective-permute-start.4 = (bf16[2,32,384]{2,1,0:T(8,128)(2,1)}, bf16[2,32,384]{2,1,0:T(8,128)(2,1)S(1)}, u32[]{:S(2)}, u32[]{:S(2)}) collective-permute-start(bf16[2,32,384]{2,1,0:T(8,128)(2,1)} %get-tuple-element.46), channel_id=1, source_target_pairs={{0,24},{8,16},{16,8},{24,0},{1,25},{9,17},{17,9},{25,1},{2,26},{10... | collective-permute-start | bytes 147464 | tf_op jit(solution)/shard_map/ppermute | solution.py:468
  15.8 8.1 %collective-permute-start.1 = (bf16[2,128,384]{2,1,0:T(8,128)(2,1)}, bf16[2,128,384]{2,1,0:T(8,128)(2,1)S(1)}, u32[]{:S(2)}, u32[]{:S(2)}) collective-permute-start(bf16[2,128,384]{2,1,0:T(8,128)(2,1)} %get-tuple-element.44), channel_id=1, source_target_pairs={{0,4},{4,0},{1,5},{5,1},{2,6},{6,2},{3,7},{7,3},{8,12},{12,8},{9,1... | collective-permute-start | bytes 589832 | tf_op jit(solution)/shard_map/ppermute | solution.py:464
  15.8 16.4 %all-to-all-start = ((bf16[8,2,16,384]{3,2,1,0:T(8,128)(2,1)}), bf16[8,2,16,384]{3,2,1,0:T(8,128)(2,1)S(1)}, u32[]{:S(2)}, u32[]{:S(2)}) async-start(bf16[8,2,16,384]{3,2,1,0:T(8,128)(2,1)} %get-tuple-element.43), calls=%async_computation | async-start | bytes 393216 | tf_op jit(solution)/shard_map/all_to_all | solution.py:489
  23.6 20.9 %copy-start.12 = (bf16[2,128,384]{2,1,0:T(8,128)(2,1)}, bf16[2,128,384]{2,1,0:T(8,128)(2,1)S(1)}, u32[]{:S(2)}) copy-start(bf16[2,128,384]{2,1,0:T(8,128)(2,1)S(1)} %constant_dynamic-update-slice_fusion.wr) | copy-start | bytes 589828
  23.6 5.4 %collective-permute-start.5 = (bf16[2,128,384]{2,1,0:T(8,128)(2,1)S(1)}, bf16[2,128,384]{2,1,0:T(8,128)(2,1)S(1)}, u32[]{:S(2)}, u32[]{:S(2)}) collective-permute-start(bf16[2,128,384]{2,1,0:T(8,128)(2,1)S(1)} %constant_dynamic-update-slice_fusion.wr), channel_id=1, source_target_pairs={{0,4},{4,0},{1,5},{5,1},{2,6},{6,2},{3,7},{7,3},{8,12},{12,8},{9,1... | collective-permute-start | bytes 589832 | tf_op jit(solution)/shard_map/ppermute | solution.py:464
  23.9 15.4 %copy-start.7 = (bf16[256,768]{1,0:T(8,128)(2,1)}, bf16[256,768]{1,0:T(8,128)(2,1)S(1)}, u32[]{:S(2)}) copy-start(bf16[256,768]{1,0:T(8,128)(2,1)S(1)} %collective-permute-done.6.ct_oth) | copy-start | bytes 1179652
  23.9 20.6 %copy-start.13 = (bf16[2,128,384]{2,1,0:T(8,128)(2,1)}, bf16[2,128,384]{2,1,0:T(8,128)(2,1)S(1)}, u32[]{:S(2)}) copy-start(bf16[2,128,384]{2,1,0:T(8,128)(2,1)S(1)} %collective-permute-done.1.yr) | copy-start | bytes 589828
  29.0 15.5 %copy-start.14 = (bf16[2,128,384]{2,1,0:T(8,128)(2,1)}, bf16[2,128,384]{2,1,0:T(8,128)(2,1)S(1)}, u32[]{:S(2)}) copy-start(bf16[2,128,384]{2,1,0:T(8,128)(2,1)S(1)} %collective-permute-done.5.wy) | copy-start | bytes 589828
  32.2 0.7 copy-start.9
  35.5 11.3 %all-to-all-start.1 = ((bf16[8,2,48,384]{3,2,1,0:T(8,128)(2,1)}), bf16[8,2,48,384]{3,2,1,0:T(8,128)(2,1)S(1)}, u32[]{:S(2)}, u32[]{:S(2)}) async-start(bf16[8,2,48,384]{3,2,1,0:T(8,128)(2,1)} %shard_map.86), calls=%async_computation.1 | async-start | bytes 1179648 | tf_op jit(solution)/shard_map/all_to_all | solution.py:491
  46.8 0.9 copy-start.2
  65.5 22.0 %all-to-all-start.2 = ((bf16[8,2,48,384]{3,2,1,0:T(8,128)(2,1)}), bf16[8,2,48,384]{3,2,1,0:T(8,128)(2,1)S(1)}, u32[]{:S(2)}, u32[]{:S(2)}) async-start(bf16[8,2,48,384]{3,2,1,0:T(8,128)(2,1)} %get-tuple-element.55), calls=%async_computation.2 | async-start | bytes 1179648 | tf_op jit(solution)/shard_map/all_to_all | solution.py:495
  69.0 5.7 %collective-permute-start.7 = (bf16[2,256,384]{2,1,0:T(8,128)(2,1)}, bf16[2,256,384]{2,1,0:T(8,128)(2,1)S(1)}, u32[]{:S(2)}, u32[]{:S(2)}) collective-permute-start(bf16[2,256,384]{2,1,0:T(8,128)(2,1)} %get-tuple-element.56.att_own), channel_id=1, source_target_pairs={{0,2},{2,0},{1,3},{3,1},{4,6},{6,4},{5,7},{7,5},{8,10},{10,8},{9,1... | collective-permute-start | bytes 1179656 | tf_op jit(solution)/shard_map/ppermute | solution.py:464
  73.2 14.3 %collective-permute-start.8 = (bf16[2,256,384]{2,1,0:T(8,128)(2,1)}, bf16[2,256,384]{2,1,0:T(8,128)(2,1)S(1)}, u32[]{:S(2)}, u32[]{:S(2)}) collective-permute-start(bf16[2,256,384]{2,1,0:T(8,128)(2,1)} %get-tuple-element.59), channel_id=1, source_target_pairs={{0,4},{4,0},{1,5},{5,1},{2,6},{6,2},{3,7},{7,3},{8,12},{12,8},{9,1... | collective-permute-start | bytes 1179656 | tf_op jit(solution)/shard_map/ppermute | solution.py:464
  74.8 0.8 copy-start.5
  87.5 7.5 %copy-start.4 = (bf16[2,256,384]{2,1,0:T(8,128)(2,1)}, bf16[2,256,384]{2,1,0:T(8,128)(2,1)S(1)}, u32[]{:S(2)}) copy-start(bf16[2,256,384]{2,1,0:T(8,128)(2,1)S(1)} %collective-permute-done.8.dy) | copy-start | bytes 1179652
  87.5 0.9 copy-start.1
  91.0 14.0 %all-to-all-start.3 = ((bf16[8,2,16,384]{3,2,1,0:T(8,128)(2,1)}), bf16[8,2,16,384]{3,2,1,0:T(8,128)(2,1)S(1)}, u32[]{:S(2)}, u32[]{:S(2)}) async-start(bf16[8,2,16,384]{3,2,1,0:T(8,128)(2,1)} %shard_map.89), calls=%async_computation.3 | async-start | bytes 393216 | tf_op jit(solution)/shard_map/all_to_all | solution.py:500
  97.4 7.5 %collective-permute-start.9 = (bf16[2,64,384]{2,1,0:T(8,128)(2,1)}, bf16[2,64,384]{2,1,0:T(8,128)(2,1)S(1)}, u32[]{:S(2)}, u32[]{:S(2)}) collective-permute-start(bf16[2,64,384]{2,1,0:T(8,128)(2,1)} %get-tuple-element.63), channel_id=1, source_target_pairs={{0,8},{8,0},{16,24},{24,16},{1,9},{9,1},{17,25},{25,17},{2,10},{10... | collective-permute-start | bytes 294920 | tf_op jit(solution)/shard_map/ppermute | solution.py:468
  98.6 4.8 %collective-permute-start.10 = (bf16[2,32,384]{2,1,0:T(8,128)(2,1)}, bf16[2,32,384]{2,1,0:T(8,128)(2,1)S(1)}, u32[]{:S(2)}, u32[]{:S(2)}) collective-permute-start(bf16[2,32,384]{2,1,0:T(8,128)(2,1)} %get-tuple-element.64), channel_id=1, source_target_pairs={{0,16},{8,24},{16,0},{24,8},{1,17},{9,25},{17,1},{25,9},{2,18},{10... | collective-permute-start | bytes 147464 | tf_op jit(solution)/shard_map/ppermute | solution.py:468
  100.3 4.7 %collective-permute-start.11 = (bf16[2,32,384]{2,1,0:T(8,128)(2,1)}, bf16[2,32,384]{2,1,0:T(8,128)(2,1)S(1)}, u32[]{:S(2)}, u32[]{:S(2)}) collective-permute-start(bf16[2,32,384]{2,1,0:T(8,128)(2,1)} %get-tuple-element.65), channel_id=1, source_target_pairs={{0,24},{8,16},{16,8},{24,0},{1,25},{9,17},{17,9},{25,1},{2,26},{10... | collective-permute-start | bytes 147464 | tf_op jit(solution)/shard_map/ppermute | solution.py:468
  103.4 1.6 copy-start.16
  105.0 0.6 copy-start.17
  105.0 0.7 copy-start.15
  105.0 0.7 copy-start.10
  112.0 4.9 %copy-start.8 = (bf16[2,256,1152]{2,1,0:T(8,128)(2,1)S(1)}, bf16[2,256,1152]{2,1,0:T(8,128)(2,1)}, u32[]{:S(2)}) copy-start(bf16[2,256,1152]{2,1,0:T(8,128)(2,1)} %get-tuple-element.74) | copy-start | bytes 3538948
  112.0 33.3 %all-to-all-start.4 = ((bf16[16,2,96,384]{3,2,1,0:T(8,128)(2,1)}), bf16[16,2,96,384]{3,2,1,0:T(8,128)(2,1)S(1)}, u32[]{:S(2)}, u32[]{:S(2)}) async-start(bf16[16,2,96,384]{3,2,1,0:T(8,128)(2,1)} %bitcast.13), calls=%async_computation.4 | async-start | bytes 4718592 | tf_op jit(solution)/shard_map/all_to_all | solution.py:505
  117.8 6.9 %collective-permute-start.12 = (bf16[256,1152]{1,0:T(8,128)(2,1)S(1)}, bf16[256,1152]{1,0:T(8,128)(2,1)S(1)}, u32[]{:S(2)}, u32[]{:S(2)}) collective-permute-start(bf16[256,1152]{1,0:T(8,128)(2,1)S(1)} %get-tuple-element.82), channel_id=1, source_target_pairs={{0,2},{2,0},{1,3},{3,1},{4,6},{6,4},{5,7},{7,5},{8,10},{10,8},{9,1... | collective-permute-start | bytes 1769480 | tf_op jit(solution)/shard_map/ppermute | solution.py:464
  124.7 0.8 copy-start.11
  145.3 1.4 copy-start
  166.8 15.1 %collective-permute-start.13 = (bf16[16,384]{1,0:T(8,128)(2,1)}, bf16[16,384]{1,0:T(8,128)(2,1)S(1)}, u32[]{:S(2)}, u32[]{:S(2)}) collective-permute-start(bf16[16,384]{1,0:T(8,128)(2,1)} %get-tuple-element.78.own), channel_id=1, source_target_pairs={{0,1},{1,0},{2,3},{3,2},{4,5},{5,4},{6,7},{7,6},{8,9},{9,8},{10,11... | collective-permute-start | bytes 36872 | tf_op jit(solution)/shard_map/ppermute | solution.py:468
  168.2 13.6 %collective-permute-start.14 = (bf16[16,384]{1,0:T(8,128)(2,1)}, bf16[16,384]{1,0:T(8,128)(2,1)S(1)}, u32[]{:S(2)}, u32[]{:S(2)}) collective-permute-start(bf16[16,384]{1,0:T(8,128)(2,1)} %get-tuple-element.79), channel_id=1, source_target_pairs={{0,2},{1,3},{2,0},{3,1},{4,6},{5,7},{6,4},{7,5},{8,10},{9,11},{10,... | collective-permute-start | bytes 36872 | tf_op jit(solution)/shard_map/ppermute | solution.py:468
  179.2 4.8 %collective-permute-start.15 = (bf16[16,384]{1,0:T(8,128)(2,1)}, bf16[16,384]{1,0:T(8,128)(2,1)S(1)}, u32[]{:S(2)}, u32[]{:S(2)}) collective-permute-start(bf16[16,384]{1,0:T(8,128)(2,1)} %get-tuple-element.79), channel_id=1, source_target_pairs={{0,3},{1,2},{2,1},{3,0},{4,7},{5,6},{6,5},{7,4},{8,11},{9,10},{10,... | collective-permute-start | bytes 36872 | tf_op jit(solution)/shard_map/ppermute | solution.py:468
  181.9 2.2 %copy-start.18 = (bf16[16,384]{1,0:T(8,128)(2,1)}, bf16[16,384]{1,0:T(8,128)(2,1)S(1)}, u32[]{:S(2)}) copy-start(bf16[16,384]{1,0:T(8,128)(2,1)S(1)} %collective-permute-done.13.from_dp) | copy-start | bytes 36868
  181.9 2.2 %copy-start.19 = (bf16[16,384]{1,0:T(8,128)(2,1)}, bf16[16,384]{1,0:T(8,128)(2,1)S(1)}, u32[]{:S(2)}) copy-start(bf16[16,384]{1,0:T(8,128)(2,1)S(1)} %collective-permute-done.14.from_core) | copy-start | bytes 36868
  184.1 0.6 copy-start.20

commit v6 on v5

--- a/solution.py
+++ b/solution.py
@@ -51,7 +51,7 @@
     return pl.BlockSpec(shape, lambda *_: (0,) * len(shape))
 
 
-def call(body, grid, ins, outs, scratch=(), aliases={}):
+def call(body, grid, ins, outs, scratch=()):
     return pl.pallas_call(
         body,
         grid_spec=pltpu.PrefetchScalarGridSpec(
@@ -62,7 +62,6 @@
             scratch_shapes=list(scratch),
         ),
         out_shape=[jax.ShapeDtypeStruct(shape, kind) for _, (shape, kind) in outs],
-        input_output_aliases=dict(aliases),
         compiler_params=pltpu.CompilerParams(vmem_limit_bytes=VMEM),
     )
 
@@ -158,7 +157,7 @@
     )(pos, zr)[0]
 
 
-def attention_body(pos, q, ag, kv, n1, yr, wr, wy, xr, att_out, dq_out, dkv_out, dn1_out, dy_out, dw_out, dx_out, keys, keys_t, s_ref, dw_ref, w_ref, ds_ref, drem):
+def attention_body(pos, q, ag, kv, n1, yr, wr, wy, xr, att_out, dq_out, dkv_out, dn1_out, dy_out, dwy_out, dw_out, dx_out, keys, keys_t, s_ref, dw_ref, w_ref, ds_ref, drem):
     for p in range(2):
         for e in range(2):
             keys[e, p, :256] = kv[e, p]
@@ -220,8 +219,8 @@
                 drem[p] = drem[p] + grad[384:]
     for p in range(2):
         rows = drem[p].astype(BF16)
-        dy_out[p, :NR] = rows[:128]
-        dy_out[p, NR:] = rows[256:384]
+        dy_out[p] = rows[:128]
+        dwy_out[p] = rows[256:384]
         dw_out[p] = drem[p, 128:256]
         for slot in range(8):
             start = 384 + ZR * slot
@@ -233,7 +232,7 @@
         return pl.BlockSpec(lead + (128,), lambda i, s: (0,) * len(lead) + (i,))
 
     outs = [
-        ((2, TOK), BF16), ((2, TOK), BF16), ((2, 2, TOK), F32), ((2, 2, NR), F32), ((2, 2 * NR), BF16),
+        ((2, TOK), BF16), ((2, TOK), BF16), ((2, 2, TOK), F32), ((2, 2, NR), F32), ((2, NR), BF16), ((2, NR), BF16),
         ((2, NR), F32), ((8, 2, ZR), BF16),
     ]
     n = 1152
@@ -264,33 +263,51 @@
     )(pos, att_own, att_oth, w_out, w_out)[0]
 
 
-def terms_body(pos, att_own, att_oth, ct_own, ct_oth, dq, xt, p_own, p_oth, out):
-    c = pos[0]
+def terms_body(pos, att_own, att_oth, ct_own, ct_oth, dq, xt, p_own, p_oth, *rest):
+    c, x = pos[0], pos[2] >> 1
+    slots = rest[-1]
     total = dot(xt[0], dq[0]) + dot(xt[1], dq[1])
-    out[:, 0, 0] = total.astype(BF16).reshape(8, 96, H)
+    slots[:, :, 0] = total.astype(BF16).reshape(XN, YN, 96, H)
     total = None
     for e, ct in ((c, ct_own), (1 - c, ct_oth)):
         att_t = (dot_nt(p_own[...], att_own[e]) + dot_nt(p_oth[...], att_oth[e])).astype(BF16)
         term = dot(att_t, ct[...])
         total = term if total is None else total + term
-    out[:, 1, 0] = total.astype(BF16).reshape(8, 96, H)
-
-
-TERMS = (8, 2, 2, 96, H)
-
-
-def terms_half(index):
-    return pl.BlockSpec((8, 2, 1, 96, H), lambda i, s: (0, 0, index, 0, 0))
+    slots[:, :, 1] = total.astype(BF16).reshape(XN, YN, 96, H)
+    for far in range(XN):
+        rest[far][...] = slots[x ^ far]
 
 
 def output_terms(pos, att_own, att_oth, ct_own, ct_oth, dq, xt, perm):
     col = lambda flip, rows: pl.BlockSpec((rows, H), lambda i, s: (0, s[0] ^ flip))
+    slot = (YN, 2, 96, H)
     return call(
         terms_body,
         (1,),
         [whole(2, TOK, H)] * 2 + [col(0, TOK)] * 2 + [whole(2, TOK, H), whole(2, D, TOK), col(0, D), col(1, D)],
-        [(terms_half(0), (TERMS, BF16))],
-    )(pos, att_own, att_oth, ct_own, ct_oth, dq, xt, perm, perm)[0]
+        [(whole(*slot), (slot, BF16))] * XN,
+        [pltpu.VMEM((XN,) + slot, BF16)],
+    )(pos, att_own, att_oth, ct_own, ct_oth, dq, xt, perm, perm)
+
+
+def x_sum_body(pos, t0, t1, t2, t3, *rest):
+    y, dp = pos[2] & 1, pos[3]
+    slots = rest[-1]
+    total = (t0[...].astype(F32) + t1[...].astype(F32)) + (t2[...].astype(F32) + t3[...].astype(F32))
+    slots[...] = total.astype(BF16)
+    for far in range(4):
+        rest[far][...] = slots[y ^ (far >> 1), dp ^ (far & 1)]
+
+
+def x_sum(pos, *terms):
+    shape = (YN, 2, 96, H)
+    return call(
+        x_sum_body,
+        (1,),
+        [whole(*shape)] * 4,
+        [(whole(96, H), ((96, H), BF16))] * 4,
+        [pltpu.VMEM(shape, BF16)],
+    )(pos, *terms)
 
 
 def back_body(pos, xr, out):
@@ -311,26 +328,26 @@
     )(pos, xr)[0]
 
 
-def hand_back_body(pos, dw, dy, *outs):
+def hand_back_body(pos, dw, dwy, *outs):
     start = 0
     for out in outs:
         rows = out.shape[1]
         for p in range(2):
-            total = dw[p, start : start + rows] + dy[p, NR + start : NR + start + rows].astype(F32)
+            total = dw[p, start : start + rows] + dwy[p, start : start + rows].astype(F32)
             out[p] = total.astype(BF16)
         start += rows
 
 
-def hand_back(pos, dw, dy):
+def hand_back(pos, dw, dwy):
     return call(
         hand_back_body,
         (1,),
-        [whole(2, NR, H), whole(2, 2 * NR, H)],
+        [whole(2, NR, H)] * 2,
         [(whole(2, rows, H), ((2, rows, H), BF16)) for rows in (64, 32, 32)],
-    )(pos, dw, dy)
-
-
-def leaf_body(pos, zr, dkv, dn1, dy, g3, g4_a, g4_b, dq, xt, _, pg_out, grad_out):
+    )(pos, dw, dwy)
+
+
+def leaf_body(pos, zr, dkv, dn1, dy, g3, g4_a, g4_b, dq, xt, pg_out, grad_out):
     def split(grad):
         high = grad.astype(BF16)
         return [high, (grad - high.astype(F32)).astype(BF16)]
@@ -343,7 +360,7 @@
 
     zs = jnp.concatenate([zr[:, p].reshape(128, H) for p in range(2)], axis=1)
     ws = jnp.concatenate([wide(g3), wide(g4_a), wide(g4_b)], axis=0)
-    ys = jnp.concatenate([dy[p, :NR] for p in range(2)], axis=1)
+    ys = wide(dy)
     for e in range(2):
         t, k = iota((TOK, 128), 0), iota((TOK, 128), 1)
         far, row, chip = (k >> 4) ^ pos[1], k & 15, t + TOK * e
@@ -361,20 +378,19 @@
     for p in range(2):
         cols = slice(H * (1 + p), H * (2 + p))
         total = dot(xt[0], pg_out[0, :, cols]) + dot(xt[1], pg_out[1, :, cols])
-        grad_out[:, p, 0] = total.astype(BF16).reshape(8, 96, H)
-
-
-def leaf_grads(pos, zr, dkv, dn1, dy, g3, g4_a, g4_b, dq, xt, terms):
+        grad_out[:, p] = total.astype(BF16).reshape(8, 96, H)
+
+
+def leaf_grads(pos, zr, dkv, dn1, dy, g3, g4_a, g4_b, dq, xt):
     return call(
         leaf_body,
         (1,),
         [
-            whole(ZN, 2, 16, H), whole(2, 2, TOK, H), whole(2, 2, NR, H), whole(2, 2 * NR, H), whole(2, 64, H), whole(2, 32, H),
-            whole(2, 32, H), whole(2, TOK, H), whole(2, D, TOK), pl.BlockSpec(memory_space=pl.ANY),
+            whole(ZN, 2, 16, H), whole(2, 2, TOK, H), whole(2, 2, NR, H), whole(2, NR, H), whole(2, 64, H), whole(2, 32, H),
+            whole(2, 32, H), whole(2, TOK, H), whole(2, D, TOK),
         ],
-        [(whole(2, TOK, 3 * H), ((2, TOK, 3 * H), BF16)), (terms_half(1), (TERMS, BF16))],
-        aliases={10: 1},
-    )(pos, zr, dkv, dn1, dy, g3, g4_a, g4_b, dq, xt, terms)
+        [(whole(2, TOK, 3 * H), ((2, TOK, 3 * H), BF16)), (whole(8, 2, 96, H), ((8, 2, 96, H), BF16))],
+    )(pos, zr, dkv, dn1, dy, g3, g4_a, g4_b, dq, xt)
 
 
 def input_body(pos, pg_own, pg_oth, *rest):
@@ -404,21 +420,21 @@
     return total
 
 
-def middle_body(pos, terms, out):
+def middle_body(pos, f0, f1, f2, f3, second, out):
+    first = total_of([f0[...], f1[...], f2[...], f3[...]]).astype(BF16)
     i, k = iota((256, 96), 0), iota((256, 96), 1)
     row, half = i & 7, (i >> 3) & 1
     hit = (k == 6 * (i >> 4) + row) & (row < 6)
-    rows = None
-    for group in range(2):
-        total = total_of([terms[slot, group] for slot in range(16)]).astype(BF16)
-        part = dot((hit & (half == group)).astype(BF16), total)
-        rows = part if rows is None else rows + part
+    rows = dot((hit & (half == 0)).astype(BF16), first)
+    rows = rows + dot((hit & (half == 1)).astype(BF16), total_of([second[slot] for slot in range(16)]).astype(BF16))
     out[...] = rows.astype(BF16).reshape(ZN, 2, 16, H)
 
 
-def middle_sum(pos, terms):
+def middle_sum(pos, firsts, second):
     shape = (ZN, 2, 16, H)
-    return call(middle_body, (1,), [whole(16, 2, 96, H)], [(whole(*shape), (shape, BF16))])(pos, terms)[0]
+    return call(
+        middle_body, (1,), [whole(96, H)] * 4 + [whole(16, 96, H)], [(whole(*shape), (shape, BF16))]
+    )(pos, *firsts, second)[0]
 
 
 def z_sum_body(pos, terms, own_out, oth_out):
@@ -490,25 +506,29 @@
     zr, yr, wy, ct_oth = lax.optimization_barrier((zr, yr, wy, ct_oth))
     xr = lax.all_to_all(plane_slots(pos, zr), ("x", "y"), 0, 0)
     q, ag, xt = project(pos, x_own, x_oth, ct_own, ct_oth, w_qkv, w_out, perm)
-    att, dq, dkv, dn1, dy, dw, dx = attention(pos, q, ag, kv, n1, yr, wr, wy, xr)
+    att, dq, dkv, dn1, dy, dwy, dw, dx = attention(pos, q, ag, kv, n1, yr, wr, wy, xr)
 
     dx_r = lax.all_to_all(dx, ("x", "y"), 0, 0)
     att_oth = swap(att, "c")
-    dy = swap(dy, "y")
-    terms = output_terms(pos, att, att_oth, ct_own, ct_oth, dq, xt, perm)
-    dx_r, terms, dy = lax.optimization_barrier((dx_r, terms, dy))
+    dwy = swap(dwy, "y")
+    first, *firsts = output_terms(pos, att, att_oth, ct_own, ct_oth, dq, xt, perm)
+    firsts = [along(firsts[far - 1], "x", far) for far in (1, 2, 3)]
+    dx_r, first, firsts[0], dwy = lax.optimization_barrier((dx_r, first, firsts[0], dwy))
     dz_r = lax.all_to_all(back_slots(pos, dx_r), "z", 0, 0)
-    g3, g4_a, g4_b = hand_back(pos, dw, dy)
+    dw, dwy, firsts = lax.optimization_barrier((dw, dwy, firsts))
+    g3, g4_a, g4_b = hand_back(pos, dw, dwy)
     g3, g4_a, g4_b = along(g3, "x", 1), along(g4_a, "x", 2), along(g4_b, "x", 3)
-    dz_r, g3, g4_a, g4_b = lax.optimization_barrier((dz_r, g3, g4_a, g4_b))
-    pg, terms = leaf_grads(pos, dz_r, dkv, dn1, dy, g3, g4_a, g4_b, dq, xt, terms)
-    terms = lax.all_to_all(terms.reshape(16, 2, 96, H), ("x", "y", "dp"), 0, 0)
+    firsts = x_sum(pos, first, *firsts)
+    firsts = list(firsts[:1]) + [along(firsts[far], ("y", "dp"), far) for far in (1, 2, 3)]
+    dz_r, g3, g4_a, g4_b, firsts = lax.optimization_barrier((dz_r, g3, g4_a, g4_b, firsts))
+    pg, terms = leaf_grads(pos, dz_r, dkv, dn1, swap(dy, "y"), g3, g4_a, g4_b, dq, xt)
+    terms = lax.all_to_all(terms.reshape(16, 96, H), ("x", "y", "dp"), 0, 0)
     pg_own = lax.dynamic_index_in_dim(pg, c, 0, keepdims=False)
     pg_oth = swap(lax.dynamic_index_in_dim(pg, 1 - c, 0, keepdims=False), "c")
     input_grad = input_side(pos, pg_own, pg_oth, w_qkv)
     layer_out = output_side(pos, att, att_oth, w_out)
     terms, input_grad, layer_out = lax.optimization_barrier((terms, input_grad, layer_out))
-    terms = lax.all_to_all(middle_sum(pos, terms), "z", 0, 0)
+    terms = lax.all_to_all(middle_sum(pos, firsts, terms), "z", 0, 0)
     own, oth = z_sum(pos, terms)
     pair = ("c", "dp")
     qkv_grad, out_grad = last_rows(pos, own, along(own, pair, 1), along(oth, pair, 2), along(oth, pair, 3))

time: 188 us -> 178 us (0.947)
  waiting for transfers between devices: 38.4 us -> 26.6 us
  Pallas kernels: 63.9 us -> 66.5 us
    all_to_all x1, waiting for transfers between devices: 14.6 us -> 0.01 us  [shards(): terms = lax.all_to_all(terms.reshape(16, 96, H), ('x', 'y', 'dp'), 0, 0)]
    ppermute x9 -> x15, waiting for transfers between devices: 5.84 us -> 13 us  [along(): return lax.ppermute(value, axes, [(i, i ^ far) for i in range(count)])]
    ppermute x7 -> x8, waiting for transfers between devices: 12.5 us -> 8.07 us  [swap(): return lax.ppermute(value, axis, [(0, 1), (1, 0)])]
    pallas_call x2 -> x3, Pallas kernels: 6.01 us -> 8.42 us  [the longest x1 3.19 us: middle_sum(): call(middle_body, (1,), [whole(96, H)] * 4 + [whole(16, 96, H)], [(whole(...]
    ppermute x7 -> x8, starting transfers between devices: 13.3 us -> 14.6 us  [swap(): return lax.ppermute(value, axis, [(0, 1), (1, 0)])]
    unnamed x44 -> x62, local copies, waits for them, and re-layouts: 7.53 us -> 6.36 us
    ppermute x9 -> x15, starting transfers between devices: 23 us -> 24 us  [along(): return lax.ppermute(value, axes, [(i, i ^ far) for i in range(count)])]
  transfers between devices with their start and end apart: 21 -> 28, of which waited for: 9 -> 12; matrix products, arithmetic and copies ran while one was open for 1% -> 1% of each run, Pallas kernels for 12% -> 15%
where the time goes in v6:
time: 178 us; the launch traced here: 177 us
  Pallas kernels  66.5 us (37%)
  starting transfers between devices  60.9 us (34%)
  waiting for transfers between devices  26.6 us (15%)
  blocking collectives  13.8 us (8%)
  local copies, waits for them, and re-layouts  7.31 us (4%)
    ppermute x15, starting transfers between devices, along(): return lax.ppermute(value, axes, [(i, i ^ far) for i in range(count)])  24 us
    pallas_call x1, Pallas kernels, attention(): call(attention_body, (H // 128,), [cut(2, TOK), cut(2, TOK), cut(2, 2, TO...  17.9 us
    ppermute x8, starting transfers between devices, swap(): return lax.ppermute(value, axis, [(0, 1), (1, 0)])  14.6 us
    all_to_all x1, blocking collectives, shards(): terms = lax.all_to_all(middle_sum(pos, firsts, terms), 'z', 0, 0)  13.8 us
    ppermute x15, waiting for transfers between devices, along(): return lax.ppermute(value, axes, [(i, i ^ far) for i in range(count)])  13 us
    ppermute x8, waiting for transfers between devices, swap(): return lax.ppermute(value, axis, [(0, 1), (1, 0)])  8.07 us
    all_to_all x1, starting transfers between devices, shards(): zr = lax.all_to_all(zs, 'z', 0, 0)  7.75 us
    unnamed x62, local copies, waits for them, and re-layouts  6.36 us
  transfers between devices with their start and end apart: 28, of which 12 were waited for; matrix products, arithmetic and copies ran while one was open for 1% of the time, Pallas kernels for 15%

profile of v6, /device:TPU:1, one launch (start us, length us, event | category | flops | bytes accessed | tf_op | source)
XLA Modules:
  0.0 176.5 jit_solution(6531096122424133352)
XLA Ops:
  0.6 3.3 %collective-permute-start = (bf16[256,768]{1,0:T(8,128)(2,1)}, bf16[256,768]{1,0:T(8,128)(2,1)S(1)}, u32[]{:S(2)}, u32[]{:S(2)}) collective-permute-start(bf16[256,768]{1,0:T(8,128)(2,1)} %bitcast.13), channel_id=1, source_target_pairs={{0,2},{2,0},{1,3},{3,1},{4,6},{6,4},{5,7},{7,5},{8,10},{10,8},{9,1... | collective-permute-start | bytes 1179656 | tf_op jit(solution)/shard_map/ppermute | solution.py:480
  4.6 1.0 collective-permute-done.x_oth
  6.3 5.0 %shard_map.84 = (bf16[2,2,256,384]{3,2,1,0:T(8,128)(2,1)}, bf16[2,2,128,384]{3,2,1,0:T(8,128)(2,1)}, bf16[2,128,384]{2,1,0:T(8,128)(2,1)}, bf16[2,64,384]{2,1,0:...) custom-call(s32[4]{0:T(128)} %pad_add_fusion.pos, bf16[256,768]{1,0:T(8,128)(2,1)} %bitcast.14, ...), custom_call_target="tpu_custom_call" | custom-call | tf_op jit(solution)/shard_map/pallas_call | solution.py:107
  11.7 2.1 %collective-permute-start.3 = (bf16[2,32,384]{2,1,0:T(8,128)(2,1)}, bf16[2,32,384]{2,1,0:T(8,128)(2,1)S(1)}, u32[]{:S(2)}, u32[]{:S(2)}) collective-permute-start(bf16[2,32,384]{2,1,0:T(8,128)(2,1)} %get-tuple-element.65), channel_id=1, source_target_pairs={{0,16},{8,24},{16,0},{24,8},{1,17},{9,25},{17,1},{25,9},{2,18},{10... | collective-permute-start | bytes 147464 | tf_op jit(solution)/shard_map/ppermute | solution.py:484
  13.9 1.9 %collective-permute-start.4 = (bf16[2,32,384]{2,1,0:T(8,128)(2,1)}, bf16[2,32,384]{2,1,0:T(8,128)(2,1)S(1)}, u32[]{:S(2)}, u32[]{:S(2)}) collective-permute-start(bf16[2,32,384]{2,1,0:T(8,128)(2,1)} %get-tuple-element.65), channel_id=1, source_target_pairs={{0,24},{8,16},{16,8},{24,0},{1,25},{9,17},{17,9},{25,1},{2,26},{10... | collective-permute-start | bytes 147464 | tf_op jit(solution)/shard_map/ppermute | solution.py:484
  15.8 7.7 %all-to-all-start = ((bf16[8,2,16,384]{3,2,1,0:T(8,128)(2,1)}), bf16[8,2,16,384]{3,2,1,0:T(8,128)(2,1)S(1)}, u32[]{:S(2)}, u32[]{:S(2)}) async-start(bf16[8,2,16,384]{3,2,1,0:T(8,128)(2,1)} %get-tuple-element.62), calls=%async_computation | async-start | bytes 393216 | tf_op jit(solution)/shard_map/all_to_all | solution.py:505
  23.9 5.1 %collective-permute-done.5.wy = bf16[2,128,384]{2,1,0:T(8,128)(2,1)S(1)} collective-permute-done((bf16[2,128,384]{2,1,0:T(8,128)(2,1)S(1)}, bf16[2,128,384]{2,1,0:T(8,128)(2,1)S(1)}, u32[]{:S(2)}, u32[]{:S(2)}) %collective-permute-start.5) | collective-permute-done | bytes 196640 | tf_op jit(solution)/shard_map/ppermute | solution.py:480
  29.0 3.2 %all-to-all-done.zr = bf16[8,2,16,384]{3,2,1,0:T(8,128)(2,1)S(1)} async-done(((bf16[8,2,16,384]{3,2,1,0:T(8,128)(2,1)}), bf16[8,2,16,384]{3,2,1,0:T(8,128)(2,1)S(1)}, u32[]{:S(2)}, u32[]{:S(2)}) %all-to-all-start) | async-done | bytes 196640 | tf_op jit(solution)/shard_map/all_to_all | solution.py:505
  32.9 2.6 %shard_map.86 = bf16[8,2,48,384]{3,2,1,0:T(8,128)(2,1)} custom-call(s32[4]{0:T(128)} %pad_add_fusion.pos, bf16[8,2,16,384]{3,2,1,0:T(8,128)(2,1)} %copy-done.9), custom_call_target="tpu_custom_call" | custom-call | tf_op jit(solution)/shard_map/pallas_call | solution.py:152
  35.5 3.8 %all-to-all-start.1 = ((bf16[8,2,48,384]{3,2,1,0:T(8,128)(2,1)}), bf16[8,2,48,384]{3,2,1,0:T(8,128)(2,1)S(1)}, u32[]{:S(2)}, u32[]{:S(2)}) async-start(bf16[8,2,48,384]{3,2,1,0:T(8,128)(2,1)} %shard_map.86), calls=%async_computation.1 | async-start | bytes 1179648 | tf_op jit(solution)/shard_map/all_to_all | solution.py:507
  39.3 5.3 %shard_map.85 = (bf16[2,256,384]{2,1,0:T(8,128)(2,1)}, bf16[2,256,384]{2,1,0:T(8,128)(2,1)}, bf16[2,768,256]{2,1,0:T(8,128)(2,1)}) custom-call(s32[4]{0:T(128)} %pad_add_fusion.pos, bf16[256,768]{1,0:T(8,128)(2,1)} %bitcast.15, bf16[256,768]{1,0:T(8,128)(2,1)} %copy-done.3, bf16[256,768]{1,0:T(8,128)(2,1)} %bitcast.16, bf16[256,768]{1,0:T(8,128)(2,1)} %copy-done.6, ...), custom_call_target="tpu_custom_call" | custom-call | tf_op jit(solution)/shard_map/pallas_call | solution.py:125
  44.5 2.3 %all-to-all-done.1.xr = bf16[8,2,48,384]{3,2,1,0:T(8,128)(2,1)S(1)} async-done(((bf16[8,2,48,384]{3,2,1,0:T(8,128)(2,1)}), bf16[8,2,48,384]{3,2,1,0:T(8,128)(2,1)S(1)}, u32[]{:S(2)}, u32[]{:S(2)}) %all-to-all-start.1) | async-done | bytes 589856 | tf_op jit(solution)/shard_map/all_to_all | solution.py:507
  47.6 17.9 %shard_map.87 = (bf16[2,256,384]{2,1,0:T(8,128)(2,1)}, bf16[2,256,384]{2,1,0:T(8,128)(2,1)}, f32[2,2,256,384]{3,2,1,0:T(8,128)}, f32[2,2,128,384]{3,2,1,0:T(8,12...) custom-call(s32[4]{0:T(128)} %pad_add_fusion.pos, ...), custom_call_target="tpu_custom_call" | custom-call | tf_op jit(solution)/shard_map/pallas_call | solution.py:239
  65.5 4.2 %collective-permute-start.7 = (bf16[2,256,384]{2,1,0:T(8,128)(2,1)}, bf16[2,256,384]{2,1,0:T(8,128)(2,1)S(1)}, u32[]{:S(2)}, u32[]{:S(2)}) collective-permute-start(bf16[2,256,384]{2,1,0:T(8,128)(2,1)} %get-tuple-element.75.att_own), channel_id=1, source_target_pairs={{0,2},{2,0},{1,3},{3,1},{4,6},{6,4},{5,7},{7,5},{8,10},{10,8},{9,1... | collective-permute-start | bytes 1179656 | tf_op jit(solution)/shard_map/ppermute | solution.py:480
  69.7 3.5 %all-to-all-start.2 = ((bf16[8,2,48,384]{3,2,1,0:T(8,128)(2,1)}), bf16[8,2,48,384]{3,2,1,0:T(8,128)(2,1)S(1)}, u32[]{:S(2)}, u32[]{:S(2)}) async-start(bf16[8,2,48,384]{3,2,1,0:T(8,128)(2,1)} %get-tuple-element.74), calls=%async_computation.2 | async-start | bytes 1179648 | tf_op jit(solution)/shard_map/all_to_all | solution.py:511
  74.0 5.6 %shard_map.88 = (bf16[2,2,96,384]{3,2,1,0:T(8,128)(2,1)}, bf16[2,2,96,384]{3,2,1,0:T(8,128)(2,1)}, bf16[2,2,96,384]{3,2,1,0:T(8,128)(2,1)}, bf16[2,2,96,384]{3,2,1,0:T(8,128)(2,1)}) custom-call(s32[4]{0:T(128)} %pad_add_fusion.pos, bf16[2,256,384]{2,1,0:T(8,128)(2,1)} %get-tuple-element.75.att_own, bf16[2,256,384]{2,1,0:T(8,128)(2,1)} %copy-done.4, ...), custom_call_target="tpu_custom_call" | custom-call | tf_op jit(solution)/shard_map/pallas_call | solution.py:284
  79.6 1.4 collective-permute-start.8
  80.9 1.2 collective-permute-start.9
  82.1 2.4 %collective-permute-start.10 = (bf16[2,2,96,384]{3,2,1,0:T(8,128)(2,1)}, bf16[2,2,96,384]{3,2,1,0:T(8,128)(2,1)S(1)}, u32[]{:S(2)}, u32[]{:S(2)}) collective-permute-start(bf16[2,2,96,384]{3,2,1,0:T(8,128)(2,1)} %get-tuple-element.85), channel_id=1, source_target_pairs={{0,16},{8,24},{16,0},{24,8},{1,17},{9,25},{17,1},{25,9},{2,18},{10... | collective-permute-start | bytes 884744 | tf_op jit(solution)/shard_map/ppermute | solution.py:484
  84.8 2.0 %collective-permute-done.9.dwy = bf16[2,128,384]{2,1,0:T(8,128)(2,1)S(1)} collective-permute-done((bf16[2,128,384]{2,1,0:T(8,128)(2,1)S(1)}, bf16[2,128,384]{2,1,0:T(8,128)(2,1)S(1)}, u32[]{:S(2)}, u32[]{:S(2)}) %collective-permute-start.9) | collective-permute-done | bytes 196640 | tf_op jit(solution)/shard_map/ppermute | solution.py:480
  86.8 1.6 collective-permute-done.8.t1
  88.4 2.7 %shard_map.89 = bf16[8,2,16,384]{3,2,1,0:T(8,128)(2,1)} custom-call(s32[4]{0:T(128)} %pad_add_fusion.pos, bf16[8,2,48,384]{3,2,1,0:T(8,128)(2,1)} %copy-done.1), custom_call_target="tpu_custom_call" | custom-call | tf_op jit(solution)/shard_map/pallas_call | solution.py:323
  91.1 3.4 %all-to-all-start.3 = ((bf16[8,2,16,384]{3,2,1,0:T(8,128)(2,1)}), bf16[8,2,16,384]{3,2,1,0:T(8,128)(2,1)S(1)}, u32[]{:S(2)}, u32[]{:S(2)}) async-start(bf16[8,2,16,384]{3,2,1,0:T(8,128)(2,1)} %shard_map.89), calls=%async_computation.3 | async-start | bytes 393216 | tf_op jit(solution)/shard_map/all_to_all | solution.py:517
  94.5 1.1 collective-permute-start.18
  95.6 1.2 collective-permute-done.10.t2
  96.8 2.9 %collective-permute-done.11.t3 = bf16[2,2,96,384]{3,2,1,0:T(8,128)(2,1)S(1)} collective-permute-done((bf16[2,2,96,384]{3,2,1,0:T(8,128)(2,1)}, bf16[2,2,96,384]{3,2,1,0:T(8,128)(2,1)S(1)}, u32[]{:S(2)}, u32[]{:S(2)}) %collective-permute-start.11) | collective-permute-done | bytes 294944 | tf_op jit(solution)/shard_map/ppermute | solution.py:484
  99.7 2.4 %shard_map.90 = (bf16[2,64,384]{2,1,0:T(8,128)(2,1)}, bf16[2,32,384]{2,1,0:T(8,128)(2,1)}, bf16[2,32,384]{2,1,0:T(8,128)(2,1)}) custom-call(s32[4]{0:T(128)} %pad_add_fusion.pos, f32[2,128,384]{2,1,0:T(8,128)} %get-tuple-element.87.dw, bf16[2,128,384]{2,1,0:T(8,128)(2,1)} %copy-done.16), custom_call_target="tpu_custom_call" | custom-call | tf_op jit(solution)/shard_map/pallas_call | solution.py:342
  102.1 1.1 collective-permute-start.14
  103.2 1.5 collective-permute-start.12
  104.7 2.8 %shard_map.91 = (bf16[96,384]{1,0:T(8,128)(2,1)}, bf16[96,384]{1,0:T(8,128)(2,1)}, bf16[96,384]{1,0:T(8,128)(2,1)}, bf16[96,384]{1,0:T(8,128)(2,1)}) custom-call(s32[4]{0:T(128)} %pad_add_fusion.pos, bf16[2,2,96,384]{3,2,1,0:T(8,128)(2,1)} %get-tuple-element.92.t0, bf16[2,2,96,384]{3,2,1,0:T(8,128)(2,1)} %copy-done.12, bf16[2,2,96,384]{3,2,1,0:T(8,128)(2,1)} %copy-done.13, ...), custom_call_target="tpu_custom_call" | custom-call | tf_op jit(solution)/shard_map/pallas_call | solution.py:304
  107.5 2.8 %collective-permute-start.15 = (bf16[96,384]{1,0:T(8,128)(2,1)}, bf16[96,384]{1,0:T(8,128)(2,1)S(1)}, u32[]{:S(2)}, u32[]{:S(2)}) collective-permute-start(bf16[96,384]{1,0:T(8,128)(2,1)} %get-tuple-element.97), channel_id=1, source_target_pairs={{0,1},{1,0},{4,5},{5,4},{2,3},{3,2},{6,7},{7,6},{8,9},{9,8},{12,13... | collective-permute-start | bytes 221192 | tf_op jit(solution)/shard_map/ppermute | solution.py:484
  110.8 1.7 collective-permute-done.15.f1
  112.5 1.3 collective-permute-done.16.f2
  113.8 1.6 collective-permute-done.17.f3
  116.2 6.2 %shard_map.92 = (bf16[2,256,1152]{2,1,0:T(8,128)(2,1)}, bf16[8,2,96,384]{3,2,1,0:T(8,128)(2,1)}) custom-call(s32[4]{0:T(128)} %pad_add_fusion.pos, bf16[8,2,16,384]{3,2,1,0:T(8,128)(2,1)} %copy-done.8, f32[2,2,256,384]{3,2,1,0:T(8,128)} %get-tuple-element.101.dkv, f32[2,2,128,384]{3,2,1,0:T(8,128)} %get-tuple-element.102.dn1, ...), custom_call_target="tpu_custom_call" | custom-call | tf_op jit(solution)/shard_map/pallas_call | solution.py:385
  122.4 3.8 %all-to-all-start.4 = ((bf16[16,96,384]{2,1,0:T(8,128)(2,1)}), bf16[16,96,384]{2,1,0:T(8,128)(2,1)S(1)}, u32[]{:S(2)}, u32[]{:S(2)}) async-start(bf16[16,96,384]{2,1,0:T(8,128)(2,1)} %bitcast.19), calls=%async_computation.4 | async-start | bytes 2359296 | tf_op jit(solution)/shard_map/all_to_all | solution.py:525
  127.2 4.1 %collective-permute-start.19 = (bf16[256,1152]{1,0:T(8,128)(2,1)S(1)}, bf16[256,1152]{1,0:T(8,128)(2,1)S(1)}, u32[]{:S(2)}, u32[]{:S(2)}) collective-permute-start(bf16[256,1152]{1,0:T(8,128)(2,1)S(1)} %get-tuple-element.120), channel_id=1, source_target_pairs={{0,2},{2,0},{1,3},{3,1},{4,6},{6,4},{5,7},{7,5},{8,10},{10,8},{9,1... | collective-permute-start | bytes 1769480 | tf_op jit(solution)/shard_map/ppermute | solution.py:480
  131.3 3.5 %shard_map.94 = bf16[256,768]{1,0:T(8,128)(2,1)} custom-call(s32[4]{0:T(128)} %pad_add_fusion.pos, bf16[2,256,384]{2,1,0:T(8,128)(2,1)} %get-tuple-element.75.att_own, bf16[2,256,384]{2,1,0:T(8,128)(2,1)} %copy-done.4, bf16[768,768]{1,0:T(8,128)(2,1)} %w_oth.1, bf16[768,768]{1,0:T(8,128)(2,1)} %w_oth.1), custom_call_target="tpu_custom_call" | custom-call | tf_op jit(solution)/shard_map/pallas_call | solution.py:258
  135.6 5.1 %shard_map.93 = bf16[256,768]{1,0:T(8,128)(2,1)} custom-call(s32[4]{0:T(128)} %pad_add_fusion.pos, bf16[256,1152]{1,0:T(8,128)(2,1)} %get-tuple-element.121.pg_own, bf16[256,1152]{1,0:T(8,128)(2,1)} %copy-done.10, bf16[768,2304]{1,0:T(8,128)(2,1)} %rest_5_.1, bf16[768,2304]{1,0:T(8,128)(2,1)} %rest_5_.1, bf16[768,2304]{1,0:T(8,128)(2,1)} %rest_5_.1, ...), custom_call_target="tpu_custom_call" | custom-call | tf_op jit(solution)/shard_map/pallas_call | solution.py:408
  140.8 1.0 copy-done
  141.8 3.2 %shard_map.95 = bf16[8,2,16,384]{3,2,1,0:T(8,128)(2,1)} custom-call(s32[4]{0:T(128)} %pad_add_fusion.pos, bf16[96,384]{1,0:T(8,128)(2,1)} %get-tuple-element.111.f0, bf16[96,384]{1,0:T(8,128)(2,1)} %copy-done.20, bf16[96,384]{1,0:T(8,128)(2,1)} %copy-done.21, bf16[96,384]{1,0:T(8,128)(2,1)} %copy-done.22, bf16[16,96,384]{2,1,0:T(8,128)(2,1)} %copy-done), custom_call_target="tpu_custom_call" | custom-call | tf_op jit(solution)/shard_map/pallas_call | solution.py:435
  145.0 13.8 %all_to_all.30.terms = bf16[8,2,16,384]{3,2,1,0:T(8,128)(2,1)} all-to-all(bf16[8,2,16,384]{3,2,1,0:T(8,128)(2,1)} %shard_map.95), channel_id=1, replica_groups=mesh['z'=8,'x'=4,'y'=2,'c'=2,'dp'=2] {'z'}, dimensions={0} | all-to-all | bytes 393216 | tf_op jit(solution)/shard_map/all_to_all | solution.py:531
  158.8 2.2 %shard_map.96 = (bf16[16,384]{1,0:T(8,128)(2,1)}, bf16[16,384]{1,0:T(8,128)(2,1)}) custom-call(s32[4]{0:T(128)} %pad_add_fusion.pos, bf16[8,2,16,384]{3,2,1,0:T(8,128)(2,1)} %all_to_all.30.terms), custom_call_target="tpu_custom_call" | custom-call | tf_op jit(solution)/shard_map/pallas_call | solution.py:446
  161.0 3.2 %collective-permute-start.20 = (bf16[16,384]{1,0:T(8,128)(2,1)}, bf16[16,384]{1,0:T(8,128)(2,1)S(1)}, u32[]{:S(2)}, u32[]{:S(2)}) collective-permute-start(bf16[16,384]{1,0:T(8,128)(2,1)} %get-tuple-element.116.own), channel_id=1, source_target_pairs={{0,1},{1,0},{2,3},{3,2},{4,5},{5,4},{6,7},{7,6},{8,9},{9,8},{10,11... | collective-permute-start | bytes 36872 | tf_op jit(solution)/shard_map/ppermute | solution.py:484
  164.3 4.7 %collective-permute-start.21 = (bf16[16,384]{1,0:T(8,128)(2,1)}, bf16[16,384]{1,0:T(8,128)(2,1)S(1)}, u32[]{:S(2)}, u32[]{:S(2)}) collective-permute-start(bf16[16,384]{1,0:T(8,128)(2,1)} %get-tuple-element.117), channel_id=1, source_target_pairs={{0,2},{1,3},{2,0},{3,1},{4,6},{5,7},{6,4},{7,5},{8,10},{9,11},{10,... | collective-permute-start | bytes 36872 | tf_op jit(solution)/shard_map/ppermute | solution.py:484
  169.0 2.0 %collective-permute-start.22 = (bf16[16,384]{1,0:T(8,128)(2,1)}, bf16[16,384]{1,0:T(8,128)(2,1)S(1)}, u32[]{:S(2)}, u32[]{:S(2)}) collective-permute-start(bf16[16,384]{1,0:T(8,128)(2,1)} %get-tuple-element.117), channel_id=1, source_target_pairs={{0,3},{1,2},{2,1},{3,0},{4,7},{5,6},{6,5},{7,4},{8,11},{9,10},{10,... | collective-permute-start | bytes 36872 | tf_op jit(solution)/shard_map/ppermute | solution.py:484
  171.1 2.8 %collective-permute-done.22.from_both = bf16[16,384]{1,0:T(8,128)(2,1)S(1)} collective-permute-done((bf16[16,384]{1,0:T(8,128)(2,1)}, bf16[16,384]{1,0:T(8,128)(2,1)S(1)}, u32[]{:S(2)}, u32[]{:S(2)}) %collective-permute-start.22) | collective-permute-done | bytes 12320 | tf_op jit(solution)/shard_map/ppermute | solution.py:484
  174.5 2.1 %shard_map.97 = (f32[6,2304]{1,0:T(8,128)}, f32[6,768]{1,0:T(8,128)}) custom-call(s32[4]{0:T(128)} %pad_add_fusion.pos, bf16[16,384]{1,0:T(8,128)(2,1)} %get-tuple-element.116.own, bf16[16,384]{1,0:T(8,128)(2,1)} %copy-done.25, bf16[16,384]{1,0:T(8,128)(2,1)} %copy-done.26, bf16[16,384]{1,0:T(8,128)(2,1)} %copy-done.27), custom_call_target="tpu_custom_call" | custom-call | tf_op jit(solution)/shard_map/pallas_call | solution.py:470
  (88 shorter events, 8.3 us)
Async XLA Ops:
  0.6 4.9 %collective-permute-start = (bf16[256,768]{1,0:T(8,128)(2,1)}, bf16[256,768]{1,0:T(8,128)(2,1)S(1)}, u32[]{:S(2)}, u32[]{:S(2)}) collective-permute-start(bf16[256,768]{1,0:T(8,128)(2,1)} %bitcast.13), channel_id=1, source_target_pairs={{0,2},{2,0},{1,3},{3,1},{4,6},{6,4},{5,7},{7,5},{8,10},{10,8},{9,1... | collective-permute-start | bytes 1179656 | tf_op jit(solution)/shard_map/ppermute | solution.py:480
  4.6 6.7 %copy-start.5 = (bf16[1,256,768]{2,1,0:T(8,128)(2,1)S(1)}, bf16[1,256,768]{2,1,0:T(8,128)(2,1)}, u32[]{:S(2)}) copy-start(bf16[1,256,768]{2,1,0:T(8,128)(2,1)} %param.6) | copy-start | bytes 1179652
  11.3 12.3 %collective-permute-start.2 = (bf16[2,64,384]{2,1,0:T(8,128)(2,1)}, bf16[2,64,384]{2,1,0:T(8,128)(2,1)S(1)}, u32[]{:S(2)}, u32[]{:S(2)}) collective-permute-start(bf16[2,64,384]{2,1,0:T(8,128)(2,1)} %get-tuple-element.64), channel_id=1, source_target_pairs={{0,8},{8,0},{16,24},{24,16},{1,9},{9,1},{17,25},{25,17},{2,10},{10... | collective-permute-start | bytes 294920 | tf_op jit(solution)/shard_map/ppermute | solution.py:484
  11.3 12.6 %collective-permute-start.6 = (bf16[256,768]{1,0:T(8,128)(2,1)S(1)}, bf16[256,768]{1,0:T(8,128)(2,1)S(1)}, u32[]{:S(2)}, u32[]{:S(2)}) collective-permute-start(bf16[256,768]{1,0:T(8,128)(2,1)S(1)} %bitcast.18), channel_id=1, source_target_pairs={{0,2},{2,0},{1,3},{3,1},{4,6},{6,4},{5,7},{7,5},{8,10},{10,8},{9,1... | collective-permute-start | bytes 1179656 | tf_op jit(solution)/shard_map/ppermute | solution.py:480
  11.7 11.8 %collective-permute-start.3 = (bf16[2,32,384]{2,1,0:T(8,128)(2,1)}, bf16[2,32,384]{2,1,0:T(8,128)(2,1)S(1)}, u32[]{:S(2)}, u32[]{:S(2)}) collective-permute-start(bf16[2,32,384]{2,1,0:T(8,128)(2,1)} %get-tuple-element.65), channel_id=1, source_target_pairs={{0,16},{8,24},{16,0},{24,8},{1,17},{9,25},{17,1},{25,9},{2,18},{10... | collective-permute-start | bytes 147464 | tf_op jit(solution)/shard_map/ppermute | solution.py:484
  13.9 9.7 %collective-permute-start.4 = (bf16[2,32,384]{2,1,0:T(8,128)(2,1)}, bf16[2,32,384]{2,1,0:T(8,128)(2,1)S(1)}, u32[]{:S(2)}, u32[]{:S(2)}) collective-permute-start(bf16[2,32,384]{2,1,0:T(8,128)(2,1)} %get-tuple-element.65), channel_id=1, source_target_pairs={{0,24},{8,16},{16,8},{24,0},{1,25},{9,17},{17,9},{25,1},{2,26},{10... | collective-permute-start | bytes 147464 | tf_op jit(solution)/shard_map/ppermute | solution.py:484
  15.8 8.1 %collective-permute-start.1 = (bf16[2,128,384]{2,1,0:T(8,128)(2,1)}, bf16[2,128,384]{2,1,0:T(8,128)(2,1)S(1)}, u32[]{:S(2)}, u32[]{:S(2)}) collective-permute-start(bf16[2,128,384]{2,1,0:T(8,128)(2,1)} %get-tuple-element.63), channel_id=1, source_target_pairs={{0,4},{4,0},{1,5},{5,1},{2,6},{6,2},{3,7},{7,3},{8,12},{12,8},{9,1... | collective-permute-start | bytes 589832 | tf_op jit(solution)/shard_map/ppermute | solution.py:480
  15.8 16.4 %all-to-all-start = ((bf16[8,2,16,384]{3,2,1,0:T(8,128)(2,1)}), bf16[8,2,16,384]{3,2,1,0:T(8,128)(2,1)S(1)}, u32[]{:S(2)}, u32[]{:S(2)}) async-start(bf16[8,2,16,384]{3,2,1,0:T(8,128)(2,1)} %get-tuple-element.62), calls=%async_computation | async-start | bytes 393216 | tf_op jit(solution)/shard_map/all_to_all | solution.py:505
  23.6 20.9 %copy-start.11 = (bf16[2,128,384]{2,1,0:T(8,128)(2,1)}, bf16[2,128,384]{2,1,0:T(8,128)(2,1)S(1)}, u32[]{:S(2)}) copy-start(bf16[2,128,384]{2,1,0:T(8,128)(2,1)S(1)} %constant_dynamic-update-slice_fusion.wr) | copy-start | bytes 589828
  23.6 5.4 %collective-permute-start.5 = (bf16[2,128,384]{2,1,0:T(8,128)(2,1)S(1)}, bf16[2,128,384]{2,1,0:T(8,128)(2,1)S(1)}, u32[]{:S(2)}, u32[]{:S(2)}) collective-permute-start(bf16[2,128,384]{2,1,0:T(8,128)(2,1)S(1)} %constant_dynamic-update-slice_fusion.wr), channel_id=1, source_target_pairs={{0,4},{4,0},{1,5},{5,1},{2,6},{6,2},{3,7},{7,3},{8,12},{12,8},{9,1... | collective-permute-start | bytes 589832 | tf_op jit(solution)/shard_map/ppermute | solution.py:480
  23.9 15.4 %copy-start.6 = (bf16[256,768]{1,0:T(8,128)(2,1)}, bf16[256,768]{1,0:T(8,128)(2,1)S(1)}, u32[]{:S(2)}) copy-start(bf16[256,768]{1,0:T(8,128)(2,1)S(1)} %collective-permute-done.6.ct_oth) | copy-start | bytes 1179652
  23.9 20.6 %copy-start.17 = (bf16[2,128,384]{2,1,0:T(8,128)(2,1)}, bf16[2,128,384]{2,1,0:T(8,128)(2,1)S(1)}, u32[]{:S(2)}) copy-start(bf16[2,128,384]{2,1,0:T(8,128)(2,1)S(1)} %collective-permute-done.1.yr) | copy-start | bytes 589828
  29.0 15.6 %copy-start.18 = (bf16[2,128,384]{2,1,0:T(8,128)(2,1)}, bf16[2,128,384]{2,1,0:T(8,128)(2,1)S(1)}, u32[]{:S(2)}) copy-start(bf16[2,128,384]{2,1,0:T(8,128)(2,1)S(1)} %collective-permute-done.5.wy) | copy-start | bytes 589828
  35.5 11.3 %all-to-all-start.1 = ((bf16[8,2,48,384]{3,2,1,0:T(8,128)(2,1)}), bf16[8,2,48,384]{3,2,1,0:T(8,128)(2,1)S(1)}, u32[]{:S(2)}, u32[]{:S(2)}) async-start(bf16[8,2,48,384]{3,2,1,0:T(8,128)(2,1)} %shard_map.86), calls=%async_computation.1 | async-start | bytes 1179648 | tf_op jit(solution)/shard_map/all_to_all | solution.py:507
  65.5 7.7 %collective-permute-start.7 = (bf16[2,256,384]{2,1,0:T(8,128)(2,1)}, bf16[2,256,384]{2,1,0:T(8,128)(2,1)S(1)}, u32[]{:S(2)}, u32[]{:S(2)}) collective-permute-start(bf16[2,256,384]{2,1,0:T(8,128)(2,1)} %get-tuple-element.75.att_own), channel_id=1, source_target_pairs={{0,2},{2,0},{1,3},{3,1},{4,6},{6,4},{5,7},{7,5},{8,10},{10,8},{9,1... | collective-permute-start | bytes 1179656 | tf_op jit(solution)/shard_map/ppermute | solution.py:480
  69.7 17.1 %all-to-all-start.2 = ((bf16[8,2,48,384]{3,2,1,0:T(8,128)(2,1)}), bf16[8,2,48,384]{3,2,1,0:T(8,128)(2,1)S(1)}, u32[]{:S(2)}, u32[]{:S(2)}) async-start(bf16[8,2,48,384]{3,2,1,0:T(8,128)(2,1)} %get-tuple-element.74), calls=%async_computation.2 | async-start | bytes 1179648 | tf_op jit(solution)/shard_map/all_to_all | solution.py:511
  74.0 6.9 %copy-start.29 = (bf16[2,128,384]{2,1,0:T(8,128)(2,1)S(1)}, bf16[2,128,384]{2,1,0:T(8,128)(2,1)}, u32[]{:S(2)}) copy-start(bf16[2,128,384]{2,1,0:T(8,128)(2,1)} %get-tuple-element.80) | copy-start | bytes 589828
  79.6 14.9 %copy-start.28 = (bf16[2,128,384]{2,1,0:T(8,128)(2,1)S(1)}, bf16[2,128,384]{2,1,0:T(8,128)(2,1)}, u32[]{:S(2)}) copy-start(bf16[2,128,384]{2,1,0:T(8,128)(2,1)} %get-tuple-element.103) | copy-start | bytes 589828
  79.6 8.8 %collective-permute-start.8 = (bf16[2,2,96,384]{3,2,1,0:T(8,128)(2,1)}, bf16[2,2,96,384]{3,2,1,0:T(8,128)(2,1)S(1)}, u32[]{:S(2)}, u32[]{:S(2)}) collective-permute-start(bf16[2,2,96,384]{3,2,1,0:T(8,128)(2,1)} %get-tuple-element.79), channel_id=1, source_target_pairs={{0,8},{8,0},{16,24},{24,16},{1,9},{9,1},{17,25},{25,17},{2,10},{10... | collective-permute-start | bytes 884744 | tf_op jit(solution)/shard_map/ppermute | solution.py:484
  80.9 5.9 %collective-permute-start.9 = (bf16[2,128,384]{2,1,0:T(8,128)(2,1)S(1)}, bf16[2,128,384]{2,1,0:T(8,128)(2,1)S(1)}, u32[]{:S(2)}, u32[]{:S(2)}) collective-permute-start(bf16[2,128,384]{2,1,0:T(8,128)(2,1)S(1)} %copy-done.29), channel_id=1, source_target_pairs={{0,4},{4,0},{1,5},{5,1},{2,6},{6,2},{3,7},{7,3},{8,12},{12,8},{9,1... | collective-permute-start | bytes 589832 | tf_op jit(solution)/shard_map/ppermute | solution.py:480
  82.1 14.6 %collective-permute-start.10 = (bf16[2,2,96,384]{3,2,1,0:T(8,128)(2,1)}, bf16[2,2,96,384]{3,2,1,0:T(8,128)(2,1)S(1)}, u32[]{:S(2)}, u32[]{:S(2)}) collective-permute-start(bf16[2,2,96,384]{3,2,1,0:T(8,128)(2,1)} %get-tuple-element.85), channel_id=1, source_target_pairs={{0,16},{8,24},{16,0},{24,8},{1,17},{9,25},{17,1},{25,9},{2,18},{10... | collective-permute-start | bytes 884744 | tf_op jit(solution)/shard_map/ppermute | solution.py:484
  84.6 15.1 %collective-permute-start.11 = (bf16[2,2,96,384]{3,2,1,0:T(8,128)(2,1)}, bf16[2,2,96,384]{3,2,1,0:T(8,128)(2,1)S(1)}, u32[]{:S(2)}, u32[]{:S(2)}) collective-permute-start(bf16[2,2,96,384]{3,2,1,0:T(8,128)(2,1)} %get-tuple-element.86), channel_id=1, source_target_pairs={{0,24},{8,16},{16,8},{24,0},{1,25},{9,17},{17,9},{25,1},{2,26},{10... | collective-permute-start | bytes 884744 | tf_op jit(solution)/shard_map/ppermute | solution.py:484
  86.8 12.8 %copy-start.16 = (bf16[2,128,384]{2,1,0:T(8,128)(2,1)}, bf16[2,128,384]{2,1,0:T(8,128)(2,1)S(1)}, u32[]{:S(2)}) copy-start(bf16[2,128,384]{2,1,0:T(8,128)(2,1)S(1)} %collective-permute-done.9.dwy) | copy-start | bytes 589828
  86.8 1.6 copy-start.1
  88.4 16.3 %copy-start.12 = (bf16[2,2,96,384]{3,2,1,0:T(8,128)(2,1)}, bf16[2,2,96,384]{3,2,1,0:T(8,128)(2,1)S(1)}, u32[]{:S(2)}) copy-start(bf16[2,2,96,384]{3,2,1,0:T(8,128)(2,1)S(1)} %collective-permute-done.8.t1) | copy-start | bytes 884740
  91.1 24.3 %all-to-all-start.3 = ((bf16[8,2,16,384]{3,2,1,0:T(8,128)(2,1)}), bf16[8,2,16,384]{3,2,1,0:T(8,128)(2,1)S(1)}, u32[]{:S(2)}, u32[]{:S(2)}) async-start(bf16[8,2,16,384]{3,2,1,0:T(8,128)(2,1)} %shard_map.89), calls=%async_computation.3 | async-start | bytes 393216 | tf_op jit(solution)/shard_map/all_to_all | solution.py:517
  94.5 20.9 %collective-permute-start.18 = (bf16[2,128,384]{2,1,0:T(8,128)(2,1)S(1)}, bf16[2,128,384]{2,1,0:T(8,128)(2,1)S(1)}, u32[]{:S(2)}, u32[]{:S(2)}) collective-permute-start(bf16[2,128,384]{2,1,0:T(8,128)(2,1)S(1)} %copy-done.28), channel_id=1, source_target_pairs={{0,4},{4,0},{1,5},{5,1},{2,6},{6,2},{3,7},{7,3},{8,12},{12,8},{9,1... | collective-permute-start | bytes 589832 | tf_op jit(solution)/shard_map/ppermute | solution.py:480
  96.8 8.0 %copy-start.13 = (bf16[2,2,96,384]{3,2,1,0:T(8,128)(2,1)}, bf16[2,2,96,384]{3,2,1,0:T(8,128)(2,1)S(1)}, u32[]{:S(2)}) copy-start(bf16[2,2,96,384]{3,2,1,0:T(8,128)(2,1)S(1)} %collective-permute-done.10.t2) | copy-start | bytes 884740
  99.6 5.1 %copy-start.14 = (bf16[2,2,96,384]{3,2,1,0:T(8,128)(2,1)}, bf16[2,2,96,384]{3,2,1,0:T(8,128)(2,1)S(1)}, u32[]{:S(2)}) copy-start(bf16[2,2,96,384]{3,2,1,0:T(8,128)(2,1)S(1)} %collective-permute-done.11.t3) | copy-start | bytes 884740
  102.1 8.3 %collective-permute-start.13 = (bf16[2,32,384]{2,1,0:T(8,128)(2,1)}, bf16[2,32,384]{2,1,0:T(8,128)(2,1)S(1)}, u32[]{:S(2)}, u32[]{:S(2)}) collective-permute-start(bf16[2,32,384]{2,1,0:T(8,128)(2,1)} %get-tuple-element.90), channel_id=1, source_target_pairs={{0,16},{8,24},{16,0},{24,8},{1,17},{9,25},{17,1},{25,9},{2,18},{10... | collective-permute-start | bytes 147464 | tf_op jit(solution)/shard_map/ppermute | solution.py:484
  102.1 8.3 %collective-permute-start.14 = (bf16[2,32,384]{2,1,0:T(8,128)(2,1)}, bf16[2,32,384]{2,1,0:T(8,128)(2,1)S(1)}, u32[]{:S(2)}, u32[]{:S(2)}) collective-permute-start(bf16[2,32,384]{2,1,0:T(8,128)(2,1)} %get-tuple-element.91), channel_id=1, source_target_pairs={{0,24},{8,16},{16,8},{24,0},{1,25},{9,17},{17,9},{25,1},{2,26},{10... | collective-permute-start | bytes 147464 | tf_op jit(solution)/shard_map/ppermute | solution.py:484
  103.2 12.2 %collective-permute-start.12 = (bf16[2,64,384]{2,1,0:T(8,128)(2,1)}, bf16[2,64,384]{2,1,0:T(8,128)(2,1)S(1)}, u32[]{:S(2)}, u32[]{:S(2)}) collective-permute-start(bf16[2,64,384]{2,1,0:T(8,128)(2,1)} %get-tuple-element.89), channel_id=1, source_target_pairs={{0,8},{8,0},{16,24},{24,16},{1,9},{9,1},{17,25},{25,17},{2,10},{10... | collective-permute-start | bytes 294920 | tf_op jit(solution)/shard_map/ppermute | solution.py:484
  107.5 4.9 %collective-permute-start.15 = (bf16[96,384]{1,0:T(8,128)(2,1)}, bf16[96,384]{1,0:T(8,128)(2,1)S(1)}, u32[]{:S(2)}, u32[]{:S(2)}) collective-permute-start(bf16[96,384]{1,0:T(8,128)(2,1)} %get-tuple-element.97), channel_id=1, source_target_pairs={{0,1},{1,0},{4,5},{5,4},{2,3},{3,2},{6,7},{7,6},{8,9},{9,8},{12,13... | collective-permute-start | bytes 221192 | tf_op jit(solution)/shard_map/ppermute | solution.py:484
  110.4 5.1 %copy-start.23 = (bf16[2,32,384]{2,1,0:T(8,128)(2,1)}, bf16[2,32,384]{2,1,0:T(8,128)(2,1)S(1)}, u32[]{:S(2)}) copy-start(bf16[2,32,384]{2,1,0:T(8,128)(2,1)S(1)} %collective-permute-done.13.g4_a) | copy-start | bytes 147460
  110.4 3.4 %collective-permute-start.16 = (bf16[96,384]{1,0:T(8,128)(2,1)}, bf16[96,384]{1,0:T(8,128)(2,1)S(1)}, u32[]{:S(2)}, u32[]{:S(2)}) collective-permute-start(bf16[96,384]{1,0:T(8,128)(2,1)} %get-tuple-element.98), channel_id=1, source_target_pairs={{0,4},{1,5},{4,0},{5,1},{2,6},{3,7},{6,2},{7,3},{8,12},{9,13},{12,... | collective-permute-start | bytes 221192 | tf_op jit(solution)/shard_map/ppermute | solution.py:484
  110.4 5.1 %copy-start.24 = (bf16[2,32,384]{2,1,0:T(8,128)(2,1)}, bf16[2,32,384]{2,1,0:T(8,128)(2,1)S(1)}, u32[]{:S(2)}) copy-start(bf16[2,32,384]{2,1,0:T(8,128)(2,1)S(1)} %collective-permute-done.14.g4_b) | copy-start | bytes 147460
  110.4 5.0 %collective-permute-start.17 = (bf16[96,384]{1,0:T(8,128)(2,1)}, bf16[96,384]{1,0:T(8,128)(2,1)S(1)}, u32[]{:S(2)}, u32[]{:S(2)}) collective-permute-start(bf16[96,384]{1,0:T(8,128)(2,1)} %get-tuple-element.99), channel_id=1, source_target_pairs={{0,5},{1,4},{4,1},{5,0},{2,7},{3,6},{6,3},{7,2},{8,13},{9,12},{12,... | collective-permute-start | bytes 221192 | tf_op jit(solution)/shard_map/ppermute | solution.py:484
  112.5 14.7 %copy-start.20 = (bf16[96,384]{1,0:T(8,128)(2,1)}, bf16[96,384]{1,0:T(8,128)(2,1)S(1)}, u32[]{:S(2)}) copy-start(bf16[96,384]{1,0:T(8,128)(2,1)S(1)} %collective-permute-done.15.f1) | copy-start | bytes 221188
  113.8 13.4 %copy-start.21 = (bf16[96,384]{1,0:T(8,128)(2,1)}, bf16[96,384]{1,0:T(8,128)(2,1)S(1)}, u32[]{:S(2)}) copy-start(bf16[96,384]{1,0:T(8,128)(2,1)S(1)} %collective-permute-done.16.f2) | copy-start | bytes 221188
  115.4 11.8 %copy-start.22 = (bf16[96,384]{1,0:T(8,128)(2,1)}, bf16[96,384]{1,0:T(8,128)(2,1)S(1)}, u32[]{:S(2)}) copy-start(bf16[96,384]{1,0:T(8,128)(2,1)S(1)} %collective-permute-done.17.f3) | copy-start | bytes 221188
  122.4 3.8 %copy-start.7 = (bf16[2,256,1152]{2,1,0:T(8,128)(2,1)S(1)}, bf16[2,256,1152]{2,1,0:T(8,128)(2,1)}, u32[]{:S(2)}) copy-start(bf16[2,256,1152]{2,1,0:T(8,128)(2,1)} %get-tuple-element.108) | copy-start | bytes 3538948
  122.4 18.4 %all-to-all-start.4 = ((bf16[16,96,384]{2,1,0:T(8,128)(2,1)}), bf16[16,96,384]{2,1,0:T(8,128)(2,1)S(1)}, u32[]{:S(2)}, u32[]{:S(2)}) async-start(bf16[16,96,384]{2,1,0:T(8,128)(2,1)} %bitcast.19), calls=%async_computation.4 | async-start | bytes 2359296 | tf_op jit(solution)/shard_map/all_to_all | solution.py:525
  127.2 7.6 %collective-permute-start.19 = (bf16[256,1152]{1,0:T(8,128)(2,1)S(1)}, bf16[256,1152]{1,0:T(8,128)(2,1)S(1)}, u32[]{:S(2)}, u32[]{:S(2)}) collective-permute-start(bf16[256,1152]{1,0:T(8,128)(2,1)S(1)} %get-tuple-element.120), channel_id=1, source_target_pairs={{0,2},{2,0},{1,3},{3,1},{4,6},{6,4},{5,7},{7,5},{8,10},{10,8},{9,1... | collective-permute-start | bytes 1769480 | tf_op jit(solution)/shard_map/ppermute | solution.py:480
  161.0 10.0 %collective-permute-start.20 = (bf16[16,384]{1,0:T(8,128)(2,1)}, bf16[16,384]{1,0:T(8,128)(2,1)S(1)}, u32[]{:S(2)}, u32[]{:S(2)}) collective-permute-start(bf16[16,384]{1,0:T(8,128)(2,1)} %get-tuple-element.116.own), channel_id=1, source_target_pairs={{0,1},{1,0},{2,3},{3,2},{4,5},{5,4},{6,7},{7,6},{8,9},{9,8},{10,11... | collective-permute-start | bytes 36872 | tf_op jit(solution)/shard_map/ppermute | solution.py:484
  164.3 6.8 %collective-permute-start.21 = (bf16[16,384]{1,0:T(8,128)(2,1)}, bf16[16,384]{1,0:T(8,128)(2,1)S(1)}, u32[]{:S(2)}, u32[]{:S(2)}) collective-permute-start(bf16[16,384]{1,0:T(8,128)(2,1)} %get-tuple-element.117), channel_id=1, source_target_pairs={{0,2},{1,3},{2,0},{3,1},{4,6},{5,7},{6,4},{7,5},{8,10},{9,11},{10,... | collective-permute-start | bytes 36872 | tf_op jit(solution)/shard_map/ppermute | solution.py:484
  169.0 4.8 %collective-permute-start.22 = (bf16[16,384]{1,0:T(8,128)(2,1)}, bf16[16,384]{1,0:T(8,128)(2,1)S(1)}, u32[]{:S(2)}, u32[]{:S(2)}) collective-permute-start(bf16[16,384]{1,0:T(8,128)(2,1)} %get-tuple-element.117), channel_id=1, source_target_pairs={{0,3},{1,2},{2,1},{3,0},{4,7},{5,6},{6,5},{7,4},{8,11},{9,10},{10,... | collective-permute-start | bytes 36872 | tf_op jit(solution)/shard_map/ppermute | solution.py:484
  171.1 2.8 %copy-start.25 = (bf16[16,384]{1,0:T(8,128)(2,1)}, bf16[16,384]{1,0:T(8,128)(2,1)S(1)}, u32[]{:S(2)}) copy-start(bf16[16,384]{1,0:T(8,128)(2,1)S(1)} %collective-permute-done.20.from_dp) | copy-start | bytes 36868
  171.1 2.8 %copy-start.26 = (bf16[16,384]{1,0:T(8,128)(2,1)}, bf16[16,384]{1,0:T(8,128)(2,1)S(1)}, u32[]{:S(2)}) copy-start(bf16[16,384]{1,0:T(8,128)(2,1)S(1)} %collective-permute-done.21.from_core) | copy-start | bytes 36868
  (10 other events, 7.7 us)

commit v7 on v6

--- a/solution.py
+++ b/solution.py
@@ -513,15 +513,15 @@
     dwy = swap(dwy, "y")
     first, *firsts = output_terms(pos, att, att_oth, ct_own, ct_oth, dq, xt, perm)
     firsts = [along(firsts[far - 1], "x", far) for far in (1, 2, 3)]
-    dx_r, first, firsts[0], dwy = lax.optimization_barrier((dx_r, first, firsts[0], dwy))
+    g3, g4_a, g4_b = hand_back(pos, dw, dwy)
+    dx_r, first, firsts[0], g3, g4_a, g4_b = lax.optimization_barrier((dx_r, first, firsts[0], g3, g4_a, g4_b))
     dz_r = lax.all_to_all(back_slots(pos, dx_r), "z", 0, 0)
-    dw, dwy, firsts = lax.optimization_barrier((dw, dwy, firsts))
-    g3, g4_a, g4_b = hand_back(pos, dw, dwy)
     g3, g4_a, g4_b = along(g3, "x", 1), along(g4_a, "x", 2), along(g4_b, "x", 3)
     firsts = x_sum(pos, first, *firsts)
+    dz_r, g3, g4_a, g4_b, firsts = lax.optimization_barrier((dz_r, g3, g4_a, g4_b, firsts))
     firsts = list(firsts[:1]) + [along(firsts[far], ("y", "dp"), far) for far in (1, 2, 3)]
-    dz_r, g3, g4_a, g4_b, firsts = lax.optimization_barrier((dz_r, g3, g4_a, g4_b, firsts))
     pg, terms = leaf_grads(pos, dz_r, dkv, dn1, swap(dy, "y"), g3, g4_a, g4_b, dq, xt)
+    terms, firsts = lax.optimization_barrier((terms, firsts))
     terms = lax.all_to_all(terms.reshape(16, 96, H), ("x", "y", "dp"), 0, 0)
     pg_own = lax.dynamic_index_in_dim(pg, c, 0, keepdims=False)
     pg_oth = swap(lax.dynamic_index_in_dim(pg, 1 - c, 0, keepdims=False), "c")

time: 178 us -> 180 us (1.011)
  waiting for transfers between devices: 26.6 us -> 22 us
  local copies, waits for them, and re-layouts: 7.31 us -> 10.1 us
  starting transfers between devices: 60.9 us -> 63.3 us
    ppermute x15, waiting for transfers between devices: 13 us -> 5.85 us  [along(): return lax.ppermute(value, axes, [(i, i ^ far) for i in range(count)])]
    unnamed x62 -> x70, local copies, waits for them, and re-layouts: 6.36 us -> 9.1 us
    ppermute x8, waiting for transfers between devices: 8.07 us -> 10.7 us  [swap(): return lax.ppermute(value, axis, [(0, 1), (1, 0)])]
  transfers between devices with their start and end apart: 28 -> 28, of which waited for: 12 -> 7; matrix products, arithmetic and copies ran while one was open for 1% -> 1% of each run, Pallas kernels for 15% -> 19%
where the time goes in v7:
time: 180 us; the launch traced here: 179 us
  Pallas kernels  66.5 us (37%)
  starting transfers between devices  63.3 us (35%)
  waiting for transfers between devices  22 us (12%)
  blocking collectives  15.2 us (8%)
  local copies, waits for them, and re-layouts  10.1 us (6%)
    ppermute x15, starting transfers between devices, along(): return lax.ppermute(value, axes, [(i, i ^ far) for i in range(count)])  25.7 us
    pallas_call x1, Pallas kernels, attention(): call(attention_body, (H // 128,), [cut(2, TOK), cut(2, TOK), cut(2, 2, TO...  17.8 us
    all_to_all x1, blocking collectives, shards(): terms = lax.all_to_all(middle_sum(pos, firsts, terms), 'z', 0, 0)  15.2 us
    ppermute x8, starting transfers between devices, swap(): return lax.ppermute(value, axis, [(0, 1), (1, 0)])  15 us
    ppermute x8, waiting for transfers between devices, swap(): return lax.ppermute(value, axis, [(0, 1), (1, 0)])  10.7 us
    unnamed x70, local copies, waits for them, and re-layouts  9.1 us
    all_to_all x1, starting transfers between devices, shards(): zr = lax.all_to_all(zs, 'z', 0, 0)  7.75 us
    pallas_call x1, Pallas kernels, leaf_grads(): call(leaf_body, (1,), [whole(ZN, 2, 16, H), whole(2, 2, TOK, H), whole(2,...  6.19 us
  transfers between devices with their start and end apart: 28, of which 7 were waited for; matrix products, arithmetic and copies ran while one was open for 1% of the time, Pallas kernels for 19%

profile of v7, /device:TPU:1, one launch (start us, length us, event | category | flops | bytes accessed | tf_op | source)
XLA Modules:
  0.0 178.7 jit_solution(11717966854308225204)
XLA Ops:
  0.6 3.3 %collective-permute-start = (bf16[256,768]{1,0:T(8,128)(2,1)}, bf16[256,768]{1,0:T(8,128)(2,1)S(1)}, u32[]{:S(2)}, u32[]{:S(2)}) collective-permute-start(bf16[256,768]{1,0:T(8,128)(2,1)} %bitcast.13), channel_id=1, source_target_pairs={{0,2},{2,0},{1,3},{3,1},{4,6},{6,4},{5,7},{7,5},{8,10},{10,8},{9,1... | collective-permute-start | bytes 1179656 | tf_op jit(solution)/shard_map/ppermute | solution.py:480
  4.6 1.0 collective-permute-done.x_oth
  5.5 0.7 copy-done.3
  6.3 5.0 %shard_map.84 = (bf16[2,2,256,384]{3,2,1,0:T(8,128)(2,1)}, bf16[2,2,128,384]{3,2,1,0:T(8,128)(2,1)}, bf16[2,128,384]{2,1,0:T(8,128)(2,1)}, bf16[2,64,384]{2,1,0:...) custom-call(s32[4]{0:T(128)} %pad_add_fusion.pos, bf16[256,768]{1,0:T(8,128)(2,1)} %bitcast.14, ...), custom_call_target="tpu_custom_call" | custom-call | tf_op jit(solution)/shard_map/pallas_call | solution.py:107
  11.7 2.1 %collective-permute-start.3 = (bf16[2,32,384]{2,1,0:T(8,128)(2,1)}, bf16[2,32,384]{2,1,0:T(8,128)(2,1)S(1)}, u32[]{:S(2)}, u32[]{:S(2)}) collective-permute-start(bf16[2,32,384]{2,1,0:T(8,128)(2,1)} %get-tuple-element.67), channel_id=1, source_target_pairs={{0,16},{8,24},{16,0},{24,8},{1,17},{9,25},{17,1},{25,9},{2,18},{10... | collective-permute-start | bytes 147464 | tf_op jit(solution)/shard_map/ppermute | solution.py:484
  13.8 1.9 %collective-permute-start.4 = (bf16[2,32,384]{2,1,0:T(8,128)(2,1)}, bf16[2,32,384]{2,1,0:T(8,128)(2,1)S(1)}, u32[]{:S(2)}, u32[]{:S(2)}) collective-permute-start(bf16[2,32,384]{2,1,0:T(8,128)(2,1)} %get-tuple-element.67), channel_id=1, source_target_pairs={{0,24},{8,16},{16,8},{24,0},{1,25},{9,17},{17,9},{25,1},{2,26},{10... | collective-permute-start | bytes 147464 | tf_op jit(solution)/shard_map/ppermute | solution.py:484
  15.8 7.7 %all-to-all-start = ((bf16[8,2,16,384]{3,2,1,0:T(8,128)(2,1)}), bf16[8,2,16,384]{3,2,1,0:T(8,128)(2,1)S(1)}, u32[]{:S(2)}, u32[]{:S(2)}) async-start(bf16[8,2,16,384]{3,2,1,0:T(8,128)(2,1)} %get-tuple-element.64), calls=%async_computation | async-start | bytes 393216 | tf_op jit(solution)/shard_map/all_to_all | solution.py:505
  23.9 5.1 %collective-permute-done.5.wy = bf16[2,128,384]{2,1,0:T(8,128)(2,1)S(1)} collective-permute-done((bf16[2,128,384]{2,1,0:T(8,128)(2,1)S(1)}, bf16[2,128,384]{2,1,0:T(8,128)(2,1)S(1)}, u32[]{:S(2)}, u32[]{:S(2)}) %collective-permute-start.5) | collective-permute-done | bytes 196640 | tf_op jit(solution)/shard_map/ppermute | solution.py:480
  29.0 3.2 %all-to-all-done.zr = bf16[8,2,16,384]{3,2,1,0:T(8,128)(2,1)S(1)} async-done(((bf16[8,2,16,384]{3,2,1,0:T(8,128)(2,1)}), bf16[8,2,16,384]{3,2,1,0:T(8,128)(2,1)S(1)}, u32[]{:S(2)}, u32[]{:S(2)}) %all-to-all-start) | async-done | bytes 196640 | tf_op jit(solution)/shard_map/all_to_all | solution.py:505
  32.9 2.6 %shard_map.86 = bf16[8,2,48,384]{3,2,1,0:T(8,128)(2,1)} custom-call(s32[4]{0:T(128)} %pad_add_fusion.pos, bf16[8,2,16,384]{3,2,1,0:T(8,128)(2,1)} %copy-done.9), custom_call_target="tpu_custom_call" | custom-call | tf_op jit(solution)/shard_map/pallas_call | solution.py:152
  35.5 3.8 %all-to-all-start.1 = ((bf16[8,2,48,384]{3,2,1,0:T(8,128)(2,1)}), bf16[8,2,48,384]{3,2,1,0:T(8,128)(2,1)S(1)}, u32[]{:S(2)}, u32[]{:S(2)}) async-start(bf16[8,2,48,384]{3,2,1,0:T(8,128)(2,1)} %shard_map.86), calls=%async_computation.1 | async-start | bytes 1179648 | tf_op jit(solution)/shard_map/all_to_all | solution.py:507
  39.3 5.3 %shard_map.85 = (bf16[2,256,384]{2,1,0:T(8,128)(2,1)}, bf16[2,256,384]{2,1,0:T(8,128)(2,1)}, bf16[2,768,256]{2,1,0:T(8,128)(2,1)}) custom-call(s32[4]{0:T(128)} %pad_add_fusion.pos, bf16[256,768]{1,0:T(8,128)(2,1)} %bitcast.15, bf16[256,768]{1,0:T(8,128)(2,1)} %copy-done.3, bf16[256,768]{1,0:T(8,128)(2,1)} %bitcast.16, bf16[256,768]{1,0:T(8,128)(2,1)} %copy-done.6, ...), custom_call_target="tpu_custom_call" | custom-call | tf_op jit(solution)/shard_map/pallas_call | solution.py:125
  44.6 2.3 %all-to-all-done.1.xr = bf16[8,2,48,384]{3,2,1,0:T(8,128)(2,1)S(1)} async-done(((bf16[8,2,48,384]{3,2,1,0:T(8,128)(2,1)}), bf16[8,2,48,384]{3,2,1,0:T(8,128)(2,1)S(1)}, u32[]{:S(2)}, u32[]{:S(2)}) %all-to-all-start.1) | async-done | bytes 589856 | tf_op jit(solution)/shard_map/all_to_all | solution.py:507
  46.8 0.8 copy-done.2
  47.6 17.8 %shard_map.87 = (bf16[2,256,384]{2,1,0:T(8,128)(2,1)}, bf16[2,256,384]{2,1,0:T(8,128)(2,1)}, f32[2,2,256,384]{3,2,1,0:T(8,128)}, f32[2,2,128,384]{3,2,1,0:T(8,12...) custom-call(s32[4]{0:T(128)} %pad_add_fusion.pos, ...), custom_call_target="tpu_custom_call" | custom-call | tf_op jit(solution)/shard_map/pallas_call | solution.py:239
  65.5 4.2 %collective-permute-start.7 = (bf16[2,256,384]{2,1,0:T(8,128)(2,1)}, bf16[2,256,384]{2,1,0:T(8,128)(2,1)S(1)}, u32[]{:S(2)}, u32[]{:S(2)}) collective-permute-start(bf16[2,256,384]{2,1,0:T(8,128)(2,1)} %get-tuple-element.77.att_own), channel_id=1, source_target_pairs={{0,2},{2,0},{1,3},{3,1},{4,6},{6,4},{5,7},{7,5},{8,10},{10,8},{9,1... | collective-permute-start | bytes 1179656 | tf_op jit(solution)/shard_map/ppermute | solution.py:480
  69.7 3.5 %all-to-all-start.2 = ((bf16[8,2,48,384]{3,2,1,0:T(8,128)(2,1)}), bf16[8,2,48,384]{3,2,1,0:T(8,128)(2,1)S(1)}, u32[]{:S(2)}, u32[]{:S(2)}) async-start(bf16[8,2,48,384]{3,2,1,0:T(8,128)(2,1)} %get-tuple-element.76), calls=%async_computation.2 | async-start | bytes 1179648 | tf_op jit(solution)/shard_map/all_to_all | solution.py:511
  73.2 0.7 copy-done.4
  74.0 5.6 %shard_map.88 = (bf16[2,2,96,384]{3,2,1,0:T(8,128)(2,1)}, bf16[2,2,96,384]{3,2,1,0:T(8,128)(2,1)}, bf16[2,2,96,384]{3,2,1,0:T(8,128)(2,1)}, bf16[2,2,96,384]{3,2,1,0:T(8,128)(2,1)}) custom-call(s32[4]{0:T(128)} %pad_add_fusion.pos, bf16[2,256,384]{2,1,0:T(8,128)(2,1)} %get-tuple-element.77.att_own, bf16[2,256,384]{2,1,0:T(8,128)(2,1)} %copy-done.4, ...), custom_call_target="tpu_custom_call" | custom-call | tf_op jit(solution)/shard_map/pallas_call | solution.py:284
  79.6 1.4 collective-permute-start.8
  81.0 1.2 collective-permute-start.9
  82.2 4.7 %collective-permute-done.9.dwy = bf16[2,128,384]{2,1,0:T(8,128)(2,1)S(1)} collective-permute-done((bf16[2,128,384]{2,1,0:T(8,128)(2,1)S(1)}, bf16[2,128,384]{2,1,0:T(8,128)(2,1)S(1)}, u32[]{:S(2)}, u32[]{:S(2)}) %collective-permute-start.9) | collective-permute-done | bytes 196640 | tf_op jit(solution)/shard_map/ppermute | solution.py:480
  87.6 2.4 %shard_map.89 = (bf16[2,64,384]{2,1,0:T(8,128)(2,1)}, bf16[2,32,384]{2,1,0:T(8,128)(2,1)}, bf16[2,32,384]{2,1,0:T(8,128)(2,1)}) custom-call(s32[4]{0:T(128)} %pad_add_fusion.pos, f32[2,128,384]{2,1,0:T(8,128)} %get-tuple-element.82.dw, bf16[2,128,384]{2,1,0:T(8,128)(2,1)} %copy-done.16), custom_call_target="tpu_custom_call" | custom-call | tf_op jit(solution)/shard_map/pallas_call | solution.py:342
  90.0 2.5 %collective-permute-start.13 = (bf16[2,2,96,384]{3,2,1,0:T(8,128)(2,1)}, bf16[2,2,96,384]{3,2,1,0:T(8,128)(2,1)S(1)}, u32[]{:S(2)}, u32[]{:S(2)}) collective-permute-start(bf16[2,2,96,384]{3,2,1,0:T(8,128)(2,1)} %get-tuple-element.93), channel_id=1, source_target_pairs={{0,16},{8,24},{16,0},{24,8},{1,17},{9,25},{17,1},{25,9},{2,18},{10... | collective-permute-start | bytes 884744 | tf_op jit(solution)/shard_map/ppermute | solution.py:484
  92.5 0.8 copy-done.1
  93.3 2.7 %shard_map.90 = bf16[8,2,16,384]{3,2,1,0:T(8,128)(2,1)} custom-call(s32[4]{0:T(128)} %pad_add_fusion.pos, bf16[8,2,48,384]{3,2,1,0:T(8,128)(2,1)} %copy-done.1), custom_call_target="tpu_custom_call" | custom-call | tf_op jit(solution)/shard_map/pallas_call | solution.py:323
  95.9 3.4 %all-to-all-start.3 = ((bf16[8,2,16,384]{3,2,1,0:T(8,128)(2,1)}), bf16[8,2,16,384]{3,2,1,0:T(8,128)(2,1)S(1)}, u32[]{:S(2)}, u32[]{:S(2)}) async-start(bf16[8,2,16,384]{3,2,1,0:T(8,128)(2,1)} %shard_map.90), calls=%async_computation.3 | async-start | bytes 393216 | tf_op jit(solution)/shard_map/all_to_all | solution.py:518
  99.8 1.0 collective-permute-start.15
  100.9 3.6 %collective-permute-start.11 = (bf16[2,32,384]{2,1,0:T(8,128)(2,1)S(1)}, bf16[2,32,384]{2,1,0:T(8,128)(2,1)S(1)}, u32[]{:S(2)}, u32[]{:S(2)}) collective-permute-start(bf16[2,32,384]{2,1,0:T(8,128)(2,1)S(1)} %copy-done.33), channel_id=1, source_target_pairs={{0,16},{8,24},{16,0},{24,8},{1,17},{9,25},{17,1},{25,9},{2,18},{10... | collective-permute-start | bytes 147464 | tf_op jit(solution)/shard_map/ppermute | solution.py:484
  104.8 3.1 %collective-permute-done.14.t3 = bf16[2,2,96,384]{3,2,1,0:T(8,128)(2,1)S(1)} collective-permute-done((bf16[2,2,96,384]{3,2,1,0:T(8,128)(2,1)S(1)}, bf16[2,2,96,384]{3,2,1,0:T(8,128)(2,1)S(1)}, u32[]{:S(2)}, u32[]{:S(2)}) %collective-permute-start.14) | collective-permute-done | bytes 294944 | tf_op jit(solution)/shard_map/ppermute | solution.py:484
  108.7 2.8 %shard_map.91 = (bf16[96,384]{1,0:T(8,128)(2,1)}, bf16[96,384]{1,0:T(8,128)(2,1)}, bf16[96,384]{1,0:T(8,128)(2,1)}, bf16[96,384]{1,0:T(8,128)(2,1)}) custom-call(s32[4]{0:T(128)} %pad_add_fusion.pos, bf16[2,2,96,384]{3,2,1,0:T(8,128)(2,1)} %get-tuple-element.91.t0, bf16[2,2,96,384]{3,2,1,0:T(8,128)(2,1)} %copy-done.12, bf16[2,2,96,384]{3,2,1,0:T(8,128)(2,1)} %copy-done.13, ...), custom_call_target="tpu_custom_call" | custom-call | tf_op jit(solution)/shard_map/pallas_call | solution.py:304
  111.6 2.9 %collective-permute-start.16 = (bf16[96,384]{1,0:T(8,128)(2,1)}, bf16[96,384]{1,0:T(8,128)(2,1)S(1)}, u32[]{:S(2)}, u32[]{:S(2)}) collective-permute-start(bf16[96,384]{1,0:T(8,128)(2,1)} %get-tuple-element.108), channel_id=1, source_target_pairs={{0,1},{1,0},{4,5},{5,4},{2,3},{3,2},{6,7},{7,6},{8,9},{9,8},{12,13... | collective-permute-start | bytes 221192 | tf_op jit(solution)/shard_map/ppermute | solution.py:484
  115.9 6.2 %shard_map.92 = (bf16[2,256,1152]{2,1,0:T(8,128)(2,1)}, bf16[8,2,96,384]{3,2,1,0:T(8,128)(2,1)}) custom-call(s32[4]{0:T(128)} %pad_add_fusion.pos, bf16[8,2,16,384]{3,2,1,0:T(8,128)(2,1)} %copy-done.8, f32[2,2,256,384]{3,2,1,0:T(8,128)} %get-tuple-element.100.dkv, f32[2,2,128,384]{3,2,1,0:T(8,128)} %get-tuple-element.101.dn1, ...), custom_call_target="tpu_custom_call" | custom-call | tf_op jit(solution)/shard_map/pallas_call | solution.py:385
  122.8 4.3 %all-to-all-start.4 = ((bf16[16,96,384]{2,1,0:T(8,128)(2,1)}), bf16[16,96,384]{2,1,0:T(8,128)(2,1)S(1)}, u32[]{:S(2)}, u32[]{:S(2)}) async-start(bf16[16,96,384]{2,1,0:T(8,128)(2,1)} %bitcast.19), calls=%async_computation.4 | async-start | bytes 2359296 | tf_op jit(solution)/shard_map/all_to_all | solution.py:525
  127.1 0.9 dynamic-slice_bitcast_fusion
  128.1 4.5 %collective-permute-start.19 = (bf16[256,1152]{1,0:T(8,128)(2,1)S(1)}, bf16[256,1152]{1,0:T(8,128)(2,1)S(1)}, u32[]{:S(2)}, u32[]{:S(2)}) collective-permute-start(bf16[256,1152]{1,0:T(8,128)(2,1)S(1)} %get-tuple-element.124), channel_id=1, source_target_pairs={{0,2},{2,0},{1,3},{3,1},{4,6},{6,4},{5,7},{7,5},{8,10},{10,8},{9,1... | collective-permute-start | bytes 1769480 | tf_op jit(solution)/shard_map/ppermute | solution.py:480
  132.6 3.5 %shard_map.94 = bf16[256,768]{1,0:T(8,128)(2,1)} custom-call(s32[4]{0:T(128)} %pad_add_fusion.pos, bf16[2,256,384]{2,1,0:T(8,128)(2,1)} %get-tuple-element.77.att_own, bf16[2,256,384]{2,1,0:T(8,128)(2,1)} %copy-done.4, bf16[768,768]{1,0:T(8,128)(2,1)} %w_oth.1, bf16[768,768]{1,0:T(8,128)(2,1)} %w_oth.1), custom_call_target="tpu_custom_call" | custom-call | tf_op jit(solution)/shard_map/pallas_call | solution.py:258
  136.0 0.8 copy-done.10
  136.9 5.1 %shard_map.93 = bf16[256,768]{1,0:T(8,128)(2,1)} custom-call(s32[4]{0:T(128)} %pad_add_fusion.pos, bf16[256,1152]{1,0:T(8,128)(2,1)} %get-tuple-element.125.pg_own, bf16[256,1152]{1,0:T(8,128)(2,1)} %copy-done.10, bf16[768,2304]{1,0:T(8,128)(2,1)} %rest_5_.1, bf16[768,2304]{1,0:T(8,128)(2,1)} %rest_5_.1, bf16[768,2304]{1,0:T(8,128)(2,1)} %rest_5_.1, ...), custom_call_target="tpu_custom_call" | custom-call | tf_op jit(solution)/shard_map/pallas_call | solution.py:408
  142.0 1.0 copy-done
  143.1 3.2 %shard_map.95 = bf16[8,2,16,384]{3,2,1,0:T(8,128)(2,1)} custom-call(s32[4]{0:T(128)} %pad_add_fusion.pos, bf16[96,384]{1,0:T(8,128)(2,1)} %get-tuple-element.115.f0, bf16[96,384]{1,0:T(8,128)(2,1)} %copy-done.20, bf16[96,384]{1,0:T(8,128)(2,1)} %copy-done.21, bf16[96,384]{1,0:T(8,128)(2,1)} %copy-done.22, bf16[16,96,384]{2,1,0:T(8,128)(2,1)} %copy-done), custom_call_target="tpu_custom_call" | custom-call | tf_op jit(solution)/shard_map/pallas_call | solution.py:435
  146.3 15.2 %all_to_all.30.terms = bf16[8,2,16,384]{3,2,1,0:T(8,128)(2,1)} all-to-all(bf16[8,2,16,384]{3,2,1,0:T(8,128)(2,1)} %shard_map.95), channel_id=1, replica_groups=mesh['z'=8,'x'=4,'y'=2,'c'=2,'dp'=2] {'z'}, dimensions={0} | all-to-all | bytes 393216 | tf_op jit(solution)/shard_map/all_to_all | solution.py:531
  161.5 2.2 %shard_map.96 = (bf16[16,384]{1,0:T(8,128)(2,1)}, bf16[16,384]{1,0:T(8,128)(2,1)}) custom-call(s32[4]{0:T(128)} %pad_add_fusion.pos, bf16[8,2,16,384]{3,2,1,0:T(8,128)(2,1)} %all_to_all.30.terms), custom_call_target="tpu_custom_call" | custom-call | tf_op jit(solution)/shard_map/pallas_call | solution.py:446
  163.7 3.2 %collective-permute-start.20 = (bf16[16,384]{1,0:T(8,128)(2,1)}, bf16[16,384]{1,0:T(8,128)(2,1)S(1)}, u32[]{:S(2)}, u32[]{:S(2)}) collective-permute-start(bf16[16,384]{1,0:T(8,128)(2,1)} %get-tuple-element.120.own), channel_id=1, source_target_pairs={{0,1},{1,0},{2,3},{3,2},{4,5},{5,4},{6,7},{7,6},{8,9},{9,8},{10,11... | collective-permute-start | bytes 36872 | tf_op jit(solution)/shard_map/ppermute | solution.py:484
  166.9 4.2 %collective-permute-start.21 = (bf16[16,384]{1,0:T(8,128)(2,1)}, bf16[16,384]{1,0:T(8,128)(2,1)S(1)}, u32[]{:S(2)}, u32[]{:S(2)}) collective-permute-start(bf16[16,384]{1,0:T(8,128)(2,1)} %get-tuple-element.121), channel_id=1, source_target_pairs={{0,2},{1,3},{2,0},{3,1},{4,6},{5,7},{6,4},{7,5},{8,10},{9,11},{10,... | collective-permute-start | bytes 36872 | tf_op jit(solution)/shard_map/ppermute | solution.py:484
  171.2 2.1 %collective-permute-start.22 = (bf16[16,384]{1,0:T(8,128)(2,1)}, bf16[16,384]{1,0:T(8,128)(2,1)S(1)}, u32[]{:S(2)}, u32[]{:S(2)}) collective-permute-start(bf16[16,384]{1,0:T(8,128)(2,1)} %get-tuple-element.121), channel_id=1, source_target_pairs={{0,3},{1,2},{2,1},{3,0},{4,7},{5,6},{6,5},{7,4},{8,11},{9,10},{10,... | collective-permute-start | bytes 36872 | tf_op jit(solution)/shard_map/ppermute | solution.py:484
  173.3 2.7 %collective-permute-done.22.from_both = bf16[16,384]{1,0:T(8,128)(2,1)S(1)} collective-permute-done((bf16[16,384]{1,0:T(8,128)(2,1)}, bf16[16,384]{1,0:T(8,128)(2,1)S(1)}, u32[]{:S(2)}, u32[]{:S(2)}) %collective-permute-start.22) | collective-permute-done | bytes 12320 | tf_op jit(solution)/shard_map/ppermute | solution.py:484
  176.6 2.1 %shard_map.97 = (f32[6,2304]{1,0:T(8,128)}, f32[6,768]{1,0:T(8,128)}) custom-call(s32[4]{0:T(128)} %pad_add_fusion.pos, bf16[16,384]{1,0:T(8,128)(2,1)} %get-tuple-element.120.own, bf16[16,384]{1,0:T(8,128)(2,1)} %copy-done.25, bf16[16,384]{1,0:T(8,128)(2,1)} %copy-done.26, bf16[16,384]{1,0:T(8,128)(2,1)} %copy-done.27), custom_call_target="tpu_custom_call" | custom-call | tf_op jit(solution)/shard_map/pallas_call | solution.py:470
  (96 shorter events, 7.1 us)
Async XLA Ops:
  0.6 4.9 %collective-permute-start = (bf16[256,768]{1,0:T(8,128)(2,1)}, bf16[256,768]{1,0:T(8,128)(2,1)S(1)}, u32[]{:S(2)}, u32[]{:S(2)}) collective-permute-start(bf16[256,768]{1,0:T(8,128)(2,1)} %bitcast.13), channel_id=1, source_target_pairs={{0,2},{2,0},{1,3},{3,1},{4,6},{6,4},{5,7},{7,5},{8,10},{10,8},{9,1... | collective-permute-start | bytes 1179656 | tf_op jit(solution)/shard_map/ppermute | solution.py:480
  4.6 6.7 %copy-start.5 = (bf16[1,256,768]{2,1,0:T(8,128)(2,1)S(1)}, bf16[1,256,768]{2,1,0:T(8,128)(2,1)}, u32[]{:S(2)}) copy-start(bf16[1,256,768]{2,1,0:T(8,128)(2,1)} %param.6) | copy-start | bytes 1179652
  11.3 12.3 %collective-permute-start.2 = (bf16[2,64,384]{2,1,0:T(8,128)(2,1)}, bf16[2,64,384]{2,1,0:T(8,128)(2,1)S(1)}, u32[]{:S(2)}, u32[]{:S(2)}) collective-permute-start(bf16[2,64,384]{2,1,0:T(8,128)(2,1)} %get-tuple-element.66), channel_id=1, source_target_pairs={{0,8},{8,0},{16,24},{24,16},{1,9},{9,1},{17,25},{25,17},{2,10},{10... | collective-permute-start | bytes 294920 | tf_op jit(solution)/shard_map/ppermute | solution.py:484
  11.3 12.6 %collective-permute-start.6 = (bf16[256,768]{1,0:T(8,128)(2,1)S(1)}, bf16[256,768]{1,0:T(8,128)(2,1)S(1)}, u32[]{:S(2)}, u32[]{:S(2)}) collective-permute-start(bf16[256,768]{1,0:T(8,128)(2,1)S(1)} %bitcast.18), channel_id=1, source_target_pairs={{0,2},{2,0},{1,3},{3,1},{4,6},{6,4},{5,7},{7,5},{8,10},{10,8},{9,1... | collective-permute-start | bytes 1179656 | tf_op jit(solution)/shard_map/ppermute | solution.py:480
  11.7 11.8 %collective-permute-start.3 = (bf16[2,32,384]{2,1,0:T(8,128)(2,1)}, bf16[2,32,384]{2,1,0:T(8,128)(2,1)S(1)}, u32[]{:S(2)}, u32[]{:S(2)}) collective-permute-start(bf16[2,32,384]{2,1,0:T(8,128)(2,1)} %get-tuple-element.67), channel_id=1, source_target_pairs={{0,16},{8,24},{16,0},{24,8},{1,17},{9,25},{17,1},{25,9},{2,18},{10... | collective-permute-start | bytes 147464 | tf_op jit(solution)/shard_map/ppermute | solution.py:484
  13.8 9.7 %collective-permute-start.4 = (bf16[2,32,384]{2,1,0:T(8,128)(2,1)}, bf16[2,32,384]{2,1,0:T(8,128)(2,1)S(1)}, u32[]{:S(2)}, u32[]{:S(2)}) collective-permute-start(bf16[2,32,384]{2,1,0:T(8,128)(2,1)} %get-tuple-element.67), channel_id=1, source_target_pairs={{0,24},{8,16},{16,8},{24,0},{1,25},{9,17},{17,9},{25,1},{2,26},{10... | collective-permute-start | bytes 147464 | tf_op jit(solution)/shard_map/ppermute | solution.py:484
  15.8 8.1 %collective-permute-start.1 = (bf16[2,128,384]{2,1,0:T(8,128)(2,1)}, bf16[2,128,384]{2,1,0:T(8,128)(2,1)S(1)}, u32[]{:S(2)}, u32[]{:S(2)}) collective-permute-start(bf16[2,128,384]{2,1,0:T(8,128)(2,1)} %get-tuple-element.65), channel_id=1, source_target_pairs={{0,4},{4,0},{1,5},{5,1},{2,6},{6,2},{3,7},{7,3},{8,12},{12,8},{9,1... | collective-permute-start | bytes 589832 | tf_op jit(solution)/shard_map/ppermute | solution.py:480
  15.8 16.4 %all-to-all-start = ((bf16[8,2,16,384]{3,2,1,0:T(8,128)(2,1)}), bf16[8,2,16,384]{3,2,1,0:T(8,128)(2,1)S(1)}, u32[]{:S(2)}, u32[]{:S(2)}) async-start(bf16[8,2,16,384]{3,2,1,0:T(8,128)(2,1)} %get-tuple-element.64), calls=%async_computation | async-start | bytes 393216 | tf_op jit(solution)/shard_map/all_to_all | solution.py:505
  23.6 20.9 %copy-start.11 = (bf16[2,128,384]{2,1,0:T(8,128)(2,1)}, bf16[2,128,384]{2,1,0:T(8,128)(2,1)S(1)}, u32[]{:S(2)}) copy-start(bf16[2,128,384]{2,1,0:T(8,128)(2,1)S(1)} %constant_dynamic-update-slice_fusion.wr) | copy-start | bytes 589828
  23.6 5.4 %collective-permute-start.5 = (bf16[2,128,384]{2,1,0:T(8,128)(2,1)S(1)}, bf16[2,128,384]{2,1,0:T(8,128)(2,1)S(1)}, u32[]{:S(2)}, u32[]{:S(2)}) collective-permute-start(bf16[2,128,384]{2,1,0:T(8,128)(2,1)S(1)} %constant_dynamic-update-slice_fusion.wr), channel_id=1, source_target_pairs={{0,4},{4,0},{1,5},{5,1},{2,6},{6,2},{3,7},{7,3},{8,12},{12,8},{9,1... | collective-permute-start | bytes 589832 | tf_op jit(solution)/shard_map/ppermute | solution.py:480
  23.9 15.4 %copy-start.6 = (bf16[256,768]{1,0:T(8,128)(2,1)}, bf16[256,768]{1,0:T(8,128)(2,1)S(1)}, u32[]{:S(2)}) copy-start(bf16[256,768]{1,0:T(8,128)(2,1)S(1)} %collective-permute-done.6.ct_oth) | copy-start | bytes 1179652
  23.9 20.7 %copy-start.17 = (bf16[2,128,384]{2,1,0:T(8,128)(2,1)}, bf16[2,128,384]{2,1,0:T(8,128)(2,1)S(1)}, u32[]{:S(2)}) copy-start(bf16[2,128,384]{2,1,0:T(8,128)(2,1)S(1)} %collective-permute-done.1.yr) | copy-start | bytes 589828
  29.0 15.6 %copy-start.18 = (bf16[2,128,384]{2,1,0:T(8,128)(2,1)}, bf16[2,128,384]{2,1,0:T(8,128)(2,1)S(1)}, u32[]{:S(2)}) copy-start(bf16[2,128,384]{2,1,0:T(8,128)(2,1)S(1)} %collective-permute-done.5.wy) | copy-start | bytes 589828
  35.5 11.3 %all-to-all-start.1 = ((bf16[8,2,48,384]{3,2,1,0:T(8,128)(2,1)}), bf16[8,2,48,384]{3,2,1,0:T(8,128)(2,1)S(1)}, u32[]{:S(2)}, u32[]{:S(2)}) async-start(bf16[8,2,48,384]{3,2,1,0:T(8,128)(2,1)} %shard_map.86), calls=%async_computation.1 | async-start | bytes 1179648 | tf_op jit(solution)/shard_map/all_to_all | solution.py:507
  65.5 7.7 %collective-permute-start.7 = (bf16[2,256,384]{2,1,0:T(8,128)(2,1)}, bf16[2,256,384]{2,1,0:T(8,128)(2,1)S(1)}, u32[]{:S(2)}, u32[]{:S(2)}) collective-permute-start(bf16[2,256,384]{2,1,0:T(8,128)(2,1)} %get-tuple-element.77.att_own), channel_id=1, source_target_pairs={{0,2},{2,0},{1,3},{3,1},{4,6},{6,4},{5,7},{7,5},{8,10},{10,8},{9,1... | collective-permute-start | bytes 1179656 | tf_op jit(solution)/shard_map/ppermute | solution.py:480
  69.7 22.8 %all-to-all-start.2 = ((bf16[8,2,48,384]{3,2,1,0:T(8,128)(2,1)}), bf16[8,2,48,384]{3,2,1,0:T(8,128)(2,1)S(1)}, u32[]{:S(2)}, u32[]{:S(2)}) async-start(bf16[8,2,48,384]{3,2,1,0:T(8,128)(2,1)} %get-tuple-element.76), calls=%async_computation.2 | async-start | bytes 1179648 | tf_op jit(solution)/shard_map/all_to_all | solution.py:511
  74.0 7.1 %copy-start.30 = (bf16[2,128,384]{2,1,0:T(8,128)(2,1)S(1)}, bf16[2,128,384]{2,1,0:T(8,128)(2,1)}, u32[]{:S(2)}) copy-start(bf16[2,128,384]{2,1,0:T(8,128)(2,1)} %get-tuple-element.83) | copy-start | bytes 589828
  79.6 19.8 %copy-start.28 = (bf16[2,2,96,384]{3,2,1,0:T(8,128)(2,1)S(1)}, bf16[2,2,96,384]{3,2,1,0:T(8,128)(2,1)}, u32[]{:S(2)}) copy-start(bf16[2,2,96,384]{3,2,1,0:T(8,128)(2,1)} %get-tuple-element.94) | copy-start | bytes 884740
  79.6 20.3 %copy-start.29 = (bf16[2,128,384]{2,1,0:T(8,128)(2,1)S(1)}, bf16[2,128,384]{2,1,0:T(8,128)(2,1)}, u32[]{:S(2)}) copy-start(bf16[2,128,384]{2,1,0:T(8,128)(2,1)} %get-tuple-element.102) | copy-start | bytes 589828
  79.6 12.9 %collective-permute-start.8 = (bf16[2,2,96,384]{3,2,1,0:T(8,128)(2,1)}, bf16[2,2,96,384]{3,2,1,0:T(8,128)(2,1)S(1)}, u32[]{:S(2)}, u32[]{:S(2)}) collective-permute-start(bf16[2,2,96,384]{3,2,1,0:T(8,128)(2,1)} %get-tuple-element.81), channel_id=1, source_target_pairs={{0,8},{8,0},{16,24},{24,16},{1,9},{9,1},{17,25},{25,17},{2,10},{10... | collective-permute-start | bytes 884744 | tf_op jit(solution)/shard_map/ppermute | solution.py:484
  81.0 5.9 %collective-permute-start.9 = (bf16[2,128,384]{2,1,0:T(8,128)(2,1)S(1)}, bf16[2,128,384]{2,1,0:T(8,128)(2,1)S(1)}, u32[]{:S(2)}, u32[]{:S(2)}) collective-permute-start(bf16[2,128,384]{2,1,0:T(8,128)(2,1)S(1)} %copy-done.30), channel_id=1, source_target_pairs={{0,4},{4,0},{1,5},{5,1},{2,6},{6,2},{3,7},{7,3},{8,12},{12,8},{9,1... | collective-permute-start | bytes 589832 | tf_op jit(solution)/shard_map/ppermute | solution.py:480
  89.9 10.9 %copy-start.31 = (bf16[2,64,384]{2,1,0:T(8,128)(2,1)S(1)}, bf16[2,64,384]{2,1,0:T(8,128)(2,1)}, u32[]{:S(2)}) copy-start(bf16[2,64,384]{2,1,0:T(8,128)(2,1)} %get-tuple-element.88) | copy-start | bytes 294916
  89.9 10.9 %copy-start.33 = (bf16[2,32,384]{2,1,0:T(8,128)(2,1)S(1)}, bf16[2,32,384]{2,1,0:T(8,128)(2,1)}, u32[]{:S(2)}) copy-start(bf16[2,32,384]{2,1,0:T(8,128)(2,1)} %get-tuple-element.89) | copy-start | bytes 147460
  89.9 14.6 %copy-start.32 = (bf16[2,32,384]{2,1,0:T(8,128)(2,1)S(1)}, bf16[2,32,384]{2,1,0:T(8,128)(2,1)}, u32[]{:S(2)}) copy-start(bf16[2,32,384]{2,1,0:T(8,128)(2,1)} %get-tuple-element.90) | copy-start | bytes 147460
  90.0 14.6 %collective-permute-start.13 = (bf16[2,2,96,384]{3,2,1,0:T(8,128)(2,1)}, bf16[2,2,96,384]{3,2,1,0:T(8,128)(2,1)S(1)}, u32[]{:S(2)}, u32[]{:S(2)}) collective-permute-start(bf16[2,2,96,384]{3,2,1,0:T(8,128)(2,1)} %get-tuple-element.93), channel_id=1, source_target_pairs={{0,16},{8,24},{16,0},{24,8},{1,17},{9,25},{17,1},{25,9},{2,18},{10... | collective-permute-start | bytes 884744 | tf_op jit(solution)/shard_map/ppermute | solution.py:484
  92.5 15.5 %copy-start.12 = (bf16[2,2,96,384]{3,2,1,0:T(8,128)(2,1)}, bf16[2,2,96,384]{3,2,1,0:T(8,128)(2,1)S(1)}, u32[]{:S(2)}) copy-start(bf16[2,2,96,384]{3,2,1,0:T(8,128)(2,1)S(1)} %collective-permute-done.8.t1) | copy-start | bytes 884740
  95.9 15.6 %all-to-all-start.3 = ((bf16[8,2,16,384]{3,2,1,0:T(8,128)(2,1)}), bf16[8,2,16,384]{3,2,1,0:T(8,128)(2,1)S(1)}, u32[]{:S(2)}, u32[]{:S(2)}) async-start(bf16[8,2,16,384]{3,2,1,0:T(8,128)(2,1)} %shard_map.90), calls=%async_computation.3 | async-start | bytes 393216 | tf_op jit(solution)/shard_map/all_to_all | solution.py:518
  99.4 8.6 %collective-permute-start.14 = (bf16[2,2,96,384]{3,2,1,0:T(8,128)(2,1)S(1)}, bf16[2,2,96,384]{3,2,1,0:T(8,128)(2,1)S(1)}, u32[]{:S(2)}, u32[]{:S(2)}) collective-permute-start(bf16[2,2,96,384]{3,2,1,0:T(8,128)(2,1)S(1)} %copy-done.28), channel_id=1, source_target_pairs={{0,24},{8,16},{16,8},{24,0},{1,25},{9,17},{17,9},{25,1},{2,26},{10... | collective-permute-start | bytes 884744 | tf_op jit(solution)/shard_map/ppermute | solution.py:484
  99.8 15.4 %collective-permute-start.15 = (bf16[2,128,384]{2,1,0:T(8,128)(2,1)S(1)}, bf16[2,128,384]{2,1,0:T(8,128)(2,1)S(1)}, u32[]{:S(2)}, u32[]{:S(2)}) collective-permute-start(bf16[2,128,384]{2,1,0:T(8,128)(2,1)S(1)} %copy-done.29), channel_id=1, source_target_pairs={{0,4},{4,0},{1,5},{5,1},{2,6},{6,2},{3,7},{7,3},{8,12},{12,8},{9,1... | collective-permute-start | bytes 589832 | tf_op jit(solution)/shard_map/ppermute | solution.py:480
  100.9 10.7 %collective-permute-start.10 = (bf16[2,64,384]{2,1,0:T(8,128)(2,1)S(1)}, bf16[2,64,384]{2,1,0:T(8,128)(2,1)S(1)}, u32[]{:S(2)}, u32[]{:S(2)}) collective-permute-start(bf16[2,64,384]{2,1,0:T(8,128)(2,1)S(1)} %copy-done.31), channel_id=1, source_target_pairs={{0,8},{8,0},{16,24},{24,16},{1,9},{9,1},{17,25},{25,17},{2,10},{10... | collective-permute-start | bytes 294920 | tf_op jit(solution)/shard_map/ppermute | solution.py:484
  100.9 10.6 %collective-permute-start.11 = (bf16[2,32,384]{2,1,0:T(8,128)(2,1)S(1)}, bf16[2,32,384]{2,1,0:T(8,128)(2,1)S(1)}, u32[]{:S(2)}, u32[]{:S(2)}) collective-permute-start(bf16[2,32,384]{2,1,0:T(8,128)(2,1)S(1)} %copy-done.33), channel_id=1, source_target_pairs={{0,16},{8,24},{16,0},{24,8},{1,17},{9,25},{17,1},{25,9},{2,18},{10... | collective-permute-start | bytes 147464 | tf_op jit(solution)/shard_map/ppermute | solution.py:484
  104.5 3.4 %copy-start.13 = (bf16[2,2,96,384]{3,2,1,0:T(8,128)(2,1)}, bf16[2,2,96,384]{3,2,1,0:T(8,128)(2,1)S(1)}, u32[]{:S(2)}) copy-start(bf16[2,2,96,384]{3,2,1,0:T(8,128)(2,1)S(1)} %collective-permute-done.13.t2) | copy-start | bytes 884740
  104.5 7.0 %collective-permute-start.12 = (bf16[2,32,384]{2,1,0:T(8,128)(2,1)S(1)}, bf16[2,32,384]{2,1,0:T(8,128)(2,1)S(1)}, u32[]{:S(2)}, u32[]{:S(2)}) collective-permute-start(bf16[2,32,384]{2,1,0:T(8,128)(2,1)S(1)} %copy-done.32), channel_id=1, source_target_pairs={{0,24},{8,16},{16,8},{24,0},{1,25},{9,17},{17,9},{25,1},{2,26},{10... | collective-permute-start | bytes 147464 | tf_op jit(solution)/shard_map/ppermute | solution.py:484
  111.5 3.8 %copy-start.23 = (bf16[2,32,384]{2,1,0:T(8,128)(2,1)}, bf16[2,32,384]{2,1,0:T(8,128)(2,1)S(1)}, u32[]{:S(2)}) copy-start(bf16[2,32,384]{2,1,0:T(8,128)(2,1)S(1)} %collective-permute-done.11.g4_a) | copy-start | bytes 147460
  111.5 3.7 %copy-start.24 = (bf16[2,32,384]{2,1,0:T(8,128)(2,1)}, bf16[2,32,384]{2,1,0:T(8,128)(2,1)S(1)}, u32[]{:S(2)}) copy-start(bf16[2,32,384]{2,1,0:T(8,128)(2,1)S(1)} %collective-permute-done.12.g4_b) | copy-start | bytes 147460
  111.5 3.7 %copy-start.19 = (bf16[2,64,384]{2,1,0:T(8,128)(2,1)}, bf16[2,64,384]{2,1,0:T(8,128)(2,1)S(1)}, u32[]{:S(2)}) copy-start(bf16[2,64,384]{2,1,0:T(8,128)(2,1)S(1)} %collective-permute-done.10.g3) | copy-start | bytes 294916
  111.6 3.7 %copy-start.8 = (bf16[8,2,16,384]{3,2,1,0:T(8,128)(2,1)}, bf16[8,2,16,384]{3,2,1,0:T(8,128)(2,1)S(1)}, u32[]{:S(2)}) copy-start(bf16[8,2,16,384]{3,2,1,0:T(8,128)(2,1)S(1)} %all-to-all-done.3.zr) | copy-start | bytes 589828
  111.6 10.6 %collective-permute-start.16 = (bf16[96,384]{1,0:T(8,128)(2,1)}, bf16[96,384]{1,0:T(8,128)(2,1)S(1)}, u32[]{:S(2)}, u32[]{:S(2)}) collective-permute-start(bf16[96,384]{1,0:T(8,128)(2,1)} %get-tuple-element.108), channel_id=1, source_target_pairs={{0,1},{1,0},{4,5},{5,4},{2,3},{3,2},{6,7},{7,6},{8,9},{9,8},{12,13... | collective-permute-start | bytes 221192 | tf_op jit(solution)/shard_map/ppermute | solution.py:484
  114.5 7.7 %collective-permute-start.17 = (bf16[96,384]{1,0:T(8,128)(2,1)}, bf16[96,384]{1,0:T(8,128)(2,1)S(1)}, u32[]{:S(2)}, u32[]{:S(2)}) collective-permute-start(bf16[96,384]{1,0:T(8,128)(2,1)} %get-tuple-element.109), channel_id=1, source_target_pairs={{0,4},{1,5},{4,0},{5,1},{2,6},{3,7},{6,2},{7,3},{8,12},{9,13},{12,... | collective-permute-start | bytes 221192 | tf_op jit(solution)/shard_map/ppermute | solution.py:484
  115.1 7.1 %collective-permute-start.18 = (bf16[96,384]{1,0:T(8,128)(2,1)}, bf16[96,384]{1,0:T(8,128)(2,1)S(1)}, u32[]{:S(2)}, u32[]{:S(2)}) collective-permute-start(bf16[96,384]{1,0:T(8,128)(2,1)} %get-tuple-element.110), channel_id=1, source_target_pairs={{0,5},{1,4},{4,1},{5,0},{2,7},{3,6},{6,3},{7,2},{8,13},{9,12},{12,... | collective-permute-start | bytes 221192 | tf_op jit(solution)/shard_map/ppermute | solution.py:484
  122.2 4.9 %copy-start.7 = (bf16[2,256,1152]{2,1,0:T(8,128)(2,1)S(1)}, bf16[2,256,1152]{2,1,0:T(8,128)(2,1)}, u32[]{:S(2)}) copy-start(bf16[2,256,1152]{2,1,0:T(8,128)(2,1)} %get-tuple-element.112) | copy-start | bytes 3538948
  122.8 19.2 %all-to-all-start.4 = ((bf16[16,96,384]{2,1,0:T(8,128)(2,1)}), bf16[16,96,384]{2,1,0:T(8,128)(2,1)S(1)}, u32[]{:S(2)}, u32[]{:S(2)}) async-start(bf16[16,96,384]{2,1,0:T(8,128)(2,1)} %bitcast.19), calls=%async_computation.4 | async-start | bytes 2359296 | tf_op jit(solution)/shard_map/all_to_all | solution.py:525
  128.1 8.0 %collective-permute-start.19 = (bf16[256,1152]{1,0:T(8,128)(2,1)S(1)}, bf16[256,1152]{1,0:T(8,128)(2,1)S(1)}, u32[]{:S(2)}, u32[]{:S(2)}) collective-permute-start(bf16[256,1152]{1,0:T(8,128)(2,1)S(1)} %get-tuple-element.124), channel_id=1, source_target_pairs={{0,2},{2,0},{1,3},{3,1},{4,6},{6,4},{5,7},{7,5},{8,10},{10,8},{9,1... | collective-permute-start | bytes 1769480 | tf_op jit(solution)/shard_map/ppermute | solution.py:480
  163.7 9.6 %collective-permute-start.20 = (bf16[16,384]{1,0:T(8,128)(2,1)}, bf16[16,384]{1,0:T(8,128)(2,1)S(1)}, u32[]{:S(2)}, u32[]{:S(2)}) collective-permute-start(bf16[16,384]{1,0:T(8,128)(2,1)} %get-tuple-element.120.own), channel_id=1, source_target_pairs={{0,1},{1,0},{2,3},{3,2},{4,5},{5,4},{6,7},{7,6},{8,9},{9,8},{10,11... | collective-permute-start | bytes 36872 | tf_op jit(solution)/shard_map/ppermute | solution.py:484
  166.9 6.4 %collective-permute-start.21 = (bf16[16,384]{1,0:T(8,128)(2,1)}, bf16[16,384]{1,0:T(8,128)(2,1)S(1)}, u32[]{:S(2)}, u32[]{:S(2)}) collective-permute-start(bf16[16,384]{1,0:T(8,128)(2,1)} %get-tuple-element.121), channel_id=1, source_target_pairs={{0,2},{1,3},{2,0},{3,1},{4,6},{5,7},{6,4},{7,5},{8,10},{9,11},{10,... | collective-permute-start | bytes 36872 | tf_op jit(solution)/shard_map/ppermute | solution.py:484
  171.2 4.8 %collective-permute-start.22 = (bf16[16,384]{1,0:T(8,128)(2,1)}, bf16[16,384]{1,0:T(8,128)(2,1)S(1)}, u32[]{:S(2)}, u32[]{:S(2)}) collective-permute-start(bf16[16,384]{1,0:T(8,128)(2,1)} %get-tuple-element.121), channel_id=1, source_target_pairs={{0,3},{1,2},{2,1},{3,0},{4,7},{5,6},{6,5},{7,4},{8,11},{9,10},{10,... | collective-permute-start | bytes 36872 | tf_op jit(solution)/shard_map/ppermute | solution.py:484
  173.3 2.7 %copy-start.25 = (bf16[16,384]{1,0:T(8,128)(2,1)}, bf16[16,384]{1,0:T(8,128)(2,1)S(1)}, u32[]{:S(2)}) copy-start(bf16[16,384]{1,0:T(8,128)(2,1)S(1)} %collective-permute-done.20.from_dp) | copy-start | bytes 36868
  173.3 2.7 %copy-start.26 = (bf16[16,384]{1,0:T(8,128)(2,1)}, bf16[16,384]{1,0:T(8,128)(2,1)S(1)}, u32[]{:S(2)}) copy-start(bf16[16,384]{1,0:T(8,128)(2,1)S(1)} %collective-permute-done.21.from_core) | copy-start | bytes 36868
  (14 other events, 10.3 us)

commit v8 on v6

--- a/solution.py
+++ b/solution.py
@@ -182,7 +182,7 @@
         ah = jnp.where(mine, ag[e], jnp.zeros((), BF16))
         masked[step] = (qh, ah)
         s_ref[step % 2] = dot_nt(keys[e, 0], qh)
-        dw_ref[step % 2] = dot_nt(keys[e, 1], ah)
+        dw_ref[step % 2] = dot_nt(keys[e, 1], ah * jnp.asarray(DH ** -0.5, BF16))
 
     scores(0)
     for step, (e, h) in enumerate(steps):
@@ -190,7 +190,6 @@
             scores(step + 1)
         if h == 0:
             att_t, dq_t = [], []
-            dk = dv = None
         s, dw, b = s_ref.at[step % 2], dw_ref.at[step % 2], step % 2
         qh, ah = masked[step]
         top = jnp.max(s[...], axis=0, keepdims=True)
@@ -199,15 +198,15 @@
         inverse = 1.0 / jnp.sum(un, axis=0, keepdims=True)
         delta = jnp.sum(un * dw[...], axis=0, keepdims=True) * inverse
         prob = s[...] * inverse
-        w_ref[b] = prob.astype(BF16)
-        ds_ref[b] = (prob * ((dw[...] - delta) * DH ** -0.5)).astype(BF16)
-        att_t.append(dot(keys_t[e, 1, 64 * h : 64 * h + 64], w_ref[b]))
-        dq_t.append(dot(keys_t[e, 0, 64 * h : 64 * h + 64], ds_ref[b]))
-        dkh, dvh = dot(ds_ref[b], qh), dot(w_ref[b], ah)
-        dk = dkh if dk is None else dk + dkh
-        dv = dvh if dv is None else dv + dvh
+        cols = slice(TOK * h, TOK * h + TOK)
+        w_ref[e, :, cols] = prob.astype(BF16)
+        ds_ref[e, :, cols] = (prob * (dw[...] - delta)).astype(BF16)
+        att_t.append(dot(keys_t[e, 1, 64 * h : 64 * h + 64], w_ref[e, :, cols]))
+        dq_t.append(dot(keys_t[e, 0, 64 * h : 64 * h + 64], ds_ref[e, :, cols]))
         if h == 0:
             continue
+        dk = dot(ds_ref[e], jnp.concatenate([masked[step - 1][0], qh], axis=0))
+        dv = dot(w_ref[e], jnp.concatenate([masked[step - 1][1], ah], axis=0))
         att_out[e] = jnp.concatenate(att_t, axis=0).T.astype(BF16)
         dq_out[e] = jnp.concatenate(dq_t, axis=0).T.astype(BF16)
         for p, grad in ((0, dk), (1, dv)):
@@ -243,7 +242,7 @@
         [(cut(*lead), (lead + (H,), kind)) for lead, kind in outs],
         [
             pltpu.VMEM((2, 2, n, 128), BF16), pltpu.VMEM((2, 2, 128, n), BF16), pltpu.VMEM((2, n, TOK), F32), pltpu.VMEM((2, n, TOK), F32),
-            pltpu.VMEM((2, n, TOK), BF16), pltpu.VMEM((2, n, TOK), BF16), pltpu.VMEM((2, 768, 128), F32),
+            pltpu.VMEM((2, n, 2 * TOK), BF16), pltpu.VMEM((2, n, 2 * TOK), BF16), pltpu.VMEM((2, 768, 128), F32),
         ],
     )(pos, q, ag, kv, n1, yr, wr, wy, xr)
 
@@ -427,7 +426,9 @@
     hit = (k == 6 * (i >> 4) + row) & (row < 6)
     rows = dot((hit & (half == 0)).astype(BF16), first)
     rows = rows + dot((hit & (half == 1)).astype(BF16), total_of([second[slot] for slot in range(16)]).astype(BF16))
-    out[...] = rows.astype(BF16).reshape(ZN, 2, 16, H)
+    rows = rows.astype(BF16).reshape(ZN, 2, 16, H)
+    for core in range(2):
+        out[:, core ^ pos[0]] = rows[:, core]
 
 
 def middle_sum(pos, firsts, second):
@@ -435,20 +436,6 @@
     return call(
         middle_body, (1,), [whole(96, H)] * 4 + [whole(16, 96, H)], [(whole(*shape), (shape, BF16))]
     )(pos, *firsts, second)[0]
-
-
-def z_sum_body(pos, terms, own_out, oth_out):
-    for core, out in ((pos[0], own_out), (1 - pos[0], oth_out)):
-        out[...] = total_of([terms[z, core] for z in range(ZN)]).astype(BF16)
-
-
-def z_sum(pos, terms):
-    return call(
-        z_sum_body,
-        (1,),
-        [whole(ZN, 2, 16, H)],
-        [(whole(16, H), ((16, H), BF16))] * 2,
-    )(pos, terms)
 
 
 def last_body(pos, own, from_dp, from_core, from_both, qkv_out, out_out, parts):
@@ -515,13 +502,14 @@
     firsts = [along(firsts[far - 1], "x", far) for far in (1, 2, 3)]
     dx_r, first, firsts[0], dwy = lax.optimization_barrier((dx_r, first, firsts[0], dwy))
     dz_r = lax.all_to_all(back_slots(pos, dx_r), "z", 0, 0)
-    dw, dwy, firsts = lax.optimization_barrier((dw, dwy, firsts))
     g3, g4_a, g4_b = hand_back(pos, dw, dwy)
+    g3, g4_a, g4_b, firsts = lax.optimization_barrier((g3, g4_a, g4_b, firsts))
     g3, g4_a, g4_b = along(g3, "x", 1), along(g4_a, "x", 2), along(g4_b, "x", 3)
     firsts = x_sum(pos, first, *firsts)
-    firsts = list(firsts[:1]) + [along(firsts[far], ("y", "dp"), far) for far in (1, 2, 3)]
-    dz_r, g3, g4_a, g4_b, firsts = lax.optimization_barrier((dz_r, g3, g4_a, g4_b, firsts))
+    dz_r, g3, g4_a, g4_b, first = lax.optimization_barrier((dz_r, g3, g4_a, g4_b, firsts[0]))
+    firsts = [first] + [along(firsts[far], ("y", "dp"), far) for far in (1, 2, 3)]
     pg, terms = leaf_grads(pos, dz_r, dkv, dn1, swap(dy, "y"), g3, g4_a, g4_b, dq, xt)
+    terms, firsts = lax.optimization_barrier((terms, firsts))
     terms = lax.all_to_all(terms.reshape(16, 96, H), ("x", "y", "dp"), 0, 0)
     pg_own = lax.dynamic_index_in_dim(pg, c, 0, keepdims=False)
     pg_oth = swap(lax.dynamic_index_in_dim(pg, 1 - c, 0, keepdims=False), "c")
@@ -529,7 +517,7 @@
     layer_out = output_side(pos, att, att_oth, w_out)
     terms, input_grad, layer_out = lax.optimization_barrier((terms, input_grad, layer_out))
     terms = lax.all_to_all(middle_sum(pos, firsts, terms), "z", 0, 0)
-    own, oth = z_sum(pos, terms)
+    own, oth = (jnp.sum(terms[:, core].astype(F32), axis=0).astype(BF16) for core in range(2))
     pair = ("c", "dp")
     qkv_grad, out_grad = last_rows(pos, own, along(own, pair, 1), along(oth, pair, 2), along(oth, pair, 3))
     return (layer_out[None], input_grad[None], qkv_grad, out_grad)

time: 178 us -> 173 us (0.972)
  waiting for transfers between devices: 26.6 us -> 19.4 us
  starting transfers between devices: 60.9 us -> 64.1 us
  Pallas kernels: 66.5 us -> 64 us
    ppermute x15, waiting for transfers between devices: 13 us -> 5.88 us  [along(): return lax.ppermute(value, axes, [(i, i ^ far) for i in range(count)])]
    all_to_all x1, starting transfers between devices: 3.83 us -> 6.26 us  [shards(): terms = lax.all_to_all(terms.reshape(16, 96, H), ('x', 'y', 'dp'), 0, 0)]
    pallas_call x1 -> x0, Pallas kernels: 2.22 us -> none  [z_sum(): call(z_sum_body, (1,), [whole(ZN, 2, 16, H)], [(whole(16, H), ((16, H), B...]
    unnamed x62 -> x64, local copies, waits for them, and re-layouts: 6.36 us -> 6.94 us
  transfers between devices with their start and end apart: 28 -> 28, of which waited for: 12 -> 8; matrix products, arithmetic and copies ran while one was open for 1% -> 1% of each run, Pallas kernels for 15% -> 19%
where the time goes in v8:
time: 173 us; the launch traced here: 172 us
  starting transfers between devices  64.1 us (37%)
  Pallas kernels  64 us (37%)
  waiting for transfers between devices  19.4 us (11%)
  blocking collectives  15.4 us (9%)
  local copies, waits for them, and re-layouts  7.87 us (5%)
    ppermute x15, starting transfers between devices, along(): return lax.ppermute(value, axes, [(i, i ^ far) for i in range(count)])  24.6 us
    pallas_call x1, Pallas kernels, attention(): call(attention_body, (H // 128,), [cut(2, TOK), cut(2, TOK), cut(2, 2, TO...  17.6 us
    all_to_all x1, blocking collectives, shards(): terms = lax.all_to_all(middle_sum(pos, firsts, terms), 'z', 0, 0)  15.4 us
    ppermute x8, starting transfers between devices, swap(): return lax.ppermute(value, axis, [(0, 1), (1, 0)])  14.8 us
    ppermute x8, waiting for transfers between devices, swap(): return lax.ppermute(value, axis, [(0, 1), (1, 0)])  8.05 us
    all_to_all x1, starting transfers between devices, shards(): zr = lax.all_to_all(zs, 'z', 0, 0)  7.75 us
    unnamed x64, local copies, waits for them, and re-layouts  6.94 us
    all_to_all x1, starting transfers between devices, shards(): terms = lax.all_to_all(terms.reshape(16, 96, H), ('x', 'y', 'dp'), 0, 0)  6.26 us
  transfers between devices with their start and end apart: 28, of which 8 were waited for; matrix products, arithmetic and copies ran while one was open for 1% of the time, Pallas kernels for 19%

profile of v8, /device:TPU:1, one launch (start us, length us, event | category | flops | bytes accessed | tf_op | source)
XLA Modules:
  0.0 172.4 jit_solution(17266403354050368304)
XLA Ops:
  0.6 3.3 %collective-permute-start = (bf16[256,768]{1,0:T(8,128)(2,1)}, bf16[256,768]{1,0:T(8,128)(2,1)S(1)}, u32[]{:S(2)}, u32[]{:S(2)}) collective-permute-start(bf16[256,768]{1,0:T(8,128)(2,1)} %bitcast.13), channel_id=1, source_target_pairs={{0,2},{2,0},{1,3},{3,1},{4,6},{6,4},{5,7},{7,5},{8,10},{10,8},{9,1... | collective-permute-start | bytes 1179656 | tf_op jit(solution)/shard_map/ppermute | solution.py:467
  4.6 0.9 collective-permute-done.x_oth
  5.5 0.7 copy-done.3
  6.3 5.0 %shard_map.84 = (bf16[2,2,256,384]{3,2,1,0:T(8,128)(2,1)}, bf16[2,2,128,384]{3,2,1,0:T(8,128)(2,1)}, bf16[2,128,384]{2,1,0:T(8,128)(2,1)}, bf16[2,64,384]{2,1,0:...) custom-call(s32[4]{0:T(128)} %pad_add_fusion.pos, bf16[256,768]{1,0:T(8,128)(2,1)} %bitcast.14, ...), custom_call_target="tpu_custom_call" | custom-call | tf_op jit(solution)/shard_map/pallas_call | solution.py:107
  11.7 2.1 %collective-permute-start.3 = (bf16[2,32,384]{2,1,0:T(8,128)(2,1)}, bf16[2,32,384]{2,1,0:T(8,128)(2,1)S(1)}, u32[]{:S(2)}, u32[]{:S(2)}) collective-permute-start(bf16[2,32,384]{2,1,0:T(8,128)(2,1)} %get-tuple-element.66), channel_id=1, source_target_pairs={{0,16},{8,24},{16,0},{24,8},{1,17},{9,25},{17,1},{25,9},{2,18},{10... | collective-permute-start | bytes 147464 | tf_op jit(solution)/shard_map/ppermute | solution.py:471
  13.8 1.9 %collective-permute-start.4 = (bf16[2,32,384]{2,1,0:T(8,128)(2,1)}, bf16[2,32,384]{2,1,0:T(8,128)(2,1)S(1)}, u32[]{:S(2)}, u32[]{:S(2)}) collective-permute-start(bf16[2,32,384]{2,1,0:T(8,128)(2,1)} %get-tuple-element.66), channel_id=1, source_target_pairs={{0,24},{8,16},{16,8},{24,0},{1,25},{9,17},{17,9},{25,1},{2,26},{10... | collective-permute-start | bytes 147464 | tf_op jit(solution)/shard_map/ppermute | solution.py:471
  15.8 7.7 %all-to-all-start = ((bf16[8,2,16,384]{3,2,1,0:T(8,128)(2,1)}), bf16[8,2,16,384]{3,2,1,0:T(8,128)(2,1)S(1)}, u32[]{:S(2)}, u32[]{:S(2)}) async-start(bf16[8,2,16,384]{3,2,1,0:T(8,128)(2,1)} %get-tuple-element.63), calls=%async_computation | async-start | bytes 393216 | tf_op jit(solution)/shard_map/all_to_all | solution.py:492
  23.9 5.1 %collective-permute-done.5.wy = bf16[2,128,384]{2,1,0:T(8,128)(2,1)S(1)} collective-permute-done((bf16[2,128,384]{2,1,0:T(8,128)(2,1)S(1)}, bf16[2,128,384]{2,1,0:T(8,128)(2,1)S(1)}, u32[]{:S(2)}, u32[]{:S(2)}) %collective-permute-start.5) | collective-permute-done | bytes 196640 | tf_op jit(solution)/shard_map/ppermute | solution.py:467
  29.0 3.2 %all-to-all-done.zr = bf16[8,2,16,384]{3,2,1,0:T(8,128)(2,1)S(1)} async-done(((bf16[8,2,16,384]{3,2,1,0:T(8,128)(2,1)}), bf16[8,2,16,384]{3,2,1,0:T(8,128)(2,1)S(1)}, u32[]{:S(2)}, u32[]{:S(2)}) %all-to-all-start) | async-done | bytes 196640 | tf_op jit(solution)/shard_map/all_to_all | solution.py:492
  32.9 2.6 %shard_map.86 = bf16[8,2,48,384]{3,2,1,0:T(8,128)(2,1)} custom-call(s32[4]{0:T(128)} %pad_add_fusion.pos, bf16[8,2,16,384]{3,2,1,0:T(8,128)(2,1)} %copy-done.9), custom_call_target="tpu_custom_call" | custom-call | tf_op jit(solution)/shard_map/pallas_call | solution.py:152
  35.5 3.8 %all-to-all-start.1 = ((bf16[8,2,48,384]{3,2,1,0:T(8,128)(2,1)}), bf16[8,2,48,384]{3,2,1,0:T(8,128)(2,1)S(1)}, u32[]{:S(2)}, u32[]{:S(2)}) async-start(bf16[8,2,48,384]{3,2,1,0:T(8,128)(2,1)} %shard_map.86), calls=%async_computation.1 | async-start | bytes 1179648 | tf_op jit(solution)/shard_map/all_to_all | solution.py:494
  39.2 5.3 %shard_map.85 = (bf16[2,256,384]{2,1,0:T(8,128)(2,1)}, bf16[2,256,384]{2,1,0:T(8,128)(2,1)}, bf16[2,768,256]{2,1,0:T(8,128)(2,1)}) custom-call(s32[4]{0:T(128)} %pad_add_fusion.pos, bf16[256,768]{1,0:T(8,128)(2,1)} %bitcast.15, bf16[256,768]{1,0:T(8,128)(2,1)} %copy-done.3, bf16[256,768]{1,0:T(8,128)(2,1)} %bitcast.16, bf16[256,768]{1,0:T(8,128)(2,1)} %copy-done.6, ...), custom_call_target="tpu_custom_call" | custom-call | tf_op jit(solution)/shard_map/pallas_call | solution.py:125
  44.5 2.3 %all-to-all-done.1.xr = bf16[8,2,48,384]{3,2,1,0:T(8,128)(2,1)S(1)} async-done(((bf16[8,2,48,384]{3,2,1,0:T(8,128)(2,1)}), bf16[8,2,48,384]{3,2,1,0:T(8,128)(2,1)S(1)}, u32[]{:S(2)}, u32[]{:S(2)}) %all-to-all-start.1) | async-done | bytes 589856 | tf_op jit(solution)/shard_map/all_to_all | solution.py:494
  46.8 0.8 copy-done.2
  47.6 17.6 %shard_map.87 = (bf16[2,256,384]{2,1,0:T(8,128)(2,1)}, bf16[2,256,384]{2,1,0:T(8,128)(2,1)}, f32[2,2,256,384]{3,2,1,0:T(8,128)}, f32[2,2,128,384]{3,2,1,0:T(8,12...) custom-call(s32[4]{0:T(128)} %pad_add_fusion.pos, ...), custom_call_target="tpu_custom_call" | custom-call | tf_op jit(solution)/shard_map/pallas_call | solution.py:238
  65.2 4.4 %collective-permute-start.7 = (bf16[2,256,384]{2,1,0:T(8,128)(2,1)}, bf16[2,256,384]{2,1,0:T(8,128)(2,1)S(1)}, u32[]{:S(2)}, u32[]{:S(2)}) collective-permute-start(bf16[2,256,384]{2,1,0:T(8,128)(2,1)} %get-tuple-element.76.att_own), channel_id=1, source_target_pairs={{0,2},{2,0},{1,3},{3,1},{4,6},{6,4},{5,7},{7,5},{8,10},{10,8},{9,1... | collective-permute-start | bytes 1179656 | tf_op jit(solution)/shard_map/ppermute | solution.py:467
  69.6 3.5 %all-to-all-start.2 = ((bf16[8,2,48,384]{3,2,1,0:T(8,128)(2,1)}), bf16[8,2,48,384]{3,2,1,0:T(8,128)(2,1)S(1)}, u32[]{:S(2)}, u32[]{:S(2)}) async-start(bf16[8,2,48,384]{3,2,1,0:T(8,128)(2,1)} %get-tuple-element.75), calls=%async_computation.2 | async-start | bytes 1179648 | tf_op jit(solution)/shard_map/all_to_all | solution.py:498
  73.1 0.7 copy-done.4
  73.9 5.6 %shard_map.88 = (bf16[2,2,96,384]{3,2,1,0:T(8,128)(2,1)}, bf16[2,2,96,384]{3,2,1,0:T(8,128)(2,1)}, bf16[2,2,96,384]{3,2,1,0:T(8,128)(2,1)}, bf16[2,2,96,384]{3,2,1,0:T(8,128)(2,1)}) custom-call(s32[4]{0:T(128)} %pad_add_fusion.pos, bf16[2,256,384]{2,1,0:T(8,128)(2,1)} %get-tuple-element.76.att_own, bf16[2,256,384]{2,1,0:T(8,128)(2,1)} %copy-done.4, ...), custom_call_target="tpu_custom_call" | custom-call | tf_op jit(solution)/shard_map/pallas_call | solution.py:283
  79.5 1.4 collective-permute-start.8
  80.8 1.2 collective-permute-start.9
  82.0 2.4 %collective-permute-start.10 = (bf16[2,2,96,384]{3,2,1,0:T(8,128)(2,1)}, bf16[2,2,96,384]{3,2,1,0:T(8,128)(2,1)S(1)}, u32[]{:S(2)}, u32[]{:S(2)}) collective-permute-start(bf16[2,2,96,384]{3,2,1,0:T(8,128)(2,1)} %get-tuple-element.89), channel_id=1, source_target_pairs={{0,16},{8,24},{16,0},{24,8},{1,17},{9,25},{17,1},{25,9},{2,18},{10... | collective-permute-start | bytes 884744 | tf_op jit(solution)/shard_map/ppermute | solution.py:471
  84.7 2.0 %collective-permute-done.9.dwy = bf16[2,128,384]{2,1,0:T(8,128)(2,1)S(1)} collective-permute-done((bf16[2,128,384]{2,1,0:T(8,128)(2,1)S(1)}, bf16[2,128,384]{2,1,0:T(8,128)(2,1)S(1)}, u32[]{:S(2)}, u32[]{:S(2)}) %collective-permute-start.9) | collective-permute-done | bytes 196640 | tf_op jit(solution)/shard_map/ppermute | solution.py:467
  86.7 1.6 collective-permute-done.8.t1
  88.3 2.6 %shard_map.89 = bf16[8,2,16,384]{3,2,1,0:T(8,128)(2,1)} custom-call(s32[4]{0:T(128)} %pad_add_fusion.pos, bf16[8,2,48,384]{3,2,1,0:T(8,128)(2,1)} %copy-done.1), custom_call_target="tpu_custom_call" | custom-call | tf_op jit(solution)/shard_map/pallas_call | solution.py:322
  91.0 3.4 %all-to-all-start.3 = ((bf16[8,2,16,384]{3,2,1,0:T(8,128)(2,1)}), bf16[8,2,16,384]{3,2,1,0:T(8,128)(2,1)S(1)}, u32[]{:S(2)}, u32[]{:S(2)}) async-start(bf16[8,2,16,384]{3,2,1,0:T(8,128)(2,1)} %shard_map.89), calls=%async_computation.3 | async-start | bytes 393216 | tf_op jit(solution)/shard_map/all_to_all | solution.py:504
  94.4 1.1 collective-permute-start.15
  95.5 2.4 %shard_map.90 = (bf16[2,64,384]{2,1,0:T(8,128)(2,1)}, bf16[2,32,384]{2,1,0:T(8,128)(2,1)}, bf16[2,32,384]{2,1,0:T(8,128)(2,1)}) custom-call(s32[4]{0:T(128)} %pad_add_fusion.pos, f32[2,128,384]{2,1,0:T(8,128)} %get-tuple-element.83.dw, bf16[2,128,384]{2,1,0:T(8,128)(2,1)} %copy-done.16), custom_call_target="tpu_custom_call" | custom-call | tf_op jit(solution)/shard_map/pallas_call | solution.py:341
  97.9 1.7 collective-permute-done.11.t3
  99.6 1.2 collective-permute-start.13
  100.7 0.9 collective-permute-start.14
  102.2 2.8 %shard_map.91 = (bf16[96,384]{1,0:T(8,128)(2,1)}, bf16[96,384]{1,0:T(8,128)(2,1)}, bf16[96,384]{1,0:T(8,128)(2,1)}, bf16[96,384]{1,0:T(8,128)(2,1)}) custom-call(s32[4]{0:T(128)} %pad_add_fusion.pos, bf16[2,2,96,384]{3,2,1,0:T(8,128)(2,1)} %get-tuple-element.94.t0, bf16[2,2,96,384]{3,2,1,0:T(8,128)(2,1)} %copy-done.12, bf16[2,2,96,384]{3,2,1,0:T(8,128)(2,1)} %copy-done.13, ...), custom_call_target="tpu_custom_call" | custom-call | tf_op jit(solution)/shard_map/pallas_call | solution.py:303
  105.0 2.8 %collective-permute-start.16 = (bf16[96,384]{1,0:T(8,128)(2,1)}, bf16[96,384]{1,0:T(8,128)(2,1)S(1)}, u32[]{:S(2)}, u32[]{:S(2)}) collective-permute-start(bf16[96,384]{1,0:T(8,128)(2,1)} %get-tuple-element.108), channel_id=1, source_target_pairs={{0,1},{1,0},{4,5},{5,4},{2,3},{3,2},{6,7},{7,6},{8,9},{9,8},{12,13... | collective-permute-start | bytes 221192 | tf_op jit(solution)/shard_map/ppermute | solution.py:471
  109.1 6.2 %shard_map.92 = (bf16[2,256,1152]{2,1,0:T(8,128)(2,1)}, bf16[8,2,96,384]{3,2,1,0:T(8,128)(2,1)}) custom-call(s32[4]{0:T(128)} %pad_add_fusion.pos, bf16[8,2,16,384]{3,2,1,0:T(8,128)(2,1)} %copy-done.8, f32[2,2,256,384]{3,2,1,0:T(8,128)} %get-tuple-element.100.dkv, f32[2,2,128,384]{3,2,1,0:T(8,128)} %get-tuple-element.101.dn1, ...), custom_call_target="tpu_custom_call" | custom-call | tf_op jit(solution)/shard_map/pallas_call | solution.py:384
  116.0 6.3 %all-to-all-start.4 = ((bf16[16,96,384]{2,1,0:T(8,128)(2,1)}), bf16[16,96,384]{2,1,0:T(8,128)(2,1)S(1)}, u32[]{:S(2)}, u32[]{:S(2)}) async-start(bf16[16,96,384]{2,1,0:T(8,128)(2,1)} %bitcast.19), calls=%async_computation.4 | async-start | bytes 2359296 | tf_op jit(solution)/shard_map/all_to_all | solution.py:513
  122.3 0.9 dynamic-slice_bitcast_fusion
  123.2 4.1 %collective-permute-start.19 = (bf16[256,1152]{1,0:T(8,128)(2,1)S(1)}, bf16[256,1152]{1,0:T(8,128)(2,1)S(1)}, u32[]{:S(2)}, u32[]{:S(2)}) collective-permute-start(bf16[256,1152]{1,0:T(8,128)(2,1)S(1)} %get-tuple-element.124), channel_id=1, source_target_pairs={{0,2},{2,0},{1,3},{3,1},{4,6},{6,4},{5,7},{7,5},{8,10},{10,8},{9,1... | collective-permute-start | bytes 1769480 | tf_op jit(solution)/shard_map/ppermute | solution.py:467
  127.3 3.5 %shard_map.94 = bf16[256,768]{1,0:T(8,128)(2,1)} custom-call(s32[4]{0:T(128)} %pad_add_fusion.pos, bf16[2,256,384]{2,1,0:T(8,128)(2,1)} %get-tuple-element.76.att_own, bf16[2,256,384]{2,1,0:T(8,128)(2,1)} %copy-done.4, bf16[768,768]{1,0:T(8,128)(2,1)} %w_oth.1, bf16[768,768]{1,0:T(8,128)(2,1)} %w_oth.1), custom_call_target="tpu_custom_call" | custom-call | tf_op jit(solution)/shard_map/pallas_call | solution.py:257
  130.7 0.8 copy-done.10
  131.6 5.1 %shard_map.93 = bf16[256,768]{1,0:T(8,128)(2,1)} custom-call(s32[4]{0:T(128)} %pad_add_fusion.pos, bf16[256,1152]{1,0:T(8,128)(2,1)} %get-tuple-element.125.pg_own, bf16[256,1152]{1,0:T(8,128)(2,1)} %copy-done.10, bf16[768,2304]{1,0:T(8,128)(2,1)} %rest_5_.1, bf16[768,2304]{1,0:T(8,128)(2,1)} %rest_5_.1, bf16[768,2304]{1,0:T(8,128)(2,1)} %rest_5_.1, ...), custom_call_target="tpu_custom_call" | custom-call | tf_op jit(solution)/shard_map/pallas_call | solution.py:407
  136.7 1.1 copy-done
  137.8 3.2 %shard_map.95 = bf16[8,2,16,384]{3,2,1,0:T(8,128)(2,1)} custom-call(s32[4]{0:T(128)} %pad_add_fusion.pos, bf16[96,384]{1,0:T(8,128)(2,1)} %get-tuple-element.115.f0, bf16[96,384]{1,0:T(8,128)(2,1)} %copy-done.20, bf16[96,384]{1,0:T(8,128)(2,1)} %copy-done.21, bf16[96,384]{1,0:T(8,128)(2,1)} %copy-done.22, bf16[16,96,384]{2,1,0:T(8,128)(2,1)} %copy-done), custom_call_target="tpu_custom_call" | custom-call | tf_op jit(solution)/shard_map/pallas_call | solution.py:436
  141.0 15.4 %all_to_all.30 = bf16[8,2,16,384]{3,2,1,0:T(8,128)(2,1)S(1)} all-to-all(bf16[8,2,16,384]{3,2,1,0:T(8,128)(2,1)} %shard_map.95), channel_id=1, replica_groups=mesh['z'=8,'x'=4,'y'=2,'c'=2,'dp'=2] {'z'}, dimensions={0} | all-to-all | bytes 393216 | tf_op jit(solution)/shard_map/all_to_all | solution.py:519
  156.4 3.3 %collective-permute-start.20 = (bf16[16,384]{1,0:T(8,128)(2,1)S(1)}, bf16[16,384]{1,0:T(8,128)(2,1)S(1)}, u32[]{:S(2)}, u32[]{:S(2)}) collective-permute-start(bf16[16,384]{1,0:T(8,128)(2,1)S(1)} %get-tuple-element.123.own), channel_id=1, source_target_pairs={{0,1},{1,0},{2,3},{3,2},{4,5},{5,4},{6,7},{7,6},{8,9},{9,8},{10,11... | collective-permute-start | bytes 36872 | tf_op jit(solution)/shard_map/ppermute | solution.py:471
  159.7 5.3 %collective-permute-start.21 = (bf16[16,384]{1,0:T(8,128)(2,1)S(1)}, bf16[16,384]{1,0:T(8,128)(2,1)S(1)}, u32[]{:S(2)}, u32[]{:S(2)}) collective-permute-start(bf16[16,384]{1,0:T(8,128)(2,1)S(1)} %get-tuple-element.122), channel_id=1, source_target_pairs={{0,2},{1,3},{2,0},{3,1},{4,6},{5,7},{6,4},{7,5},{8,10},{9,11},{10,... | collective-permute-start | bytes 36872 | tf_op jit(solution)/shard_map/ppermute | solution.py:471
  165.1 2.0 %collective-permute-start.22 = (bf16[16,384]{1,0:T(8,128)(2,1)S(1)}, bf16[16,384]{1,0:T(8,128)(2,1)S(1)}, u32[]{:S(2)}, u32[]{:S(2)}) collective-permute-start(bf16[16,384]{1,0:T(8,128)(2,1)S(1)} %get-tuple-element.122), channel_id=1, source_target_pairs={{0,3},{1,2},{2,1},{3,0},{4,7},{5,6},{6,5},{7,4},{8,11},{9,10},{10,... | collective-permute-start | bytes 36872 | tf_op jit(solution)/shard_map/ppermute | solution.py:471
  167.1 2.6 %collective-permute-done.22.from_both = bf16[16,384]{1,0:T(8,128)(2,1)S(1)} collective-permute-done((bf16[16,384]{1,0:T(8,128)(2,1)S(1)}, bf16[16,384]{1,0:T(8,128)(2,1)S(1)}, u32[]{:S(2)}, u32[]{:S(2)}) %collective-permute-start.22) | collective-permute-done | bytes 12320 | tf_op jit(solution)/shard_map/ppermute | solution.py:471
  170.3 2.1 %shard_map.96 = (f32[6,2304]{1,0:T(8,128)}, f32[6,768]{1,0:T(8,128)}) custom-call(s32[4]{0:T(128)} %pad_add_fusion.pos, bf16[16,384]{1,0:T(8,128)(2,1)} %copy-done.25, bf16[16,384]{1,0:T(8,128)(2,1)} %copy-done.26, bf16[16,384]{1,0:T(8,128)(2,1)} %copy-done.27, bf16[16,384]{1,0:T(8,128)(2,1)} %copy-done.28), custom_call_target="tpu_custom_call" | custom-call | tf_op jit(solution)/shard_map/pallas_call | solution.py:457
  (90 shorter events, 5.5 us)
Async XLA Ops:
  0.6 4.9 %collective-permute-start = (bf16[256,768]{1,0:T(8,128)(2,1)}, bf16[256,768]{1,0:T(8,128)(2,1)S(1)}, u32[]{:S(2)}, u32[]{:S(2)}) collective-permute-start(bf16[256,768]{1,0:T(8,128)(2,1)} %bitcast.13), channel_id=1, source_target_pairs={{0,2},{2,0},{1,3},{3,1},{4,6},{6,4},{5,7},{7,5},{8,10},{10,8},{9,1... | collective-permute-start | bytes 1179656 | tf_op jit(solution)/shard_map/ppermute | solution.py:467
  4.6 6.7 %copy-start.5 = (bf16[1,256,768]{2,1,0:T(8,128)(2,1)S(1)}, bf16[1,256,768]{2,1,0:T(8,128)(2,1)}, u32[]{:S(2)}) copy-start(bf16[1,256,768]{2,1,0:T(8,128)(2,1)} %param.6) | copy-start | bytes 1179652
  11.3 12.3 %collective-permute-start.2 = (bf16[2,64,384]{2,1,0:T(8,128)(2,1)}, bf16[2,64,384]{2,1,0:T(8,128)(2,1)S(1)}, u32[]{:S(2)}, u32[]{:S(2)}) collective-permute-start(bf16[2,64,384]{2,1,0:T(8,128)(2,1)} %get-tuple-element.65), channel_id=1, source_target_pairs={{0,8},{8,0},{16,24},{24,16},{1,9},{9,1},{17,25},{25,17},{2,10},{10... | collective-permute-start | bytes 294920 | tf_op jit(solution)/shard_map/ppermute | solution.py:471
  11.3 12.6 %collective-permute-start.6 = (bf16[256,768]{1,0:T(8,128)(2,1)S(1)}, bf16[256,768]{1,0:T(8,128)(2,1)S(1)}, u32[]{:S(2)}, u32[]{:S(2)}) collective-permute-start(bf16[256,768]{1,0:T(8,128)(2,1)S(1)} %bitcast.18), channel_id=1, source_target_pairs={{0,2},{2,0},{1,3},{3,1},{4,6},{6,4},{5,7},{7,5},{8,10},{10,8},{9,1... | collective-permute-start | bytes 1179656 | tf_op jit(solution)/shard_map/ppermute | solution.py:467
  11.7 11.8 %collective-permute-start.3 = (bf16[2,32,384]{2,1,0:T(8,128)(2,1)}, bf16[2,32,384]{2,1,0:T(8,128)(2,1)S(1)}, u32[]{:S(2)}, u32[]{:S(2)}) collective-permute-start(bf16[2,32,384]{2,1,0:T(8,128)(2,1)} %get-tuple-element.66), channel_id=1, source_target_pairs={{0,16},{8,24},{16,0},{24,8},{1,17},{9,25},{17,1},{25,9},{2,18},{10... | collective-permute-start | bytes 147464 | tf_op jit(solution)/shard_map/ppermute | solution.py:471
  13.8 9.7 %collective-permute-start.4 = (bf16[2,32,384]{2,1,0:T(8,128)(2,1)}, bf16[2,32,384]{2,1,0:T(8,128)(2,1)S(1)}, u32[]{:S(2)}, u32[]{:S(2)}) collective-permute-start(bf16[2,32,384]{2,1,0:T(8,128)(2,1)} %get-tuple-element.66), channel_id=1, source_target_pairs={{0,24},{8,16},{16,8},{24,0},{1,25},{9,17},{17,9},{25,1},{2,26},{10... | collective-permute-start | bytes 147464 | tf_op jit(solution)/shard_map/ppermute | solution.py:471
  15.8 8.1 %collective-permute-start.1 = (bf16[2,128,384]{2,1,0:T(8,128)(2,1)}, bf16[2,128,384]{2,1,0:T(8,128)(2,1)S(1)}, u32[]{:S(2)}, u32[]{:S(2)}) collective-permute-start(bf16[2,128,384]{2,1,0:T(8,128)(2,1)} %get-tuple-element.64), channel_id=1, source_target_pairs={{0,4},{4,0},{1,5},{5,1},{2,6},{6,2},{3,7},{7,3},{8,12},{12,8},{9,1... | collective-permute-start | bytes 589832 | tf_op jit(solution)/shard_map/ppermute | solution.py:467
  15.8 16.4 %all-to-all-start = ((bf16[8,2,16,384]{3,2,1,0:T(8,128)(2,1)}), bf16[8,2,16,384]{3,2,1,0:T(8,128)(2,1)S(1)}, u32[]{:S(2)}, u32[]{:S(2)}) async-start(bf16[8,2,16,384]{3,2,1,0:T(8,128)(2,1)} %get-tuple-element.63), calls=%async_computation | async-start | bytes 393216 | tf_op jit(solution)/shard_map/all_to_all | solution.py:492
  23.6 20.9 %copy-start.11 = (bf16[2,128,384]{2,1,0:T(8,128)(2,1)}, bf16[2,128,384]{2,1,0:T(8,128)(2,1)S(1)}, u32[]{:S(2)}) copy-start(bf16[2,128,384]{2,1,0:T(8,128)(2,1)S(1)} %constant_dynamic-update-slice_fusion.wr) | copy-start | bytes 589828
  23.6 5.4 %collective-permute-start.5 = (bf16[2,128,384]{2,1,0:T(8,128)(2,1)S(1)}, bf16[2,128,384]{2,1,0:T(8,128)(2,1)S(1)}, u32[]{:S(2)}, u32[]{:S(2)}) collective-permute-start(bf16[2,128,384]{2,1,0:T(8,128)(2,1)S(1)} %constant_dynamic-update-slice_fusion.wr), channel_id=1, source_target_pairs={{0,4},{4,0},{1,5},{5,1},{2,6},{6,2},{3,7},{7,3},{8,12},{12,8},{9,1... | collective-permute-start | bytes 589832 | tf_op jit(solution)/shard_map/ppermute | solution.py:467
  23.9 15.4 %copy-start.6 = (bf16[256,768]{1,0:T(8,128)(2,1)}, bf16[256,768]{1,0:T(8,128)(2,1)S(1)}, u32[]{:S(2)}) copy-start(bf16[256,768]{1,0:T(8,128)(2,1)S(1)} %collective-permute-done.6.ct_oth) | copy-start | bytes 1179652
  23.9 20.6 %copy-start.17 = (bf16[2,128,384]{2,1,0:T(8,128)(2,1)}, bf16[2,128,384]{2,1,0:T(8,128)(2,1)S(1)}, u32[]{:S(2)}) copy-start(bf16[2,128,384]{2,1,0:T(8,128)(2,1)S(1)} %collective-permute-done.1.yr) | copy-start | bytes 589828
  29.0 15.5 %copy-start.18 = (bf16[2,128,384]{2,1,0:T(8,128)(2,1)}, bf16[2,128,384]{2,1,0:T(8,128)(2,1)S(1)}, u32[]{:S(2)}) copy-start(bf16[2,128,384]{2,1,0:T(8,128)(2,1)S(1)} %collective-permute-done.5.wy) | copy-start | bytes 589828
  35.5 11.3 %all-to-all-start.1 = ((bf16[8,2,48,384]{3,2,1,0:T(8,128)(2,1)}), bf16[8,2,48,384]{3,2,1,0:T(8,128)(2,1)S(1)}, u32[]{:S(2)}, u32[]{:S(2)}) async-start(bf16[8,2,48,384]{3,2,1,0:T(8,128)(2,1)} %shard_map.86), calls=%async_computation.1 | async-start | bytes 1179648 | tf_op jit(solution)/shard_map/all_to_all | solution.py:494
  46.8 0.8 copy-start.2
  65.2 7.9 %collective-permute-start.7 = (bf16[2,256,384]{2,1,0:T(8,128)(2,1)}, bf16[2,256,384]{2,1,0:T(8,128)(2,1)S(1)}, u32[]{:S(2)}, u32[]{:S(2)}) collective-permute-start(bf16[2,256,384]{2,1,0:T(8,128)(2,1)} %get-tuple-element.76.att_own), channel_id=1, source_target_pairs={{0,2},{2,0},{1,3},{3,1},{4,6},{6,4},{5,7},{7,5},{8,10},{10,8},{9,1... | collective-permute-start | bytes 1179656 | tf_op jit(solution)/shard_map/ppermute | solution.py:467
  69.6 17.1 %all-to-all-start.2 = ((bf16[8,2,48,384]{3,2,1,0:T(8,128)(2,1)}), bf16[8,2,48,384]{3,2,1,0:T(8,128)(2,1)S(1)}, u32[]{:S(2)}, u32[]{:S(2)}) async-start(bf16[8,2,48,384]{3,2,1,0:T(8,128)(2,1)} %get-tuple-element.75), calls=%async_computation.2 | async-start | bytes 1179648 | tf_op jit(solution)/shard_map/all_to_all | solution.py:498
  73.1 0.8 copy-start.4
  73.9 7.0 %copy-start.30 = (bf16[2,128,384]{2,1,0:T(8,128)(2,1)S(1)}, bf16[2,128,384]{2,1,0:T(8,128)(2,1)}, u32[]{:S(2)}) copy-start(bf16[2,128,384]{2,1,0:T(8,128)(2,1)} %get-tuple-element.81) | copy-start | bytes 589828
  79.5 14.9 %copy-start.29 = (bf16[2,128,384]{2,1,0:T(8,128)(2,1)S(1)}, bf16[2,128,384]{2,1,0:T(8,128)(2,1)}, u32[]{:S(2)}) copy-start(bf16[2,128,384]{2,1,0:T(8,128)(2,1)} %get-tuple-element.102) | copy-start | bytes 589828
  79.5 8.8 %collective-permute-start.8 = (bf16[2,2,96,384]{3,2,1,0:T(8,128)(2,1)}, bf16[2,2,96,384]{3,2,1,0:T(8,128)(2,1)S(1)}, u32[]{:S(2)}, u32[]{:S(2)}) collective-permute-start(bf16[2,2,96,384]{3,2,1,0:T(8,128)(2,1)} %get-tuple-element.80), channel_id=1, source_target_pairs={{0,8},{8,0},{16,24},{24,16},{1,9},{9,1},{17,25},{25,17},{2,10},{10... | collective-permute-start | bytes 884744 | tf_op jit(solution)/shard_map/ppermute | solution.py:471
  80.8 5.9 %collective-permute-start.9 = (bf16[2,128,384]{2,1,0:T(8,128)(2,1)S(1)}, bf16[2,128,384]{2,1,0:T(8,128)(2,1)S(1)}, u32[]{:S(2)}, u32[]{:S(2)}) collective-permute-start(bf16[2,128,384]{2,1,0:T(8,128)(2,1)S(1)} %copy-done.30), channel_id=1, source_target_pairs={{0,4},{4,0},{1,5},{5,1},{2,6},{6,2},{3,7},{7,3},{8,12},{12,8},{9,1... | collective-permute-start | bytes 589832 | tf_op jit(solution)/shard_map/ppermute | solution.py:467
  82.0 15.9 %collective-permute-start.10 = (bf16[2,2,96,384]{3,2,1,0:T(8,128)(2,1)}, bf16[2,2,96,384]{3,2,1,0:T(8,128)(2,1)S(1)}, u32[]{:S(2)}, u32[]{:S(2)}) collective-permute-start(bf16[2,2,96,384]{3,2,1,0:T(8,128)(2,1)} %get-tuple-element.89), channel_id=1, source_target_pairs={{0,16},{8,24},{16,0},{24,8},{1,17},{9,25},{17,1},{25,9},{2,18},{10... | collective-permute-start | bytes 884744 | tf_op jit(solution)/shard_map/ppermute | solution.py:471
  84.5 15.1 %collective-permute-start.11 = (bf16[2,2,96,384]{3,2,1,0:T(8,128)(2,1)}, bf16[2,2,96,384]{3,2,1,0:T(8,128)(2,1)S(1)}, u32[]{:S(2)}, u32[]{:S(2)}) collective-permute-start(bf16[2,2,96,384]{3,2,1,0:T(8,128)(2,1)} %get-tuple-element.90), channel_id=1, source_target_pairs={{0,24},{8,16},{16,8},{24,0},{1,25},{9,17},{17,9},{25,1},{2,26},{10... | collective-permute-start | bytes 884744 | tf_op jit(solution)/shard_map/ppermute | solution.py:471
  86.7 8.8 %copy-start.16 = (bf16[2,128,384]{2,1,0:T(8,128)(2,1)}, bf16[2,128,384]{2,1,0:T(8,128)(2,1)S(1)}, u32[]{:S(2)}) copy-start(bf16[2,128,384]{2,1,0:T(8,128)(2,1)S(1)} %collective-permute-done.9.dwy) | copy-start | bytes 589828
  86.7 1.6 copy-start.1
  88.3 13.9 %copy-start.12 = (bf16[2,2,96,384]{3,2,1,0:T(8,128)(2,1)}, bf16[2,2,96,384]{3,2,1,0:T(8,128)(2,1)S(1)}, u32[]{:S(2)}) copy-start(bf16[2,2,96,384]{3,2,1,0:T(8,128)(2,1)S(1)} %collective-permute-done.8.t1) | copy-start | bytes 884740
  91.0 17.4 %all-to-all-start.3 = ((bf16[8,2,16,384]{3,2,1,0:T(8,128)(2,1)}), bf16[8,2,16,384]{3,2,1,0:T(8,128)(2,1)S(1)}, u32[]{:S(2)}, u32[]{:S(2)}) async-start(bf16[8,2,16,384]{3,2,1,0:T(8,128)(2,1)} %shard_map.89), calls=%async_computation.3 | async-start | bytes 393216 | tf_op jit(solution)/shard_map/all_to_all | solution.py:504
  94.4 14.0 %collective-permute-start.15 = (bf16[2,128,384]{2,1,0:T(8,128)(2,1)S(1)}, bf16[2,128,384]{2,1,0:T(8,128)(2,1)S(1)}, u32[]{:S(2)}, u32[]{:S(2)}) collective-permute-start(bf16[2,128,384]{2,1,0:T(8,128)(2,1)S(1)} %copy-done.29), channel_id=1, source_target_pairs={{0,4},{4,0},{1,5},{5,1},{2,6},{6,2},{3,7},{7,3},{8,12},{12,8},{9,1... | collective-permute-start | bytes 589832 | tf_op jit(solution)/shard_map/ppermute | solution.py:467
  97.9 4.3 %copy-start.13 = (bf16[2,2,96,384]{3,2,1,0:T(8,128)(2,1)}, bf16[2,2,96,384]{3,2,1,0:T(8,128)(2,1)S(1)}, u32[]{:S(2)}) copy-start(bf16[2,2,96,384]{3,2,1,0:T(8,128)(2,1)S(1)} %collective-permute-done.10.t2) | copy-start | bytes 884740
  99.6 2.7 %copy-start.14 = (bf16[2,2,96,384]{3,2,1,0:T(8,128)(2,1)}, bf16[2,2,96,384]{3,2,1,0:T(8,128)(2,1)S(1)}, u32[]{:S(2)}) copy-start(bf16[2,2,96,384]{3,2,1,0:T(8,128)(2,1)S(1)} %collective-permute-done.11.t3) | copy-start | bytes 884740
  99.6 8.3 %collective-permute-start.13 = (bf16[2,32,384]{2,1,0:T(8,128)(2,1)}, bf16[2,32,384]{2,1,0:T(8,128)(2,1)S(1)}, u32[]{:S(2)}, u32[]{:S(2)}) collective-permute-start(bf16[2,32,384]{2,1,0:T(8,128)(2,1)} %get-tuple-element.92), channel_id=1, source_target_pairs={{0,16},{8,24},{16,0},{24,8},{1,17},{9,25},{17,1},{25,9},{2,18},{10... | collective-permute-start | bytes 147464 | tf_op jit(solution)/shard_map/ppermute | solution.py:471
  100.7 7.1 %collective-permute-start.14 = (bf16[2,32,384]{2,1,0:T(8,128)(2,1)}, bf16[2,32,384]{2,1,0:T(8,128)(2,1)S(1)}, u32[]{:S(2)}, u32[]{:S(2)}) collective-permute-start(bf16[2,32,384]{2,1,0:T(8,128)(2,1)} %get-tuple-element.93), channel_id=1, source_target_pairs={{0,24},{8,16},{16,8},{24,0},{1,25},{9,17},{17,9},{25,1},{2,26},{10... | collective-permute-start | bytes 147464 | tf_op jit(solution)/shard_map/ppermute | solution.py:471
  101.6 6.7 %collective-permute-start.12 = (bf16[2,64,384]{2,1,0:T(8,128)(2,1)}, bf16[2,64,384]{2,1,0:T(8,128)(2,1)S(1)}, u32[]{:S(2)}, u32[]{:S(2)}) collective-permute-start(bf16[2,64,384]{2,1,0:T(8,128)(2,1)} %get-tuple-element.91), channel_id=1, source_target_pairs={{0,8},{8,0},{16,24},{24,16},{1,9},{9,1},{17,25},{25,17},{2,10},{10... | collective-permute-start | bytes 294920 | tf_op jit(solution)/shard_map/ppermute | solution.py:471
  105.0 10.2 %collective-permute-start.16 = (bf16[96,384]{1,0:T(8,128)(2,1)}, bf16[96,384]{1,0:T(8,128)(2,1)S(1)}, u32[]{:S(2)}, u32[]{:S(2)}) collective-permute-start(bf16[96,384]{1,0:T(8,128)(2,1)} %get-tuple-element.108), channel_id=1, source_target_pairs={{0,1},{1,0},{4,5},{5,4},{2,3},{3,2},{6,7},{7,6},{8,9},{9,8},{12,13... | collective-permute-start | bytes 221192 | tf_op jit(solution)/shard_map/ppermute | solution.py:471
  107.8 7.4 %collective-permute-start.17 = (bf16[96,384]{1,0:T(8,128)(2,1)}, bf16[96,384]{1,0:T(8,128)(2,1)S(1)}, u32[]{:S(2)}, u32[]{:S(2)}) collective-permute-start(bf16[96,384]{1,0:T(8,128)(2,1)} %get-tuple-element.109), channel_id=1, source_target_pairs={{0,4},{1,5},{4,0},{5,1},{2,6},{3,7},{6,2},{7,3},{8,12},{9,13},{12,... | collective-permute-start | bytes 221192 | tf_op jit(solution)/shard_map/ppermute | solution.py:471
  107.9 7.4 %collective-permute-start.18 = (bf16[96,384]{1,0:T(8,128)(2,1)}, bf16[96,384]{1,0:T(8,128)(2,1)S(1)}, u32[]{:S(2)}, u32[]{:S(2)}) collective-permute-start(bf16[96,384]{1,0:T(8,128)(2,1)} %get-tuple-element.110), channel_id=1, source_target_pairs={{0,5},{1,4},{4,1},{5,0},{2,7},{3,6},{6,3},{7,2},{8,13},{9,12},{12,... | collective-permute-start | bytes 221192 | tf_op jit(solution)/shard_map/ppermute | solution.py:471
  115.3 6.9 %copy-start.7 = (bf16[2,256,1152]{2,1,0:T(8,128)(2,1)S(1)}, bf16[2,256,1152]{2,1,0:T(8,128)(2,1)}, u32[]{:S(2)}) copy-start(bf16[2,256,1152]{2,1,0:T(8,128)(2,1)} %get-tuple-element.112) | copy-start | bytes 3538948
  116.0 20.7 %all-to-all-start.4 = ((bf16[16,96,384]{2,1,0:T(8,128)(2,1)}), bf16[16,96,384]{2,1,0:T(8,128)(2,1)S(1)}, u32[]{:S(2)}, u32[]{:S(2)}) async-start(bf16[16,96,384]{2,1,0:T(8,128)(2,1)} %bitcast.19), calls=%async_computation.4 | async-start | bytes 2359296 | tf_op jit(solution)/shard_map/all_to_all | solution.py:513
  123.2 7.6 %collective-permute-start.19 = (bf16[256,1152]{1,0:T(8,128)(2,1)S(1)}, bf16[256,1152]{1,0:T(8,128)(2,1)S(1)}, u32[]{:S(2)}, u32[]{:S(2)}) collective-permute-start(bf16[256,1152]{1,0:T(8,128)(2,1)S(1)} %get-tuple-element.124), channel_id=1, source_target_pairs={{0,2},{2,0},{1,3},{3,1},{4,6},{6,4},{5,7},{7,5},{8,10},{10,8},{9,1... | collective-permute-start | bytes 1769480 | tf_op jit(solution)/shard_map/ppermute | solution.py:467
  130.7 0.8 copy-start.10
  136.7 1.1 copy-start
  156.4 13.3 %copy-start.25 = (bf16[16,384]{1,0:T(8,128)(2,1)}, bf16[16,384]{1,0:T(8,128)(2,1)S(1)}, u32[]{:S(2)}) copy-start(bf16[16,384]{1,0:T(8,128)(2,1)S(1)} %get-tuple-element.123.own) | copy-start | bytes 36868
  156.4 10.7 %collective-permute-start.20 = (bf16[16,384]{1,0:T(8,128)(2,1)S(1)}, bf16[16,384]{1,0:T(8,128)(2,1)S(1)}, u32[]{:S(2)}, u32[]{:S(2)}) collective-permute-start(bf16[16,384]{1,0:T(8,128)(2,1)S(1)} %get-tuple-element.123.own), channel_id=1, source_target_pairs={{0,1},{1,0},{2,3},{3,2},{4,5},{5,4},{6,7},{7,6},{8,9},{9,8},{10,11... | collective-permute-start | bytes 36872 | tf_op jit(solution)/shard_map/ppermute | solution.py:471
  159.7 7.3 %collective-permute-start.21 = (bf16[16,384]{1,0:T(8,128)(2,1)S(1)}, bf16[16,384]{1,0:T(8,128)(2,1)S(1)}, u32[]{:S(2)}, u32[]{:S(2)}) collective-permute-start(bf16[16,384]{1,0:T(8,128)(2,1)S(1)} %get-tuple-element.122), channel_id=1, source_target_pairs={{0,2},{1,3},{2,0},{3,1},{4,6},{5,7},{6,4},{7,5},{8,10},{9,11},{10,... | collective-permute-start | bytes 36872 | tf_op jit(solution)/shard_map/ppermute | solution.py:471
  165.1 4.6 %collective-permute-start.22 = (bf16[16,384]{1,0:T(8,128)(2,1)S(1)}, bf16[16,384]{1,0:T(8,128)(2,1)S(1)}, u32[]{:S(2)}, u32[]{:S(2)}) collective-permute-start(bf16[16,384]{1,0:T(8,128)(2,1)S(1)} %get-tuple-element.122), channel_id=1, source_target_pairs={{0,3},{1,2},{2,1},{3,0},{4,7},{5,6},{6,5},{7,4},{8,11},{9,10},{10,... | collective-permute-start | bytes 36872 | tf_op jit(solution)/shard_map/ppermute | solution.py:471
  167.1 2.6 %copy-start.26 = (bf16[16,384]{1,0:T(8,128)(2,1)}, bf16[16,384]{1,0:T(8,128)(2,1)S(1)}, u32[]{:S(2)}) copy-start(bf16[16,384]{1,0:T(8,128)(2,1)S(1)} %collective-permute-done.20.from_dp) | copy-start | bytes 36868
  167.1 2.6 %copy-start.27 = (bf16[16,384]{1,0:T(8,128)(2,1)}, bf16[16,384]{1,0:T(8,128)(2,1)S(1)}, u32[]{:S(2)}) copy-start(bf16[16,384]{1,0:T(8,128)(2,1)S(1)} %collective-permute-done.21.from_core) | copy-start | bytes 36868
  (11 other events, 7.3 us)

commit v9 on v8

--- a/solution.py
+++ b/solution.py
@@ -309,41 +309,29 @@
     )(pos, *terms)
 
 
-def back_body(pos, xr, out):
+def back_body(pos, xr, dw, dwy, out, *tiers):
     hot = (iota((128, ZR), 0) == z_source(pos[1], 1, (128, ZR))).astype(BF16)
     for p in range(2):
         total = xr[0, p].astype(F32)
         for slot in range(1, 8):
             total = total + xr[slot, p].astype(F32)
         out[:, p] = dot(hot, total.astype(BF16)).astype(BF16).reshape(8, 16, H)
-
-
-def back_slots(pos, xr):
+        start = 0
+        for tier in tiers:
+            rows = tier.shape[1]
+            total = dw[p, start : start + rows] + dwy[p, start : start + rows].astype(F32)
+            tier[p] = total.astype(BF16)
+            start += rows
+
+
+def back_slots(pos, xr, dw, dwy):
+    outs = [(ZN, 2, 16, H), (2, 64, H), (2, 32, H), (2, 32, H)]
     return call(
         back_body,
         (1,),
-        [whole(8, 2, ZR, H)],
-        [(whole(ZN, 2, 16, H), ((ZN, 2, 16, H), BF16))],
-    )(pos, xr)[0]
-
-
-def hand_back_body(pos, dw, dwy, *outs):
-    start = 0
-    for out in outs:
-        rows = out.shape[1]
-        for p in range(2):
-            total = dw[p, start : start + rows] + dwy[p, start : start + rows].astype(F32)
-            out[p] = total.astype(BF16)
-        start += rows
-
-
-def hand_back(pos, dw, dwy):
-    return call(
-        hand_back_body,
-        (1,),
-        [whole(2, NR, H)] * 2,
-        [(whole(2, rows, H), ((2, rows, H), BF16)) for rows in (64, 32, 32)],
-    )(pos, dw, dwy)
+        [whole(8, 2, ZR, H), whole(2, NR, H), whole(2, NR, H)],
+        [(whole(*shape), (shape, BF16)) for shape in outs],
+    )(pos, xr, dw, dwy)
 
 
 def leaf_body(pos, zr, dkv, dn1, dy, g3, g4_a, g4_b, dq, xt, pg_out, grad_out):
@@ -488,9 +476,9 @@
     kv, n1, n2, n3, n4, zs = tree(pos, x_own, x_oth, w_qkv)
     yr = swap(n2, "y")
     wr = jnp.concatenate([along(n3, "x", 1), along(n4, "x", 2), along(n4, "x", 3)], axis=1)
+    zr = lax.all_to_all(zs, "z", 0, 0)
+    zr, yr, wr, ct_oth = lax.optimization_barrier((zr, yr, wr, ct_oth))
     wy = swap(wr, "y")
-    zr = lax.all_to_all(zs, "z", 0, 0)
-    zr, yr, wy, ct_oth = lax.optimization_barrier((zr, yr, wy, ct_oth))
     xr = lax.all_to_all(plane_slots(pos, zr), ("x", "y"), 0, 0)
     q, ag, xt = project(pos, x_own, x_oth, ct_own, ct_oth, w_qkv, w_out, perm)
     att, dq, dkv, dn1, dy, dwy, dw, dx = attention(pos, q, ag, kv, n1, yr, wr, wy, xr)
@@ -501,8 +489,8 @@
     first, *firsts = output_terms(pos, att, att_oth, ct_own, ct_oth, dq, xt, perm)
     firsts = [along(firsts[far - 1], "x", far) for far in (1, 2, 3)]
     dx_r, first, firsts[0], dwy = lax.optimization_barrier((dx_r, first, firsts[0], dwy))
-    dz_r = lax.all_to_all(back_slots(pos, dx_r), "z", 0, 0)
-    g3, g4_a, g4_b = hand_back(pos, dw, dwy)
+    dz, g3, g4_a, g4_b = back_slots(pos, dx_r, dw, dwy)
+    dz_r = lax.all_to_all(dz, "z", 0, 0)
     g3, g4_a, g4_b, firsts = lax.optimization_barrier((g3, g4_a, g4_b, firsts))
     g3, g4_a, g4_b = along(g3, "x", 1), along(g4_a, "x", 2), along(g4_b, "x", 3)
     firsts = x_sum(pos, first, *firsts)

time: 173 us -> 172 us (level)
  starting transfers between devices: 64.1 us -> 67.3 us
  waiting for transfers between devices: 19.4 us -> 16.5 us
  Pallas kernels: 64 us -> 61.8 us
    ppermute x15, waiting for transfers between devices: 5.88 us -> 10.3 us  [along(): return lax.ppermute(value, axes, [(i, i ^ far) for i in range(count)])]
    all_to_all x1, waiting for transfers between devices: 3.21 us -> 0.01 us  [shards(): zr = lax.all_to_all(zs, 'z', 0, 0)]
    ppermute x8, starting transfers between devices: 14.8 us -> 17.3 us  [swap(): return lax.ppermute(value, axis, [(0, 1), (1, 0)])]
    all_to_all x1, waiting for transfers between devices: 2.27 us -> 0.01 us  [shards(): xr = lax.all_to_all(plane_slots(pos, zr), ('x', 'y'), 0, 0)]
    pallas_call x2 -> x1, Pallas kernels: 5.05 us -> 2.8 us  [back_slots(): call(back_body, (1,), [whole(8, 2, ZR, H), whole(2, NR, H), whole(2, NR,...]
    all_to_all x1, starting transfers between devices: 3.39 us -> 5.47 us  [shards(): dz_r = lax.all_to_all(dz, 'z', 0, 0)]
    ppermute x8, waiting for transfers between devices: 8.05 us -> 6.21 us  [swap(): return lax.ppermute(value, axis, [(0, 1), (1, 0)])]
    unnamed x64 -> x60, local copies, waits for them, and re-layouts: 6.94 us -> 7.04 us
  transfers between devices with their start and end apart: 28 -> 28, of which waited for: 8 -> 8; matrix products, arithmetic and copies ran while one was open for 1% -> 1% of each run, Pallas kernels for 19% -> 21%
where the time goes in v9:
time: 172 us; the launch traced here: 171 us
  starting transfers between devices  67.3 us (39%)
  Pallas kernels  61.8 us (36%)
  waiting for transfers between devices  16.5 us (10%)
  blocking collectives  15.5 us (9%)
  local copies, waits for them, and re-layouts  7.97 us (5%)
    ppermute x15, starting transfers between devices, along(): return lax.ppermute(value, axes, [(i, i ^ far) for i in range(count)])  23.5 us
    pallas_call x1, Pallas kernels, attention(): call(attention_body, (H // 128,), [cut(2, TOK), cut(2, TOK), cut(2, 2, TO...  17.6 us
    ppermute x8, starting transfers between devices, swap(): return lax.ppermute(value, axis, [(0, 1), (1, 0)])  17.3 us
    all_to_all x1, blocking collectives, shards(): terms = lax.all_to_all(middle_sum(pos, firsts, terms), 'z', 0, 0)  15.5 us
    ppermute x15, waiting for transfers between devices, along(): return lax.ppermute(value, axes, [(i, i ^ far) for i in range(count)])  10.3 us
    unnamed x60, local copies, waits for them, and re-layouts  7.04 us
    all_to_all x1, starting transfers between devices, shards(): zr = lax.all_to_all(zs, 'z', 0, 0)  6.45 us
    ppermute x8, waiting for transfers between devices, swap(): return lax.ppermute(value, axis, [(0, 1), (1, 0)])  6.21 us
  transfers between devices with their start and end apart: 28, of which 8 were waited for; matrix products, arithmetic and copies ran while one was open for 1% of the time, Pallas kernels for 21%

profile of v9, /device:TPU:1, one launch (start us, length us, event | category | flops | bytes accessed | tf_op | source)
XLA Modules:
  0.0 170.6 jit_solution(10728021951436887139)
XLA Ops:
  0.6 3.3 %collective-permute-start = (bf16[256,768]{1,0:T(8,128)(2,1)}, bf16[256,768]{1,0:T(8,128)(2,1)S(1)}, u32[]{:S(2)}, u32[]{:S(2)}) collective-permute-start(bf16[256,768]{1,0:T(8,128)(2,1)} %bitcast.13), channel_id=1, source_target_pairs={{0,2},{2,0},{1,3},{3,1},{4,6},{6,4},{5,7},{7,5},{8,10},{10,8},{9,1... | collective-permute-start | bytes 1179656 | tf_op jit(solution)/shard_map/ppermute | solution.py:455
  4.7 0.9 collective-permute-done.x_oth
  6.3 5.0 %shard_map.84 = (bf16[2,2,256,384]{3,2,1,0:T(8,128)(2,1)}, bf16[2,2,128,384]{3,2,1,0:T(8,128)(2,1)}, bf16[2,128,384]{2,1,0:T(8,128)(2,1)}, bf16[2,64,384]{2,1,0:...) custom-call(s32[4]{0:T(128)} %pad_add_fusion.pos, bf16[256,768]{1,0:T(8,128)(2,1)} %bitcast.14, ...), custom_call_target="tpu_custom_call" | custom-call | tf_op jit(solution)/shard_map/pallas_call | solution.py:107
  11.3 6.5 %all-to-all-start = ((bf16[8,2,16,384]{3,2,1,0:T(8,128)(2,1)}), bf16[8,2,16,384]{3,2,1,0:T(8,128)(2,1)S(1)}, u32[]{:S(2)}, u32[]{:S(2)}) async-start(bf16[8,2,16,384]{3,2,1,0:T(8,128)(2,1)} %get-tuple-element.64), calls=%async_computation | async-start | bytes 393216 | tf_op jit(solution)/shard_map/all_to_all | solution.py:479
  17.7 1.2 collective-permute-start.2
  18.9 1.3 collective-permute-start.1
  20.2 2.5 %collective-permute-start.3 = (bf16[2,32,384]{2,1,0:T(8,128)(2,1)}, bf16[2,32,384]{2,1,0:T(8,128)(2,1)S(1)}, u32[]{:S(2)}, u32[]{:S(2)}) collective-permute-start(bf16[2,32,384]{2,1,0:T(8,128)(2,1)} %get-tuple-element.67), channel_id=1, source_target_pairs={{0,16},{8,24},{16,0},{24,8},{1,17},{9,25},{17,1},{25,9},{2,18},{10... | collective-permute-start | bytes 147464 | tf_op jit(solution)/shard_map/ppermute | solution.py:459
  22.9 2.7 %collective-permute-done.3 = bf16[2,32,384]{2,1,0:T(8,128)(2,1)S(1)} collective-permute-done((bf16[2,32,384]{2,1,0:T(8,128)(2,1)}, bf16[2,32,384]{2,1,0:T(8,128)(2,1)S(1)}, u32[]{:S(2)}, u32[]{:S(2)}) %collective-permute-start.3) | collective-permute-done | bytes 49184 | tf_op jit(solution)/shard_map/ppermute | solution.py:459
  25.5 1.6 collective-permute-done.4
  27.2 0.8 copy-done.8
  27.9 2.6 %shard_map.86 = bf16[8,2,48,384]{3,2,1,0:T(8,128)(2,1)} custom-call(s32[4]{0:T(128)} %pad_add_fusion.pos, bf16[8,2,16,384]{3,2,1,0:T(8,128)(2,1)} %copy-done.8), custom_call_target="tpu_custom_call" | custom-call | tf_op jit(solution)/shard_map/pallas_call | solution.py:152
  30.6 4.9 %all-to-all-start.1 = ((bf16[8,2,48,384]{3,2,1,0:T(8,128)(2,1)}), bf16[8,2,48,384]{3,2,1,0:T(8,128)(2,1)S(1)}, u32[]{:S(2)}, u32[]{:S(2)}) async-start(bf16[8,2,48,384]{3,2,1,0:T(8,128)(2,1)} %shard_map.86), calls=%async_computation.1 | async-start | bytes 1179648 | tf_op jit(solution)/shard_map/all_to_all | solution.py:482
  35.5 1.5 collective-permute-start.6
  36.9 5.3 %shard_map.85 = (bf16[2,256,384]{2,1,0:T(8,128)(2,1)}, bf16[2,256,384]{2,1,0:T(8,128)(2,1)}, bf16[2,768,256]{2,1,0:T(8,128)(2,1)}) custom-call(s32[4]{0:T(128)} %pad_add_fusion.pos, bf16[256,768]{1,0:T(8,128)(2,1)} %bitcast.15, bf16[256,768]{1,0:T(8,128)(2,1)} %copy-done.3, bf16[256,768]{1,0:T(8,128)(2,1)} %bitcast.17, bf16[256,768]{1,0:T(8,128)(2,1)} %copy-done.5, ...), custom_call_target="tpu_custom_call" | custom-call | tf_op jit(solution)/shard_map/pallas_call | solution.py:125
  42.2 3.6 %collective-permute-done.6.wy = bf16[2,128,384]{2,1,0:T(8,128)(2,1)S(1)} collective-permute-done((bf16[2,128,384]{2,1,0:T(8,128)(2,1)S(1)}, bf16[2,128,384]{2,1,0:T(8,128)(2,1)S(1)}, u32[]{:S(2)}, u32[]{:S(2)}) %collective-permute-start.6) | collective-permute-done | bytes 196640 | tf_op jit(solution)/shard_map/ppermute | solution.py:455
  46.7 17.6 %shard_map.87 = (bf16[2,256,384]{2,1,0:T(8,128)(2,1)}, bf16[2,256,384]{2,1,0:T(8,128)(2,1)}, f32[2,2,256,384]{3,2,1,0:T(8,128)}, f32[2,2,128,384]{3,2,1,0:T(8,12...) custom-call(s32[4]{0:T(128)} %pad_add_fusion.pos, ...), custom_call_target="tpu_custom_call" | custom-call | tf_op jit(solution)/shard_map/pallas_call | solution.py:238
  64.4 3.7 %collective-permute-start.7 = (bf16[2,256,384]{2,1,0:T(8,128)(2,1)}, bf16[2,256,384]{2,1,0:T(8,128)(2,1)S(1)}, u32[]{:S(2)}, u32[]{:S(2)}) collective-permute-start(bf16[2,256,384]{2,1,0:T(8,128)(2,1)} %get-tuple-element.77.att_own), channel_id=1, source_target_pairs={{0,2},{2,0},{1,3},{3,1},{4,6},{6,4},{5,7},{7,5},{8,10},{10,8},{9,1... | collective-permute-start | bytes 1179656 | tf_op jit(solution)/shard_map/ppermute | solution.py:455
  68.1 4.0 %all-to-all-start.2 = ((bf16[8,2,48,384]{3,2,1,0:T(8,128)(2,1)}), bf16[8,2,48,384]{3,2,1,0:T(8,128)(2,1)S(1)}, u32[]{:S(2)}, u32[]{:S(2)}) async-start(bf16[8,2,48,384]{3,2,1,0:T(8,128)(2,1)} %get-tuple-element.76), calls=%async_computation.2 | async-start | bytes 1179648 | tf_op jit(solution)/shard_map/all_to_all | solution.py:486
  72.1 0.8 copy-done.4
  72.8 5.6 %shard_map.88 = (bf16[2,2,96,384]{3,2,1,0:T(8,128)(2,1)}, bf16[2,2,96,384]{3,2,1,0:T(8,128)(2,1)}, bf16[2,2,96,384]{3,2,1,0:T(8,128)(2,1)}, bf16[2,2,96,384]{3,2,1,0:T(8,128)(2,1)}) custom-call(s32[4]{0:T(128)} %pad_add_fusion.pos, bf16[2,256,384]{2,1,0:T(8,128)(2,1)} %get-tuple-element.77.att_own, bf16[2,256,384]{2,1,0:T(8,128)(2,1)} %copy-done.4, ...), custom_call_target="tpu_custom_call" | custom-call | tf_op jit(solution)/shard_map/pallas_call | solution.py:283
  78.4 1.5 collective-permute-start.8
  79.9 1.2 collective-permute-start.9
  81.1 2.4 %collective-permute-start.10 = (bf16[2,2,96,384]{3,2,1,0:T(8,128)(2,1)}, bf16[2,2,96,384]{3,2,1,0:T(8,128)(2,1)S(1)}, u32[]{:S(2)}, u32[]{:S(2)}) collective-permute-start(bf16[2,2,96,384]{3,2,1,0:T(8,128)(2,1)} %get-tuple-element.91), channel_id=1, source_target_pairs={{0,16},{8,24},{16,0},{24,8},{1,17},{9,25},{17,1},{25,9},{2,18},{10... | collective-permute-start | bytes 884744 | tf_op jit(solution)/shard_map/ppermute | solution.py:459
  83.8 1.7 collective-permute-done.9.dwy
  85.5 1.5 collective-permute-done.8.t1
  86.9 2.8 %shard_map.89 = (bf16[8,2,16,384]{3,2,1,0:T(8,128)(2,1)}, bf16[2,64,384]{2,1,0:T(8,128)(2,1)}, bf16[2,32,384]{2,1,0:T(8,128)(2,1)}, bf16[2,32,384]{2,1,0:T(8,128)(2,1)}) custom-call(s32[4]{0:T(128)} %pad_add_fusion.pos, bf16[8,2,48,384]{3,2,1,0:T(8,128)(2,1)} %copy-done.1, f32[2,128,384]{2,1,0:T(8,128)} %get-tuple-element.84.dw, bf16[2,128,384]{2,1,0:T(8,128)(2,1)} %copy-done.15), custom_call_target="tpu_custom_call" | custom-call | tf_op jit(solution)/shard_map/pallas_call | solution.py:329
  89.8 5.5 %all-to-all-start.3 = ((bf16[8,2,16,384]{3,2,1,0:T(8,128)(2,1)}), bf16[8,2,16,384]{3,2,1,0:T(8,128)(2,1)S(1)}, u32[]{:S(2)}, u32[]{:S(2)}) async-start(bf16[8,2,16,384]{3,2,1,0:T(8,128)(2,1)} %get-tuple-element.86), calls=%async_computation.3 | async-start | bytes 393216 | tf_op jit(solution)/shard_map/all_to_all | solution.py:493
  95.2 1.2 collective-permute-start.15
  96.5 2.1 %collective-permute-done.11.t3 = bf16[2,2,96,384]{3,2,1,0:T(8,128)(2,1)S(1)} collective-permute-done((bf16[2,2,96,384]{3,2,1,0:T(8,128)(2,1)}, bf16[2,2,96,384]{3,2,1,0:T(8,128)(2,1)S(1)}, u32[]{:S(2)}, u32[]{:S(2)}) %collective-permute-start.11) | collective-permute-done | bytes 294944 | tf_op jit(solution)/shard_map/ppermute | solution.py:459
  99.3 0.9 collective-permute-start.14
  100.1 1.0 collective-permute-start.12
  101.2 2.8 %shard_map.90 = (bf16[96,384]{1,0:T(8,128)(2,1)}, bf16[96,384]{1,0:T(8,128)(2,1)}, bf16[96,384]{1,0:T(8,128)(2,1)}, bf16[96,384]{1,0:T(8,128)(2,1)}) custom-call(s32[4]{0:T(128)} %pad_add_fusion.pos, bf16[2,2,96,384]{3,2,1,0:T(8,128)(2,1)} %get-tuple-element.96.t0, bf16[2,2,96,384]{3,2,1,0:T(8,128)(2,1)} %copy-done.11, bf16[2,2,96,384]{3,2,1,0:T(8,128)(2,1)} %copy-done.12, ...), custom_call_target="tpu_custom_call" | custom-call | tf_op jit(solution)/shard_map/pallas_call | solution.py:303
  104.0 2.6 %collective-permute-start.16 = (bf16[96,384]{1,0:T(8,128)(2,1)}, bf16[96,384]{1,0:T(8,128)(2,1)S(1)}, u32[]{:S(2)}, u32[]{:S(2)}) collective-permute-start(bf16[96,384]{1,0:T(8,128)(2,1)} %get-tuple-element.110), channel_id=1, source_target_pairs={{0,1},{1,0},{4,5},{5,4},{2,3},{3,2},{6,7},{7,6},{8,9},{9,8},{12,13... | collective-permute-start | bytes 221192 | tf_op jit(solution)/shard_map/ppermute | solution.py:459
  108.1 6.2 %shard_map.91 = (bf16[2,256,1152]{2,1,0:T(8,128)(2,1)}, bf16[8,2,96,384]{3,2,1,0:T(8,128)(2,1)}) custom-call(s32[4]{0:T(128)} %pad_add_fusion.pos, bf16[8,2,16,384]{3,2,1,0:T(8,128)(2,1)} %copy-done.7, f32[2,2,256,384]{3,2,1,0:T(8,128)} %get-tuple-element.102.dkv, f32[2,2,128,384]{3,2,1,0:T(8,128)} %get-tuple-element.103.dn1, ...), custom_call_target="tpu_custom_call" | custom-call | tf_op jit(solution)/shard_map/pallas_call | solution.py:372
  115.0 5.6 %all-to-all-start.4 = ((bf16[16,96,384]{2,1,0:T(8,128)(2,1)}), bf16[16,96,384]{2,1,0:T(8,128)(2,1)S(1)}, u32[]{:S(2)}, u32[]{:S(2)}) async-start(bf16[16,96,384]{2,1,0:T(8,128)(2,1)} %bitcast.19), calls=%async_computation.4 | async-start | bytes 2359296 | tf_op jit(solution)/shard_map/all_to_all | solution.py:501
  120.6 0.9 dynamic-slice_bitcast_fusion
  121.6 5.0 %collective-permute-start.19 = (bf16[256,1152]{1,0:T(8,128)(2,1)S(1)}, bf16[256,1152]{1,0:T(8,128)(2,1)S(1)}, u32[]{:S(2)}, u32[]{:S(2)}) collective-permute-start(bf16[256,1152]{1,0:T(8,128)(2,1)S(1)} %get-tuple-element.126), channel_id=1, source_target_pairs={{0,2},{2,0},{1,3},{3,1},{4,6},{6,4},{5,7},{7,5},{8,10},{10,8},{9,1... | collective-permute-start | bytes 1769480 | tf_op jit(solution)/shard_map/ppermute | solution.py:455
  126.6 3.5 %shard_map.93 = bf16[256,768]{1,0:T(8,128)(2,1)} custom-call(s32[4]{0:T(128)} %pad_add_fusion.pos, bf16[2,256,384]{2,1,0:T(8,128)(2,1)} %get-tuple-element.77.att_own, bf16[2,256,384]{2,1,0:T(8,128)(2,1)} %copy-done.4, bf16[768,768]{1,0:T(8,128)(2,1)} %w_oth.1, bf16[768,768]{1,0:T(8,128)(2,1)} %w_oth.1), custom_call_target="tpu_custom_call" | custom-call | tf_op jit(solution)/shard_map/pallas_call | solution.py:257
  130.0 0.8 copy-done.10
  130.8 5.1 %shard_map.92 = bf16[256,768]{1,0:T(8,128)(2,1)} custom-call(s32[4]{0:T(128)} %pad_add_fusion.pos, bf16[256,1152]{1,0:T(8,128)(2,1)} %get-tuple-element.127.pg_own, bf16[256,1152]{1,0:T(8,128)(2,1)} %copy-done.10, bf16[768,2304]{1,0:T(8,128)(2,1)} %rest_5_.1, bf16[768,2304]{1,0:T(8,128)(2,1)} %rest_5_.1, bf16[768,2304]{1,0:T(8,128)(2,1)} %rest_5_.1, ...), custom_call_target="tpu_custom_call" | custom-call | tf_op jit(solution)/shard_map/pallas_call | solution.py:395
  136.0 1.0 copy-done
  137.0 3.2 %shard_map.94 = bf16[8,2,16,384]{3,2,1,0:T(8,128)(2,1)} custom-call(s32[4]{0:T(128)} %pad_add_fusion.pos, bf16[96,384]{1,0:T(8,128)(2,1)} %get-tuple-element.117.f0, bf16[96,384]{1,0:T(8,128)(2,1)} %copy-done.19, bf16[96,384]{1,0:T(8,128)(2,1)} %copy-done.20, bf16[96,384]{1,0:T(8,128)(2,1)} %copy-done.21, bf16[16,96,384]{2,1,0:T(8,128)(2,1)} %copy-done), custom_call_target="tpu_custom_call" | custom-call | tf_op jit(solution)/shard_map/pallas_call | solution.py:424
  140.2 15.5 %all_to_all.30 = bf16[8,2,16,384]{3,2,1,0:T(8,128)(2,1)S(1)} all-to-all(bf16[8,2,16,384]{3,2,1,0:T(8,128)(2,1)} %shard_map.94), channel_id=1, replica_groups=mesh['z'=8,'x'=4,'y'=2,'c'=2,'dp'=2] {'z'}, dimensions={0} | all-to-all | bytes 393216 | tf_op jit(solution)/shard_map/all_to_all | solution.py:507
  155.8 3.3 %collective-permute-start.20 = (bf16[16,384]{1,0:T(8,128)(2,1)S(1)}, bf16[16,384]{1,0:T(8,128)(2,1)S(1)}, u32[]{:S(2)}, u32[]{:S(2)}) collective-permute-start(bf16[16,384]{1,0:T(8,128)(2,1)S(1)} %get-tuple-element.125.own), channel_id=1, source_target_pairs={{0,1},{1,0},{2,3},{3,2},{4,5},{5,4},{6,7},{7,6},{8,9},{9,8},{10,11... | collective-permute-start | bytes 36872 | tf_op jit(solution)/shard_map/ppermute | solution.py:459
  159.1 4.2 %collective-permute-start.21 = (bf16[16,384]{1,0:T(8,128)(2,1)S(1)}, bf16[16,384]{1,0:T(8,128)(2,1)S(1)}, u32[]{:S(2)}, u32[]{:S(2)}) collective-permute-start(bf16[16,384]{1,0:T(8,128)(2,1)S(1)} %get-tuple-element.124), channel_id=1, source_target_pairs={{0,2},{1,3},{2,0},{3,1},{4,6},{5,7},{6,4},{7,5},{8,10},{9,11},{10,... | collective-permute-start | bytes 36872 | tf_op jit(solution)/shard_map/ppermute | solution.py:459
  163.3 2.1 %collective-permute-start.22 = (bf16[16,384]{1,0:T(8,128)(2,1)S(1)}, bf16[16,384]{1,0:T(8,128)(2,1)S(1)}, u32[]{:S(2)}, u32[]{:S(2)}) collective-permute-start(bf16[16,384]{1,0:T(8,128)(2,1)S(1)} %get-tuple-element.124), channel_id=1, source_target_pairs={{0,3},{1,2},{2,1},{3,0},{4,7},{5,6},{6,5},{7,4},{8,11},{9,10},{10,... | collective-permute-start | bytes 36872 | tf_op jit(solution)/shard_map/ppermute | solution.py:459
  165.4 2.5 %collective-permute-done.22.from_both = bf16[16,384]{1,0:T(8,128)(2,1)S(1)} collective-permute-done((bf16[16,384]{1,0:T(8,128)(2,1)S(1)}, bf16[16,384]{1,0:T(8,128)(2,1)S(1)}, u32[]{:S(2)}, u32[]{:S(2)}) %collective-permute-start.22) | collective-permute-done | bytes 12320 | tf_op jit(solution)/shard_map/ppermute | solution.py:459
  168.5 2.1 %shard_map.95 = (f32[6,2304]{1,0:T(8,128)}, f32[6,768]{1,0:T(8,128)}) custom-call(s32[4]{0:T(128)} %pad_add_fusion.pos, bf16[16,384]{1,0:T(8,128)(2,1)} %copy-done.24, bf16[16,384]{1,0:T(8,128)(2,1)} %copy-done.25, bf16[16,384]{1,0:T(8,128)(2,1)} %copy-done.26, bf16[16,384]{1,0:T(8,128)(2,1)} %copy-done.27), custom_call_target="tpu_custom_call" | custom-call | tf_op jit(solution)/shard_map/pallas_call | solution.py:445
  (85 shorter events, 6.3 us)
Async XLA Ops:
  0.6 4.9 %collective-permute-start = (bf16[256,768]{1,0:T(8,128)(2,1)}, bf16[256,768]{1,0:T(8,128)(2,1)S(1)}, u32[]{:S(2)}, u32[]{:S(2)}) collective-permute-start(bf16[256,768]{1,0:T(8,128)(2,1)} %bitcast.13), channel_id=1, source_target_pairs={{0,2},{2,0},{1,3},{3,1},{4,6},{6,4},{5,7},{7,5},{8,10},{10,8},{9,1... | collective-permute-start | bytes 1179656 | tf_op jit(solution)/shard_map/ppermute | solution.py:455
  4.0 23.1 %collective-permute-start.5 = (bf16[256,768]{1,0:T(8,128)(2,1)}, bf16[256,768]{1,0:T(8,128)(2,1)S(1)}, u32[]{:S(2)}, u32[]{:S(2)}) collective-permute-start(bf16[256,768]{1,0:T(8,128)(2,1)} %bitcast.16), channel_id=1, source_target_pairs={{0,2},{2,0},{1,3},{3,1},{4,6},{6,4},{5,7},{7,5},{8,10},{10,8},{9,1... | collective-permute-start | bytes 1179656 | tf_op jit(solution)/shard_map/ppermute | solution.py:455
  5.5 0.7 copy-start.3
  11.3 15.9 %all-to-all-start = ((bf16[8,2,16,384]{3,2,1,0:T(8,128)(2,1)}), bf16[8,2,16,384]{3,2,1,0:T(8,128)(2,1)S(1)}, u32[]{:S(2)}, u32[]{:S(2)}) async-start(bf16[8,2,16,384]{3,2,1,0:T(8,128)(2,1)} %get-tuple-element.64), calls=%async_computation | async-start | bytes 393216 | tf_op jit(solution)/shard_map/all_to_all | solution.py:479
  17.7 9.4 %collective-permute-start.2 = (bf16[2,64,384]{2,1,0:T(8,128)(2,1)}, bf16[2,64,384]{2,1,0:T(8,128)(2,1)S(1)}, u32[]{:S(2)}, u32[]{:S(2)}) collective-permute-start(bf16[2,64,384]{2,1,0:T(8,128)(2,1)} %get-tuple-element.66), channel_id=1, source_target_pairs={{0,8},{8,0},{16,24},{24,16},{1,9},{9,1},{17,25},{25,17},{2,10},{10... | collective-permute-start | bytes 294920 | tf_op jit(solution)/shard_map/ppermute | solution.py:459
  18.9 8.2 %collective-permute-start.1 = (bf16[2,128,384]{2,1,0:T(8,128)(2,1)}, bf16[2,128,384]{2,1,0:T(8,128)(2,1)S(1)}, u32[]{:S(2)}, u32[]{:S(2)}) collective-permute-start(bf16[2,128,384]{2,1,0:T(8,128)(2,1)} %get-tuple-element.65), channel_id=1, source_target_pairs={{0,4},{4,0},{1,5},{5,1},{2,6},{6,2},{3,7},{7,3},{8,12},{12,8},{9,1... | collective-permute-start | bytes 589832 | tf_op jit(solution)/shard_map/ppermute | solution.py:455
  20.2 5.3 %collective-permute-start.3 = (bf16[2,32,384]{2,1,0:T(8,128)(2,1)}, bf16[2,32,384]{2,1,0:T(8,128)(2,1)S(1)}, u32[]{:S(2)}, u32[]{:S(2)}) collective-permute-start(bf16[2,32,384]{2,1,0:T(8,128)(2,1)} %get-tuple-element.67), channel_id=1, source_target_pairs={{0,16},{8,24},{16,0},{24,8},{1,17},{9,25},{17,1},{25,9},{2,18},{10... | collective-permute-start | bytes 147464 | tf_op jit(solution)/shard_map/ppermute | solution.py:459
  22.7 4.4 %collective-permute-start.4 = (bf16[2,32,384]{2,1,0:T(8,128)(2,1)}, bf16[2,32,384]{2,1,0:T(8,128)(2,1)S(1)}, u32[]{:S(2)}, u32[]{:S(2)}) collective-permute-start(bf16[2,32,384]{2,1,0:T(8,128)(2,1)} %get-tuple-element.67), channel_id=1, source_target_pairs={{0,24},{8,16},{16,8},{24,0},{1,25},{9,17},{17,9},{25,1},{2,26},{10... | collective-permute-start | bytes 147464 | tf_op jit(solution)/shard_map/ppermute | solution.py:459
  27.1 15.1 %copy-start.9 = (bf16[2,128,384]{2,1,0:T(8,128)(2,1)}, bf16[2,128,384]{2,1,0:T(8,128)(2,1)S(1)}, u32[]{:S(2)}) copy-start(bf16[2,128,384]{2,1,0:T(8,128)(2,1)S(1)} %pad_maximum_fusion.wr) | copy-start | bytes 589828
  27.1 9.8 %copy-start.5 = (bf16[256,768]{1,0:T(8,128)(2,1)}, bf16[256,768]{1,0:T(8,128)(2,1)S(1)}, u32[]{:S(2)}) copy-start(bf16[256,768]{1,0:T(8,128)(2,1)S(1)} %collective-permute-done.5.ct_oth) | copy-start | bytes 1179652
  27.1 15.1 %copy-start.16 = (bf16[2,128,384]{2,1,0:T(8,128)(2,1)}, bf16[2,128,384]{2,1,0:T(8,128)(2,1)S(1)}, u32[]{:S(2)}) copy-start(bf16[2,128,384]{2,1,0:T(8,128)(2,1)S(1)} %collective-permute-done.1.yr) | copy-start | bytes 589828
  27.2 0.8 copy-start.8
  30.6 15.3 %all-to-all-start.1 = ((bf16[8,2,48,384]{3,2,1,0:T(8,128)(2,1)}), bf16[8,2,48,384]{3,2,1,0:T(8,128)(2,1)S(1)}, u32[]{:S(2)}, u32[]{:S(2)}) async-start(bf16[8,2,48,384]{3,2,1,0:T(8,128)(2,1)} %shard_map.86), calls=%async_computation.1 | async-start | bytes 1179648 | tf_op jit(solution)/shard_map/all_to_all | solution.py:482
  35.5 10.4 %collective-permute-start.6 = (bf16[2,128,384]{2,1,0:T(8,128)(2,1)S(1)}, bf16[2,128,384]{2,1,0:T(8,128)(2,1)S(1)}, u32[]{:S(2)}, u32[]{:S(2)}) collective-permute-start(bf16[2,128,384]{2,1,0:T(8,128)(2,1)S(1)} %pad_maximum_fusion.wr), channel_id=1, source_target_pairs={{0,4},{4,0},{1,5},{5,1},{2,6},{6,2},{3,7},{7,3},{8,12},{12,8},{9,1... | collective-permute-start | bytes 589832 | tf_op jit(solution)/shard_map/ppermute | solution.py:455
  45.9 0.9 copy-start.2
  64.4 7.7 %collective-permute-start.7 = (bf16[2,256,384]{2,1,0:T(8,128)(2,1)}, bf16[2,256,384]{2,1,0:T(8,128)(2,1)S(1)}, u32[]{:S(2)}, u32[]{:S(2)}) collective-permute-start(bf16[2,256,384]{2,1,0:T(8,128)(2,1)} %get-tuple-element.77.att_own), channel_id=1, source_target_pairs={{0,2},{2,0},{1,3},{3,1},{4,6},{6,4},{5,7},{7,5},{8,10},{10,8},{9,1... | collective-permute-start | bytes 1179656 | tf_op jit(solution)/shard_map/ppermute | solution.py:455
  68.1 17.4 %all-to-all-start.2 = ((bf16[8,2,48,384]{3,2,1,0:T(8,128)(2,1)}), bf16[8,2,48,384]{3,2,1,0:T(8,128)(2,1)S(1)}, u32[]{:S(2)}, u32[]{:S(2)}) async-start(bf16[8,2,48,384]{3,2,1,0:T(8,128)(2,1)} %get-tuple-element.76), calls=%async_computation.2 | async-start | bytes 1179648 | tf_op jit(solution)/shard_map/all_to_all | solution.py:486
  72.1 0.8 copy-start.4
  72.8 7.1 %copy-start.29 = (bf16[2,128,384]{2,1,0:T(8,128)(2,1)S(1)}, bf16[2,128,384]{2,1,0:T(8,128)(2,1)}, u32[]{:S(2)}) copy-start(bf16[2,128,384]{2,1,0:T(8,128)(2,1)} %get-tuple-element.82) | copy-start | bytes 589828
  78.4 16.8 %copy-start.28 = (bf16[2,128,384]{2,1,0:T(8,128)(2,1)S(1)}, bf16[2,128,384]{2,1,0:T(8,128)(2,1)}, u32[]{:S(2)}) copy-start(bf16[2,128,384]{2,1,0:T(8,128)(2,1)} %get-tuple-element.104) | copy-start | bytes 589828
  78.4 8.5 %collective-permute-start.8 = (bf16[2,2,96,384]{3,2,1,0:T(8,128)(2,1)}, bf16[2,2,96,384]{3,2,1,0:T(8,128)(2,1)S(1)}, u32[]{:S(2)}, u32[]{:S(2)}) collective-permute-start(bf16[2,2,96,384]{3,2,1,0:T(8,128)(2,1)} %get-tuple-element.81), channel_id=1, source_target_pairs={{0,8},{8,0},{16,24},{24,16},{1,9},{9,1},{17,25},{25,17},{2,10},{10... | collective-permute-start | bytes 884744 | tf_op jit(solution)/shard_map/ppermute | solution.py:459
  79.9 5.6 %collective-permute-start.9 = (bf16[2,128,384]{2,1,0:T(8,128)(2,1)S(1)}, bf16[2,128,384]{2,1,0:T(8,128)(2,1)S(1)}, u32[]{:S(2)}, u32[]{:S(2)}) collective-permute-start(bf16[2,128,384]{2,1,0:T(8,128)(2,1)S(1)} %copy-done.29), channel_id=1, source_target_pairs={{0,4},{4,0},{1,5},{5,1},{2,6},{6,2},{3,7},{7,3},{8,12},{12,8},{9,1... | collective-permute-start | bytes 589832 | tf_op jit(solution)/shard_map/ppermute | solution.py:455
  81.1 15.4 %collective-permute-start.10 = (bf16[2,2,96,384]{3,2,1,0:T(8,128)(2,1)}, bf16[2,2,96,384]{3,2,1,0:T(8,128)(2,1)S(1)}, u32[]{:S(2)}, u32[]{:S(2)}) collective-permute-start(bf16[2,2,96,384]{3,2,1,0:T(8,128)(2,1)} %get-tuple-element.91), channel_id=1, source_target_pairs={{0,16},{8,24},{16,0},{24,8},{1,17},{9,25},{17,1},{25,9},{2,18},{10... | collective-permute-start | bytes 884744 | tf_op jit(solution)/shard_map/ppermute | solution.py:459
  83.5 15.1 %collective-permute-start.11 = (bf16[2,2,96,384]{3,2,1,0:T(8,128)(2,1)}, bf16[2,2,96,384]{3,2,1,0:T(8,128)(2,1)S(1)}, u32[]{:S(2)}, u32[]{:S(2)}) collective-permute-start(bf16[2,2,96,384]{3,2,1,0:T(8,128)(2,1)} %get-tuple-element.92), channel_id=1, source_target_pairs={{0,24},{8,16},{16,8},{24,0},{1,25},{9,17},{17,9},{25,1},{2,26},{10... | collective-permute-start | bytes 884744 | tf_op jit(solution)/shard_map/ppermute | solution.py:459
  85.4 1.5 copy-start.15
  85.5 1.5 copy-start.1
  86.9 14.2 %copy-start.11 = (bf16[2,2,96,384]{3,2,1,0:T(8,128)(2,1)}, bf16[2,2,96,384]{3,2,1,0:T(8,128)(2,1)S(1)}, u32[]{:S(2)}) copy-start(bf16[2,2,96,384]{3,2,1,0:T(8,128)(2,1)S(1)} %collective-permute-done.8.t1) | copy-start | bytes 884740
  89.8 17.5 %all-to-all-start.3 = ((bf16[8,2,16,384]{3,2,1,0:T(8,128)(2,1)}), bf16[8,2,16,384]{3,2,1,0:T(8,128)(2,1)S(1)}, u32[]{:S(2)}, u32[]{:S(2)}) async-start(bf16[8,2,16,384]{3,2,1,0:T(8,128)(2,1)} %get-tuple-element.86), calls=%async_computation.3 | async-start | bytes 393216 | tf_op jit(solution)/shard_map/all_to_all | solution.py:493
  95.2 12.1 %collective-permute-start.15 = (bf16[2,128,384]{2,1,0:T(8,128)(2,1)S(1)}, bf16[2,128,384]{2,1,0:T(8,128)(2,1)S(1)}, u32[]{:S(2)}, u32[]{:S(2)}) collective-permute-start(bf16[2,128,384]{2,1,0:T(8,128)(2,1)S(1)} %copy-done.28), channel_id=1, source_target_pairs={{0,4},{4,0},{1,5},{5,1},{2,6},{6,2},{3,7},{7,3},{8,12},{12,8},{9,1... | collective-permute-start | bytes 589832 | tf_op jit(solution)/shard_map/ppermute | solution.py:455
  96.5 4.7 %copy-start.12 = (bf16[2,2,96,384]{3,2,1,0:T(8,128)(2,1)}, bf16[2,2,96,384]{3,2,1,0:T(8,128)(2,1)S(1)}, u32[]{:S(2)}) copy-start(bf16[2,2,96,384]{3,2,1,0:T(8,128)(2,1)S(1)} %collective-permute-done.10.t2) | copy-start | bytes 884740
  98.5 2.7 %copy-start.13 = (bf16[2,2,96,384]{3,2,1,0:T(8,128)(2,1)}, bf16[2,2,96,384]{3,2,1,0:T(8,128)(2,1)S(1)}, u32[]{:S(2)}) copy-start(bf16[2,2,96,384]{3,2,1,0:T(8,128)(2,1)S(1)} %collective-permute-done.11.t3) | copy-start | bytes 884740
  98.5 8.1 %collective-permute-start.13 = (bf16[2,32,384]{2,1,0:T(8,128)(2,1)}, bf16[2,32,384]{2,1,0:T(8,128)(2,1)S(1)}, u32[]{:S(2)}, u32[]{:S(2)}) collective-permute-start(bf16[2,32,384]{2,1,0:T(8,128)(2,1)} %get-tuple-element.94), channel_id=1, source_target_pairs={{0,16},{8,24},{16,0},{24,8},{1,17},{9,25},{17,1},{25,9},{2,18},{10... | collective-permute-start | bytes 147464 | tf_op jit(solution)/shard_map/ppermute | solution.py:459
  99.3 7.4 %collective-permute-start.14 = (bf16[2,32,384]{2,1,0:T(8,128)(2,1)}, bf16[2,32,384]{2,1,0:T(8,128)(2,1)S(1)}, u32[]{:S(2)}, u32[]{:S(2)}) collective-permute-start(bf16[2,32,384]{2,1,0:T(8,128)(2,1)} %get-tuple-element.95), channel_id=1, source_target_pairs={{0,24},{8,16},{16,8},{24,0},{1,25},{9,17},{17,9},{25,1},{2,26},{10... | collective-permute-start | bytes 147464 | tf_op jit(solution)/shard_map/ppermute | solution.py:459
  100.1 7.2 %collective-permute-start.12 = (bf16[2,64,384]{2,1,0:T(8,128)(2,1)}, bf16[2,64,384]{2,1,0:T(8,128)(2,1)S(1)}, u32[]{:S(2)}, u32[]{:S(2)}) collective-permute-start(bf16[2,64,384]{2,1,0:T(8,128)(2,1)} %get-tuple-element.93), channel_id=1, source_target_pairs={{0,8},{8,0},{16,24},{24,16},{1,9},{9,1},{17,25},{25,17},{2,10},{10... | collective-permute-start | bytes 294920 | tf_op jit(solution)/shard_map/ppermute | solution.py:459
  104.0 10.2 %collective-permute-start.16 = (bf16[96,384]{1,0:T(8,128)(2,1)}, bf16[96,384]{1,0:T(8,128)(2,1)S(1)}, u32[]{:S(2)}, u32[]{:S(2)}) collective-permute-start(bf16[96,384]{1,0:T(8,128)(2,1)} %get-tuple-element.110), channel_id=1, source_target_pairs={{0,1},{1,0},{4,5},{5,4},{2,3},{3,2},{6,7},{7,6},{8,9},{9,8},{12,13... | collective-permute-start | bytes 221192 | tf_op jit(solution)/shard_map/ppermute | solution.py:459
  106.7 7.6 %collective-permute-start.17 = (bf16[96,384]{1,0:T(8,128)(2,1)}, bf16[96,384]{1,0:T(8,128)(2,1)S(1)}, u32[]{:S(2)}, u32[]{:S(2)}) collective-permute-start(bf16[96,384]{1,0:T(8,128)(2,1)} %get-tuple-element.111), channel_id=1, source_target_pairs={{0,4},{1,5},{4,0},{5,1},{2,6},{3,7},{6,2},{7,3},{8,12},{9,13},{12,... | collective-permute-start | bytes 221192 | tf_op jit(solution)/shard_map/ppermute | solution.py:459
  106.7 7.6 %collective-permute-start.18 = (bf16[96,384]{1,0:T(8,128)(2,1)}, bf16[96,384]{1,0:T(8,128)(2,1)S(1)}, u32[]{:S(2)}, u32[]{:S(2)}) collective-permute-start(bf16[96,384]{1,0:T(8,128)(2,1)} %get-tuple-element.112), channel_id=1, source_target_pairs={{0,5},{1,4},{4,1},{5,0},{2,7},{3,6},{6,3},{7,2},{8,13},{9,12},{12,... | collective-permute-start | bytes 221192 | tf_op jit(solution)/shard_map/ppermute | solution.py:459
  114.3 6.3 %copy-start.6 = (bf16[2,256,1152]{2,1,0:T(8,128)(2,1)S(1)}, bf16[2,256,1152]{2,1,0:T(8,128)(2,1)}, u32[]{:S(2)}) copy-start(bf16[2,256,1152]{2,1,0:T(8,128)(2,1)} %get-tuple-element.114) | copy-start | bytes 3538948
  115.0 21.0 %all-to-all-start.4 = ((bf16[16,96,384]{2,1,0:T(8,128)(2,1)}), bf16[16,96,384]{2,1,0:T(8,128)(2,1)S(1)}, u32[]{:S(2)}, u32[]{:S(2)}) async-start(bf16[16,96,384]{2,1,0:T(8,128)(2,1)} %bitcast.19), calls=%async_computation.4 | async-start | bytes 2359296 | tf_op jit(solution)/shard_map/all_to_all | solution.py:501
  121.6 8.5 %collective-permute-start.19 = (bf16[256,1152]{1,0:T(8,128)(2,1)S(1)}, bf16[256,1152]{1,0:T(8,128)(2,1)S(1)}, u32[]{:S(2)}, u32[]{:S(2)}) collective-permute-start(bf16[256,1152]{1,0:T(8,128)(2,1)S(1)} %get-tuple-element.126), channel_id=1, source_target_pairs={{0,2},{2,0},{1,3},{3,1},{4,6},{6,4},{5,7},{7,5},{8,10},{10,8},{9,1... | collective-permute-start | bytes 1769480 | tf_op jit(solution)/shard_map/ppermute | solution.py:455
  130.0 0.8 copy-start.10
  136.0 1.1 copy-start
  155.8 12.1 %copy-start.24 = (bf16[16,384]{1,0:T(8,128)(2,1)}, bf16[16,384]{1,0:T(8,128)(2,1)S(1)}, u32[]{:S(2)}) copy-start(bf16[16,384]{1,0:T(8,128)(2,1)S(1)} %get-tuple-element.125.own) | copy-start | bytes 36868
  155.8 9.6 %collective-permute-start.20 = (bf16[16,384]{1,0:T(8,128)(2,1)S(1)}, bf16[16,384]{1,0:T(8,128)(2,1)S(1)}, u32[]{:S(2)}, u32[]{:S(2)}) collective-permute-start(bf16[16,384]{1,0:T(8,128)(2,1)S(1)} %get-tuple-element.125.own), channel_id=1, source_target_pairs={{0,1},{1,0},{2,3},{3,2},{4,5},{5,4},{6,7},{7,6},{8,9},{9,8},{10,11... | collective-permute-start | bytes 36872 | tf_op jit(solution)/shard_map/ppermute | solution.py:459
  159.1 6.3 %collective-permute-start.21 = (bf16[16,384]{1,0:T(8,128)(2,1)S(1)}, bf16[16,384]{1,0:T(8,128)(2,1)S(1)}, u32[]{:S(2)}, u32[]{:S(2)}) collective-permute-start(bf16[16,384]{1,0:T(8,128)(2,1)S(1)} %get-tuple-element.124), channel_id=1, source_target_pairs={{0,2},{1,3},{2,0},{3,1},{4,6},{5,7},{6,4},{7,5},{8,10},{9,11},{10,... | collective-permute-start | bytes 36872 | tf_op jit(solution)/shard_map/ppermute | solution.py:459
  163.3 4.6 %collective-permute-start.22 = (bf16[16,384]{1,0:T(8,128)(2,1)S(1)}, bf16[16,384]{1,0:T(8,128)(2,1)S(1)}, u32[]{:S(2)}, u32[]{:S(2)}) collective-permute-start(bf16[16,384]{1,0:T(8,128)(2,1)S(1)} %get-tuple-element.124), channel_id=1, source_target_pairs={{0,3},{1,2},{2,1},{3,0},{4,7},{5,6},{6,5},{7,4},{8,11},{9,10},{10,... | collective-permute-start | bytes 36872 | tf_op jit(solution)/shard_map/ppermute | solution.py:459
  165.4 2.5 %copy-start.25 = (bf16[16,384]{1,0:T(8,128)(2,1)}, bf16[16,384]{1,0:T(8,128)(2,1)S(1)}, u32[]{:S(2)}) copy-start(bf16[16,384]{1,0:T(8,128)(2,1)S(1)} %collective-permute-done.20.from_dp) | copy-start | bytes 36868
  165.4 2.5 %copy-start.26 = (bf16[16,384]{1,0:T(8,128)(2,1)}, bf16[16,384]{1,0:T(8,128)(2,1)S(1)}, u32[]{:S(2)}) copy-start(bf16[16,384]{1,0:T(8,128)(2,1)S(1)} %collective-permute-done.21.from_core) | copy-start | bytes 36868
  (10 other events, 6.6 us)

commit v10 on v9

--- a/solution.py
+++ b/solution.py
@@ -479,7 +479,8 @@
     zr = lax.all_to_all(zs, "z", 0, 0)
     zr, yr, wr, ct_oth = lax.optimization_barrier((zr, yr, wr, ct_oth))
     wy = swap(wr, "y")
-    xr = lax.all_to_all(plane_slots(pos, zr), ("x", "y"), 0, 0)
+    xs, wy = lax.optimization_barrier((plane_slots(pos, zr), wy))
+    xr = lax.all_to_all(xs, ("x", "y"), 0, 0)
     q, ag, xt = project(pos, x_own, x_oth, ct_own, ct_oth, w_qkv, w_out, perm)
     att, dq, dkv, dn1, dy, dwy, dw, dx = attention(pos, q, ag, kv, n1, yr, wr, wy, xr)
 
@@ -493,18 +494,18 @@
     dz_r = lax.all_to_all(dz, "z", 0, 0)
     g3, g4_a, g4_b, firsts = lax.optimization_barrier((g3, g4_a, g4_b, firsts))
     g3, g4_a, g4_b = along(g3, "x", 1), along(g4_a, "x", 2), along(g4_b, "x", 3)
+    pg, terms = leaf_grads(pos, dz_r, dkv, dn1, swap(dy, "y"), g3, g4_a, g4_b, dq, xt)
+    terms, first, firsts = lax.optimization_barrier((terms, first, firsts))
     firsts = x_sum(pos, first, *firsts)
-    dz_r, g3, g4_a, g4_b, first = lax.optimization_barrier((dz_r, g3, g4_a, g4_b, firsts[0]))
-    firsts = [first] + [along(firsts[far], ("y", "dp"), far) for far in (1, 2, 3)]
-    pg, terms = leaf_grads(pos, dz_r, dkv, dn1, swap(dy, "y"), g3, g4_a, g4_b, dq, xt)
-    terms, firsts = lax.optimization_barrier((terms, firsts))
+    firsts = list(firsts[:1]) + [along(firsts[far], ("y", "dp"), far) for far in (1, 2, 3)]
     terms = lax.all_to_all(terms.reshape(16, 96, H), ("x", "y", "dp"), 0, 0)
     pg_own = lax.dynamic_index_in_dim(pg, c, 0, keepdims=False)
     pg_oth = swap(lax.dynamic_index_in_dim(pg, 1 - c, 0, keepdims=False), "c")
     input_grad = input_side(pos, pg_own, pg_oth, w_qkv)
-    layer_out = output_side(pos, att, att_oth, w_out)
-    terms, input_grad, layer_out = lax.optimization_barrier((terms, input_grad, layer_out))
-    terms = lax.all_to_all(middle_sum(pos, firsts, terms), "z", 0, 0)
+    terms, input_grad = lax.optimization_barrier((terms, input_grad))
+    terms, att, att_oth = lax.optimization_barrier((middle_sum(pos, firsts, terms), att, att_oth))
+    terms = lax.all_to_all(terms, "z", 0, 0)
+    terms, layer_out = lax.optimization_barrier((terms, output_side(pos, att, att_oth, w_out)))
     own, oth = (jnp.sum(terms[:, core].astype(F32), axis=0).astype(BF16) for core in range(2))
     pair = ("c", "dp")
     qkv_grad, out_grad = last_rows(pos, own, along(own, pair, 1), along(oth, pair, 2), along(oth, pair, 3))

time: 172 us -> 171 us (level)
  blocking collectives: 15.5 us -> 0 us
  waiting for transfers between devices: 16.5 us -> 29.8 us
  starting transfers between devices: 67.3 us -> 70.7 us
  local copies, waits for them, and re-layouts: 7.97 us -> 6.11 us
    all_to_all x1 -> x0, blocking collectives: 15.5 us -> none  [shards(): terms = lax.all_to_all(middle_sum(pos, firsts, terms), 'z', 0, 0)]
    ppermute x15, waiting for transfers between devices: 10.3 us -> 18.8 us  [along(): return lax.ppermute(value, axes, [(i, i ^ far) for i in range(count)])]
    all_to_all x1 -> x2, waiting for transfers between devices: 0.01 us -> 7.4 us  [the longest x1 5.12 us: shards(): terms = lax.all_to_all(terms, 'z', 0, 0)]
    all_to_all x1 -> x2, starting transfers between devices: 4.91 us -> 10.4 us  [the longest x1 5.51 us: shards(): terms = lax.all_to_all(terms, 'z', 0, 0)]
    ppermute x8, waiting for transfers between devices: 6.21 us -> 3.54 us  [swap(): return lax.ppermute(value, axis, [(0, 1), (1, 0)])]
    unnamed x60, local copies, waits for them, and re-layouts: 7.04 us -> 5.17 us
  transfers between devices with their start and end apart: 28 -> 29, of which waited for: 8 -> 15; matrix products, arithmetic and copies ran while one was open for 1% -> 1% of each run, Pallas kernels for 21% -> 19%
where the time goes in v10:
time: 171 us; the launch traced here: 170 us
  starting transfers between devices  70.7 us (41%)
  Pallas kernels  61.8 us (36%)
  waiting for transfers between devices  29.8 us (17%)
  local copies, waits for them, and re-layouts  6.11 us (4%)
    ppermute x15, starting transfers between devices, along(): return lax.ppermute(value, axes, [(i, i ^ far) for i in range(count)])  21.9 us
    ppermute x15, waiting for transfers between devices, along(): return lax.ppermute(value, axes, [(i, i ^ far) for i in range(count)])  18.8 us
    pallas_call x1, Pallas kernels, attention(): call(attention_body, (H // 128,), [cut(2, TOK), cut(2, TOK), cut(2, 2, TO...  17.6 us
    ppermute x8, starting transfers between devices, swap(): return lax.ppermute(value, axis, [(0, 1), (1, 0)])  16.8 us
    all_to_all x1, starting transfers between devices, shards(): zr = lax.all_to_all(zs, 'z', 0, 0)  6.45 us
    pallas_call x1, Pallas kernels, leaf_grads(): call(leaf_body, (1,), [whole(ZN, 2, 16, H), whole(2, 2, TOK, H), whole(2,...  6.2 us
    all_to_all x1, starting transfers between devices, shards(): terms = lax.all_to_all(terms.reshape(16, 96, H), ('x', 'y', 'dp'), 0, 0)  5.81 us
    all_to_all x1, starting transfers between devices, shards(): dz_r = lax.all_to_all(dz, 'z', 0, 0)  5.79 us
  transfers between devices with their start and end apart: 29, of which 15 were waited for; matrix products, arithmetic and copies ran while one was open for 1% of the time, Pallas kernels for 19%

profile of v10, /device:TPU:1, one launch (start us, length us, event | category | flops | bytes accessed | tf_op | source)
XLA Modules:
  0.0 169.9 jit_solution(5070436605455290487)
XLA Ops:
  0.6 3.3 %collective-permute-start = (bf16[256,768]{1,0:T(8,128)(2,1)}, bf16[256,768]{1,0:T(8,128)(2,1)S(1)}, u32[]{:S(2)}, u32[]{:S(2)}) collective-permute-start(bf16[256,768]{1,0:T(8,128)(2,1)} %bitcast.13), channel_id=1, source_target_pairs={{0,2},{2,0},{1,3},{3,1},{4,6},{6,4},{5,7},{7,5},{8,10},{10,8},{9,1... | collective-permute-start | bytes 1179656 | tf_op jit(solution)/shard_map/ppermute | solution.py:455
  6.3 5.0 %shard_map.84 = (bf16[2,2,256,384]{3,2,1,0:T(8,128)(2,1)}, bf16[2,2,128,384]{3,2,1,0:T(8,128)(2,1)}, bf16[2,128,384]{2,1,0:T(8,128)(2,1)}, bf16[2,64,384]{2,1,0:...) custom-call(s32[4]{0:T(128)} %pad_add_fusion.pos, bf16[256,768]{1,0:T(8,128)(2,1)} %bitcast.14, ...), custom_call_target="tpu_custom_call" | custom-call | tf_op jit(solution)/shard_map/pallas_call | solution.py:107
  11.3 6.5 %all-to-all-start = ((bf16[8,2,16,384]{3,2,1,0:T(8,128)(2,1)}), bf16[8,2,16,384]{3,2,1,0:T(8,128)(2,1)S(1)}, u32[]{:S(2)}, u32[]{:S(2)}) async-start(bf16[8,2,16,384]{3,2,1,0:T(8,128)(2,1)} %get-tuple-element.65), calls=%async_computation | async-start | bytes 393216 | tf_op jit(solution)/shard_map/all_to_all | solution.py:479
  17.7 1.2 collective-permute-start.2
  18.9 1.3 collective-permute-start.1
  20.2 2.5 %collective-permute-start.3 = (bf16[2,32,384]{2,1,0:T(8,128)(2,1)}, bf16[2,32,384]{2,1,0:T(8,128)(2,1)S(1)}, u32[]{:S(2)}, u32[]{:S(2)}) collective-permute-start(bf16[2,32,384]{2,1,0:T(8,128)(2,1)} %get-tuple-element.68), channel_id=1, source_target_pairs={{0,16},{8,24},{16,0},{24,8},{1,17},{9,25},{17,1},{25,9},{2,18},{10... | collective-permute-start | bytes 147464 | tf_op jit(solution)/shard_map/ppermute | solution.py:459
  22.9 2.7 %collective-permute-done.3 = bf16[2,32,384]{2,1,0:T(8,128)(2,1)S(1)} collective-permute-done((bf16[2,32,384]{2,1,0:T(8,128)(2,1)}, bf16[2,32,384]{2,1,0:T(8,128)(2,1)S(1)}, u32[]{:S(2)}, u32[]{:S(2)}) %collective-permute-start.3) | collective-permute-done | bytes 49184 | tf_op jit(solution)/shard_map/ppermute | solution.py:459
  25.5 1.6 collective-permute-done.4
  27.2 1.3 collective-permute-start.6
  28.4 2.6 %shard_map.86 = bf16[8,2,48,384]{3,2,1,0:T(8,128)(2,1)} custom-call(s32[4]{0:T(128)} %pad_add_fusion.pos, bf16[8,2,16,384]{3,2,1,0:T(8,128)(2,1)} %copy-done.8), custom_call_target="tpu_custom_call" | custom-call | tf_op jit(solution)/shard_map/pallas_call | solution.py:152
  31.8 4.9 %all-to-all-start.1 = ((bf16[8,2,48,384]{3,2,1,0:T(8,128)(2,1)}), bf16[8,2,48,384]{3,2,1,0:T(8,128)(2,1)S(1)}, u32[]{:S(2)}, u32[]{:S(2)}) async-start(bf16[8,2,48,384]{3,2,1,0:T(8,128)(2,1)} %shard_map.86), calls=%async_computation.1 | async-start | bytes 1179648 | tf_op jit(solution)/shard_map/all_to_all | solution.py:483
  36.7 5.3 %shard_map.85 = (bf16[2,256,384]{2,1,0:T(8,128)(2,1)}, bf16[2,256,384]{2,1,0:T(8,128)(2,1)}, bf16[2,768,256]{2,1,0:T(8,128)(2,1)}) custom-call(s32[4]{0:T(128)} %pad_add_fusion.pos, bf16[256,768]{1,0:T(8,128)(2,1)} %bitcast.15, bf16[256,768]{1,0:T(8,128)(2,1)} %copy-done.3, bf16[256,768]{1,0:T(8,128)(2,1)} %bitcast.17, bf16[256,768]{1,0:T(8,128)(2,1)} %copy-done.5, ...), custom_call_target="tpu_custom_call" | custom-call | tf_op jit(solution)/shard_map/pallas_call | solution.py:125
  42.0 2.3 %all-to-all-done.1.xr = bf16[8,2,48,384]{3,2,1,0:T(8,128)(2,1)S(1)} async-done(((bf16[8,2,48,384]{3,2,1,0:T(8,128)(2,1)}), bf16[8,2,48,384]{3,2,1,0:T(8,128)(2,1)S(1)}, u32[]{:S(2)}, u32[]{:S(2)}) %all-to-all-start.1) | async-done | bytes 589856 | tf_op jit(solution)/shard_map/all_to_all | solution.py:483
  45.1 17.6 %shard_map.87 = (bf16[2,256,384]{2,1,0:T(8,128)(2,1)}, bf16[2,256,384]{2,1,0:T(8,128)(2,1)}, f32[2,2,256,384]{3,2,1,0:T(8,128)}, f32[2,2,128,384]{3,2,1,0:T(8,12...) custom-call(s32[4]{0:T(128)} %pad_add_fusion.pos, ...), custom_call_target="tpu_custom_call" | custom-call | tf_op jit(solution)/shard_map/pallas_call | solution.py:238
  62.7 4.7 %collective-permute-start.7 = (bf16[2,256,384]{2,1,0:T(8,128)(2,1)}, bf16[2,256,384]{2,1,0:T(8,128)(2,1)S(1)}, u32[]{:S(2)}, u32[]{:S(2)}) collective-permute-start(bf16[2,256,384]{2,1,0:T(8,128)(2,1)} %get-tuple-element.119.att_own), channel_id=1, source_target_pairs={{0,2},{2,0},{1,3},{3,1},{4,6},{6,4},{5,7},{7,5},{8,10},{10,8},{9,1... | collective-permute-start | bytes 1179656 | tf_op jit(solution)/shard_map/ppermute | solution.py:455
  67.4 3.5 %all-to-all-start.2 = ((bf16[8,2,48,384]{3,2,1,0:T(8,128)(2,1)}), bf16[8,2,48,384]{3,2,1,0:T(8,128)(2,1)S(1)}, u32[]{:S(2)}, u32[]{:S(2)}) async-start(bf16[8,2,48,384]{3,2,1,0:T(8,128)(2,1)} %get-tuple-element.79), calls=%async_computation.2 | async-start | bytes 1179648 | tf_op jit(solution)/shard_map/all_to_all | solution.py:487
  71.7 5.6 %shard_map.88 = (bf16[2,2,96,384]{3,2,1,0:T(8,128)(2,1)}, bf16[2,2,96,384]{3,2,1,0:T(8,128)(2,1)}, bf16[2,2,96,384]{3,2,1,0:T(8,128)(2,1)}, bf16[2,2,96,384]{3,2,1,0:T(8,128)(2,1)}) custom-call(s32[4]{0:T(128)} %pad_add_fusion.pos, bf16[2,256,384]{2,1,0:T(8,128)(2,1)} %get-tuple-element.119.att_own, bf16[2,256,384]{2,1,0:T(8,128)(2,1)} %copy-done.4, ...), custom_call_target="tpu_custom_call" | custom-call | tf_op jit(solution)/shard_map/pallas_call | solution.py:283
  77.3 1.4 collective-permute-start.8
  78.7 1.2 collective-permute-start.9
  79.9 2.4 %collective-permute-start.11 = (bf16[2,2,96,384]{3,2,1,0:T(8,128)(2,1)}, bf16[2,2,96,384]{3,2,1,0:T(8,128)(2,1)S(1)}, u32[]{:S(2)}, u32[]{:S(2)}) collective-permute-start(bf16[2,2,96,384]{3,2,1,0:T(8,128)(2,1)} %get-tuple-element.97), channel_id=1, source_target_pairs={{0,16},{8,24},{16,0},{24,8},{1,17},{9,25},{17,1},{25,9},{2,18},{10... | collective-permute-start | bytes 884744 | tf_op jit(solution)/shard_map/ppermute | solution.py:459
  82.6 2.0 %collective-permute-done.9.dwy = bf16[2,128,384]{2,1,0:T(8,128)(2,1)S(1)} collective-permute-done((bf16[2,128,384]{2,1,0:T(8,128)(2,1)S(1)}, bf16[2,128,384]{2,1,0:T(8,128)(2,1)S(1)}, u32[]{:S(2)}, u32[]{:S(2)}) %collective-permute-start.9) | collective-permute-done | bytes 196640 | tf_op jit(solution)/shard_map/ppermute | solution.py:455
  84.6 1.6 collective-permute-done.8.t1
  86.2 2.8 %shard_map.89 = (bf16[8,2,16,384]{3,2,1,0:T(8,128)(2,1)}, bf16[2,64,384]{2,1,0:T(8,128)(2,1)}, bf16[2,32,384]{2,1,0:T(8,128)(2,1)}, bf16[2,32,384]{2,1,0:T(8,128)(2,1)}) custom-call(s32[4]{0:T(128)} %pad_add_fusion.pos, bf16[8,2,48,384]{3,2,1,0:T(8,128)(2,1)} %copy-done.1, f32[2,128,384]{2,1,0:T(8,128)} %get-tuple-element.87.dw, bf16[2,128,384]{2,1,0:T(8,128)(2,1)} %copy-done.15), custom_call_target="tpu_custom_call" | custom-call | tf_op jit(solution)/shard_map/pallas_call | solution.py:329
  89.0 5.8 %all-to-all-start.3 = ((bf16[8,2,16,384]{3,2,1,0:T(8,128)(2,1)}), bf16[8,2,16,384]{3,2,1,0:T(8,128)(2,1)S(1)}, u32[]{:S(2)}, u32[]{:S(2)}) async-start(bf16[8,2,16,384]{3,2,1,0:T(8,128)(2,1)} %get-tuple-element.89), calls=%async_computation.3 | async-start | bytes 393216 | tf_op jit(solution)/shard_map/all_to_all | solution.py:494
  94.8 1.1 collective-permute-start.10
  95.9 1.5 collective-permute-done.12.t3
  97.4 2.2 %collective-permute-start.14 = (bf16[2,32,384]{2,1,0:T(8,128)(2,1)}, bf16[2,32,384]{2,1,0:T(8,128)(2,1)S(1)}, u32[]{:S(2)}, u32[]{:S(2)}) collective-permute-start(bf16[2,32,384]{2,1,0:T(8,128)(2,1)} %get-tuple-element.100), channel_id=1, source_target_pairs={{0,16},{8,24},{16,0},{24,8},{1,17},{9,25},{17,1},{25,9},{2,18},{10... | collective-permute-start | bytes 147464 | tf_op jit(solution)/shard_map/ppermute | solution.py:459
  99.6 1.6 collective-permute-start.15
  101.3 1.4 collective-permute-done.14.g4_a
  102.7 1.3 collective-permute-done.15.g4_b
  104.8 6.2 %shard_map.90 = (bf16[2,256,1152]{2,1,0:T(8,128)(2,1)}, bf16[8,2,96,384]{3,2,1,0:T(8,128)(2,1)}) custom-call(s32[4]{0:T(128)} %pad_add_fusion.pos, bf16[8,2,16,384]{3,2,1,0:T(8,128)(2,1)} %copy-done.7, f32[2,2,256,384]{3,2,1,0:T(8,128)} %get-tuple-element.90.dkv, f32[2,2,128,384]{3,2,1,0:T(8,128)} %get-tuple-element.91.dn1, bf16[2,128,384]{2,1,0:T(8,128)(2,1)} %copy-done.14, ...), custom_call_target="tpu_custom_call" | custom-call | tf_op jit(solution)/shard_map/pallas_call | solution.py:372
  111.0 5.8 %all-to-all-start.4 = ((bf16[16,96,384]{2,1,0:T(8,128)(2,1)}), bf16[16,96,384]{2,1,0:T(8,128)(2,1)S(1)}, u32[]{:S(2)}, u32[]{:S(2)}) async-start(bf16[16,96,384]{2,1,0:T(8,128)(2,1)} %bitcast.19), calls=%async_computation.4 | async-start | bytes 2359296 | tf_op jit(solution)/shard_map/all_to_all | solution.py:501
  116.8 0.9 dynamic-slice_bitcast_fusion
  117.7 3.8 %collective-permute-start.19 = (bf16[256,1152]{1,0:T(8,128)(2,1)S(1)}, bf16[256,1152]{1,0:T(8,128)(2,1)S(1)}, u32[]{:S(2)}, u32[]{:S(2)}) collective-permute-start(bf16[256,1152]{1,0:T(8,128)(2,1)S(1)} %get-tuple-element.128), channel_id=1, source_target_pairs={{0,2},{2,0},{1,3},{3,1},{4,6},{6,4},{5,7},{7,5},{8,10},{10,8},{9,1... | collective-permute-start | bytes 1769480 | tf_op jit(solution)/shard_map/ppermute | solution.py:455
  121.5 2.8 %shard_map.91 = (bf16[96,384]{1,0:T(8,128)(2,1)}, bf16[96,384]{1,0:T(8,128)(2,1)}, bf16[96,384]{1,0:T(8,128)(2,1)}, bf16[96,384]{1,0:T(8,128)(2,1)}) custom-call(s32[4]{0:T(128)} %pad_add_fusion.pos, bf16[2,2,96,384]{3,2,1,0:T(8,128)(2,1)} %get-tuple-element.107.t0, bf16[2,2,96,384]{3,2,1,0:T(8,128)(2,1)} %copy-done.11, bf16[2,2,96,384]{3,2,1,0:T(8,128)(2,1)} %copy-done.12, ...), custom_call_target="tpu_custom_call" | custom-call | tf_op jit(solution)/shard_map/pallas_call | solution.py:303
  124.3 3.1 %collective-permute-start.16 = (bf16[96,384]{1,0:T(8,128)(2,1)}, bf16[96,384]{1,0:T(8,128)(2,1)S(1)}, u32[]{:S(2)}, u32[]{:S(2)}) collective-permute-start(bf16[96,384]{1,0:T(8,128)(2,1)} %get-tuple-element.112), channel_id=1, source_target_pairs={{0,1},{1,0},{4,5},{5,4},{2,3},{3,2},{6,7},{7,6},{8,9},{9,8},{12,13... | collective-permute-start | bytes 221192 | tf_op jit(solution)/shard_map/ppermute | solution.py:459
  128.4 0.8 copy-done.10
  129.2 5.1 %shard_map.92 = bf16[256,768]{1,0:T(8,128)(2,1)} custom-call(s32[4]{0:T(128)} %pad_add_fusion.pos, bf16[256,1152]{1,0:T(8,128)(2,1)} %get-tuple-element.129.pg_own, bf16[256,1152]{1,0:T(8,128)(2,1)} %copy-done.10, bf16[768,2304]{1,0:T(8,128)(2,1)} %rest_5_.1, bf16[768,2304]{1,0:T(8,128)(2,1)} %rest_5_.1, bf16[768,2304]{1,0:T(8,128)(2,1)} %rest_5_.1, ...), custom_call_target="tpu_custom_call" | custom-call | tf_op jit(solution)/shard_map/pallas_call | solution.py:395
  134.3 3.2 %collective-permute-done.16.f1 = bf16[96,384]{1,0:T(8,128)(2,1)S(1)} collective-permute-done((bf16[96,384]{1,0:T(8,128)(2,1)}, bf16[96,384]{1,0:T(8,128)(2,1)S(1)}, u32[]{:S(2)}, u32[]{:S(2)}) %collective-permute-start.16) | collective-permute-done | bytes 73760 | tf_op jit(solution)/shard_map/ppermute | solution.py:459
  137.5 1.5 collective-permute-done.17.f2
  139.7 3.2 %shard_map.93 = bf16[8,2,16,384]{3,2,1,0:T(8,128)(2,1)} custom-call(s32[4]{0:T(128)} %pad_add_fusion.pos, bf16[96,384]{1,0:T(8,128)(2,1)} %get-tuple-element.111.f0, bf16[96,384]{1,0:T(8,128)(2,1)} %copy-done.19, bf16[96,384]{1,0:T(8,128)(2,1)} %copy-done.20, bf16[96,384]{1,0:T(8,128)(2,1)} %copy-done.21, bf16[16,96,384]{2,1,0:T(8,128)(2,1)} %copy-done), custom_call_target="tpu_custom_call" | custom-call | tf_op jit(solution)/shard_map/pallas_call | solution.py:424
  142.9 5.5 %all-to-all-start.5 = ((bf16[8,2,16,384]{3,2,1,0:T(8,128)(2,1)}), bf16[8,2,16,384]{3,2,1,0:T(8,128)(2,1)S(1)}, u32[]{:S(2)}, u32[]{:S(2)}) async-start(bf16[8,2,16,384]{3,2,1,0:T(8,128)(2,1)} %shard_map.93), calls=%async_computation.5 | async-start | bytes 393216 | tf_op jit(solution)/shard_map/all_to_all | solution.py:507
  148.4 3.5 %shard_map.94 = bf16[256,768]{1,0:T(8,128)(2,1)} custom-call(s32[4]{0:T(128)} %pad_add_fusion.pos, bf16[2,256,384]{2,1,0:T(8,128)(2,1)} %get-tuple-element.119.att_own, bf16[2,256,384]{2,1,0:T(8,128)(2,1)} %copy-done.4, bf16[768,768]{1,0:T(8,128)(2,1)} %w_oth.1, bf16[768,768]{1,0:T(8,128)(2,1)} %w_oth.1), custom_call_target="tpu_custom_call" | custom-call | tf_op jit(solution)/shard_map/pallas_call | solution.py:257
  151.8 5.1 %all-to-all-done.5 = bf16[8,2,16,384]{3,2,1,0:T(8,128)(2,1)S(1)} async-done(((bf16[8,2,16,384]{3,2,1,0:T(8,128)(2,1)}), bf16[8,2,16,384]{3,2,1,0:T(8,128)(2,1)S(1)}, u32[]{:S(2)}, u32[]{:S(2)}) %all-to-all-start.5) | async-done | bytes 196640 | tf_op jit(solution)/shard_map/all_to_all | solution.py:507
  157.0 3.3 %collective-permute-start.20 = (bf16[16,384]{1,0:T(8,128)(2,1)S(1)}, bf16[16,384]{1,0:T(8,128)(2,1)S(1)}, u32[]{:S(2)}, u32[]{:S(2)}) collective-permute-start(bf16[16,384]{1,0:T(8,128)(2,1)S(1)} %get-tuple-element.127.own), channel_id=1, source_target_pairs={{0,1},{1,0},{2,3},{3,2},{4,5},{5,4},{6,7},{7,6},{8,9},{9,8},{10,11... | collective-permute-start | bytes 36872 | tf_op jit(solution)/shard_map/ppermute | solution.py:459
  160.3 2.4 %collective-permute-start.21 = (bf16[16,384]{1,0:T(8,128)(2,1)S(1)}, bf16[16,384]{1,0:T(8,128)(2,1)S(1)}, u32[]{:S(2)}, u32[]{:S(2)}) collective-permute-start(bf16[16,384]{1,0:T(8,128)(2,1)S(1)} %get-tuple-element.126), channel_id=1, source_target_pairs={{0,2},{1,3},{2,0},{3,1},{4,6},{5,7},{6,4},{7,5},{8,10},{9,11},{10,... | collective-permute-start | bytes 36872 | tf_op jit(solution)/shard_map/ppermute | solution.py:459
  163.5 3.8 %collective-permute-done.22.from_both = bf16[16,384]{1,0:T(8,128)(2,1)S(1)} collective-permute-done((bf16[16,384]{1,0:T(8,128)(2,1)S(1)}, bf16[16,384]{1,0:T(8,128)(2,1)S(1)}, u32[]{:S(2)}, u32[]{:S(2)}) %collective-permute-start.22) | collective-permute-done | bytes 12320 | tf_op jit(solution)/shard_map/ppermute | solution.py:459
  167.9 2.1 %shard_map.95 = (f32[6,2304]{1,0:T(8,128)}, f32[6,768]{1,0:T(8,128)}) custom-call(s32[4]{0:T(128)} %pad_add_fusion.pos, bf16[16,384]{1,0:T(8,128)(2,1)} %copy-done.24, bf16[16,384]{1,0:T(8,128)(2,1)} %copy-done.25, bf16[16,384]{1,0:T(8,128)(2,1)} %copy-done.26, bf16[16,384]{1,0:T(8,128)(2,1)} %copy-done.27), custom_call_target="tpu_custom_call" | custom-call | tf_op jit(solution)/shard_map/pallas_call | solution.py:445
  (86 shorter events, 8.9 us)
Async XLA Ops:
  0.6 4.9 %collective-permute-start = (bf16[256,768]{1,0:T(8,128)(2,1)}, bf16[256,768]{1,0:T(8,128)(2,1)S(1)}, u32[]{:S(2)}, u32[]{:S(2)}) collective-permute-start(bf16[256,768]{1,0:T(8,128)(2,1)} %bitcast.13), channel_id=1, source_target_pairs={{0,2},{2,0},{1,3},{3,1},{4,6},{6,4},{5,7},{7,5},{8,10},{10,8},{9,1... | collective-permute-start | bytes 1179656 | tf_op jit(solution)/shard_map/ppermute | solution.py:455
  4.0 23.2 %collective-permute-start.5 = (bf16[256,768]{1,0:T(8,128)(2,1)}, bf16[256,768]{1,0:T(8,128)(2,1)S(1)}, u32[]{:S(2)}, u32[]{:S(2)}) collective-permute-start(bf16[256,768]{1,0:T(8,128)(2,1)} %bitcast.16), channel_id=1, source_target_pairs={{0,2},{2,0},{1,3},{3,1},{4,6},{6,4},{5,7},{7,5},{8,10},{10,8},{9,1... | collective-permute-start | bytes 1179656 | tf_op jit(solution)/shard_map/ppermute | solution.py:455
  11.3 15.9 %all-to-all-start = ((bf16[8,2,16,384]{3,2,1,0:T(8,128)(2,1)}), bf16[8,2,16,384]{3,2,1,0:T(8,128)(2,1)S(1)}, u32[]{:S(2)}, u32[]{:S(2)}) async-start(bf16[8,2,16,384]{3,2,1,0:T(8,128)(2,1)} %get-tuple-element.65), calls=%async_computation | async-start | bytes 393216 | tf_op jit(solution)/shard_map/all_to_all | solution.py:479
  17.7 9.4 %collective-permute-start.2 = (bf16[2,64,384]{2,1,0:T(8,128)(2,1)}, bf16[2,64,384]{2,1,0:T(8,128)(2,1)S(1)}, u32[]{:S(2)}, u32[]{:S(2)}) collective-permute-start(bf16[2,64,384]{2,1,0:T(8,128)(2,1)} %get-tuple-element.67), channel_id=1, source_target_pairs={{0,8},{8,0},{16,24},{24,16},{1,9},{9,1},{17,25},{25,17},{2,10},{10... | collective-permute-start | bytes 294920 | tf_op jit(solution)/shard_map/ppermute | solution.py:459
  18.9 8.2 %collective-permute-start.1 = (bf16[2,128,384]{2,1,0:T(8,128)(2,1)}, bf16[2,128,384]{2,1,0:T(8,128)(2,1)S(1)}, u32[]{:S(2)}, u32[]{:S(2)}) collective-permute-start(bf16[2,128,384]{2,1,0:T(8,128)(2,1)} %get-tuple-element.66), channel_id=1, source_target_pairs={{0,4},{4,0},{1,5},{5,1},{2,6},{6,2},{3,7},{7,3},{8,12},{12,8},{9,1... | collective-permute-start | bytes 589832 | tf_op jit(solution)/shard_map/ppermute | solution.py:455
  20.2 5.3 %collective-permute-start.3 = (bf16[2,32,384]{2,1,0:T(8,128)(2,1)}, bf16[2,32,384]{2,1,0:T(8,128)(2,1)S(1)}, u32[]{:S(2)}, u32[]{:S(2)}) collective-permute-start(bf16[2,32,384]{2,1,0:T(8,128)(2,1)} %get-tuple-element.68), channel_id=1, source_target_pairs={{0,16},{8,24},{16,0},{24,8},{1,17},{9,25},{17,1},{25,9},{2,18},{10... | collective-permute-start | bytes 147464 | tf_op jit(solution)/shard_map/ppermute | solution.py:459
  22.7 4.4 %collective-permute-start.4 = (bf16[2,32,384]{2,1,0:T(8,128)(2,1)}, bf16[2,32,384]{2,1,0:T(8,128)(2,1)S(1)}, u32[]{:S(2)}, u32[]{:S(2)}) collective-permute-start(bf16[2,32,384]{2,1,0:T(8,128)(2,1)} %get-tuple-element.68), channel_id=1, source_target_pairs={{0,24},{8,16},{16,8},{24,0},{1,25},{9,17},{17,9},{25,1},{2,26},{10... | collective-permute-start | bytes 147464 | tf_op jit(solution)/shard_map/ppermute | solution.py:459
  27.1 14.9 %copy-start.9 = (bf16[2,128,384]{2,1,0:T(8,128)(2,1)}, bf16[2,128,384]{2,1,0:T(8,128)(2,1)S(1)}, u32[]{:S(2)}) copy-start(bf16[2,128,384]{2,1,0:T(8,128)(2,1)S(1)} %pad_maximum_fusion.wr) | copy-start | bytes 589828
  27.1 9.6 %copy-start.5 = (bf16[256,768]{1,0:T(8,128)(2,1)}, bf16[256,768]{1,0:T(8,128)(2,1)S(1)}, u32[]{:S(2)}) copy-start(bf16[256,768]{1,0:T(8,128)(2,1)S(1)} %collective-permute-done.5.ct_oth) | copy-start | bytes 1179652
  27.1 14.8 %copy-start.16 = (bf16[2,128,384]{2,1,0:T(8,128)(2,1)}, bf16[2,128,384]{2,1,0:T(8,128)(2,1)S(1)}, u32[]{:S(2)}) copy-start(bf16[2,128,384]{2,1,0:T(8,128)(2,1)S(1)} %collective-permute-done.1.yr) | copy-start | bytes 589828
  27.2 4.6 %collective-permute-start.6 = (bf16[2,128,384]{2,1,0:T(8,128)(2,1)S(1)}, bf16[2,128,384]{2,1,0:T(8,128)(2,1)S(1)}, u32[]{:S(2)}, u32[]{:S(2)}) collective-permute-start(bf16[2,128,384]{2,1,0:T(8,128)(2,1)S(1)} %pad_maximum_fusion.wr), channel_id=1, source_target_pairs={{0,4},{4,0},{1,5},{5,1},{2,6},{6,2},{3,7},{7,3},{8,12},{12,8},{9,1... | collective-permute-start | bytes 589832 | tf_op jit(solution)/shard_map/ppermute | solution.py:455
  31.8 10.2 %copy-start.17 = (bf16[2,128,384]{2,1,0:T(8,128)(2,1)}, bf16[2,128,384]{2,1,0:T(8,128)(2,1)S(1)}, u32[]{:S(2)}) copy-start(bf16[2,128,384]{2,1,0:T(8,128)(2,1)S(1)} %collective-permute-done.6.wy) | copy-start | bytes 589828
  31.8 12.5 %all-to-all-start.1 = ((bf16[8,2,48,384]{3,2,1,0:T(8,128)(2,1)}), bf16[8,2,48,384]{3,2,1,0:T(8,128)(2,1)S(1)}, u32[]{:S(2)}, u32[]{:S(2)}) async-start(bf16[8,2,48,384]{3,2,1,0:T(8,128)(2,1)} %shard_map.86), calls=%async_computation.1 | async-start | bytes 1179648 | tf_op jit(solution)/shard_map/all_to_all | solution.py:483
  62.7 8.3 %collective-permute-start.7 = (bf16[2,256,384]{2,1,0:T(8,128)(2,1)}, bf16[2,256,384]{2,1,0:T(8,128)(2,1)S(1)}, u32[]{:S(2)}, u32[]{:S(2)}) collective-permute-start(bf16[2,256,384]{2,1,0:T(8,128)(2,1)} %get-tuple-element.119.att_own), channel_id=1, source_target_pairs={{0,2},{2,0},{1,3},{3,1},{4,6},{6,4},{5,7},{7,5},{8,10},{10,8},{9,1... | collective-permute-start | bytes 1179656 | tf_op jit(solution)/shard_map/ppermute | solution.py:455
  67.4 17.2 %all-to-all-start.2 = ((bf16[8,2,48,384]{3,2,1,0:T(8,128)(2,1)}), bf16[8,2,48,384]{3,2,1,0:T(8,128)(2,1)S(1)}, u32[]{:S(2)}, u32[]{:S(2)}) async-start(bf16[8,2,48,384]{3,2,1,0:T(8,128)(2,1)} %get-tuple-element.79), calls=%async_computation.2 | async-start | bytes 1179648 | tf_op jit(solution)/shard_map/all_to_all | solution.py:487
  71.7 7.0 %copy-start.29 = (bf16[2,128,384]{2,1,0:T(8,128)(2,1)S(1)}, bf16[2,128,384]{2,1,0:T(8,128)(2,1)}, u32[]{:S(2)}) copy-start(bf16[2,128,384]{2,1,0:T(8,128)(2,1)} %get-tuple-element.85) | copy-start | bytes 589828
  77.3 17.4 %copy-start.28 = (bf16[2,128,384]{2,1,0:T(8,128)(2,1)S(1)}, bf16[2,128,384]{2,1,0:T(8,128)(2,1)}, u32[]{:S(2)}) copy-start(bf16[2,128,384]{2,1,0:T(8,128)(2,1)} %get-tuple-element.92) | copy-start | bytes 589828
  77.3 8.8 %collective-permute-start.8 = (bf16[2,2,96,384]{3,2,1,0:T(8,128)(2,1)}, bf16[2,2,96,384]{3,2,1,0:T(8,128)(2,1)S(1)}, u32[]{:S(2)}, u32[]{:S(2)}) collective-permute-start(bf16[2,2,96,384]{3,2,1,0:T(8,128)(2,1)} %get-tuple-element.84), channel_id=1, source_target_pairs={{0,8},{8,0},{16,24},{24,16},{1,9},{9,1},{17,25},{25,17},{2,10},{10... | collective-permute-start | bytes 884744 | tf_op jit(solution)/shard_map/ppermute | solution.py:459
  78.7 5.9 %collective-permute-start.9 = (bf16[2,128,384]{2,1,0:T(8,128)(2,1)S(1)}, bf16[2,128,384]{2,1,0:T(8,128)(2,1)S(1)}, u32[]{:S(2)}, u32[]{:S(2)}) collective-permute-start(bf16[2,128,384]{2,1,0:T(8,128)(2,1)S(1)} %copy-done.29), channel_id=1, source_target_pairs={{0,4},{4,0},{1,5},{5,1},{2,6},{6,2},{3,7},{7,3},{8,12},{12,8},{9,1... | collective-permute-start | bytes 589832 | tf_op jit(solution)/shard_map/ppermute | solution.py:455
  79.9 16.0 %collective-permute-start.11 = (bf16[2,2,96,384]{3,2,1,0:T(8,128)(2,1)}, bf16[2,2,96,384]{3,2,1,0:T(8,128)(2,1)S(1)}, u32[]{:S(2)}, u32[]{:S(2)}) collective-permute-start(bf16[2,2,96,384]{3,2,1,0:T(8,128)(2,1)} %get-tuple-element.97), channel_id=1, source_target_pairs={{0,16},{8,24},{16,0},{24,8},{1,17},{9,25},{17,1},{25,9},{2,18},{10... | collective-permute-start | bytes 884744 | tf_op jit(solution)/shard_map/ppermute | solution.py:459
  82.3 15.1 %collective-permute-start.12 = (bf16[2,2,96,384]{3,2,1,0:T(8,128)(2,1)}, bf16[2,2,96,384]{3,2,1,0:T(8,128)(2,1)S(1)}, u32[]{:S(2)}, u32[]{:S(2)}) collective-permute-start(bf16[2,2,96,384]{3,2,1,0:T(8,128)(2,1)} %get-tuple-element.98), channel_id=1, source_target_pairs={{0,24},{8,16},{16,8},{24,0},{1,25},{9,17},{17,9},{25,1},{2,26},{10... | collective-permute-start | bytes 884744 | tf_op jit(solution)/shard_map/ppermute | solution.py:459
  84.6 1.6 copy-start.15
  84.6 1.6 copy-start.1
  86.2 24.8 %copy-start.11 = (bf16[2,2,96,384]{3,2,1,0:T(8,128)(2,1)}, bf16[2,2,96,384]{3,2,1,0:T(8,128)(2,1)S(1)}, u32[]{:S(2)}) copy-start(bf16[2,2,96,384]{3,2,1,0:T(8,128)(2,1)S(1)} %collective-permute-done.8.t1) | copy-start | bytes 884740
  89.0 15.0 %all-to-all-start.3 = ((bf16[8,2,16,384]{3,2,1,0:T(8,128)(2,1)}), bf16[8,2,16,384]{3,2,1,0:T(8,128)(2,1)S(1)}, u32[]{:S(2)}, u32[]{:S(2)}) async-start(bf16[8,2,16,384]{3,2,1,0:T(8,128)(2,1)} %get-tuple-element.89), calls=%async_computation.3 | async-start | bytes 393216 | tf_op jit(solution)/shard_map/all_to_all | solution.py:494
  94.8 6.5 %collective-permute-start.10 = (bf16[2,128,384]{2,1,0:T(8,128)(2,1)S(1)}, bf16[2,128,384]{2,1,0:T(8,128)(2,1)S(1)}, u32[]{:S(2)}, u32[]{:S(2)}) collective-permute-start(bf16[2,128,384]{2,1,0:T(8,128)(2,1)S(1)} %copy-done.28), channel_id=1, source_target_pairs={{0,4},{4,0},{1,5},{5,1},{2,6},{6,2},{3,7},{7,3},{8,12},{12,8},{9,1... | collective-permute-start | bytes 589832 | tf_op jit(solution)/shard_map/ppermute | solution.py:455
  95.9 21.8 %copy-start.12 = (bf16[2,2,96,384]{3,2,1,0:T(8,128)(2,1)}, bf16[2,2,96,384]{3,2,1,0:T(8,128)(2,1)S(1)}, u32[]{:S(2)}) copy-start(bf16[2,2,96,384]{3,2,1,0:T(8,128)(2,1)S(1)} %collective-permute-done.11.t2) | copy-start | bytes 884740
  97.4 13.6 %copy-start.13 = (bf16[2,2,96,384]{3,2,1,0:T(8,128)(2,1)}, bf16[2,2,96,384]{3,2,1,0:T(8,128)(2,1)S(1)}, u32[]{:S(2)}) copy-start(bf16[2,2,96,384]{3,2,1,0:T(8,128)(2,1)S(1)} %collective-permute-done.12.t3) | copy-start | bytes 884740
  97.4 6.6 %collective-permute-start.13 = (bf16[2,64,384]{2,1,0:T(8,128)(2,1)}, bf16[2,64,384]{2,1,0:T(8,128)(2,1)S(1)}, u32[]{:S(2)}, u32[]{:S(2)}) collective-permute-start(bf16[2,64,384]{2,1,0:T(8,128)(2,1)} %get-tuple-element.99), channel_id=1, source_target_pairs={{0,8},{8,0},{16,24},{24,16},{1,9},{9,1},{17,25},{25,17},{2,10},{10... | collective-permute-start | bytes 294920 | tf_op jit(solution)/shard_map/ppermute | solution.py:459
  97.4 5.2 %collective-permute-start.14 = (bf16[2,32,384]{2,1,0:T(8,128)(2,1)}, bf16[2,32,384]{2,1,0:T(8,128)(2,1)S(1)}, u32[]{:S(2)}, u32[]{:S(2)}) collective-permute-start(bf16[2,32,384]{2,1,0:T(8,128)(2,1)} %get-tuple-element.100), channel_id=1, source_target_pairs={{0,16},{8,24},{16,0},{24,8},{1,17},{9,25},{17,1},{25,9},{2,18},{10... | collective-permute-start | bytes 147464 | tf_op jit(solution)/shard_map/ppermute | solution.py:459
  99.6 4.4 %collective-permute-start.15 = (bf16[2,32,384]{2,1,0:T(8,128)(2,1)}, bf16[2,32,384]{2,1,0:T(8,128)(2,1)S(1)}, u32[]{:S(2)}, u32[]{:S(2)}) collective-permute-start(bf16[2,32,384]{2,1,0:T(8,128)(2,1)} %get-tuple-element.101), channel_id=1, source_target_pairs={{0,24},{8,16},{16,8},{24,0},{1,25},{9,17},{17,9},{25,1},{2,26},{10... | collective-permute-start | bytes 147464 | tf_op jit(solution)/shard_map/ppermute | solution.py:459
  101.3 2.7 %copy-start.14 = (bf16[2,128,384]{2,1,0:T(8,128)(2,1)}, bf16[2,128,384]{2,1,0:T(8,128)(2,1)S(1)}, u32[]{:S(2)}) copy-start(bf16[2,128,384]{2,1,0:T(8,128)(2,1)S(1)} %collective-permute-done.10.dy) | copy-start | bytes 589828
  102.7 1.4 copy-start.22
  111.0 5.8 %copy-start.6 = (bf16[2,256,1152]{2,1,0:T(8,128)(2,1)S(1)}, bf16[2,256,1152]{2,1,0:T(8,128)(2,1)}, u32[]{:S(2)}) copy-start(bf16[2,256,1152]{2,1,0:T(8,128)(2,1)} %get-tuple-element.116) | copy-start | bytes 3538948
  111.0 23.4 %all-to-all-start.4 = ((bf16[16,96,384]{2,1,0:T(8,128)(2,1)}), bf16[16,96,384]{2,1,0:T(8,128)(2,1)S(1)}, u32[]{:S(2)}, u32[]{:S(2)}) async-start(bf16[16,96,384]{2,1,0:T(8,128)(2,1)} %bitcast.19), calls=%async_computation.4 | async-start | bytes 2359296 | tf_op jit(solution)/shard_map/all_to_all | solution.py:501
  117.7 10.6 %collective-permute-start.19 = (bf16[256,1152]{1,0:T(8,128)(2,1)S(1)}, bf16[256,1152]{1,0:T(8,128)(2,1)S(1)}, u32[]{:S(2)}, u32[]{:S(2)}) collective-permute-start(bf16[256,1152]{1,0:T(8,128)(2,1)S(1)} %get-tuple-element.128), channel_id=1, source_target_pairs={{0,2},{2,0},{1,3},{3,1},{4,6},{6,4},{5,7},{7,5},{8,10},{10,8},{9,1... | collective-permute-start | bytes 1769480 | tf_op jit(solution)/shard_map/ppermute | solution.py:455
  124.3 13.2 %collective-permute-start.16 = (bf16[96,384]{1,0:T(8,128)(2,1)}, bf16[96,384]{1,0:T(8,128)(2,1)S(1)}, u32[]{:S(2)}, u32[]{:S(2)}) collective-permute-start(bf16[96,384]{1,0:T(8,128)(2,1)} %get-tuple-element.112), channel_id=1, source_target_pairs={{0,1},{1,0},{4,5},{5,4},{2,3},{3,2},{6,7},{7,6},{8,9},{9,8},{12,13... | collective-permute-start | bytes 221192 | tf_op jit(solution)/shard_map/ppermute | solution.py:459
  127.5 11.5 %collective-permute-start.17 = (bf16[96,384]{1,0:T(8,128)(2,1)}, bf16[96,384]{1,0:T(8,128)(2,1)S(1)}, u32[]{:S(2)}, u32[]{:S(2)}) collective-permute-start(bf16[96,384]{1,0:T(8,128)(2,1)} %get-tuple-element.113), channel_id=1, source_target_pairs={{0,4},{1,5},{4,0},{5,1},{2,6},{3,7},{6,2},{7,3},{8,12},{9,13},{12,... | collective-permute-start | bytes 221192 | tf_op jit(solution)/shard_map/ppermute | solution.py:459
  127.8 11.2 %collective-permute-start.18 = (bf16[96,384]{1,0:T(8,128)(2,1)}, bf16[96,384]{1,0:T(8,128)(2,1)S(1)}, u32[]{:S(2)}, u32[]{:S(2)}) collective-permute-start(bf16[96,384]{1,0:T(8,128)(2,1)} %get-tuple-element.114), channel_id=1, source_target_pairs={{0,5},{1,4},{4,1},{5,0},{2,7},{3,6},{6,3},{7,2},{8,13},{9,12},{12,... | collective-permute-start | bytes 221192 | tf_op jit(solution)/shard_map/ppermute | solution.py:459
  134.3 4.7 %copy-start = (bf16[16,96,384]{2,1,0:T(8,128)(2,1)}, bf16[16,96,384]{2,1,0:T(8,128)(2,1)S(1)}, u32[]{:S(2)}) copy-start(bf16[16,96,384]{2,1,0:T(8,128)(2,1)S(1)} %all-to-all-done.4.second) | copy-start | bytes 3538948
  137.5 1.5 copy-start.19
  142.9 14.1 %all-to-all-start.5 = ((bf16[8,2,16,384]{3,2,1,0:T(8,128)(2,1)}), bf16[8,2,16,384]{3,2,1,0:T(8,128)(2,1)S(1)}, u32[]{:S(2)}, u32[]{:S(2)}) async-start(bf16[8,2,16,384]{3,2,1,0:T(8,128)(2,1)} %shard_map.93), calls=%async_computation.5 | async-start | bytes 393216 | tf_op jit(solution)/shard_map/all_to_all | solution.py:507
  157.0 10.3 %copy-start.24 = (bf16[16,384]{1,0:T(8,128)(2,1)}, bf16[16,384]{1,0:T(8,128)(2,1)S(1)}, u32[]{:S(2)}) copy-start(bf16[16,384]{1,0:T(8,128)(2,1)S(1)} %get-tuple-element.127.own) | copy-start | bytes 36868
  157.0 6.1 %collective-permute-start.20 = (bf16[16,384]{1,0:T(8,128)(2,1)S(1)}, bf16[16,384]{1,0:T(8,128)(2,1)S(1)}, u32[]{:S(2)}, u32[]{:S(2)}) collective-permute-start(bf16[16,384]{1,0:T(8,128)(2,1)S(1)} %get-tuple-element.127.own), channel_id=1, source_target_pairs={{0,1},{1,0},{2,3},{3,2},{4,5},{5,4},{6,7},{7,6},{8,9},{9,8},{10,11... | collective-permute-start | bytes 36872 | tf_op jit(solution)/shard_map/ppermute | solution.py:459
  160.3 3.2 %collective-permute-start.21 = (bf16[16,384]{1,0:T(8,128)(2,1)S(1)}, bf16[16,384]{1,0:T(8,128)(2,1)S(1)}, u32[]{:S(2)}, u32[]{:S(2)}) collective-permute-start(bf16[16,384]{1,0:T(8,128)(2,1)S(1)} %get-tuple-element.126), channel_id=1, source_target_pairs={{0,2},{1,3},{2,0},{3,1},{4,6},{5,7},{6,4},{7,5},{8,10},{9,11},{10,... | collective-permute-start | bytes 36872 | tf_op jit(solution)/shard_map/ppermute | solution.py:459
  162.6 4.6 %collective-permute-start.22 = (bf16[16,384]{1,0:T(8,128)(2,1)S(1)}, bf16[16,384]{1,0:T(8,128)(2,1)S(1)}, u32[]{:S(2)}, u32[]{:S(2)}) collective-permute-start(bf16[16,384]{1,0:T(8,128)(2,1)S(1)} %get-tuple-element.126), channel_id=1, source_target_pairs={{0,3},{1,2},{2,1},{3,0},{4,7},{5,6},{6,5},{7,4},{8,11},{9,10},{10,... | collective-permute-start | bytes 36872 | tf_op jit(solution)/shard_map/ppermute | solution.py:459
  163.1 4.2 %copy-start.25 = (bf16[16,384]{1,0:T(8,128)(2,1)}, bf16[16,384]{1,0:T(8,128)(2,1)S(1)}, u32[]{:S(2)}) copy-start(bf16[16,384]{1,0:T(8,128)(2,1)S(1)} %collective-permute-done.20.from_dp) | copy-start | bytes 36868
  163.5 3.8 %copy-start.26 = (bf16[16,384]{1,0:T(8,128)(2,1)}, bf16[16,384]{1,0:T(8,128)(2,1)S(1)}, u32[]{:S(2)}) copy-start(bf16[16,384]{1,0:T(8,128)(2,1)S(1)} %collective-permute-done.21.from_core) | copy-start | bytes 36868
  (11 other events, 8.3 us)

commit v11 on v10

--- a/solution.py
+++ b/solution.py
@@ -66,39 +66,45 @@
     )
 
 
-def tree_body(pos, x_own, x_oth, wk, wv, kv_out, n1_out, n2_out, n3_out, n4_out, zs_out):
+def tree_body(pos, x_own, x_oth, wk, wv, kv_out, n1_out, n2_out, n3_out, n4_out, zs_out, rows, pad):
     c, z = pos[0], pos[1]
     for e, x in ((c, x_own), (1 - c, x_oth)):
-        kv_out[e, 0] = dot(x[...], wk[...]).astype(BF16)
-        kv_out[e, 1] = dot(x[...], wv[...]).astype(BF16)
-
-    def store(ref, *index):
-        def put(node):
-            for p in range(2):
-                ref[index + (p,)] = node[:, H * p : H * p + H]
-
-        return put
-
-    halves = []
-    for e in range(2):
-        n1 = coarsen(jnp.concatenate([kv_out[e, 0], kv_out[e, 1]], axis=1))
-        store(n1_out, e)(n1)
-        halves.append(coarsen(n1))
-    n2 = jnp.concatenate(halves, axis=0)
-    store(n2_out)(n2)
-    n3 = coarsen(n2)
-    store(n3_out)(n3)
-    n4 = coarsen(n3)
-    store(n4_out)(n4)
-    n5 = coarsen(n4)
-    n6 = coarsen(n5, 16, 8)
-    n7 = coarsen(n6, 16, 4)
-    store(zs_out, z)(jnp.zeros_like(n5))
-    store(zs_out, z ^ 1)(n5)
-    for far in (2, 3):
-        store(zs_out, z ^ far)(n6)
-    for far in (4, 5, 6, 7):
-        store(zs_out, z ^ far)(n7)
+        for p, w in ((0, wk), (1, wv)):
+            part = dot(x[...], w[...]).astype(BF16)
+            kv_out[e, p] = part
+            for n in range(3):
+                rows[e, 3 * p + n] = part[:, 128 * n : 128 * n + 128].astype(F32)
+
+    def coarser(ref, n):
+        node = ((ref[pl.ds(0, n, stride=2), :] + ref[pl.ds(1, n, stride=2), :]) * HALF_ROOT).astype(BF16)
+        return node, node.astype(F32)
+
+    for p in range(2):
+        for n in range(3):
+            cols, block = slice(128 * n, 128 * n + 128), 3 * p + n
+            top = pad.at[block]
+            for e in range(2):
+                ref = rows.at[e, block]
+                n1_out[e, p, :, cols], wide = coarser(ref, NR)
+                ref[:NR] = wide
+                n2_out[p, 64 * e : 64 * e + 64, cols], wide = coarser(ref, 64)
+                top[64 * e : 64 * e + 64] = wide
+            n3_out[p, :, cols], wide = coarser(top, 64)
+            top[:64] = wide
+            n4_out[p, :, cols], wide = coarser(top, 32)
+            top[:32] = wide
+            n5, wide = coarser(top, 16)
+            top[:16] = wide
+            top[16:48] = jnp.zeros((32, 128), F32)
+            top[16:24] = coarser(top, 8)[1]
+            top[32:36] = coarser(top.at[pl.ds(16, 8)], 4)[1]
+            n6, n7 = top[16:32].astype(BF16), top[32:48].astype(BF16)
+            zs_out[z, p, :, cols] = jnp.zeros_like(n5)
+            zs_out[z ^ 1, p, :, cols] = n5
+            for far in (2, 3):
+                zs_out[z ^ far, p, :, cols] = n6
+            for far in (4, 5, 6, 7):
+                zs_out[z ^ far, p, :, cols] = n7
 
 
 def tree(pos, x_own, x_oth, w_qkv):
@@ -109,6 +115,7 @@
         (1,),
         [whole(TOK, D)] * 2 + [col(1), col(2)],
         [(whole(*shape), (shape, BF16)) for shape in outs],
+        [pltpu.VMEM((2, 6, TOK, 128), F32), pltpu.VMEM((6, NR, 128), F32)],
     )(pos, x_own, x_oth, w_qkv, w_qkv)
 
 
@@ -157,20 +164,19 @@
     )(pos, zr)[0]
 
 
-def attention_body(pos, q, ag, kv, n1, yr, wr, wy, xr, att_out, dq_out, dkv_out, dn1_out, dy_out, dwy_out, dw_out, dx_out, keys, keys_t, s_ref, dw_ref, w_ref, ds_ref, drem):
+def attention_body(pos, q, ag, kv, n1, yr, wr, wy, xr, att_out, dq_out, dkv_out, dn1_out, dy_out, dwy_out, dw_out, dx_out, near, near_t, shared, shared_t, s_ref, dw_ref, w_ref, ds_ref, drem):
     for p in range(2):
         for e in range(2):
-            keys[e, p, :256] = kv[e, p]
-            keys[e, p, 256:384] = n1[1 - e, p]
-            keys[e, p, 384:512] = yr[p]
-            keys[e, p, 512:640] = wr[p]
-            keys[e, p, 640:768] = wy[p]
-            for slot in range(8):
-                start = 768 + ZR * slot
-                keys[e, p, start : start + ZR] = xr[slot, p]
-    for p in range(2):
-        for e in range(2):
-            keys_t[e, p] = keys[e, p].T
+            near[e, p, :256] = kv[e, p]
+            near[e, p, 256:] = n1[1 - e, p]
+            near_t[e, p] = near[e, p].T
+        shared[p, :128] = yr[p]
+        shared[p, 128:256] = wr[p]
+        shared[p, 256:384] = wy[p]
+        for slot in range(8):
+            start = 384 + ZR * slot
+            shared[p, start : start + ZR] = xr[slot, p]
+        shared_t[p] = shared[p].T
     lane = iota((TOK, 128), 1)
     steps = [(e, h) for e in range(2) for h in range(2)]
     masked = {}
@@ -181,8 +187,9 @@
         qh = jnp.where(mine, q[e], jnp.zeros((), BF16))
         ah = jnp.where(mine, ag[e], jnp.zeros((), BF16))
         masked[step] = (qh, ah)
-        s_ref[step % 2] = dot_nt(keys[e, 0], qh)
-        dw_ref[step % 2] = dot_nt(keys[e, 1], ah * jnp.asarray(DH ** -0.5, BF16))
+        for ref, p, token in ((s_ref, 0, qh), (dw_ref, 1, ah * jnp.asarray(DH ** -0.5, BF16))):
+            ref[step % 2, :384] = dot_nt(near[e, p], token)
+            ref[step % 2, 384:] = dot_nt(shared[p], token)
 
     scores(0)
     for step, (e, h) in enumerate(steps):
@@ -201,8 +208,9 @@
         cols = slice(TOK * h, TOK * h + TOK)
         w_ref[e, :, cols] = prob.astype(BF16)
         ds_ref[e, :, cols] = (prob * (dw[...] - delta)).astype(BF16)
-        att_t.append(dot(keys_t[e, 1, 64 * h : 64 * h + 64], w_ref[e, :, cols]))
-        dq_t.append(dot(keys_t[e, 0, 64 * h : 64 * h + 64], ds_ref[e, :, cols]))
+        head = slice(64 * h, 64 * h + 64)
+        for out, p, ref in ((att_t, 1, w_ref), (dq_t, 0, ds_ref)):
+            out.append(dot(near_t[e, p, head], ref[e, :384, cols]) + dot(shared_t[p, head], ref[e, 384:, cols]))
         if h == 0:
             continue
         dk = dot(ds_ref[e], jnp.concatenate([masked[step - 1][0], qh], axis=0))
@@ -241,7 +249,8 @@
         [cut(2, TOK), cut(2, TOK), cut(2, 2, TOK), cut(2, 2, NR), cut(2, NR), cut(2, NR), cut(2, NR), cut(8, 2, ZR)],
         [(cut(*lead), (lead + (H,), kind)) for lead, kind in outs],
         [
-            pltpu.VMEM((2, 2, n, 128), BF16), pltpu.VMEM((2, 2, 128, n), BF16), pltpu.VMEM((2, n, TOK), F32), pltpu.VMEM((2, n, TOK), F32),
+            pltpu.VMEM((2, 2, 384, 128), BF16), pltpu.VMEM((2, 2, 128, 384), BF16),
+            pltpu.VMEM((2, 768, 128), BF16), pltpu.VMEM((2, 128, 768), BF16), pltpu.VMEM((2, n, TOK), F32), pltpu.VMEM((2, n, TOK), F32),
             pltpu.VMEM((2, n, 2 * TOK), BF16), pltpu.VMEM((2, n, 2 * TOK), BF16), pltpu.VMEM((2, 768, 128), F32),
         ],
     )(pos, q, ag, kv, n1, yr, wr, wy, xr)
@@ -334,7 +343,7 @@
     )(pos, xr, dw, dwy)
 
 
-def leaf_body(pos, zr, dkv, dn1, dy, g3, g4_a, g4_b, dq, xt, pg_out, grad_out):
+def leaf_body(pos, zr, dkv, dn1, dy, g3, g4_a, g4_b, dq, xt, own_out, oth_out, grad_out):
     def split(grad):
         high = grad.astype(BF16)
         return [high, (grad - high.astype(F32)).astype(BF16)]
@@ -348,7 +357,8 @@
     zs = jnp.concatenate([zr[:, p].reshape(128, H) for p in range(2)], axis=1)
     ws = jnp.concatenate([wide(g3), wide(g4_a), wide(g4_b)], axis=0)
     ys = wide(dy)
-    for e in range(2):
+    sides = ((pos[0], own_out), (1 - pos[0], oth_out))
+    for e, pg_out in sides:
         t, k = iota((TOK, 128), 0), iota((TOK, 128), 1)
         far, row, chip = (k >> 4) ^ pos[1], k & 15, t + TOK * e
         first = hot(t >> 1 == k, 1.0)
@@ -360,11 +370,12 @@
         up = dot(jnp.concatenate([first, first, third, odd], axis=1), jnp.concatenate(split(wide(dn1.at[e])) + [ws, zs], axis=0))
         up = up * HALF_ROOT + dot(jnp.concatenate([second, fourth, even], axis=1), jnp.concatenate([ys, ws, zs], axis=0))
         for p in range(2):
-            pg_out[e, :, H * (1 + p) : H * (2 + p)] = (dkv[e, p] + up[:, H * p : H * p + H]).astype(BF16)
-        pg_out[e, :, :H] = dq[e]
+            pg_out[:, H * (1 + p) : H * (2 + p)] = (dkv[e, p] + up[:, H * p : H * p + H]).astype(BF16)
+        pg_out[:, :H] = dq[e]
     for p in range(2):
         cols = slice(H * (1 + p), H * (2 + p))
-        total = dot(xt[0], pg_out[0, :, cols]) + dot(xt[1], pg_out[1, :, cols])
+        first, second = (dot(xt[e], pg_out[:, cols]) for e, pg_out in sides)
+        total = first + second
         grad_out[:, p] = total.astype(BF16).reshape(8, 96, H)
 
 
@@ -376,7 +387,7 @@
             whole(ZN, 2, 16, H), whole(2, 2, TOK, H), whole(2, 2, NR, H), whole(2, NR, H), whole(2, 64, H), whole(2, 32, H),
             whole(2, 32, H), whole(2, TOK, H), whole(2, D, TOK),
         ],
-        [(whole(2, TOK, 3 * H), ((2, TOK, 3 * H), BF16)), (whole(8, 2, 96, H), ((8, 2, 96, H), BF16))],
+        [(whole(TOK, 3 * H), ((TOK, 3 * H), BF16))] * 2 + [(whole(8, 2, 96, H), ((8, 2, 96, H), BF16))],
     )(pos, zr, dkv, dn1, dy, g3, g4_a, g4_b, dq, xt)
 
 
@@ -494,14 +505,12 @@
     dz_r = lax.all_to_all(dz, "z", 0, 0)
     g3, g4_a, g4_b, firsts = lax.optimization_barrier((g3, g4_a, g4_b, firsts))
     g3, g4_a, g4_b = along(g3, "x", 1), along(g4_a, "x", 2), along(g4_b, "x", 3)
-    pg, terms = leaf_grads(pos, dz_r, dkv, dn1, swap(dy, "y"), g3, g4_a, g4_b, dq, xt)
+    pg_own, pg_oth, terms = leaf_grads(pos, dz_r, dkv, dn1, swap(dy, "y"), g3, g4_a, g4_b, dq, xt)
     terms, first, firsts = lax.optimization_barrier((terms, first, firsts))
     firsts = x_sum(pos, first, *firsts)
     firsts = list(firsts[:1]) + [along(firsts[far], ("y", "dp"), far) for far in (1, 2, 3)]
     terms = lax.all_to_all(terms.reshape(16, 96, H), ("x", "y", "dp"), 0, 0)
-    pg_own = lax.dynamic_index_in_dim(pg, c, 0, keepdims=False)
-    pg_oth = swap(lax.dynamic_index_in_dim(pg, 1 - c, 0, keepdims=False), "c")
-    input_grad = input_side(pos, pg_own, pg_oth, w_qkv)
+    input_grad = input_side(pos, pg_own, swap(pg_oth, "c"), w_qkv)
     terms, input_grad = lax.optimization_barrier((terms, input_grad))
     terms, att, att_oth = lax.optimization_barrier((middle_sum(pos, firsts, terms), att, att_oth))
     terms = lax.all_to_all(terms, "z", 0, 0)

time: 171 us -> 168 us (0.982)
  transfers between devices with their start and end apart: 29 -> 29, of which waited for: 15 -> 16; matrix products, arithmetic and copies ran while one was open for 1% -> 0% of each run, Pallas kernels for 19% -> 19%
where the time goes in v11:
time: 168 us; the launch traced here: 167 us
  starting transfers between devices  70.2 us (42%)
  Pallas kernels  60.5 us (36%)
  waiting for transfers between devices  30 us (18%)
  local copies, waits for them, and re-layouts  5.2 us (3%)
    ppermute x15, starting transfers between devices, along(): return lax.ppermute(value, axes, [(i, i ^ far) for i in range(count)])  21.4 us
    ppermute x15, waiting for transfers between devices, along(): return lax.ppermute(value, axes, [(i, i ^ far) for i in range(count)])  18.8 us
    ppermute x8, starting transfers between devices, swap(): return lax.ppermute(value, axis, [(0, 1), (1, 0)])  16.9 us
    pallas_call x1, Pallas kernels, attention(): call(attention_body, (H // 128,), [cut(2, TOK), cut(2, TOK), cut(2, 2, TO...  16.8 us
    all_to_all x1, starting transfers between devices, shards(): zr = lax.all_to_all(zs, 'z', 0, 0)  6.45 us
    pallas_call x1, Pallas kernels, leaf_grads(): call(leaf_body, (1,), [whole(ZN, 2, 16, H), whole(2, 2, TOK, H), whole(2,...  6.24 us
    all_to_all x1, starting transfers between devices, shards(): terms = lax.all_to_all(terms.reshape(16, 96, H), ('x', 'y', 'dp'), 0, 0)  6.1 us
    pallas_call x1, Pallas kernels, output_terms(): call(terms_body, (1,), [whole(2, TOK, H)] * 2 + [col(0, TOK)] * 2 + [whol...  5.59 us
  transfers between devices with their start and end apart: 29, of which 16 were waited for; matrix products, arithmetic and copies ran while one was open for 0% of the time, Pallas kernels for 19%

profile of v11, /device:TPU:1, one launch (start us, length us, event | category | flops | bytes accessed | tf_op | source)
XLA Modules:
  0.0 167.4 jit_solution(17663862946402170496)
XLA Ops:
  0.6 3.3 %collective-permute-start = (bf16[256,768]{1,0:T(8,128)(2,1)}, bf16[256,768]{1,0:T(8,128)(2,1)S(1)}, u32[]{:S(2)}, u32[]{:S(2)}) collective-permute-start(bf16[256,768]{1,0:T(8,128)(2,1)} %bitcast.9), channel_id=1, source_target_pairs={{0,2},{2,0},{1,3},{3,1},{4,6},{6,4},{5,7},{7,5},{8,10},{10,8},{9,1... | collective-permute-start | bytes 1179656 | tf_op jit(solution)/shard_map/ppermute | solution.py:466
  4.7 0.8 collective-permute-done.x_oth
  6.3 4.5 %shard_map.84 = (bf16[2,2,256,384]{3,2,1,0:T(8,128)(2,1)}, bf16[2,2,128,384]{3,2,1,0:T(8,128)(2,1)}, bf16[2,128,384]{2,1,0:T(8,128)(2,1)}, bf16[2,64,384]{2,1,0:...) custom-call(s32[4]{0:T(128)} %pad_add_fusion.pos, bf16[256,768]{1,0:T(8,128)(2,1)} %bitcast.10, ...), custom_call_target="tpu_custom_call" | custom-call | tf_op jit(solution)/shard_map/pallas_call | solution.py:113
  10.7 6.5 %all-to-all-start = ((bf16[8,2,16,384]{3,2,1,0:T(8,128)(2,1)}), bf16[8,2,16,384]{3,2,1,0:T(8,128)(2,1)S(1)}, u32[]{:S(2)}, u32[]{:S(2)}) async-start(bf16[8,2,16,384]{3,2,1,0:T(8,128)(2,1)} %get-tuple-element.66), calls=%async_computation | async-start | bytes 393216 | tf_op jit(solution)/shard_map/all_to_all | solution.py:490
  17.2 1.2 collective-permute-start.2
  18.4 1.3 collective-permute-start.1
  19.7 1.8 %collective-permute-start.4 = (bf16[2,32,384]{2,1,0:T(8,128)(2,1)}, bf16[2,32,384]{2,1,0:T(8,128)(2,1)S(1)}, u32[]{:S(2)}, u32[]{:S(2)}) collective-permute-start(bf16[2,32,384]{2,1,0:T(8,128)(2,1)} %get-tuple-element.69), channel_id=1, source_target_pairs={{0,24},{8,16},{16,8},{24,0},{1,25},{9,17},{17,9},{25,1},{2,26},{10... | collective-permute-start | bytes 147464 | tf_op jit(solution)/shard_map/ppermute | solution.py:470
  22.1 2.2 %collective-permute-done.4 = bf16[2,32,384]{2,1,0:T(8,128)(2,1)S(1)} collective-permute-done((bf16[2,32,384]{2,1,0:T(8,128)(2,1)}, bf16[2,32,384]{2,1,0:T(8,128)(2,1)S(1)}, u32[]{:S(2)}, u32[]{:S(2)}) %collective-permute-start.4) | collective-permute-done | bytes 49184 | tf_op jit(solution)/shard_map/ppermute | solution.py:470
  24.3 1.9 %collective-permute-done.3 = bf16[2,32,384]{2,1,0:T(8,128)(2,1)S(1)} collective-permute-done((bf16[2,32,384]{2,1,0:T(8,128)(2,1)}, bf16[2,32,384]{2,1,0:T(8,128)(2,1)S(1)}, u32[]{:S(2)}, u32[]{:S(2)}) %collective-permute-start.3) | collective-permute-done | bytes 49184 | tf_op jit(solution)/shard_map/ppermute | solution.py:470
  26.6 1.3 collective-permute-start.6
  27.9 2.6 %shard_map.86 = bf16[8,2,48,384]{3,2,1,0:T(8,128)(2,1)} custom-call(s32[4]{0:T(128)} %pad_add_fusion.pos, bf16[8,2,16,384]{3,2,1,0:T(8,128)(2,1)} %copy-done.7), custom_call_target="tpu_custom_call" | custom-call | tf_op jit(solution)/shard_map/pallas_call | solution.py:159
  31.1 5.0 %all-to-all-start.1 = ((bf16[8,2,48,384]{3,2,1,0:T(8,128)(2,1)}), bf16[8,2,48,384]{3,2,1,0:T(8,128)(2,1)S(1)}, u32[]{:S(2)}, u32[]{:S(2)}) async-start(bf16[8,2,48,384]{3,2,1,0:T(8,128)(2,1)} %shard_map.86), calls=%async_computation.1 | async-start | bytes 1179648 | tf_op jit(solution)/shard_map/all_to_all | solution.py:494
  36.2 5.2 %shard_map.85 = (bf16[2,256,384]{2,1,0:T(8,128)(2,1)}, bf16[2,256,384]{2,1,0:T(8,128)(2,1)}, bf16[2,768,256]{2,1,0:T(8,128)(2,1)}) custom-call(s32[4]{0:T(128)} %pad_add_fusion.pos, bf16[256,768]{1,0:T(8,128)(2,1)} %bitcast.11, bf16[256,768]{1,0:T(8,128)(2,1)} %copy-done.3, bf16[256,768]{1,0:T(8,128)(2,1)} %bitcast.13, bf16[256,768]{1,0:T(8,128)(2,1)} %copy-done.5, ...), custom_call_target="tpu_custom_call" | custom-call | tf_op jit(solution)/shard_map/pallas_call | solution.py:132
  41.4 2.3 %all-to-all-done.1.xr = bf16[8,2,48,384]{3,2,1,0:T(8,128)(2,1)S(1)} async-done(((bf16[8,2,48,384]{3,2,1,0:T(8,128)(2,1)}), bf16[8,2,48,384]{3,2,1,0:T(8,128)(2,1)S(1)}, u32[]{:S(2)}, u32[]{:S(2)}) %all-to-all-start.1) | async-done | bytes 589856 | tf_op jit(solution)/shard_map/all_to_all | solution.py:494
  44.5 16.8 %shard_map.87 = (bf16[2,256,384]{2,1,0:T(8,128)(2,1)}, bf16[2,256,384]{2,1,0:T(8,128)(2,1)}, f32[2,2,256,384]{3,2,1,0:T(8,128)}, f32[2,2,128,384]{3,2,1,0:T(8,12...) custom-call(s32[4]{0:T(128)} %pad_add_fusion.pos, ...), custom_call_target="tpu_custom_call" | custom-call | tf_op jit(solution)/shard_map/pallas_call | solution.py:246
  61.4 4.7 %collective-permute-start.7 = (bf16[2,256,384]{2,1,0:T(8,128)(2,1)}, bf16[2,256,384]{2,1,0:T(8,128)(2,1)S(1)}, u32[]{:S(2)}, u32[]{:S(2)}) collective-permute-start(bf16[2,256,384]{2,1,0:T(8,128)(2,1)} %get-tuple-element.121.att_own), channel_id=1, source_target_pairs={{0,2},{2,0},{1,3},{3,1},{4,6},{6,4},{5,7},{7,5},{8,10},{10,8},{9,1... | collective-permute-start | bytes 1179656 | tf_op jit(solution)/shard_map/ppermute | solution.py:466
  66.1 3.5 %all-to-all-start.2 = ((bf16[8,2,48,384]{3,2,1,0:T(8,128)(2,1)}), bf16[8,2,48,384]{3,2,1,0:T(8,128)(2,1)S(1)}, u32[]{:S(2)}, u32[]{:S(2)}) async-start(bf16[8,2,48,384]{3,2,1,0:T(8,128)(2,1)} %get-tuple-element.80), calls=%async_computation.2 | async-start | bytes 1179648 | tf_op jit(solution)/shard_map/all_to_all | solution.py:498
  70.4 5.6 %shard_map.88 = (bf16[2,2,96,384]{3,2,1,0:T(8,128)(2,1)}, bf16[2,2,96,384]{3,2,1,0:T(8,128)(2,1)}, bf16[2,2,96,384]{3,2,1,0:T(8,128)(2,1)}, bf16[2,2,96,384]{3,2,1,0:T(8,128)(2,1)}) custom-call(s32[4]{0:T(128)} %pad_add_fusion.pos, bf16[2,256,384]{2,1,0:T(8,128)(2,1)} %get-tuple-element.121.att_own, bf16[2,256,384]{2,1,0:T(8,128)(2,1)} %copy-done.4, ...), custom_call_target="tpu_custom_call" | custom-call | tf_op jit(solution)/shard_map/pallas_call | solution.py:292
  76.0 1.4 collective-permute-start.8
  77.4 1.2 collective-permute-start.9
  78.6 2.4 %collective-permute-start.11 = (bf16[2,2,96,384]{3,2,1,0:T(8,128)(2,1)}, bf16[2,2,96,384]{3,2,1,0:T(8,128)(2,1)S(1)}, u32[]{:S(2)}, u32[]{:S(2)}) collective-permute-start(bf16[2,2,96,384]{3,2,1,0:T(8,128)(2,1)} %get-tuple-element.98), channel_id=1, source_target_pairs={{0,16},{8,24},{16,0},{24,8},{1,17},{9,25},{17,1},{25,9},{2,18},{10... | collective-permute-start | bytes 884744 | tf_op jit(solution)/shard_map/ppermute | solution.py:470
  81.2 2.0 %collective-permute-done.9.dwy = bf16[2,128,384]{2,1,0:T(8,128)(2,1)S(1)} collective-permute-done((bf16[2,128,384]{2,1,0:T(8,128)(2,1)S(1)}, bf16[2,128,384]{2,1,0:T(8,128)(2,1)S(1)}, u32[]{:S(2)}, u32[]{:S(2)}) %collective-permute-start.9) | collective-permute-done | bytes 196640 | tf_op jit(solution)/shard_map/ppermute | solution.py:466
  83.2 1.6 collective-permute-done.8.t1
  84.8 2.8 %shard_map.89 = (bf16[8,2,16,384]{3,2,1,0:T(8,128)(2,1)}, bf16[2,64,384]{2,1,0:T(8,128)(2,1)}, bf16[2,32,384]{2,1,0:T(8,128)(2,1)}, bf16[2,32,384]{2,1,0:T(8,128)(2,1)}) custom-call(s32[4]{0:T(128)} %pad_add_fusion.pos, bf16[8,2,48,384]{3,2,1,0:T(8,128)(2,1)} %copy-done.1, f32[2,128,384]{2,1,0:T(8,128)} %get-tuple-element.88.dw, bf16[2,128,384]{2,1,0:T(8,128)(2,1)} %copy-done.14), custom_call_target="tpu_custom_call" | custom-call | tf_op jit(solution)/shard_map/pallas_call | solution.py:338
  87.7 5.4 %all-to-all-start.3 = ((bf16[8,2,16,384]{3,2,1,0:T(8,128)(2,1)}), bf16[8,2,16,384]{3,2,1,0:T(8,128)(2,1)S(1)}, u32[]{:S(2)}, u32[]{:S(2)}) async-start(bf16[8,2,16,384]{3,2,1,0:T(8,128)(2,1)} %get-tuple-element.90), calls=%async_computation.3 | async-start | bytes 393216 | tf_op jit(solution)/shard_map/all_to_all | solution.py:505
  93.1 1.1 collective-permute-start.10
  94.2 1.8 %collective-permute-done.12.t3 = bf16[2,2,96,384]{3,2,1,0:T(8,128)(2,1)S(1)} collective-permute-done((bf16[2,2,96,384]{3,2,1,0:T(8,128)(2,1)}, bf16[2,2,96,384]{3,2,1,0:T(8,128)(2,1)S(1)}, u32[]{:S(2)}, u32[]{:S(2)}) %collective-permute-start.12) | collective-permute-done | bytes 294944 | tf_op jit(solution)/shard_map/ppermute | solution.py:470
  96.1 1.9 %collective-permute-start.14 = (bf16[2,32,384]{2,1,0:T(8,128)(2,1)}, bf16[2,32,384]{2,1,0:T(8,128)(2,1)S(1)}, u32[]{:S(2)}, u32[]{:S(2)}) collective-permute-start(bf16[2,32,384]{2,1,0:T(8,128)(2,1)} %get-tuple-element.101), channel_id=1, source_target_pairs={{0,16},{8,24},{16,0},{24,8},{1,17},{9,25},{17,1},{25,9},{2,18},{10... | collective-permute-start | bytes 147464 | tf_op jit(solution)/shard_map/ppermute | solution.py:470
  98.0 2.0 %collective-permute-start.15 = (bf16[2,32,384]{2,1,0:T(8,128)(2,1)}, bf16[2,32,384]{2,1,0:T(8,128)(2,1)S(1)}, u32[]{:S(2)}, u32[]{:S(2)}) collective-permute-start(bf16[2,32,384]{2,1,0:T(8,128)(2,1)} %get-tuple-element.102), channel_id=1, source_target_pairs={{0,24},{8,16},{16,8},{24,0},{1,25},{9,17},{17,9},{25,1},{2,26},{10... | collective-permute-start | bytes 147464 | tf_op jit(solution)/shard_map/ppermute | solution.py:470
  99.9 1.1 collective-permute-done.14.g4_a
  101.0 1.3 collective-permute-done.15.g4_b
  103.1 6.2 %shard_map.90 = (bf16[256,1152]{1,0:T(8,128)(2,1)}, bf16[256,1152]{1,0:T(8,128)(2,1)}, bf16[8,2,96,384]{3,2,1,0:T(8,128)(2,1)}) custom-call(s32[4]{0:T(128)} %pad_add_fusion.pos, bf16[8,2,16,384]{3,2,1,0:T(8,128)(2,1)} %copy-done.6, f32[2,2,256,384]{3,2,1,0:T(8,128)} %get-tuple-element.91.dkv, f32[2,2,128,384]{3,2,1,0:T(8,128)} %get-tuple-element.92.dn1, ...), custom_call_target="tpu_custom_call" | custom-call | tf_op jit(solution)/shard_map/pallas_call | solution.py:383
  109.3 6.1 %all-to-all-start.4 = ((bf16[16,96,384]{2,1,0:T(8,128)(2,1)}), bf16[16,96,384]{2,1,0:T(8,128)(2,1)S(1)}, u32[]{:S(2)}, u32[]{:S(2)}) async-start(bf16[16,96,384]{2,1,0:T(8,128)(2,1)} %bitcast.15), calls=%async_computation.4 | async-start | bytes 2359296 | tf_op jit(solution)/shard_map/all_to_all | solution.py:512
  115.5 3.9 %collective-permute-start.19 = (bf16[256,1152]{1,0:T(8,128)(2,1)S(1)}, bf16[256,1152]{1,0:T(8,128)(2,1)S(1)}, u32[]{:S(2)}, u32[]{:S(2)}) collective-permute-start(bf16[256,1152]{1,0:T(8,128)(2,1)S(1)} %copy-done.27), channel_id=1, source_target_pairs={{0,2},{2,0},{1,3},{3,1},{4,6},{6,4},{5,7},{7,5},{8,10},{10,8},{9,1... | collective-permute-start | bytes 1769480 | tf_op jit(solution)/shard_map/ppermute | solution.py:466
  119.3 2.8 %shard_map.91 = (bf16[96,384]{1,0:T(8,128)(2,1)}, bf16[96,384]{1,0:T(8,128)(2,1)}, bf16[96,384]{1,0:T(8,128)(2,1)}, bf16[96,384]{1,0:T(8,128)(2,1)}) custom-call(s32[4]{0:T(128)} %pad_add_fusion.pos, bf16[2,2,96,384]{3,2,1,0:T(8,128)(2,1)} %get-tuple-element.108.t0, bf16[2,2,96,384]{3,2,1,0:T(8,128)(2,1)} %copy-done.10, bf16[2,2,96,384]{3,2,1,0:T(8,128)(2,1)} %copy-done.11, ...), custom_call_target="tpu_custom_call" | custom-call | tf_op jit(solution)/shard_map/pallas_call | solution.py:312
  122.2 3.1 %collective-permute-start.16 = (bf16[96,384]{1,0:T(8,128)(2,1)}, bf16[96,384]{1,0:T(8,128)(2,1)S(1)}, u32[]{:S(2)}, u32[]{:S(2)}) collective-permute-start(bf16[96,384]{1,0:T(8,128)(2,1)} %get-tuple-element.113), channel_id=1, source_target_pairs={{0,1},{1,0},{4,5},{5,4},{2,3},{3,2},{6,7},{7,6},{8,9},{9,8},{12,13... | collective-permute-start | bytes 221192 | tf_op jit(solution)/shard_map/ppermute | solution.py:470
  126.2 0.8 copy-done.9
  127.0 5.1 %shard_map.92 = bf16[256,768]{1,0:T(8,128)(2,1)} custom-call(s32[4]{0:T(128)} %pad_add_fusion.pos, bf16[256,1152]{1,0:T(8,128)(2,1)} %get-tuple-element.117.pg_own, bf16[256,1152]{1,0:T(8,128)(2,1)} %copy-done.9, bf16[768,2304]{1,0:T(8,128)(2,1)} %rest_5_.1, bf16[768,2304]{1,0:T(8,128)(2,1)} %rest_5_.1, bf16[768,2304]{1,0:T(8,128)(2,1)} %rest_5_.1, ...), custom_call_target="tpu_custom_call" | custom-call | tf_op jit(solution)/shard_map/pallas_call | solution.py:406
  132.2 4.0 %collective-permute-done.16.f1 = bf16[96,384]{1,0:T(8,128)(2,1)S(1)} collective-permute-done((bf16[96,384]{1,0:T(8,128)(2,1)}, bf16[96,384]{1,0:T(8,128)(2,1)S(1)}, u32[]{:S(2)}, u32[]{:S(2)}) %collective-permute-start.16) | collective-permute-done | bytes 73760 | tf_op jit(solution)/shard_map/ppermute | solution.py:470
  136.2 1.4 collective-permute-done.17.f2
  138.2 3.2 %shard_map.93 = bf16[8,2,16,384]{3,2,1,0:T(8,128)(2,1)} custom-call(s32[4]{0:T(128)} %pad_add_fusion.pos, bf16[96,384]{1,0:T(8,128)(2,1)} %get-tuple-element.112.f0, bf16[96,384]{1,0:T(8,128)(2,1)} %copy-done.18, bf16[96,384]{1,0:T(8,128)(2,1)} %copy-done.19, bf16[96,384]{1,0:T(8,128)(2,1)} %copy-done.20, bf16[16,96,384]{2,1,0:T(8,128)(2,1)} %copy-done), custom_call_target="tpu_custom_call" | custom-call | tf_op jit(solution)/shard_map/pallas_call | solution.py:435
  141.4 5.2 %all-to-all-start.5 = ((bf16[8,2,16,384]{3,2,1,0:T(8,128)(2,1)}), bf16[8,2,16,384]{3,2,1,0:T(8,128)(2,1)S(1)}, u32[]{:S(2)}, u32[]{:S(2)}) async-start(bf16[8,2,16,384]{3,2,1,0:T(8,128)(2,1)} %shard_map.93), calls=%async_computation.5 | async-start | bytes 393216 | tf_op jit(solution)/shard_map/all_to_all | solution.py:516
  146.7 3.5 %shard_map.94 = bf16[256,768]{1,0:T(8,128)(2,1)} custom-call(s32[4]{0:T(128)} %pad_add_fusion.pos, bf16[2,256,384]{2,1,0:T(8,128)(2,1)} %get-tuple-element.121.att_own, bf16[2,256,384]{2,1,0:T(8,128)(2,1)} %copy-done.4, bf16[768,768]{1,0:T(8,128)(2,1)} %w_oth.1, bf16[768,768]{1,0:T(8,128)(2,1)} %w_oth.1), custom_call_target="tpu_custom_call" | custom-call | tf_op jit(solution)/shard_map/pallas_call | solution.py:266
  150.2 5.1 %all-to-all-done.5 = bf16[8,2,16,384]{3,2,1,0:T(8,128)(2,1)S(1)} async-done(((bf16[8,2,16,384]{3,2,1,0:T(8,128)(2,1)}), bf16[8,2,16,384]{3,2,1,0:T(8,128)(2,1)S(1)}, u32[]{:S(2)}, u32[]{:S(2)}) %all-to-all-start.5) | async-done | bytes 196640 | tf_op jit(solution)/shard_map/all_to_all | solution.py:516
  155.4 5.3 %collective-permute-start.22 = (bf16[16,384]{1,0:T(8,128)(2,1)S(1)}, bf16[16,384]{1,0:T(8,128)(2,1)S(1)}, u32[]{:S(2)}, u32[]{:S(2)}) collective-permute-start(bf16[16,384]{1,0:T(8,128)(2,1)S(1)} %get-tuple-element.128), channel_id=1, source_target_pairs={{0,3},{1,2},{2,1},{3,0},{4,7},{5,6},{6,5},{7,4},{8,11},{9,10},{10,... | collective-permute-start | bytes 36872 | tf_op jit(solution)/shard_map/ppermute | solution.py:470
  161.2 0.8 collective-permute-done.22.from_both
  162.0 2.7 %collective-permute-done.20.from_dp = bf16[16,384]{1,0:T(8,128)(2,1)S(1)} collective-permute-done((bf16[16,384]{1,0:T(8,128)(2,1)S(1)}, bf16[16,384]{1,0:T(8,128)(2,1)S(1)}, u32[]{:S(2)}, u32[]{:S(2)}) %collective-permute-start.20) | collective-permute-done | bytes 12320 | tf_op jit(solution)/shard_map/ppermute | solution.py:470
  165.3 2.1 %shard_map.95 = (f32[6,2304]{1,0:T(8,128)}, f32[6,768]{1,0:T(8,128)}) custom-call(s32[4]{0:T(128)} %pad_add_fusion.pos, bf16[16,384]{1,0:T(8,128)(2,1)} %copy-done.23, bf16[16,384]{1,0:T(8,128)(2,1)} %copy-done.26, bf16[16,384]{1,0:T(8,128)(2,1)} %copy-done.25, bf16[16,384]{1,0:T(8,128)(2,1)} %copy-done.24), custom_call_target="tpu_custom_call" | custom-call | tf_op jit(solution)/shard_map/pallas_call | solution.py:456
  (85 shorter events, 8.4 us)
Async XLA Ops:
  0.6 4.9 %collective-permute-start = (bf16[256,768]{1,0:T(8,128)(2,1)}, bf16[256,768]{1,0:T(8,128)(2,1)S(1)}, u32[]{:S(2)}, u32[]{:S(2)}) collective-permute-start(bf16[256,768]{1,0:T(8,128)(2,1)} %bitcast.9), channel_id=1, source_target_pairs={{0,2},{2,0},{1,3},{3,1},{4,6},{6,4},{5,7},{7,5},{8,10},{10,8},{9,1... | collective-permute-start | bytes 1179656 | tf_op jit(solution)/shard_map/ppermute | solution.py:466
  4.0 22.3 %collective-permute-start.5 = (bf16[256,768]{1,0:T(8,128)(2,1)}, bf16[256,768]{1,0:T(8,128)(2,1)S(1)}, u32[]{:S(2)}, u32[]{:S(2)}) collective-permute-start(bf16[256,768]{1,0:T(8,128)(2,1)} %bitcast.12), channel_id=1, source_target_pairs={{0,2},{2,0},{1,3},{3,1},{4,6},{6,4},{5,7},{7,5},{8,10},{10,8},{9,1... | collective-permute-start | bytes 1179656 | tf_op jit(solution)/shard_map/ppermute | solution.py:466
  10.7 15.9 %all-to-all-start = ((bf16[8,2,16,384]{3,2,1,0:T(8,128)(2,1)}), bf16[8,2,16,384]{3,2,1,0:T(8,128)(2,1)S(1)}, u32[]{:S(2)}, u32[]{:S(2)}) async-start(bf16[8,2,16,384]{3,2,1,0:T(8,128)(2,1)} %get-tuple-element.66), calls=%async_computation | async-start | bytes 393216 | tf_op jit(solution)/shard_map/all_to_all | solution.py:490
  17.2 9.1 %collective-permute-start.2 = (bf16[2,64,384]{2,1,0:T(8,128)(2,1)}, bf16[2,64,384]{2,1,0:T(8,128)(2,1)S(1)}, u32[]{:S(2)}, u32[]{:S(2)}) collective-permute-start(bf16[2,64,384]{2,1,0:T(8,128)(2,1)} %get-tuple-element.68), channel_id=1, source_target_pairs={{0,8},{8,0},{16,24},{24,16},{1,9},{9,1},{17,25},{25,17},{2,10},{10... | collective-permute-start | bytes 294920 | tf_op jit(solution)/shard_map/ppermute | solution.py:470
  18.4 7.9 %collective-permute-start.1 = (bf16[2,128,384]{2,1,0:T(8,128)(2,1)}, bf16[2,128,384]{2,1,0:T(8,128)(2,1)S(1)}, u32[]{:S(2)}, u32[]{:S(2)}) collective-permute-start(bf16[2,128,384]{2,1,0:T(8,128)(2,1)} %get-tuple-element.67), channel_id=1, source_target_pairs={{0,4},{4,0},{1,5},{5,1},{2,6},{6,2},{3,7},{7,3},{8,12},{12,8},{9,1... | collective-permute-start | bytes 589832 | tf_op jit(solution)/shard_map/ppermute | solution.py:466
  19.7 4.7 %collective-permute-start.4 = (bf16[2,32,384]{2,1,0:T(8,128)(2,1)}, bf16[2,32,384]{2,1,0:T(8,128)(2,1)S(1)}, u32[]{:S(2)}, u32[]{:S(2)}) collective-permute-start(bf16[2,32,384]{2,1,0:T(8,128)(2,1)} %get-tuple-element.69), channel_id=1, source_target_pairs={{0,24},{8,16},{16,8},{24,0},{1,25},{9,17},{17,9},{25,1},{2,26},{10... | collective-permute-start | bytes 147464 | tf_op jit(solution)/shard_map/ppermute | solution.py:470
  21.5 4.7 %collective-permute-start.3 = (bf16[2,32,384]{2,1,0:T(8,128)(2,1)}, bf16[2,32,384]{2,1,0:T(8,128)(2,1)S(1)}, u32[]{:S(2)}, u32[]{:S(2)}) collective-permute-start(bf16[2,32,384]{2,1,0:T(8,128)(2,1)} %get-tuple-element.69), channel_id=1, source_target_pairs={{0,16},{8,24},{16,0},{24,8},{1,17},{9,25},{17,1},{25,9},{2,18},{10... | collective-permute-start | bytes 147464 | tf_op jit(solution)/shard_map/ppermute | solution.py:470
  26.3 15.1 %copy-start.8 = (bf16[2,128,384]{2,1,0:T(8,128)(2,1)}, bf16[2,128,384]{2,1,0:T(8,128)(2,1)S(1)}, u32[]{:S(2)}) copy-start(bf16[2,128,384]{2,1,0:T(8,128)(2,1)S(1)} %pad_maximum_fusion.wr) | copy-start | bytes 589828
  26.3 9.9 %copy-start.5 = (bf16[256,768]{1,0:T(8,128)(2,1)}, bf16[256,768]{1,0:T(8,128)(2,1)S(1)}, u32[]{:S(2)}) copy-start(bf16[256,768]{1,0:T(8,128)(2,1)S(1)} %collective-permute-done.5.ct_oth) | copy-start | bytes 1179652
  26.3 15.1 %copy-start.15 = (bf16[2,128,384]{2,1,0:T(8,128)(2,1)}, bf16[2,128,384]{2,1,0:T(8,128)(2,1)S(1)}, u32[]{:S(2)}) copy-start(bf16[2,128,384]{2,1,0:T(8,128)(2,1)S(1)} %collective-permute-done.1.yr) | copy-start | bytes 589828
  26.6 4.5 %collective-permute-start.6 = (bf16[2,128,384]{2,1,0:T(8,128)(2,1)S(1)}, bf16[2,128,384]{2,1,0:T(8,128)(2,1)S(1)}, u32[]{:S(2)}, u32[]{:S(2)}) collective-permute-start(bf16[2,128,384]{2,1,0:T(8,128)(2,1)S(1)} %pad_maximum_fusion.wr), channel_id=1, source_target_pairs={{0,4},{4,0},{1,5},{5,1},{2,6},{6,2},{3,7},{7,3},{8,12},{12,8},{9,1... | collective-permute-start | bytes 589832 | tf_op jit(solution)/shard_map/ppermute | solution.py:466
  31.1 10.3 %copy-start.16 = (bf16[2,128,384]{2,1,0:T(8,128)(2,1)}, bf16[2,128,384]{2,1,0:T(8,128)(2,1)S(1)}, u32[]{:S(2)}) copy-start(bf16[2,128,384]{2,1,0:T(8,128)(2,1)S(1)} %collective-permute-done.6.wy) | copy-start | bytes 589828
  31.1 12.6 %all-to-all-start.1 = ((bf16[8,2,48,384]{3,2,1,0:T(8,128)(2,1)}), bf16[8,2,48,384]{3,2,1,0:T(8,128)(2,1)S(1)}, u32[]{:S(2)}, u32[]{:S(2)}) async-start(bf16[8,2,48,384]{3,2,1,0:T(8,128)(2,1)} %shard_map.86), calls=%async_computation.1 | async-start | bytes 1179648 | tf_op jit(solution)/shard_map/all_to_all | solution.py:494
  61.4 8.3 %collective-permute-start.7 = (bf16[2,256,384]{2,1,0:T(8,128)(2,1)}, bf16[2,256,384]{2,1,0:T(8,128)(2,1)S(1)}, u32[]{:S(2)}, u32[]{:S(2)}) collective-permute-start(bf16[2,256,384]{2,1,0:T(8,128)(2,1)} %get-tuple-element.121.att_own), channel_id=1, source_target_pairs={{0,2},{2,0},{1,3},{3,1},{4,6},{6,4},{5,7},{7,5},{8,10},{10,8},{9,1... | collective-permute-start | bytes 1179656 | tf_op jit(solution)/shard_map/ppermute | solution.py:466
  66.1 17.1 %all-to-all-start.2 = ((bf16[8,2,48,384]{3,2,1,0:T(8,128)(2,1)}), bf16[8,2,48,384]{3,2,1,0:T(8,128)(2,1)S(1)}, u32[]{:S(2)}, u32[]{:S(2)}) async-start(bf16[8,2,48,384]{3,2,1,0:T(8,128)(2,1)} %get-tuple-element.80), calls=%async_computation.2 | async-start | bytes 1179648 | tf_op jit(solution)/shard_map/all_to_all | solution.py:498
  70.4 7.0 %copy-start.29 = (bf16[2,128,384]{2,1,0:T(8,128)(2,1)S(1)}, bf16[2,128,384]{2,1,0:T(8,128)(2,1)}, u32[]{:S(2)}) copy-start(bf16[2,128,384]{2,1,0:T(8,128)(2,1)} %get-tuple-element.86) | copy-start | bytes 589828
  76.0 17.1 %copy-start.28 = (bf16[2,128,384]{2,1,0:T(8,128)(2,1)S(1)}, bf16[2,128,384]{2,1,0:T(8,128)(2,1)}, u32[]{:S(2)}) copy-start(bf16[2,128,384]{2,1,0:T(8,128)(2,1)} %get-tuple-element.93) | copy-start | bytes 589828
  76.0 8.8 %collective-permute-start.8 = (bf16[2,2,96,384]{3,2,1,0:T(8,128)(2,1)}, bf16[2,2,96,384]{3,2,1,0:T(8,128)(2,1)S(1)}, u32[]{:S(2)}, u32[]{:S(2)}) collective-permute-start(bf16[2,2,96,384]{3,2,1,0:T(8,128)(2,1)} %get-tuple-element.85), channel_id=1, source_target_pairs={{0,8},{8,0},{16,24},{24,16},{1,9},{9,1},{17,25},{25,17},{2,10},{10... | collective-permute-start | bytes 884744 | tf_op jit(solution)/shard_map/ppermute | solution.py:470
  77.4 5.9 %collective-permute-start.9 = (bf16[2,128,384]{2,1,0:T(8,128)(2,1)S(1)}, bf16[2,128,384]{2,1,0:T(8,128)(2,1)S(1)}, u32[]{:S(2)}, u32[]{:S(2)}) collective-permute-start(bf16[2,128,384]{2,1,0:T(8,128)(2,1)S(1)} %copy-done.29), channel_id=1, source_target_pairs={{0,4},{4,0},{1,5},{5,1},{2,6},{6,2},{3,7},{7,3},{8,12},{12,8},{9,1... | collective-permute-start | bytes 589832 | tf_op jit(solution)/shard_map/ppermute | solution.py:466
  78.6 15.7 %collective-permute-start.11 = (bf16[2,2,96,384]{3,2,1,0:T(8,128)(2,1)}, bf16[2,2,96,384]{3,2,1,0:T(8,128)(2,1)S(1)}, u32[]{:S(2)}, u32[]{:S(2)}) collective-permute-start(bf16[2,2,96,384]{3,2,1,0:T(8,128)(2,1)} %get-tuple-element.98), channel_id=1, source_target_pairs={{0,16},{8,24},{16,0},{24,8},{1,17},{9,25},{17,1},{25,9},{2,18},{10... | collective-permute-start | bytes 884744 | tf_op jit(solution)/shard_map/ppermute | solution.py:470
  81.0 15.1 %collective-permute-start.12 = (bf16[2,2,96,384]{3,2,1,0:T(8,128)(2,1)}, bf16[2,2,96,384]{3,2,1,0:T(8,128)(2,1)S(1)}, u32[]{:S(2)}, u32[]{:S(2)}) collective-permute-start(bf16[2,2,96,384]{3,2,1,0:T(8,128)(2,1)} %get-tuple-element.99), channel_id=1, source_target_pairs={{0,24},{8,16},{16,8},{24,0},{1,25},{9,17},{17,9},{25,1},{2,26},{10... | collective-permute-start | bytes 884744 | tf_op jit(solution)/shard_map/ppermute | solution.py:470
  83.2 1.6 copy-start.14
  83.2 1.6 copy-start.1
  84.8 24.5 %copy-start.10 = (bf16[2,2,96,384]{3,2,1,0:T(8,128)(2,1)}, bf16[2,2,96,384]{3,2,1,0:T(8,128)(2,1)S(1)}, u32[]{:S(2)}) copy-start(bf16[2,2,96,384]{3,2,1,0:T(8,128)(2,1)S(1)} %collective-permute-done.8.t1) | copy-start | bytes 884740
  87.7 14.7 %all-to-all-start.3 = ((bf16[8,2,16,384]{3,2,1,0:T(8,128)(2,1)}), bf16[8,2,16,384]{3,2,1,0:T(8,128)(2,1)S(1)}, u32[]{:S(2)}, u32[]{:S(2)}) async-start(bf16[8,2,16,384]{3,2,1,0:T(8,128)(2,1)} %get-tuple-element.90), calls=%async_computation.3 | async-start | bytes 393216 | tf_op jit(solution)/shard_map/all_to_all | solution.py:505
  93.1 6.8 %collective-permute-start.10 = (bf16[2,128,384]{2,1,0:T(8,128)(2,1)S(1)}, bf16[2,128,384]{2,1,0:T(8,128)(2,1)S(1)}, u32[]{:S(2)}, u32[]{:S(2)}) collective-permute-start(bf16[2,128,384]{2,1,0:T(8,128)(2,1)S(1)} %copy-done.28), channel_id=1, source_target_pairs={{0,4},{4,0},{1,5},{5,1},{2,6},{6,2},{3,7},{7,3},{8,12},{12,8},{9,1... | collective-permute-start | bytes 589832 | tf_op jit(solution)/shard_map/ppermute | solution.py:466
  94.2 25.1 %copy-start.11 = (bf16[2,2,96,384]{3,2,1,0:T(8,128)(2,1)}, bf16[2,2,96,384]{3,2,1,0:T(8,128)(2,1)S(1)}, u32[]{:S(2)}) copy-start(bf16[2,2,96,384]{3,2,1,0:T(8,128)(2,1)S(1)} %collective-permute-done.11.t2) | copy-start | bytes 884740
  96.1 23.3 %copy-start.12 = (bf16[2,2,96,384]{3,2,1,0:T(8,128)(2,1)}, bf16[2,2,96,384]{3,2,1,0:T(8,128)(2,1)S(1)}, u32[]{:S(2)}) copy-start(bf16[2,2,96,384]{3,2,1,0:T(8,128)(2,1)S(1)} %collective-permute-done.12.t3) | copy-start | bytes 884740
  96.1 6.2 %collective-permute-start.13 = (bf16[2,64,384]{2,1,0:T(8,128)(2,1)}, bf16[2,64,384]{2,1,0:T(8,128)(2,1)S(1)}, u32[]{:S(2)}, u32[]{:S(2)}) collective-permute-start(bf16[2,64,384]{2,1,0:T(8,128)(2,1)} %get-tuple-element.100), channel_id=1, source_target_pairs={{0,8},{8,0},{16,24},{24,16},{1,9},{9,1},{17,25},{25,17},{2,10},{10... | collective-permute-start | bytes 294920 | tf_op jit(solution)/shard_map/ppermute | solution.py:470
  96.1 5.0 %collective-permute-start.14 = (bf16[2,32,384]{2,1,0:T(8,128)(2,1)}, bf16[2,32,384]{2,1,0:T(8,128)(2,1)S(1)}, u32[]{:S(2)}, u32[]{:S(2)}) collective-permute-start(bf16[2,32,384]{2,1,0:T(8,128)(2,1)} %get-tuple-element.101), channel_id=1, source_target_pairs={{0,16},{8,24},{16,0},{24,8},{1,17},{9,25},{17,1},{25,9},{2,18},{10... | collective-permute-start | bytes 147464 | tf_op jit(solution)/shard_map/ppermute | solution.py:470
  98.0 4.4 %collective-permute-start.15 = (bf16[2,32,384]{2,1,0:T(8,128)(2,1)}, bf16[2,32,384]{2,1,0:T(8,128)(2,1)S(1)}, u32[]{:S(2)}, u32[]{:S(2)}) collective-permute-start(bf16[2,32,384]{2,1,0:T(8,128)(2,1)} %get-tuple-element.102), channel_id=1, source_target_pairs={{0,24},{8,16},{16,8},{24,0},{1,25},{9,17},{17,9},{25,1},{2,26},{10... | collective-permute-start | bytes 147464 | tf_op jit(solution)/shard_map/ppermute | solution.py:470
  99.9 2.4 %copy-start.13 = (bf16[2,128,384]{2,1,0:T(8,128)(2,1)}, bf16[2,128,384]{2,1,0:T(8,128)(2,1)S(1)}, u32[]{:S(2)}) copy-start(bf16[2,128,384]{2,1,0:T(8,128)(2,1)S(1)} %collective-permute-done.10.dy) | copy-start | bytes 589828
  101.0 1.3 copy-start.21
  109.3 6.1 %copy-start.27 = (bf16[256,1152]{1,0:T(8,128)(2,1)S(1)}, bf16[256,1152]{1,0:T(8,128)(2,1)}, u32[]{:S(2)}) copy-start(bf16[256,1152]{1,0:T(8,128)(2,1)} %get-tuple-element.118) | copy-start | bytes 1769476
  109.3 22.8 %all-to-all-start.4 = ((bf16[16,96,384]{2,1,0:T(8,128)(2,1)}), bf16[16,96,384]{2,1,0:T(8,128)(2,1)S(1)}, u32[]{:S(2)}, u32[]{:S(2)}) async-start(bf16[16,96,384]{2,1,0:T(8,128)(2,1)} %bitcast.15), calls=%async_computation.4 | async-start | bytes 2359296 | tf_op jit(solution)/shard_map/all_to_all | solution.py:512
  115.5 10.8 %collective-permute-start.19 = (bf16[256,1152]{1,0:T(8,128)(2,1)S(1)}, bf16[256,1152]{1,0:T(8,128)(2,1)S(1)}, u32[]{:S(2)}, u32[]{:S(2)}) collective-permute-start(bf16[256,1152]{1,0:T(8,128)(2,1)S(1)} %copy-done.27), channel_id=1, source_target_pairs={{0,2},{2,0},{1,3},{3,1},{4,6},{6,4},{5,7},{7,5},{8,10},{10,8},{9,1... | collective-permute-start | bytes 1769480 | tf_op jit(solution)/shard_map/ppermute | solution.py:466
  122.2 14.0 %collective-permute-start.16 = (bf16[96,384]{1,0:T(8,128)(2,1)}, bf16[96,384]{1,0:T(8,128)(2,1)S(1)}, u32[]{:S(2)}, u32[]{:S(2)}) collective-permute-start(bf16[96,384]{1,0:T(8,128)(2,1)} %get-tuple-element.113), channel_id=1, source_target_pairs={{0,1},{1,0},{4,5},{5,4},{2,3},{3,2},{6,7},{7,6},{8,9},{9,8},{12,13... | collective-permute-start | bytes 221192 | tf_op jit(solution)/shard_map/ppermute | solution.py:470
  125.3 12.3 %collective-permute-start.17 = (bf16[96,384]{1,0:T(8,128)(2,1)}, bf16[96,384]{1,0:T(8,128)(2,1)S(1)}, u32[]{:S(2)}, u32[]{:S(2)}) collective-permute-start(bf16[96,384]{1,0:T(8,128)(2,1)} %get-tuple-element.114), channel_id=1, source_target_pairs={{0,4},{1,5},{4,0},{5,1},{2,6},{3,7},{6,2},{7,3},{8,12},{9,13},{12,... | collective-permute-start | bytes 221192 | tf_op jit(solution)/shard_map/ppermute | solution.py:470
  125.6 12.0 %collective-permute-start.18 = (bf16[96,384]{1,0:T(8,128)(2,1)}, bf16[96,384]{1,0:T(8,128)(2,1)S(1)}, u32[]{:S(2)}, u32[]{:S(2)}) collective-permute-start(bf16[96,384]{1,0:T(8,128)(2,1)} %get-tuple-element.115), channel_id=1, source_target_pairs={{0,5},{1,4},{4,1},{5,0},{2,7},{3,6},{6,3},{7,2},{8,13},{9,12},{12,... | collective-permute-start | bytes 221192 | tf_op jit(solution)/shard_map/ppermute | solution.py:470
  132.2 5.4 %copy-start = (bf16[16,96,384]{2,1,0:T(8,128)(2,1)}, bf16[16,96,384]{2,1,0:T(8,128)(2,1)S(1)}, u32[]{:S(2)}) copy-start(bf16[16,96,384]{2,1,0:T(8,128)(2,1)S(1)} %all-to-all-done.4.second) | copy-start | bytes 3538948
  136.2 1.4 copy-start.18
  141.4 13.9 %all-to-all-start.5 = ((bf16[8,2,16,384]{3,2,1,0:T(8,128)(2,1)}), bf16[8,2,16,384]{3,2,1,0:T(8,128)(2,1)S(1)}, u32[]{:S(2)}, u32[]{:S(2)}) async-start(bf16[8,2,16,384]{3,2,1,0:T(8,128)(2,1)} %shard_map.93), calls=%async_computation.5 | async-start | bytes 393216 | tf_op jit(solution)/shard_map/all_to_all | solution.py:516
  155.3 9.4 %copy-start.23 = (bf16[16,384]{1,0:T(8,128)(2,1)}, bf16[16,384]{1,0:T(8,128)(2,1)S(1)}, u32[]{:S(2)}) copy-start(bf16[16,384]{1,0:T(8,128)(2,1)S(1)} %get-tuple-element.129.own) | copy-start | bytes 36868
  155.4 6.7 %collective-permute-start.22 = (bf16[16,384]{1,0:T(8,128)(2,1)S(1)}, bf16[16,384]{1,0:T(8,128)(2,1)S(1)}, u32[]{:S(2)}, u32[]{:S(2)}) collective-permute-start(bf16[16,384]{1,0:T(8,128)(2,1)S(1)} %get-tuple-element.128), channel_id=1, source_target_pairs={{0,3},{1,2},{2,1},{3,0},{4,7},{5,6},{6,5},{7,4},{8,11},{9,10},{10,... | collective-permute-start | bytes 36872 | tf_op jit(solution)/shard_map/ppermute | solution.py:470
  160.6 1.4 collective-permute-start.21
  160.6 4.0 %collective-permute-start.20 = (bf16[16,384]{1,0:T(8,128)(2,1)S(1)}, bf16[16,384]{1,0:T(8,128)(2,1)S(1)}, u32[]{:S(2)}, u32[]{:S(2)}) collective-permute-start(bf16[16,384]{1,0:T(8,128)(2,1)S(1)} %get-tuple-element.129.own), channel_id=1, source_target_pairs={{0,1},{1,0},{2,3},{3,2},{4,5},{5,4},{6,7},{7,6},{8,9},{9,8},{10,11... | collective-permute-start | bytes 36872 | tf_op jit(solution)/shard_map/ppermute | solution.py:470
  162.0 2.7 %copy-start.24 = (bf16[16,384]{1,0:T(8,128)(2,1)}, bf16[16,384]{1,0:T(8,128)(2,1)S(1)}, u32[]{:S(2)}) copy-start(bf16[16,384]{1,0:T(8,128)(2,1)S(1)} %collective-permute-done.22.from_both) | copy-start | bytes 36868
  162.0 2.7 %copy-start.25 = (bf16[16,384]{1,0:T(8,128)(2,1)}, bf16[16,384]{1,0:T(8,128)(2,1)S(1)}, u32[]{:S(2)}) copy-start(bf16[16,384]{1,0:T(8,128)(2,1)S(1)} %collective-permute-done.21.from_core) | copy-start | bytes 36868
  (11 other events, 8.4 us)

commit v12 on v11

--- a/solution.py
+++ b/solution.py
@@ -500,7 +500,7 @@
     dwy = swap(dwy, "y")
     first, *firsts = output_terms(pos, att, att_oth, ct_own, ct_oth, dq, xt, perm)
     firsts = [along(firsts[far - 1], "x", far) for far in (1, 2, 3)]
-    dx_r, first, firsts[0], dwy = lax.optimization_barrier((dx_r, first, firsts[0], dwy))
+    dx_r, first, dwy = lax.optimization_barrier((dx_r, first, dwy))
     dz, g3, g4_a, g4_b = back_slots(pos, dx_r, dw, dwy)
     dz_r = lax.all_to_all(dz, "z", 0, 0)
     g3, g4_a, g4_b, firsts = lax.optimization_barrier((g3, g4_a, g4_b, firsts))

time: 168 us -> 168 us (level)
  waiting for transfers between devices: 30 us -> 28.1 us
    ppermute x8, waiting for transfers between devices: 3.48 us -> 1.41 us  [swap(): return lax.ppermute(value, axis, [(0, 1), (1, 0)])]
    unnamed x60 -> x62, local copies, waits for them, and re-layouts: 5.2 us -> 6.09 us
  transfers between devices with their start and end apart: 29 -> 29, of which waited for: 16 -> 15; matrix products, arithmetic and copies ran while one was open for 0% -> 0% of each run, Pallas kernels for 19% -> 19%
where the time goes in v12:
time: 168 us; the launch traced here: 167 us
  starting transfers between devices  71.4 us (43%)
  Pallas kernels  60.3 us (36%)
  waiting for transfers between devices  28.1 us (17%)
  local copies, waits for them, and re-layouts  6.09 us (4%)
    ppermute x15, starting transfers between devices, along(): return lax.ppermute(value, axes, [(i, i ^ far) for i in range(count)])  21.4 us
    ppermute x15, waiting for transfers between devices, along(): return lax.ppermute(value, axes, [(i, i ^ far) for i in range(count)])  19.2 us
    ppermute x8, starting transfers between devices, swap(): return lax.ppermute(value, axis, [(0, 1), (1, 0)])  17.5 us
    pallas_call x1, Pallas kernels, attention(): call(attention_body, (H // 128,), [cut(2, TOK), cut(2, TOK), cut(2, 2, TO...  16.8 us
    all_to_all x1, starting transfers between devices, shards(): zr = lax.all_to_all(zs, 'z', 0, 0)  6.45 us
    all_to_all x1, starting transfers between devices, shards(): terms = lax.all_to_all(terms.reshape(16, 96, H), ('x', 'y', 'dp'), 0, 0)  6.4 us
    pallas_call x1, Pallas kernels, leaf_grads(): call(leaf_body, (1,), [whole(ZN, 2, 16, H), whole(2, 2, TOK, H), whole(2,...  6.26 us
    unnamed x62, local copies, waits for them, and re-layouts  6.09 us
  transfers between devices with their start and end apart: 29, of which 15 were waited for; matrix products, arithmetic and copies ran while one was open for 0% of the time, Pallas kernels for 19%

profile of v12, /device:TPU:1, one launch (start us, length us, event | category | flops | bytes accessed | tf_op | source)
XLA Modules:
  0.0 167.5 jit_solution(15307228700150497746)
XLA Ops:
  0.6 3.3 %collective-permute-start = (bf16[256,768]{1,0:T(8,128)(2,1)}, bf16[256,768]{1,0:T(8,128)(2,1)S(1)}, u32[]{:S(2)}, u32[]{:S(2)}) collective-permute-start(bf16[256,768]{1,0:T(8,128)(2,1)} %bitcast.9), channel_id=1, source_target_pairs={{0,2},{2,0},{1,3},{3,1},{4,6},{6,4},{5,7},{7,5},{8,10},{10,8},{9,1... | collective-permute-start | bytes 1179656 | tf_op jit(solution)/shard_map/ppermute | solution.py:466
  4.7 0.8 collective-permute-done.x_oth
  5.5 0.7 copy-done.3
  6.3 4.5 %shard_map.84 = (bf16[2,2,256,384]{3,2,1,0:T(8,128)(2,1)}, bf16[2,2,128,384]{3,2,1,0:T(8,128)(2,1)}, bf16[2,128,384]{2,1,0:T(8,128)(2,1)}, bf16[2,64,384]{2,1,0:...) custom-call(s32[4]{0:T(128)} %pad_add_fusion.pos, bf16[256,768]{1,0:T(8,128)(2,1)} %bitcast.10, ...), custom_call_target="tpu_custom_call" | custom-call | tf_op jit(solution)/shard_map/pallas_call | solution.py:113
  10.7 6.5 %all-to-all-start = ((bf16[8,2,16,384]{3,2,1,0:T(8,128)(2,1)}), bf16[8,2,16,384]{3,2,1,0:T(8,128)(2,1)S(1)}, u32[]{:S(2)}, u32[]{:S(2)}) async-start(bf16[8,2,16,384]{3,2,1,0:T(8,128)(2,1)} %get-tuple-element.65), calls=%async_computation | async-start | bytes 393216 | tf_op jit(solution)/shard_map/all_to_all | solution.py:490
  17.2 1.2 collective-permute-start.2
  18.4 1.3 collective-permute-start.1
  19.7 1.8 %collective-permute-start.4 = (bf16[2,32,384]{2,1,0:T(8,128)(2,1)}, bf16[2,32,384]{2,1,0:T(8,128)(2,1)S(1)}, u32[]{:S(2)}, u32[]{:S(2)}) collective-permute-start(bf16[2,32,384]{2,1,0:T(8,128)(2,1)} %get-tuple-element.68), channel_id=1, source_target_pairs={{0,24},{8,16},{16,8},{24,0},{1,25},{9,17},{17,9},{25,1},{2,26},{10... | collective-permute-start | bytes 147464 | tf_op jit(solution)/shard_map/ppermute | solution.py:470
  22.1 2.2 %collective-permute-done.4 = bf16[2,32,384]{2,1,0:T(8,128)(2,1)S(1)} collective-permute-done((bf16[2,32,384]{2,1,0:T(8,128)(2,1)}, bf16[2,32,384]{2,1,0:T(8,128)(2,1)S(1)}, u32[]{:S(2)}, u32[]{:S(2)}) %collective-permute-start.4) | collective-permute-done | bytes 49184 | tf_op jit(solution)/shard_map/ppermute | solution.py:470
  24.3 1.9 %collective-permute-done.3 = bf16[2,32,384]{2,1,0:T(8,128)(2,1)S(1)} collective-permute-done((bf16[2,32,384]{2,1,0:T(8,128)(2,1)}, bf16[2,32,384]{2,1,0:T(8,128)(2,1)S(1)}, u32[]{:S(2)}, u32[]{:S(2)}) %collective-permute-start.3) | collective-permute-done | bytes 49184 | tf_op jit(solution)/shard_map/ppermute | solution.py:470
  26.6 1.3 collective-permute-start.6
  27.9 2.6 %shard_map.86 = bf16[8,2,48,384]{3,2,1,0:T(8,128)(2,1)} custom-call(s32[4]{0:T(128)} %pad_add_fusion.pos, bf16[8,2,16,384]{3,2,1,0:T(8,128)(2,1)} %copy-done.8), custom_call_target="tpu_custom_call" | custom-call | tf_op jit(solution)/shard_map/pallas_call | solution.py:159
  31.1 5.0 %all-to-all-start.1 = ((bf16[8,2,48,384]{3,2,1,0:T(8,128)(2,1)}), bf16[8,2,48,384]{3,2,1,0:T(8,128)(2,1)S(1)}, u32[]{:S(2)}, u32[]{:S(2)}) async-start(bf16[8,2,48,384]{3,2,1,0:T(8,128)(2,1)} %shard_map.86), calls=%async_computation.1 | async-start | bytes 1179648 | tf_op jit(solution)/shard_map/all_to_all | solution.py:494
  36.2 5.2 %shard_map.85 = (bf16[2,256,384]{2,1,0:T(8,128)(2,1)}, bf16[2,256,384]{2,1,0:T(8,128)(2,1)}, bf16[2,768,256]{2,1,0:T(8,128)(2,1)}) custom-call(s32[4]{0:T(128)} %pad_add_fusion.pos, bf16[256,768]{1,0:T(8,128)(2,1)} %bitcast.11, bf16[256,768]{1,0:T(8,128)(2,1)} %copy-done.3, bf16[256,768]{1,0:T(8,128)(2,1)} %bitcast.13, bf16[256,768]{1,0:T(8,128)(2,1)} %copy-done.6, ...), custom_call_target="tpu_custom_call" | custom-call | tf_op jit(solution)/shard_map/pallas_call | solution.py:132
  41.4 2.3 %all-to-all-done.1.xr = bf16[8,2,48,384]{3,2,1,0:T(8,128)(2,1)S(1)} async-done(((bf16[8,2,48,384]{3,2,1,0:T(8,128)(2,1)}), bf16[8,2,48,384]{3,2,1,0:T(8,128)(2,1)S(1)}, u32[]{:S(2)}, u32[]{:S(2)}) %all-to-all-start.1) | async-done | bytes 589856 | tf_op jit(solution)/shard_map/all_to_all | solution.py:494
  43.7 0.8 copy-done.2
  44.6 16.8 %shard_map.87 = (bf16[2,256,384]{2,1,0:T(8,128)(2,1)}, bf16[2,256,384]{2,1,0:T(8,128)(2,1)}, f32[2,2,256,384]{3,2,1,0:T(8,128)}, f32[2,2,128,384]{3,2,1,0:T(8,12...) custom-call(s32[4]{0:T(128)} %pad_add_fusion.pos, ...), custom_call_target="tpu_custom_call" | custom-call | tf_op jit(solution)/shard_map/pallas_call | solution.py:246
  61.4 3.7 %all-to-all-start.2 = ((bf16[8,2,48,384]{3,2,1,0:T(8,128)(2,1)}), bf16[8,2,48,384]{3,2,1,0:T(8,128)(2,1)S(1)}, u32[]{:S(2)}, u32[]{:S(2)}) async-start(bf16[8,2,48,384]{3,2,1,0:T(8,128)(2,1)} %get-tuple-element.79), calls=%async_computation.2 | async-start | bytes 1179648 | tf_op jit(solution)/shard_map/all_to_all | solution.py:498
  65.1 4.7 %collective-permute-start.7 = (bf16[2,256,384]{2,1,0:T(8,128)(2,1)S(1)}, bf16[2,256,384]{2,1,0:T(8,128)(2,1)S(1)}, u32[]{:S(2)}, u32[]{:S(2)}) collective-permute-start(bf16[2,256,384]{2,1,0:T(8,128)(2,1)S(1)} %copy-done.4), channel_id=1, source_target_pairs={{0,2},{2,0},{1,3},{3,1},{4,6},{6,4},{5,7},{7,5},{8,10},{10,8},{9,1... | collective-permute-start | bytes 1179656 | tf_op jit(solution)/shard_map/ppermute | solution.py:466
  69.8 1.4 collective-permute-start.8
  71.2 0.8 copy-done.5
  72.0 5.4 %shard_map.88 = (bf16[2,2,96,384]{3,2,1,0:T(8,128)(2,1)}, bf16[2,2,96,384]{3,2,1,0:T(8,128)(2,1)}, bf16[2,2,96,384]{3,2,1,0:T(8,128)(2,1)}, bf16[2,2,96,384]{3,2,1,0:T(8,128)(2,1)}) custom-call(s32[4]{0:T(128)} %pad_add_fusion.pos, bf16[2,256,384]{2,1,0:T(8,128)(2,1)} %get-tuple-element.119.att_own, bf16[2,256,384]{2,1,0:T(8,128)(2,1)} %copy-done.5, ...), custom_call_target="tpu_custom_call" | custom-call | tf_op jit(solution)/shard_map/pallas_call | solution.py:292
  77.4 1.3 collective-permute-start.10
  78.8 2.4 %collective-permute-start.11 = (bf16[2,2,96,384]{3,2,1,0:T(8,128)(2,1)}, bf16[2,2,96,384]{3,2,1,0:T(8,128)(2,1)S(1)}, u32[]{:S(2)}, u32[]{:S(2)}) collective-permute-start(bf16[2,2,96,384]{3,2,1,0:T(8,128)(2,1)} %get-tuple-element.96), channel_id=1, source_target_pairs={{0,16},{8,24},{16,0},{24,8},{1,17},{9,25},{17,1},{25,9},{2,18},{10... | collective-permute-start | bytes 884744 | tf_op jit(solution)/shard_map/ppermute | solution.py:470
  82.2 2.8 %shard_map.89 = (bf16[8,2,16,384]{3,2,1,0:T(8,128)(2,1)}, bf16[2,64,384]{2,1,0:T(8,128)(2,1)}, bf16[2,32,384]{2,1,0:T(8,128)(2,1)}, bf16[2,32,384]{2,1,0:T(8,128)(2,1)}) custom-call(s32[4]{0:T(128)} %pad_add_fusion.pos, bf16[8,2,48,384]{3,2,1,0:T(8,128)(2,1)} %copy-done.1, f32[2,128,384]{2,1,0:T(8,128)} %get-tuple-element.86.dw, bf16[2,128,384]{2,1,0:T(8,128)(2,1)} %copy-done.15), custom_call_target="tpu_custom_call" | custom-call | tf_op jit(solution)/shard_map/pallas_call | solution.py:338
  85.0 5.5 %all-to-all-start.3 = ((bf16[8,2,16,384]{3,2,1,0:T(8,128)(2,1)}), bf16[8,2,16,384]{3,2,1,0:T(8,128)(2,1)S(1)}, u32[]{:S(2)}, u32[]{:S(2)}) async-start(bf16[8,2,16,384]{3,2,1,0:T(8,128)(2,1)} %get-tuple-element.88), calls=%async_computation.3 | async-start | bytes 393216 | tf_op jit(solution)/shard_map/all_to_all | solution.py:505
  90.4 1.4 collective-permute-start.9
  91.9 2.6 %collective-permute-done.11.t2 = bf16[2,2,96,384]{3,2,1,0:T(8,128)(2,1)S(1)} collective-permute-done((bf16[2,2,96,384]{3,2,1,0:T(8,128)(2,1)}, bf16[2,2,96,384]{3,2,1,0:T(8,128)(2,1)S(1)}, u32[]{:S(2)}, u32[]{:S(2)}) %collective-permute-start.11) | collective-permute-done | bytes 294944 | tf_op jit(solution)/shard_map/ppermute | solution.py:470
  94.5 2.0 %collective-permute-done.12.t3 = bf16[2,2,96,384]{3,2,1,0:T(8,128)(2,1)S(1)} collective-permute-done((bf16[2,2,96,384]{3,2,1,0:T(8,128)(2,1)}, bf16[2,2,96,384]{3,2,1,0:T(8,128)(2,1)S(1)}, u32[]{:S(2)}, u32[]{:S(2)}) %collective-permute-start.12) | collective-permute-done | bytes 294944 | tf_op jit(solution)/shard_map/ppermute | solution.py:470
  96.5 1.3 collective-permute-start.14
  97.8 2.5 %collective-permute-start.15 = (bf16[2,32,384]{2,1,0:T(8,128)(2,1)}, bf16[2,32,384]{2,1,0:T(8,128)(2,1)S(1)}, u32[]{:S(2)}, u32[]{:S(2)}) collective-permute-start(bf16[2,32,384]{2,1,0:T(8,128)(2,1)} %get-tuple-element.100), channel_id=1, source_target_pairs={{0,24},{8,16},{16,8},{24,0},{1,25},{9,17},{17,9},{25,1},{2,26},{10... | collective-permute-start | bytes 147464 | tf_op jit(solution)/shard_map/ppermute | solution.py:470
  100.4 1.1 collective-permute-done.14.g4_a
  102.9 6.3 %shard_map.90 = (bf16[256,1152]{1,0:T(8,128)(2,1)}, bf16[256,1152]{1,0:T(8,128)(2,1)}, bf16[8,2,96,384]{3,2,1,0:T(8,128)(2,1)}) custom-call(s32[4]{0:T(128)} %pad_add_fusion.pos, bf16[8,2,16,384]{3,2,1,0:T(8,128)(2,1)} %copy-done.7, f32[2,2,256,384]{3,2,1,0:T(8,128)} %get-tuple-element.89.dkv, f32[2,2,128,384]{3,2,1,0:T(8,128)} %get-tuple-element.90.dn1, ...), custom_call_target="tpu_custom_call" | custom-call | tf_op jit(solution)/shard_map/pallas_call | solution.py:383
  109.2 6.4 %all-to-all-start.4 = ((bf16[16,96,384]{2,1,0:T(8,128)(2,1)}), bf16[16,96,384]{2,1,0:T(8,128)(2,1)S(1)}, u32[]{:S(2)}, u32[]{:S(2)}) async-start(bf16[16,96,384]{2,1,0:T(8,128)(2,1)} %bitcast.15), calls=%async_computation.4 | async-start | bytes 2359296 | tf_op jit(solution)/shard_map/all_to_all | solution.py:512
  115.6 3.9 %collective-permute-start.19 = (bf16[256,1152]{1,0:T(8,128)(2,1)S(1)}, bf16[256,1152]{1,0:T(8,128)(2,1)S(1)}, u32[]{:S(2)}, u32[]{:S(2)}) collective-permute-start(bf16[256,1152]{1,0:T(8,128)(2,1)S(1)} %copy-done.28), channel_id=1, source_target_pairs={{0,2},{2,0},{1,3},{3,1},{4,6},{6,4},{5,7},{7,5},{8,10},{10,8},{9,1... | collective-permute-start | bytes 1769480 | tf_op jit(solution)/shard_map/ppermute | solution.py:466
  119.6 2.8 %shard_map.91 = (bf16[96,384]{1,0:T(8,128)(2,1)}, bf16[96,384]{1,0:T(8,128)(2,1)}, bf16[96,384]{1,0:T(8,128)(2,1)}, bf16[96,384]{1,0:T(8,128)(2,1)}) custom-call(s32[4]{0:T(128)} %pad_add_fusion.pos, bf16[2,2,96,384]{3,2,1,0:T(8,128)(2,1)} %get-tuple-element.106.t0, bf16[2,2,96,384]{3,2,1,0:T(8,128)(2,1)} %copy-done.11, bf16[2,2,96,384]{3,2,1,0:T(8,128)(2,1)} %copy-done.12, ...), custom_call_target="tpu_custom_call" | custom-call | tf_op jit(solution)/shard_map/pallas_call | solution.py:312
  122.4 3.1 %collective-permute-start.16 = (bf16[96,384]{1,0:T(8,128)(2,1)}, bf16[96,384]{1,0:T(8,128)(2,1)S(1)}, u32[]{:S(2)}, u32[]{:S(2)}) collective-permute-start(bf16[96,384]{1,0:T(8,128)(2,1)} %get-tuple-element.111), channel_id=1, source_target_pairs={{0,1},{1,0},{4,5},{5,4},{2,3},{3,2},{6,7},{7,6},{8,9},{9,8},{12,13... | collective-permute-start | bytes 221192 | tf_op jit(solution)/shard_map/ppermute | solution.py:470
  126.4 0.8 copy-done.10
  127.3 5.1 %shard_map.92 = bf16[256,768]{1,0:T(8,128)(2,1)} custom-call(s32[4]{0:T(128)} %pad_add_fusion.pos, bf16[256,1152]{1,0:T(8,128)(2,1)} %get-tuple-element.115.pg_own, bf16[256,1152]{1,0:T(8,128)(2,1)} %copy-done.10, bf16[768,2304]{1,0:T(8,128)(2,1)} %rest_5_.1, bf16[768,2304]{1,0:T(8,128)(2,1)} %rest_5_.1, bf16[768,2304]{1,0:T(8,128)(2,1)} %rest_5_.1, ...), custom_call_target="tpu_custom_call" | custom-call | tf_op jit(solution)/shard_map/pallas_call | solution.py:406
  132.4 4.0 %collective-permute-done.16.f1 = bf16[96,384]{1,0:T(8,128)(2,1)S(1)} collective-permute-done((bf16[96,384]{1,0:T(8,128)(2,1)}, bf16[96,384]{1,0:T(8,128)(2,1)S(1)}, u32[]{:S(2)}, u32[]{:S(2)}) %collective-permute-start.16) | collective-permute-done | bytes 73760 | tf_op jit(solution)/shard_map/ppermute | solution.py:470
  136.4 1.3 collective-permute-done.17.f2
  138.4 3.2 %shard_map.93 = bf16[8,2,16,384]{3,2,1,0:T(8,128)(2,1)} custom-call(s32[4]{0:T(128)} %pad_add_fusion.pos, bf16[96,384]{1,0:T(8,128)(2,1)} %get-tuple-element.110.f0, bf16[96,384]{1,0:T(8,128)(2,1)} %copy-done.19, bf16[96,384]{1,0:T(8,128)(2,1)} %copy-done.20, bf16[96,384]{1,0:T(8,128)(2,1)} %copy-done.21, bf16[16,96,384]{2,1,0:T(8,128)(2,1)} %copy-done), custom_call_target="tpu_custom_call" | custom-call | tf_op jit(solution)/shard_map/pallas_call | solution.py:435
  141.6 5.5 %all-to-all-start.5 = ((bf16[8,2,16,384]{3,2,1,0:T(8,128)(2,1)}), bf16[8,2,16,384]{3,2,1,0:T(8,128)(2,1)S(1)}, u32[]{:S(2)}, u32[]{:S(2)}) async-start(bf16[8,2,16,384]{3,2,1,0:T(8,128)(2,1)} %shard_map.93), calls=%async_computation.5 | async-start | bytes 393216 | tf_op jit(solution)/shard_map/all_to_all | solution.py:516
  147.0 3.5 %shard_map.94 = bf16[256,768]{1,0:T(8,128)(2,1)} custom-call(s32[4]{0:T(128)} %pad_add_fusion.pos, bf16[2,256,384]{2,1,0:T(8,128)(2,1)} %get-tuple-element.119.att_own, bf16[2,256,384]{2,1,0:T(8,128)(2,1)} %copy-done.5, bf16[768,768]{1,0:T(8,128)(2,1)} %w_oth.1, bf16[768,768]{1,0:T(8,128)(2,1)} %w_oth.1), custom_call_target="tpu_custom_call" | custom-call | tf_op jit(solution)/shard_map/pallas_call | solution.py:266
  150.5 4.9 %all-to-all-done.5 = bf16[8,2,16,384]{3,2,1,0:T(8,128)(2,1)S(1)} async-done(((bf16[8,2,16,384]{3,2,1,0:T(8,128)(2,1)}), bf16[8,2,16,384]{3,2,1,0:T(8,128)(2,1)S(1)}, u32[]{:S(2)}, u32[]{:S(2)}) %all-to-all-start.5) | async-done | bytes 196640 | tf_op jit(solution)/shard_map/all_to_all | solution.py:516
  155.5 5.3 %collective-permute-start.22 = (bf16[16,384]{1,0:T(8,128)(2,1)S(1)}, bf16[16,384]{1,0:T(8,128)(2,1)S(1)}, u32[]{:S(2)}, u32[]{:S(2)}) collective-permute-start(bf16[16,384]{1,0:T(8,128)(2,1)S(1)} %get-tuple-element.126), channel_id=1, source_target_pairs={{0,3},{1,2},{2,1},{3,0},{4,7},{5,6},{6,5},{7,4},{8,11},{9,10},{10,... | collective-permute-start | bytes 36872 | tf_op jit(solution)/shard_map/ppermute | solution.py:470
  162.1 2.7 %collective-permute-done.20.from_dp = bf16[16,384]{1,0:T(8,128)(2,1)S(1)} collective-permute-done((bf16[16,384]{1,0:T(8,128)(2,1)S(1)}, bf16[16,384]{1,0:T(8,128)(2,1)S(1)}, u32[]{:S(2)}, u32[]{:S(2)}) %collective-permute-start.20) | collective-permute-done | bytes 12320 | tf_op jit(solution)/shard_map/ppermute | solution.py:470
  165.4 2.1 %shard_map.95 = (f32[6,2304]{1,0:T(8,128)}, f32[6,768]{1,0:T(8,128)}) custom-call(s32[4]{0:T(128)} %pad_add_fusion.pos, bf16[16,384]{1,0:T(8,128)(2,1)} %copy-done.24, bf16[16,384]{1,0:T(8,128)(2,1)} %copy-done.27, bf16[16,384]{1,0:T(8,128)(2,1)} %copy-done.26, bf16[16,384]{1,0:T(8,128)(2,1)} %copy-done.25), custom_call_target="tpu_custom_call" | custom-call | tf_op jit(solution)/shard_map/pallas_call | solution.py:456
  (87 shorter events, 8.4 us)
Async XLA Ops:
  0.6 4.9 %collective-permute-start = (bf16[256,768]{1,0:T(8,128)(2,1)}, bf16[256,768]{1,0:T(8,128)(2,1)S(1)}, u32[]{:S(2)}, u32[]{:S(2)}) collective-permute-start(bf16[256,768]{1,0:T(8,128)(2,1)} %bitcast.9), channel_id=1, source_target_pairs={{0,2},{2,0},{1,3},{3,1},{4,6},{6,4},{5,7},{7,5},{8,10},{10,8},{9,1... | collective-permute-start | bytes 1179656 | tf_op jit(solution)/shard_map/ppermute | solution.py:466
  4.0 22.3 %collective-permute-start.5 = (bf16[256,768]{1,0:T(8,128)(2,1)}, bf16[256,768]{1,0:T(8,128)(2,1)S(1)}, u32[]{:S(2)}, u32[]{:S(2)}) collective-permute-start(bf16[256,768]{1,0:T(8,128)(2,1)} %bitcast.12), channel_id=1, source_target_pairs={{0,2},{2,0},{1,3},{3,1},{4,6},{6,4},{5,7},{7,5},{8,10},{10,8},{9,1... | collective-permute-start | bytes 1179656 | tf_op jit(solution)/shard_map/ppermute | solution.py:466
  10.7 15.9 %all-to-all-start = ((bf16[8,2,16,384]{3,2,1,0:T(8,128)(2,1)}), bf16[8,2,16,384]{3,2,1,0:T(8,128)(2,1)S(1)}, u32[]{:S(2)}, u32[]{:S(2)}) async-start(bf16[8,2,16,384]{3,2,1,0:T(8,128)(2,1)} %get-tuple-element.65), calls=%async_computation | async-start | bytes 393216 | tf_op jit(solution)/shard_map/all_to_all | solution.py:490
  17.2 9.1 %collective-permute-start.2 = (bf16[2,64,384]{2,1,0:T(8,128)(2,1)}, bf16[2,64,384]{2,1,0:T(8,128)(2,1)S(1)}, u32[]{:S(2)}, u32[]{:S(2)}) collective-permute-start(bf16[2,64,384]{2,1,0:T(8,128)(2,1)} %get-tuple-element.67), channel_id=1, source_target_pairs={{0,8},{8,0},{16,24},{24,16},{1,9},{9,1},{17,25},{25,17},{2,10},{10... | collective-permute-start | bytes 294920 | tf_op jit(solution)/shard_map/ppermute | solution.py:470
  18.4 7.9 %collective-permute-start.1 = (bf16[2,128,384]{2,1,0:T(8,128)(2,1)}, bf16[2,128,384]{2,1,0:T(8,128)(2,1)S(1)}, u32[]{:S(2)}, u32[]{:S(2)}) collective-permute-start(bf16[2,128,384]{2,1,0:T(8,128)(2,1)} %get-tuple-element.66), channel_id=1, source_target_pairs={{0,4},{4,0},{1,5},{5,1},{2,6},{6,2},{3,7},{7,3},{8,12},{12,8},{9,1... | collective-permute-start | bytes 589832 | tf_op jit(solution)/shard_map/ppermute | solution.py:466
  19.7 4.7 %collective-permute-start.4 = (bf16[2,32,384]{2,1,0:T(8,128)(2,1)}, bf16[2,32,384]{2,1,0:T(8,128)(2,1)S(1)}, u32[]{:S(2)}, u32[]{:S(2)}) collective-permute-start(bf16[2,32,384]{2,1,0:T(8,128)(2,1)} %get-tuple-element.68), channel_id=1, source_target_pairs={{0,24},{8,16},{16,8},{24,0},{1,25},{9,17},{17,9},{25,1},{2,26},{10... | collective-permute-start | bytes 147464 | tf_op jit(solution)/shard_map/ppermute | solution.py:470
  21.5 4.7 %collective-permute-start.3 = (bf16[2,32,384]{2,1,0:T(8,128)(2,1)}, bf16[2,32,384]{2,1,0:T(8,128)(2,1)S(1)}, u32[]{:S(2)}, u32[]{:S(2)}) collective-permute-start(bf16[2,32,384]{2,1,0:T(8,128)(2,1)} %get-tuple-element.68), channel_id=1, source_target_pairs={{0,16},{8,24},{16,0},{24,8},{1,17},{9,25},{17,1},{25,9},{2,18},{10... | collective-permute-start | bytes 147464 | tf_op jit(solution)/shard_map/ppermute | solution.py:470
  26.3 15.1 %copy-start.9 = (bf16[2,128,384]{2,1,0:T(8,128)(2,1)}, bf16[2,128,384]{2,1,0:T(8,128)(2,1)S(1)}, u32[]{:S(2)}) copy-start(bf16[2,128,384]{2,1,0:T(8,128)(2,1)S(1)} %pad_maximum_fusion.wr) | copy-start | bytes 589828
  26.3 9.9 %copy-start.6 = (bf16[256,768]{1,0:T(8,128)(2,1)}, bf16[256,768]{1,0:T(8,128)(2,1)S(1)}, u32[]{:S(2)}) copy-start(bf16[256,768]{1,0:T(8,128)(2,1)S(1)} %collective-permute-done.5.ct_oth) | copy-start | bytes 1179652
  26.3 15.1 %copy-start.16 = (bf16[2,128,384]{2,1,0:T(8,128)(2,1)}, bf16[2,128,384]{2,1,0:T(8,128)(2,1)S(1)}, u32[]{:S(2)}) copy-start(bf16[2,128,384]{2,1,0:T(8,128)(2,1)S(1)} %collective-permute-done.1.yr) | copy-start | bytes 589828
  26.6 1.3 copy-start.8
  26.6 4.5 %collective-permute-start.6 = (bf16[2,128,384]{2,1,0:T(8,128)(2,1)S(1)}, bf16[2,128,384]{2,1,0:T(8,128)(2,1)S(1)}, u32[]{:S(2)}, u32[]{:S(2)}) collective-permute-start(bf16[2,128,384]{2,1,0:T(8,128)(2,1)S(1)} %pad_maximum_fusion.wr), channel_id=1, source_target_pairs={{0,4},{4,0},{1,5},{5,1},{2,6},{6,2},{3,7},{7,3},{8,12},{12,8},{9,1... | collective-permute-start | bytes 589832 | tf_op jit(solution)/shard_map/ppermute | solution.py:466
  31.1 10.3 %copy-start.17 = (bf16[2,128,384]{2,1,0:T(8,128)(2,1)}, bf16[2,128,384]{2,1,0:T(8,128)(2,1)S(1)}, u32[]{:S(2)}) copy-start(bf16[2,128,384]{2,1,0:T(8,128)(2,1)S(1)} %collective-permute-done.6.wy) | copy-start | bytes 589828
  31.1 12.6 %all-to-all-start.1 = ((bf16[8,2,48,384]{3,2,1,0:T(8,128)(2,1)}), bf16[8,2,48,384]{3,2,1,0:T(8,128)(2,1)S(1)}, u32[]{:S(2)}, u32[]{:S(2)}) async-start(bf16[8,2,48,384]{3,2,1,0:T(8,128)(2,1)} %shard_map.86), calls=%async_computation.1 | async-start | bytes 1179648 | tf_op jit(solution)/shard_map/all_to_all | solution.py:494
  61.4 3.7 %copy-start.4 = (bf16[2,256,384]{2,1,0:T(8,128)(2,1)S(1)}, bf16[2,256,384]{2,1,0:T(8,128)(2,1)}, u32[]{:S(2)}) copy-start(bf16[2,256,384]{2,1,0:T(8,128)(2,1)} %get-tuple-element.119.att_own) | copy-start | bytes 1179652
  61.4 8.5 %copy-start.30 = (bf16[2,128,384]{2,1,0:T(8,128)(2,1)S(1)}, bf16[2,128,384]{2,1,0:T(8,128)(2,1)}, u32[]{:S(2)}) copy-start(bf16[2,128,384]{2,1,0:T(8,128)(2,1)} %get-tuple-element.84) | copy-start | bytes 589828
  61.4 19.9 %all-to-all-start.2 = ((bf16[8,2,48,384]{3,2,1,0:T(8,128)(2,1)}), bf16[8,2,48,384]{3,2,1,0:T(8,128)(2,1)S(1)}, u32[]{:S(2)}, u32[]{:S(2)}) async-start(bf16[8,2,48,384]{3,2,1,0:T(8,128)(2,1)} %get-tuple-element.79), calls=%async_computation.2 | async-start | bytes 1179648 | tf_op jit(solution)/shard_map/all_to_all | solution.py:498
  65.1 6.1 %collective-permute-start.7 = (bf16[2,256,384]{2,1,0:T(8,128)(2,1)S(1)}, bf16[2,256,384]{2,1,0:T(8,128)(2,1)S(1)}, u32[]{:S(2)}, u32[]{:S(2)}) collective-permute-start(bf16[2,256,384]{2,1,0:T(8,128)(2,1)S(1)} %copy-done.4), channel_id=1, source_target_pairs={{0,2},{2,0},{1,3},{3,1},{4,6},{6,4},{5,7},{7,5},{8,10},{10,8},{9,1... | collective-permute-start | bytes 1179656 | tf_op jit(solution)/shard_map/ppermute | solution.py:466
  69.8 11.5 %collective-permute-start.8 = (bf16[2,128,384]{2,1,0:T(8,128)(2,1)S(1)}, bf16[2,128,384]{2,1,0:T(8,128)(2,1)S(1)}, u32[]{:S(2)}, u32[]{:S(2)}) collective-permute-start(bf16[2,128,384]{2,1,0:T(8,128)(2,1)S(1)} %copy-done.30), channel_id=1, source_target_pairs={{0,4},{4,0},{1,5},{5,1},{2,6},{6,2},{3,7},{7,3},{8,12},{12,8},{9,1... | collective-permute-start | bytes 589832 | tf_op jit(solution)/shard_map/ppermute | solution.py:466
  77.4 13.0 %copy-start.29 = (bf16[2,128,384]{2,1,0:T(8,128)(2,1)S(1)}, bf16[2,128,384]{2,1,0:T(8,128)(2,1)}, u32[]{:S(2)}) copy-start(bf16[2,128,384]{2,1,0:T(8,128)(2,1)} %get-tuple-element.91) | copy-start | bytes 589828
  77.4 14.4 %collective-permute-start.10 = (bf16[2,2,96,384]{3,2,1,0:T(8,128)(2,1)}, bf16[2,2,96,384]{3,2,1,0:T(8,128)(2,1)S(1)}, u32[]{:S(2)}, u32[]{:S(2)}) collective-permute-start(bf16[2,2,96,384]{3,2,1,0:T(8,128)(2,1)} %get-tuple-element.95), channel_id=1, source_target_pairs={{0,8},{8,0},{16,24},{24,16},{1,9},{9,1},{17,25},{25,17},{2,10},{10... | collective-permute-start | bytes 884744 | tf_op jit(solution)/shard_map/ppermute | solution.py:470
  78.8 15.8 %collective-permute-start.11 = (bf16[2,2,96,384]{3,2,1,0:T(8,128)(2,1)}, bf16[2,2,96,384]{3,2,1,0:T(8,128)(2,1)S(1)}, u32[]{:S(2)}, u32[]{:S(2)}) collective-permute-start(bf16[2,2,96,384]{3,2,1,0:T(8,128)(2,1)} %get-tuple-element.96), channel_id=1, source_target_pairs={{0,16},{8,24},{16,0},{24,8},{1,17},{9,25},{17,1},{25,9},{2,18},{10... | collective-permute-start | bytes 884744 | tf_op jit(solution)/shard_map/ppermute | solution.py:470
  81.2 15.3 %collective-permute-start.12 = (bf16[2,2,96,384]{3,2,1,0:T(8,128)(2,1)}, bf16[2,2,96,384]{3,2,1,0:T(8,128)(2,1)S(1)}, u32[]{:S(2)}, u32[]{:S(2)}) collective-permute-start(bf16[2,2,96,384]{3,2,1,0:T(8,128)(2,1)} %get-tuple-element.97), channel_id=1, source_target_pairs={{0,24},{8,16},{16,8},{24,0},{1,25},{9,17},{17,9},{25,1},{2,26},{10... | collective-permute-start | bytes 884744 | tf_op jit(solution)/shard_map/ppermute | solution.py:470
  81.3 0.9 copy-start.1
  85.0 17.2 %all-to-all-start.3 = ((bf16[8,2,16,384]{3,2,1,0:T(8,128)(2,1)}), bf16[8,2,16,384]{3,2,1,0:T(8,128)(2,1)S(1)}, u32[]{:S(2)}, u32[]{:S(2)}) async-start(bf16[8,2,16,384]{3,2,1,0:T(8,128)(2,1)} %get-tuple-element.88), calls=%async_computation.3 | async-start | bytes 393216 | tf_op jit(solution)/shard_map/all_to_all | solution.py:505
  90.4 9.9 %collective-permute-start.9 = (bf16[2,128,384]{2,1,0:T(8,128)(2,1)S(1)}, bf16[2,128,384]{2,1,0:T(8,128)(2,1)S(1)}, u32[]{:S(2)}, u32[]{:S(2)}) collective-permute-start(bf16[2,128,384]{2,1,0:T(8,128)(2,1)S(1)} %copy-done.29), channel_id=1, source_target_pairs={{0,4},{4,0},{1,5},{5,1},{2,6},{6,2},{3,7},{7,3},{8,12},{12,8},{9,1... | collective-permute-start | bytes 589832 | tf_op jit(solution)/shard_map/ppermute | solution.py:466
  91.8 27.7 %copy-start.11 = (bf16[2,2,96,384]{3,2,1,0:T(8,128)(2,1)}, bf16[2,2,96,384]{3,2,1,0:T(8,128)(2,1)S(1)}, u32[]{:S(2)}) copy-start(bf16[2,2,96,384]{3,2,1,0:T(8,128)(2,1)S(1)} %collective-permute-done.10.t1) | copy-start | bytes 884740
  94.5 25.1 %copy-start.12 = (bf16[2,2,96,384]{3,2,1,0:T(8,128)(2,1)}, bf16[2,2,96,384]{3,2,1,0:T(8,128)(2,1)S(1)}, u32[]{:S(2)}) copy-start(bf16[2,2,96,384]{3,2,1,0:T(8,128)(2,1)S(1)} %collective-permute-done.11.t2) | copy-start | bytes 884740
  96.5 23.1 %copy-start.13 = (bf16[2,2,96,384]{3,2,1,0:T(8,128)(2,1)}, bf16[2,2,96,384]{3,2,1,0:T(8,128)(2,1)S(1)}, u32[]{:S(2)}) copy-start(bf16[2,2,96,384]{3,2,1,0:T(8,128)(2,1)S(1)} %collective-permute-done.12.t3) | copy-start | bytes 884740
  96.5 5.7 %collective-permute-start.13 = (bf16[2,64,384]{2,1,0:T(8,128)(2,1)}, bf16[2,64,384]{2,1,0:T(8,128)(2,1)S(1)}, u32[]{:S(2)}, u32[]{:S(2)}) collective-permute-start(bf16[2,64,384]{2,1,0:T(8,128)(2,1)} %get-tuple-element.98), channel_id=1, source_target_pairs={{0,8},{8,0},{16,24},{24,16},{1,9},{9,1},{17,25},{25,17},{2,10},{10... | collective-permute-start | bytes 294920 | tf_op jit(solution)/shard_map/ppermute | solution.py:470
  96.5 5.0 %collective-permute-start.14 = (bf16[2,32,384]{2,1,0:T(8,128)(2,1)}, bf16[2,32,384]{2,1,0:T(8,128)(2,1)S(1)}, u32[]{:S(2)}, u32[]{:S(2)}) collective-permute-start(bf16[2,32,384]{2,1,0:T(8,128)(2,1)} %get-tuple-element.99), channel_id=1, source_target_pairs={{0,16},{8,24},{16,0},{24,8},{1,17},{9,25},{17,1},{25,9},{2,18},{10... | collective-permute-start | bytes 147464 | tf_op jit(solution)/shard_map/ppermute | solution.py:470
  97.8 4.4 %collective-permute-start.15 = (bf16[2,32,384]{2,1,0:T(8,128)(2,1)}, bf16[2,32,384]{2,1,0:T(8,128)(2,1)S(1)}, u32[]{:S(2)}, u32[]{:S(2)}) collective-permute-start(bf16[2,32,384]{2,1,0:T(8,128)(2,1)} %get-tuple-element.100), channel_id=1, source_target_pairs={{0,24},{8,16},{16,8},{24,0},{1,25},{9,17},{17,9},{25,1},{2,26},{10... | collective-permute-start | bytes 147464 | tf_op jit(solution)/shard_map/ppermute | solution.py:470
  100.4 1.8 %copy-start.14 = (bf16[2,128,384]{2,1,0:T(8,128)(2,1)}, bf16[2,128,384]{2,1,0:T(8,128)(2,1)S(1)}, u32[]{:S(2)}) copy-start(bf16[2,128,384]{2,1,0:T(8,128)(2,1)S(1)} %collective-permute-done.9.dy) | copy-start | bytes 589828
  109.2 6.4 %copy-start.28 = (bf16[256,1152]{1,0:T(8,128)(2,1)S(1)}, bf16[256,1152]{1,0:T(8,128)(2,1)}, u32[]{:S(2)}) copy-start(bf16[256,1152]{1,0:T(8,128)(2,1)} %get-tuple-element.116) | copy-start | bytes 1769476
  109.2 23.2 %all-to-all-start.4 = ((bf16[16,96,384]{2,1,0:T(8,128)(2,1)}), bf16[16,96,384]{2,1,0:T(8,128)(2,1)S(1)}, u32[]{:S(2)}, u32[]{:S(2)}) async-start(bf16[16,96,384]{2,1,0:T(8,128)(2,1)} %bitcast.15), calls=%async_computation.4 | async-start | bytes 2359296 | tf_op jit(solution)/shard_map/all_to_all | solution.py:512
  115.6 10.8 %collective-permute-start.19 = (bf16[256,1152]{1,0:T(8,128)(2,1)S(1)}, bf16[256,1152]{1,0:T(8,128)(2,1)S(1)}, u32[]{:S(2)}, u32[]{:S(2)}) collective-permute-start(bf16[256,1152]{1,0:T(8,128)(2,1)S(1)} %copy-done.28), channel_id=1, source_target_pairs={{0,2},{2,0},{1,3},{3,1},{4,6},{6,4},{5,7},{7,5},{8,10},{10,8},{9,1... | collective-permute-start | bytes 1769480 | tf_op jit(solution)/shard_map/ppermute | solution.py:466
  122.4 14.0 %collective-permute-start.16 = (bf16[96,384]{1,0:T(8,128)(2,1)}, bf16[96,384]{1,0:T(8,128)(2,1)S(1)}, u32[]{:S(2)}, u32[]{:S(2)}) collective-permute-start(bf16[96,384]{1,0:T(8,128)(2,1)} %get-tuple-element.111), channel_id=1, source_target_pairs={{0,1},{1,0},{4,5},{5,4},{2,3},{3,2},{6,7},{7,6},{8,9},{9,8},{12,13... | collective-permute-start | bytes 221192 | tf_op jit(solution)/shard_map/ppermute | solution.py:470
  125.5 12.2 %collective-permute-start.17 = (bf16[96,384]{1,0:T(8,128)(2,1)}, bf16[96,384]{1,0:T(8,128)(2,1)S(1)}, u32[]{:S(2)}, u32[]{:S(2)}) collective-permute-start(bf16[96,384]{1,0:T(8,128)(2,1)} %get-tuple-element.112), channel_id=1, source_target_pairs={{0,4},{1,5},{4,0},{5,1},{2,6},{3,7},{6,2},{7,3},{8,12},{9,13},{12,... | collective-permute-start | bytes 221192 | tf_op jit(solution)/shard_map/ppermute | solution.py:470
  125.8 11.9 %collective-permute-start.18 = (bf16[96,384]{1,0:T(8,128)(2,1)}, bf16[96,384]{1,0:T(8,128)(2,1)S(1)}, u32[]{:S(2)}, u32[]{:S(2)}) collective-permute-start(bf16[96,384]{1,0:T(8,128)(2,1)} %get-tuple-element.113), channel_id=1, source_target_pairs={{0,5},{1,4},{4,1},{5,0},{2,7},{3,6},{6,3},{7,2},{8,13},{9,12},{12,... | collective-permute-start | bytes 221192 | tf_op jit(solution)/shard_map/ppermute | solution.py:470
  132.4 5.3 %copy-start = (bf16[16,96,384]{2,1,0:T(8,128)(2,1)}, bf16[16,96,384]{2,1,0:T(8,128)(2,1)S(1)}, u32[]{:S(2)}) copy-start(bf16[16,96,384]{2,1,0:T(8,128)(2,1)S(1)} %all-to-all-done.4.second) | copy-start | bytes 3538948
  136.4 1.3 copy-start.19
  141.6 13.8 %all-to-all-start.5 = ((bf16[8,2,16,384]{3,2,1,0:T(8,128)(2,1)}), bf16[8,2,16,384]{3,2,1,0:T(8,128)(2,1)S(1)}, u32[]{:S(2)}, u32[]{:S(2)}) async-start(bf16[8,2,16,384]{3,2,1,0:T(8,128)(2,1)} %shard_map.93), calls=%async_computation.5 | async-start | bytes 393216 | tf_op jit(solution)/shard_map/all_to_all | solution.py:516
  155.4 9.3 %copy-start.24 = (bf16[16,384]{1,0:T(8,128)(2,1)}, bf16[16,384]{1,0:T(8,128)(2,1)S(1)}, u32[]{:S(2)}) copy-start(bf16[16,384]{1,0:T(8,128)(2,1)S(1)} %get-tuple-element.127.own) | copy-start | bytes 36868
  155.5 6.6 %collective-permute-start.22 = (bf16[16,384]{1,0:T(8,128)(2,1)S(1)}, bf16[16,384]{1,0:T(8,128)(2,1)S(1)}, u32[]{:S(2)}, u32[]{:S(2)}) collective-permute-start(bf16[16,384]{1,0:T(8,128)(2,1)S(1)} %get-tuple-element.126), channel_id=1, source_target_pairs={{0,3},{1,2},{2,1},{3,0},{4,7},{5,6},{6,5},{7,4},{8,11},{9,10},{10,... | collective-permute-start | bytes 36872 | tf_op jit(solution)/shard_map/ppermute | solution.py:470
  160.7 1.4 collective-permute-start.21
  160.7 4.0 %collective-permute-start.20 = (bf16[16,384]{1,0:T(8,128)(2,1)S(1)}, bf16[16,384]{1,0:T(8,128)(2,1)S(1)}, u32[]{:S(2)}, u32[]{:S(2)}) collective-permute-start(bf16[16,384]{1,0:T(8,128)(2,1)S(1)} %get-tuple-element.127.own), channel_id=1, source_target_pairs={{0,1},{1,0},{2,3},{3,2},{4,5},{5,4},{6,7},{7,6},{8,9},{9,8},{10,11... | collective-permute-start | bytes 36872 | tf_op jit(solution)/shard_map/ppermute | solution.py:470
  162.1 2.7 %copy-start.25 = (bf16[16,384]{1,0:T(8,128)(2,1)}, bf16[16,384]{1,0:T(8,128)(2,1)S(1)}, u32[]{:S(2)}) copy-start(bf16[16,384]{1,0:T(8,128)(2,1)S(1)} %collective-permute-done.22.from_both) | copy-start | bytes 36868
  162.1 2.7 %copy-start.26 = (bf16[16,384]{1,0:T(8,128)(2,1)}, bf16[16,384]{1,0:T(8,128)(2,1)S(1)}, u32[]{:S(2)}) copy-start(bf16[16,384]{1,0:T(8,128)(2,1)S(1)} %collective-permute-done.21.from_core) | copy-start | bytes 36868
  (12 other events, 8.5 us)

commit v13 on v12

--- a/solution.py
+++ b/solution.py
@@ -272,7 +272,7 @@
 
 
 def terms_body(pos, att_own, att_oth, ct_own, ct_oth, dq, xt, p_own, p_oth, *rest):
-    c, x = pos[0], pos[2] >> 1
+    c, y, dp = pos[0], pos[2] & 1, pos[3]
     slots = rest[-1]
     total = dot(xt[0], dq[0]) + dot(xt[1], dq[1])
     slots[:, :, 0] = total.astype(BF16).reshape(XN, YN, 96, H)
@@ -282,33 +282,33 @@
         term = dot(att_t, ct[...])
         total = term if total is None else total + term
     slots[:, :, 1] = total.astype(BF16).reshape(XN, YN, 96, H)
-    for far in range(XN):
-        rest[far][...] = slots[x ^ far]
+    for far in range(4):
+        rest[far][...] = slots[:, y ^ (far >> 1), dp ^ (far & 1)]
 
 
 def output_terms(pos, att_own, att_oth, ct_own, ct_oth, dq, xt, perm):
     col = lambda flip, rows: pl.BlockSpec((rows, H), lambda i, s: (0, s[0] ^ flip))
-    slot = (YN, 2, 96, H)
+    slot = (XN, 96, H)
     return call(
         terms_body,
         (1,),
         [whole(2, TOK, H)] * 2 + [col(0, TOK)] * 2 + [whole(2, TOK, H), whole(2, D, TOK), col(0, D), col(1, D)],
-        [(whole(*slot), (slot, BF16))] * XN,
-        [pltpu.VMEM((XN,) + slot, BF16)],
+        [(whole(*slot), (slot, BF16))] * 4,
+        [pltpu.VMEM((XN, YN, 2, 96, H), BF16)],
     )(pos, att_own, att_oth, ct_own, ct_oth, dq, xt, perm, perm)
 
 
 def x_sum_body(pos, t0, t1, t2, t3, *rest):
-    y, dp = pos[2] & 1, pos[3]
+    x = pos[2] >> 1
     slots = rest[-1]
     total = (t0[...].astype(F32) + t1[...].astype(F32)) + (t2[...].astype(F32) + t3[...].astype(F32))
     slots[...] = total.astype(BF16)
-    for far in range(4):
-        rest[far][...] = slots[y ^ (far >> 1), dp ^ (far & 1)]
+    for far in range(XN):
+        rest[far][...] = slots[x ^ far]
 
 
 def x_sum(pos, *terms):
-    shape = (YN, 2, 96, H)
+    shape = (XN, 96, H)
     return call(
         x_sum_body,
         (1,),
@@ -499,16 +499,17 @@
     att_oth = swap(att, "c")
     dwy = swap(dwy, "y")
     first, *firsts = output_terms(pos, att, att_oth, ct_own, ct_oth, dq, xt, perm)
-    firsts = [along(firsts[far - 1], "x", far) for far in (1, 2, 3)]
-    dx_r, first, dwy = lax.optimization_barrier((dx_r, first, dwy))
+    firsts = [along(firsts[far - 1], ("y", "dp"), far) for far in (1, 2, 3)]
+    dy = swap(dy, "y")
+    dx_r, first, dwy, dy = lax.optimization_barrier((dx_r, first, dwy, dy))
     dz, g3, g4_a, g4_b = back_slots(pos, dx_r, dw, dwy)
     dz_r = lax.all_to_all(dz, "z", 0, 0)
     g3, g4_a, g4_b, firsts = lax.optimization_barrier((g3, g4_a, g4_b, firsts))
     g3, g4_a, g4_b = along(g3, "x", 1), along(g4_a, "x", 2), along(g4_b, "x", 3)
-    pg_own, pg_oth, terms = leaf_grads(pos, dz_r, dkv, dn1, swap(dy, "y"), g3, g4_a, g4_b, dq, xt)
+    pg_own, pg_oth, terms = leaf_grads(pos, dz_r, dkv, dn1, dy, g3, g4_a, g4_b, dq, xt)
     terms, first, firsts = lax.optimization_barrier((terms, first, firsts))
     firsts = x_sum(pos, first, *firsts)
-    firsts = list(firsts[:1]) + [along(firsts[far], ("y", "dp"), far) for far in (1, 2, 3)]
+    firsts = list(firsts[:1]) + [along(firsts[far], "x", far) for far in (1, 2, 3)]
     terms = lax.all_to_all(terms.reshape(16, 96, H), ("x", "y", "dp"), 0, 0)
     input_grad = input_side(pos, pg_own, swap(pg_oth, "c"), w_qkv)
     terms, input_grad = lax.optimization_barrier((terms, input_grad))

time: 168 us -> 167 us (level)
  starting transfers between devices: 71.4 us -> 68.8 us
    ppermute x15, starting transfers between devices: 21.4 us -> 24.4 us  [along(): return lax.ppermute(value, axes, [(i, i ^ far) for i in range(count)])]
    ppermute x8, starting transfers between devices: 17.5 us -> 14.8 us  [swap(): return lax.ppermute(value, axis, [(0, 1), (1, 0)])]
    all_to_all x1, starting transfers between devices: 6.4 us -> 3.83 us  [shards(): terms = lax.all_to_all(terms.reshape(16, 96, H), ('x', 'y', 'dp'), 0, 0)]
    ppermute x8, waiting for transfers between devices: 1.41 us -> 3.57 us  [swap(): return lax.ppermute(value, axis, [(0, 1), (1, 0)])]
    ppermute x15, waiting for transfers between devices: 19.2 us -> 17.5 us  [along(): return lax.ppermute(value, axes, [(i, i ^ far) for i in range(count)])]
where the time goes in v13:
time: 167 us; the launch traced here: 166 us
  starting transfers between devices  68.8 us (41%)
  Pallas kernels  60.3 us (36%)
  waiting for transfers between devices  28.8 us (17%)
  local copies, waits for them, and re-layouts  6.1 us (4%)
    ppermute x15, starting transfers between devices, along(): return lax.ppermute(value, axes, [(i, i ^ far) for i in range(count)])  24.4 us
    ppermute x15, waiting for transfers between devices, along(): return lax.ppermute(value, axes, [(i, i ^ far) for i in range(count)])  17.5 us
    pallas_call x1, Pallas kernels, attention(): call(attention_body, (H // 128,), [cut(2, TOK), cut(2, TOK), cut(2, 2, TO...  16.8 us
    ppermute x8, starting transfers between devices, swap(): return lax.ppermute(value, axis, [(0, 1), (1, 0)])  14.8 us
    all_to_all x1, starting transfers between devices, shards(): zr = lax.all_to_all(zs, 'z', 0, 0)  6.45 us
    pallas_call x1, Pallas kernels, leaf_grads(): call(leaf_body, (1,), [whole(ZN, 2, 16, H), whole(2, 2, TOK, H), whole(2,...  6.26 us
    unnamed x62, local copies, waits for them, and re-layouts  6.1 us
    all_to_all x1, starting transfers between devices, shards(): terms = lax.all_to_all(terms, 'z', 0, 0)  5.46 us
  transfers between devices with their start and end apart: 29, of which 15 were waited for; matrix products, arithmetic and copies ran while one was open for 0% of the time, Pallas kernels for 19%

profile of v13, /device:TPU:1, one launch (start us, length us, event | category | flops | bytes accessed | tf_op | source)
XLA Modules:
  0.0 165.6 jit_solution(13713242896602625165)
XLA Ops:
  0.6 3.3 %collective-permute-start = (bf16[256,768]{1,0:T(8,128)(2,1)}, bf16[256,768]{1,0:T(8,128)(2,1)S(1)}, u32[]{:S(2)}, u32[]{:S(2)}) collective-permute-start(bf16[256,768]{1,0:T(8,128)(2,1)} %bitcast.9), channel_id=1, source_target_pairs={{0,2},{2,0},{1,3},{3,1},{4,6},{6,4},{5,7},{7,5},{8,10},{10,8},{9,1... | collective-permute-start | bytes 1179656 | tf_op jit(solution)/shard_map/ppermute | solution.py:466
  4.7 0.8 collective-permute-done.x_oth
  6.3 4.5 %shard_map.84 = (bf16[2,2,256,384]{3,2,1,0:T(8,128)(2,1)}, bf16[2,2,128,384]{3,2,1,0:T(8,128)(2,1)}, bf16[2,128,384]{2,1,0:T(8,128)(2,1)}, bf16[2,64,384]{2,1,0:...) custom-call(s32[4]{0:T(128)} %pad_add_fusion.pos, bf16[256,768]{1,0:T(8,128)(2,1)} %bitcast.10, ...), custom_call_target="tpu_custom_call" | custom-call | tf_op jit(solution)/shard_map/pallas_call | solution.py:113
  10.7 6.5 %all-to-all-start = ((bf16[8,2,16,384]{3,2,1,0:T(8,128)(2,1)}), bf16[8,2,16,384]{3,2,1,0:T(8,128)(2,1)S(1)}, u32[]{:S(2)}, u32[]{:S(2)}) async-start(bf16[8,2,16,384]{3,2,1,0:T(8,128)(2,1)} %get-tuple-element.66), calls=%async_computation | async-start | bytes 393216 | tf_op jit(solution)/shard_map/all_to_all | solution.py:490
  17.2 1.2 collective-permute-start.2
  18.4 1.3 collective-permute-start.1
  19.7 1.8 %collective-permute-start.4 = (bf16[2,32,384]{2,1,0:T(8,128)(2,1)}, bf16[2,32,384]{2,1,0:T(8,128)(2,1)S(1)}, u32[]{:S(2)}, u32[]{:S(2)}) collective-permute-start(bf16[2,32,384]{2,1,0:T(8,128)(2,1)} %get-tuple-element.69), channel_id=1, source_target_pairs={{0,24},{8,16},{16,8},{24,0},{1,25},{9,17},{17,9},{25,1},{2,26},{10... | collective-permute-start | bytes 147464 | tf_op jit(solution)/shard_map/ppermute | solution.py:470
  22.1 2.2 %collective-permute-done.4 = bf16[2,32,384]{2,1,0:T(8,128)(2,1)S(1)} collective-permute-done((bf16[2,32,384]{2,1,0:T(8,128)(2,1)}, bf16[2,32,384]{2,1,0:T(8,128)(2,1)S(1)}, u32[]{:S(2)}, u32[]{:S(2)}) %collective-permute-start.4) | collective-permute-done | bytes 49184 | tf_op jit(solution)/shard_map/ppermute | solution.py:470
  24.3 1.9 %collective-permute-done.3 = bf16[2,32,384]{2,1,0:T(8,128)(2,1)S(1)} collective-permute-done((bf16[2,32,384]{2,1,0:T(8,128)(2,1)}, bf16[2,32,384]{2,1,0:T(8,128)(2,1)S(1)}, u32[]{:S(2)}, u32[]{:S(2)}) %collective-permute-start.3) | collective-permute-done | bytes 49184 | tf_op jit(solution)/shard_map/ppermute | solution.py:470
  26.6 1.3 collective-permute-start.6
  27.9 2.6 %shard_map.86 = bf16[8,2,48,384]{3,2,1,0:T(8,128)(2,1)} custom-call(s32[4]{0:T(128)} %pad_add_fusion.pos, bf16[8,2,16,384]{3,2,1,0:T(8,128)(2,1)} %copy-done.8), custom_call_target="tpu_custom_call" | custom-call | tf_op jit(solution)/shard_map/pallas_call | solution.py:159
  31.1 5.0 %all-to-all-start.1 = ((bf16[8,2,48,384]{3,2,1,0:T(8,128)(2,1)}), bf16[8,2,48,384]{3,2,1,0:T(8,128)(2,1)S(1)}, u32[]{:S(2)}, u32[]{:S(2)}) async-start(bf16[8,2,48,384]{3,2,1,0:T(8,128)(2,1)} %shard_map.86), calls=%async_computation.1 | async-start | bytes 1179648 | tf_op jit(solution)/shard_map/all_to_all | solution.py:494
  36.2 5.2 %shard_map.85 = (bf16[2,256,384]{2,1,0:T(8,128)(2,1)}, bf16[2,256,384]{2,1,0:T(8,128)(2,1)}, bf16[2,768,256]{2,1,0:T(8,128)(2,1)}) custom-call(s32[4]{0:T(128)} %pad_add_fusion.pos, bf16[256,768]{1,0:T(8,128)(2,1)} %bitcast.11, bf16[256,768]{1,0:T(8,128)(2,1)} %copy-done.3, bf16[256,768]{1,0:T(8,128)(2,1)} %bitcast.13, bf16[256,768]{1,0:T(8,128)(2,1)} %copy-done.6, ...), custom_call_target="tpu_custom_call" | custom-call | tf_op jit(solution)/shard_map/pallas_call | solution.py:132
  41.4 2.3 %all-to-all-done.1.xr = bf16[8,2,48,384]{3,2,1,0:T(8,128)(2,1)S(1)} async-done(((bf16[8,2,48,384]{3,2,1,0:T(8,128)(2,1)}), bf16[8,2,48,384]{3,2,1,0:T(8,128)(2,1)S(1)}, u32[]{:S(2)}, u32[]{:S(2)}) %all-to-all-start.1) | async-done | bytes 589856 | tf_op jit(solution)/shard_map/all_to_all | solution.py:494
  43.7 0.8 copy-done.2
  44.6 16.8 %shard_map.87 = (bf16[2,256,384]{2,1,0:T(8,128)(2,1)}, bf16[2,256,384]{2,1,0:T(8,128)(2,1)}, f32[2,2,256,384]{3,2,1,0:T(8,128)}, f32[2,2,128,384]{3,2,1,0:T(8,12...) custom-call(s32[4]{0:T(128)} %pad_add_fusion.pos, ...), custom_call_target="tpu_custom_call" | custom-call | tf_op jit(solution)/shard_map/pallas_call | solution.py:246
  61.4 3.7 %all-to-all-start.2 = ((bf16[8,2,48,384]{3,2,1,0:T(8,128)(2,1)}), bf16[8,2,48,384]{3,2,1,0:T(8,128)(2,1)S(1)}, u32[]{:S(2)}, u32[]{:S(2)}) async-start(bf16[8,2,48,384]{3,2,1,0:T(8,128)(2,1)} %get-tuple-element.80), calls=%async_computation.2 | async-start | bytes 1179648 | tf_op jit(solution)/shard_map/all_to_all | solution.py:498
  65.1 4.7 %collective-permute-start.7 = (bf16[2,256,384]{2,1,0:T(8,128)(2,1)S(1)}, bf16[2,256,384]{2,1,0:T(8,128)(2,1)S(1)}, u32[]{:S(2)}, u32[]{:S(2)}) collective-permute-start(bf16[2,256,384]{2,1,0:T(8,128)(2,1)S(1)} %copy-done.4), channel_id=1, source_target_pairs={{0,2},{2,0},{1,3},{3,1},{4,6},{6,4},{5,7},{7,5},{8,10},{10,8},{9,1... | collective-permute-start | bytes 1179656 | tf_op jit(solution)/shard_map/ppermute | solution.py:466
  69.8 1.4 collective-permute-start.8
  71.3 0.8 copy-done.5
  72.1 5.4 %shard_map.88 = (bf16[4,96,384]{2,1,0:T(8,128)(2,1)}, bf16[4,96,384]{2,1,0:T(8,128)(2,1)}, bf16[4,96,384]{2,1,0:T(8,128)(2,1)}, bf16[4,96,384]{2,1,0:T(8,128)(2,1)}) custom-call(s32[4]{0:T(128)} %pad_add_fusion.pos, bf16[2,256,384]{2,1,0:T(8,128)(2,1)} %get-tuple-element.121.att_own, bf16[2,256,384]{2,1,0:T(8,128)(2,1)} %copy-done.5, ...), custom_call_target="tpu_custom_call" | custom-call | tf_op jit(solution)/shard_map/pallas_call | solution.py:292
  77.5 2.6 %collective-permute-start.10 = (bf16[4,96,384]{2,1,0:T(8,128)(2,1)}, bf16[4,96,384]{2,1,0:T(8,128)(2,1)S(1)}, u32[]{:S(2)}, u32[]{:S(2)}) collective-permute-start(bf16[4,96,384]{2,1,0:T(8,128)(2,1)} %get-tuple-element.97), channel_id=1, source_target_pairs={{0,1},{1,0},{4,5},{5,4},{2,3},{3,2},{6,7},{7,6},{8,9},{9,8},{12,13... | collective-permute-start | bytes 884744 | tf_op jit(solution)/shard_map/ppermute | solution.py:470
  81.3 2.2 %collective-permute-done.9.dy = bf16[2,128,384]{2,1,0:T(8,128)(2,1)S(1)} collective-permute-done((bf16[2,128,384]{2,1,0:T(8,128)(2,1)S(1)}, bf16[2,128,384]{2,1,0:T(8,128)(2,1)S(1)}, u32[]{:S(2)}, u32[]{:S(2)}) %collective-permute-start.9) | collective-permute-done | bytes 196640 | tf_op jit(solution)/shard_map/ppermute | solution.py:466
  83.5 0.9 copy-done.1
  84.3 2.8 %shard_map.89 = (bf16[8,2,16,384]{3,2,1,0:T(8,128)(2,1)}, bf16[2,64,384]{2,1,0:T(8,128)(2,1)}, bf16[2,32,384]{2,1,0:T(8,128)(2,1)}, bf16[2,32,384]{2,1,0:T(8,128)(2,1)}) custom-call(s32[4]{0:T(128)} %pad_add_fusion.pos, bf16[8,2,48,384]{3,2,1,0:T(8,128)(2,1)} %copy-done.1, f32[2,128,384]{2,1,0:T(8,128)} %get-tuple-element.88.dw, bf16[2,128,384]{2,1,0:T(8,128)(2,1)} %copy-done.15), custom_call_target="tpu_custom_call" | custom-call | tf_op jit(solution)/shard_map/pallas_call | solution.py:338
  87.1 5.1 %all-to-all-start.3 = ((bf16[8,2,16,384]{3,2,1,0:T(8,128)(2,1)}), bf16[8,2,16,384]{3,2,1,0:T(8,128)(2,1)S(1)}, u32[]{:S(2)}, u32[]{:S(2)}) async-start(bf16[8,2,16,384]{3,2,1,0:T(8,128)(2,1)} %get-tuple-element.90), calls=%async_computation.3 | async-start | bytes 393216 | tf_op jit(solution)/shard_map/all_to_all | solution.py:506
  92.3 3.9 %collective-permute-done.11.t2 = bf16[4,96,384]{2,1,0:T(8,128)(2,1)S(1)} collective-permute-done((bf16[4,96,384]{2,1,0:T(8,128)(2,1)}, bf16[4,96,384]{2,1,0:T(8,128)(2,1)S(1)}, u32[]{:S(2)}, u32[]{:S(2)}) %collective-permute-start.11) | collective-permute-done | bytes 294944 | tf_op jit(solution)/shard_map/ppermute | solution.py:470
  96.7 1.7 %collective-permute-start.13 = (bf16[2,64,384]{2,1,0:T(8,128)(2,1)}, bf16[2,64,384]{2,1,0:T(8,128)(2,1)S(1)}, u32[]{:S(2)}, u32[]{:S(2)}) collective-permute-start(bf16[2,64,384]{2,1,0:T(8,128)(2,1)} %get-tuple-element.100), channel_id=1, source_target_pairs={{0,8},{8,0},{16,24},{24,16},{1,9},{9,1},{17,25},{25,17},{2,10},{10... | collective-permute-start | bytes 294920 | tf_op jit(solution)/shard_map/ppermute | solution.py:470
  98.4 2.0 %collective-permute-start.14 = (bf16[2,32,384]{2,1,0:T(8,128)(2,1)}, bf16[2,32,384]{2,1,0:T(8,128)(2,1)S(1)}, u32[]{:S(2)}, u32[]{:S(2)}) collective-permute-start(bf16[2,32,384]{2,1,0:T(8,128)(2,1)} %get-tuple-element.101), channel_id=1, source_target_pairs={{0,16},{8,24},{16,0},{24,8},{1,17},{9,25},{17,1},{25,9},{2,18},{10... | collective-permute-start | bytes 147464 | tf_op jit(solution)/shard_map/ppermute | solution.py:470
  100.8 2.4 %collective-permute-done.14.g4_a = bf16[2,32,384]{2,1,0:T(8,128)(2,1)S(1)} collective-permute-done((bf16[2,32,384]{2,1,0:T(8,128)(2,1)}, bf16[2,32,384]{2,1,0:T(8,128)(2,1)S(1)}, u32[]{:S(2)}, u32[]{:S(2)}) %collective-permute-start.14) | collective-permute-done | bytes 49184 | tf_op jit(solution)/shard_map/ppermute | solution.py:470
  103.2 2.1 %collective-permute-done.15.g4_b = bf16[2,32,384]{2,1,0:T(8,128)(2,1)S(1)} collective-permute-done((bf16[2,32,384]{2,1,0:T(8,128)(2,1)}, bf16[2,32,384]{2,1,0:T(8,128)(2,1)S(1)}, u32[]{:S(2)}, u32[]{:S(2)}) %collective-permute-start.15) | collective-permute-done | bytes 49184 | tf_op jit(solution)/shard_map/ppermute | solution.py:470
  106.1 6.3 %shard_map.90 = (bf16[256,1152]{1,0:T(8,128)(2,1)}, bf16[256,1152]{1,0:T(8,128)(2,1)}, bf16[8,2,96,384]{3,2,1,0:T(8,128)(2,1)}) custom-call(s32[4]{0:T(128)} %pad_add_fusion.pos, bf16[8,2,16,384]{3,2,1,0:T(8,128)(2,1)} %copy-done.7, f32[2,2,256,384]{3,2,1,0:T(8,128)} %get-tuple-element.91.dkv, f32[2,2,128,384]{3,2,1,0:T(8,128)} %get-tuple-element.92.dn1, ...), custom_call_target="tpu_custom_call" | custom-call | tf_op jit(solution)/shard_map/pallas_call | solution.py:383
  112.3 3.8 %all-to-all-start.4 = ((bf16[16,96,384]{2,1,0:T(8,128)(2,1)}), bf16[16,96,384]{2,1,0:T(8,128)(2,1)S(1)}, u32[]{:S(2)}, u32[]{:S(2)}) async-start(bf16[16,96,384]{2,1,0:T(8,128)(2,1)} %bitcast.15), calls=%async_computation.4 | async-start | bytes 2359296 | tf_op jit(solution)/shard_map/all_to_all | solution.py:513
  116.2 2.6 %collective-permute-start.19 = (bf16[256,1152]{1,0:T(8,128)(2,1)S(1)}, bf16[256,1152]{1,0:T(8,128)(2,1)S(1)}, u32[]{:S(2)}, u32[]{:S(2)}) collective-permute-start(bf16[256,1152]{1,0:T(8,128)(2,1)S(1)} %copy-done.28), channel_id=1, source_target_pairs={{0,2},{2,0},{1,3},{3,1},{4,6},{6,4},{5,7},{7,5},{8,10},{10,8},{9,1... | collective-permute-start | bytes 1769480 | tf_op jit(solution)/shard_map/ppermute | solution.py:466
  118.8 2.8 %shard_map.91 = (bf16[96,384]{1,0:T(8,128)(2,1)}, bf16[96,384]{1,0:T(8,128)(2,1)}, bf16[96,384]{1,0:T(8,128)(2,1)}, bf16[96,384]{1,0:T(8,128)(2,1)}) custom-call(s32[4]{0:T(128)} %pad_add_fusion.pos, bf16[4,96,384]{2,1,0:T(8,128)(2,1)} %get-tuple-element.108.t0, bf16[4,96,384]{2,1,0:T(8,128)(2,1)} %copy-done.11, bf16[4,96,384]{2,1,0:T(8,128)(2,1)} %copy-done.12, ...), custom_call_target="tpu_custom_call" | custom-call | tf_op jit(solution)/shard_map/pallas_call | solution.py:312
  121.6 1.6 collective-permute-start.16
  123.2 2.4 %collective-permute-start.17 = (bf16[96,384]{1,0:T(8,128)(2,1)}, bf16[96,384]{1,0:T(8,128)(2,1)S(1)}, u32[]{:S(2)}, u32[]{:S(2)}) collective-permute-start(bf16[96,384]{1,0:T(8,128)(2,1)} %get-tuple-element.114), channel_id=1, source_target_pairs={{0,16},{8,24},{16,0},{24,8},{1,17},{9,25},{17,1},{25,9},{2,18},{10... | collective-permute-start | bytes 221192 | tf_op jit(solution)/shard_map/ppermute | solution.py:470
  125.7 0.8 copy-done.10
  126.5 5.1 %shard_map.92 = bf16[256,768]{1,0:T(8,128)(2,1)} custom-call(s32[4]{0:T(128)} %pad_add_fusion.pos, bf16[256,1152]{1,0:T(8,128)(2,1)} %get-tuple-element.117.pg_own, bf16[256,1152]{1,0:T(8,128)(2,1)} %copy-done.10, bf16[768,2304]{1,0:T(8,128)(2,1)} %rest_5_.1, bf16[768,2304]{1,0:T(8,128)(2,1)} %rest_5_.1, bf16[768,2304]{1,0:T(8,128)(2,1)} %rest_5_.1, ...), custom_call_target="tpu_custom_call" | custom-call | tf_op jit(solution)/shard_map/pallas_call | solution.py:406
  131.7 1.6 collective-permute-done.17.f2
  133.9 3.2 %shard_map.93 = bf16[8,2,16,384]{3,2,1,0:T(8,128)(2,1)} custom-call(s32[4]{0:T(128)} %pad_add_fusion.pos, bf16[96,384]{1,0:T(8,128)(2,1)} %get-tuple-element.112.f0, bf16[96,384]{1,0:T(8,128)(2,1)} %copy-done.19, bf16[96,384]{1,0:T(8,128)(2,1)} %copy-done.20, bf16[96,384]{1,0:T(8,128)(2,1)} %copy-done.21, bf16[16,96,384]{2,1,0:T(8,128)(2,1)} %copy-done), custom_call_target="tpu_custom_call" | custom-call | tf_op jit(solution)/shard_map/pallas_call | solution.py:435
  137.1 5.5 %all-to-all-start.5 = ((bf16[8,2,16,384]{3,2,1,0:T(8,128)(2,1)}), bf16[8,2,16,384]{3,2,1,0:T(8,128)(2,1)S(1)}, u32[]{:S(2)}, u32[]{:S(2)}) async-start(bf16[8,2,16,384]{3,2,1,0:T(8,128)(2,1)} %shard_map.93), calls=%async_computation.5 | async-start | bytes 393216 | tf_op jit(solution)/shard_map/all_to_all | solution.py:517
  142.6 3.5 %shard_map.94 = bf16[256,768]{1,0:T(8,128)(2,1)} custom-call(s32[4]{0:T(128)} %pad_add_fusion.pos, bf16[2,256,384]{2,1,0:T(8,128)(2,1)} %get-tuple-element.121.att_own, bf16[2,256,384]{2,1,0:T(8,128)(2,1)} %copy-done.5, bf16[768,768]{1,0:T(8,128)(2,1)} %w_oth.1, bf16[768,768]{1,0:T(8,128)(2,1)} %w_oth.1), custom_call_target="tpu_custom_call" | custom-call | tf_op jit(solution)/shard_map/pallas_call | solution.py:266
  146.0 5.2 %all-to-all-done.5 = bf16[8,2,16,384]{3,2,1,0:T(8,128)(2,1)S(1)} async-done(((bf16[8,2,16,384]{3,2,1,0:T(8,128)(2,1)}), bf16[8,2,16,384]{3,2,1,0:T(8,128)(2,1)S(1)}, u32[]{:S(2)}, u32[]{:S(2)}) %all-to-all-start.5) | async-done | bytes 196640 | tf_op jit(solution)/shard_map/all_to_all | solution.py:517
  151.3 7.6 %collective-permute-start.22 = (bf16[16,384]{1,0:T(8,128)(2,1)S(1)}, bf16[16,384]{1,0:T(8,128)(2,1)S(1)}, u32[]{:S(2)}, u32[]{:S(2)}) collective-permute-start(bf16[16,384]{1,0:T(8,128)(2,1)S(1)} %get-tuple-element.128), channel_id=1, source_target_pairs={{0,3},{1,2},{2,1},{3,0},{4,7},{5,6},{6,5},{7,4},{8,11},{9,10},{10,... | collective-permute-start | bytes 36872 | tf_op jit(solution)/shard_map/ppermute | solution.py:470
  158.8 1.1 collective-permute-start.20
  160.2 2.7 %collective-permute-done.20.from_dp = bf16[16,384]{1,0:T(8,128)(2,1)S(1)} collective-permute-done((bf16[16,384]{1,0:T(8,128)(2,1)S(1)}, bf16[16,384]{1,0:T(8,128)(2,1)S(1)}, u32[]{:S(2)}, u32[]{:S(2)}) %collective-permute-start.20) | collective-permute-done | bytes 12320 | tf_op jit(solution)/shard_map/ppermute | solution.py:470
  163.5 2.1 %shard_map.95 = (f32[6,2304]{1,0:T(8,128)}, f32[6,768]{1,0:T(8,128)}) custom-call(s32[4]{0:T(128)} %pad_add_fusion.pos, bf16[16,384]{1,0:T(8,128)(2,1)} %copy-done.24, bf16[16,384]{1,0:T(8,128)(2,1)} %copy-done.27, bf16[16,384]{1,0:T(8,128)(2,1)} %copy-done.26, bf16[16,384]{1,0:T(8,128)(2,1)} %copy-done.25), custom_call_target="tpu_custom_call" | custom-call | tf_op jit(solution)/shard_map/pallas_call | solution.py:456
  (87 shorter events, 7.6 us)
Async XLA Ops:
  0.6 4.9 %collective-permute-start = (bf16[256,768]{1,0:T(8,128)(2,1)}, bf16[256,768]{1,0:T(8,128)(2,1)S(1)}, u32[]{:S(2)}, u32[]{:S(2)}) collective-permute-start(bf16[256,768]{1,0:T(8,128)(2,1)} %bitcast.9), channel_id=1, source_target_pairs={{0,2},{2,0},{1,3},{3,1},{4,6},{6,4},{5,7},{7,5},{8,10},{10,8},{9,1... | collective-permute-start | bytes 1179656 | tf_op jit(solution)/shard_map/ppermute | solution.py:466
  4.0 22.3 %collective-permute-start.5 = (bf16[256,768]{1,0:T(8,128)(2,1)}, bf16[256,768]{1,0:T(8,128)(2,1)S(1)}, u32[]{:S(2)}, u32[]{:S(2)}) collective-permute-start(bf16[256,768]{1,0:T(8,128)(2,1)} %bitcast.12), channel_id=1, source_target_pairs={{0,2},{2,0},{1,3},{3,1},{4,6},{6,4},{5,7},{7,5},{8,10},{10,8},{9,1... | collective-permute-start | bytes 1179656 | tf_op jit(solution)/shard_map/ppermute | solution.py:466
  10.7 15.9 %all-to-all-start = ((bf16[8,2,16,384]{3,2,1,0:T(8,128)(2,1)}), bf16[8,2,16,384]{3,2,1,0:T(8,128)(2,1)S(1)}, u32[]{:S(2)}, u32[]{:S(2)}) async-start(bf16[8,2,16,384]{3,2,1,0:T(8,128)(2,1)} %get-tuple-element.66), calls=%async_computation | async-start | bytes 393216 | tf_op jit(solution)/shard_map/all_to_all | solution.py:490
  17.2 9.1 %collective-permute-start.2 = (bf16[2,64,384]{2,1,0:T(8,128)(2,1)}, bf16[2,64,384]{2,1,0:T(8,128)(2,1)S(1)}, u32[]{:S(2)}, u32[]{:S(2)}) collective-permute-start(bf16[2,64,384]{2,1,0:T(8,128)(2,1)} %get-tuple-element.68), channel_id=1, source_target_pairs={{0,8},{8,0},{16,24},{24,16},{1,9},{9,1},{17,25},{25,17},{2,10},{10... | collective-permute-start | bytes 294920 | tf_op jit(solution)/shard_map/ppermute | solution.py:470
  18.4 7.9 %collective-permute-start.1 = (bf16[2,128,384]{2,1,0:T(8,128)(2,1)}, bf16[2,128,384]{2,1,0:T(8,128)(2,1)S(1)}, u32[]{:S(2)}, u32[]{:S(2)}) collective-permute-start(bf16[2,128,384]{2,1,0:T(8,128)(2,1)} %get-tuple-element.67), channel_id=1, source_target_pairs={{0,4},{4,0},{1,5},{5,1},{2,6},{6,2},{3,7},{7,3},{8,12},{12,8},{9,1... | collective-permute-start | bytes 589832 | tf_op jit(solution)/shard_map/ppermute | solution.py:466
  19.7 4.7 %collective-permute-start.4 = (bf16[2,32,384]{2,1,0:T(8,128)(2,1)}, bf16[2,32,384]{2,1,0:T(8,128)(2,1)S(1)}, u32[]{:S(2)}, u32[]{:S(2)}) collective-permute-start(bf16[2,32,384]{2,1,0:T(8,128)(2,1)} %get-tuple-element.69), channel_id=1, source_target_pairs={{0,24},{8,16},{16,8},{24,0},{1,25},{9,17},{17,9},{25,1},{2,26},{10... | collective-permute-start | bytes 147464 | tf_op jit(solution)/shard_map/ppermute | solution.py:470
  21.5 4.7 %collective-permute-start.3 = (bf16[2,32,384]{2,1,0:T(8,128)(2,1)}, bf16[2,32,384]{2,1,0:T(8,128)(2,1)S(1)}, u32[]{:S(2)}, u32[]{:S(2)}) collective-permute-start(bf16[2,32,384]{2,1,0:T(8,128)(2,1)} %get-tuple-element.69), channel_id=1, source_target_pairs={{0,16},{8,24},{16,0},{24,8},{1,17},{9,25},{17,1},{25,9},{2,18},{10... | collective-permute-start | bytes 147464 | tf_op jit(solution)/shard_map/ppermute | solution.py:470
  26.3 15.1 %copy-start.9 = (bf16[2,128,384]{2,1,0:T(8,128)(2,1)}, bf16[2,128,384]{2,1,0:T(8,128)(2,1)S(1)}, u32[]{:S(2)}) copy-start(bf16[2,128,384]{2,1,0:T(8,128)(2,1)S(1)} %pad_maximum_fusion.wr) | copy-start | bytes 589828
  26.3 9.9 %copy-start.6 = (bf16[256,768]{1,0:T(8,128)(2,1)}, bf16[256,768]{1,0:T(8,128)(2,1)S(1)}, u32[]{:S(2)}) copy-start(bf16[256,768]{1,0:T(8,128)(2,1)S(1)} %collective-permute-done.5.ct_oth) | copy-start | bytes 1179652
  26.3 15.1 %copy-start.16 = (bf16[2,128,384]{2,1,0:T(8,128)(2,1)}, bf16[2,128,384]{2,1,0:T(8,128)(2,1)S(1)}, u32[]{:S(2)}) copy-start(bf16[2,128,384]{2,1,0:T(8,128)(2,1)S(1)} %collective-permute-done.1.yr) | copy-start | bytes 589828
  26.6 4.5 %collective-permute-start.6 = (bf16[2,128,384]{2,1,0:T(8,128)(2,1)S(1)}, bf16[2,128,384]{2,1,0:T(8,128)(2,1)S(1)}, u32[]{:S(2)}, u32[]{:S(2)}) collective-permute-start(bf16[2,128,384]{2,1,0:T(8,128)(2,1)S(1)} %pad_maximum_fusion.wr), channel_id=1, source_target_pairs={{0,4},{4,0},{1,5},{5,1},{2,6},{6,2},{3,7},{7,3},{8,12},{12,8},{9,1... | collective-permute-start | bytes 589832 | tf_op jit(solution)/shard_map/ppermute | solution.py:466
  31.1 10.3 %copy-start.17 = (bf16[2,128,384]{2,1,0:T(8,128)(2,1)}, bf16[2,128,384]{2,1,0:T(8,128)(2,1)S(1)}, u32[]{:S(2)}) copy-start(bf16[2,128,384]{2,1,0:T(8,128)(2,1)S(1)} %collective-permute-done.6.wy) | copy-start | bytes 589828
  31.1 12.6 %all-to-all-start.1 = ((bf16[8,2,48,384]{3,2,1,0:T(8,128)(2,1)}), bf16[8,2,48,384]{3,2,1,0:T(8,128)(2,1)S(1)}, u32[]{:S(2)}, u32[]{:S(2)}) async-start(bf16[8,2,48,384]{3,2,1,0:T(8,128)(2,1)} %shard_map.86), calls=%async_computation.1 | async-start | bytes 1179648 | tf_op jit(solution)/shard_map/all_to_all | solution.py:494
  61.4 3.7 %copy-start.4 = (bf16[2,256,384]{2,1,0:T(8,128)(2,1)S(1)}, bf16[2,256,384]{2,1,0:T(8,128)(2,1)}, u32[]{:S(2)}) copy-start(bf16[2,256,384]{2,1,0:T(8,128)(2,1)} %get-tuple-element.121.att_own) | copy-start | bytes 1179652
  61.4 8.5 %copy-start.30 = (bf16[2,128,384]{2,1,0:T(8,128)(2,1)S(1)}, bf16[2,128,384]{2,1,0:T(8,128)(2,1)}, u32[]{:S(2)}) copy-start(bf16[2,128,384]{2,1,0:T(8,128)(2,1)} %get-tuple-element.85) | copy-start | bytes 589828
  61.4 9.8 %copy-start.29 = (bf16[2,128,384]{2,1,0:T(8,128)(2,1)S(1)}, bf16[2,128,384]{2,1,0:T(8,128)(2,1)}, u32[]{:S(2)}) copy-start(bf16[2,128,384]{2,1,0:T(8,128)(2,1)} %get-tuple-element.86) | copy-start | bytes 589828
  61.4 22.1 %all-to-all-start.2 = ((bf16[8,2,48,384]{3,2,1,0:T(8,128)(2,1)}), bf16[8,2,48,384]{3,2,1,0:T(8,128)(2,1)S(1)}, u32[]{:S(2)}, u32[]{:S(2)}) async-start(bf16[8,2,48,384]{3,2,1,0:T(8,128)(2,1)} %get-tuple-element.80), calls=%async_computation.2 | async-start | bytes 1179648 | tf_op jit(solution)/shard_map/all_to_all | solution.py:498
  65.1 6.2 %collective-permute-start.7 = (bf16[2,256,384]{2,1,0:T(8,128)(2,1)S(1)}, bf16[2,256,384]{2,1,0:T(8,128)(2,1)S(1)}, u32[]{:S(2)}, u32[]{:S(2)}) collective-permute-start(bf16[2,256,384]{2,1,0:T(8,128)(2,1)S(1)} %copy-done.4), channel_id=1, source_target_pairs={{0,2},{2,0},{1,3},{3,1},{4,6},{6,4},{5,7},{7,5},{8,10},{10,8},{9,1... | collective-permute-start | bytes 1179656 | tf_op jit(solution)/shard_map/ppermute | solution.py:466
  69.8 11.5 %collective-permute-start.8 = (bf16[2,128,384]{2,1,0:T(8,128)(2,1)S(1)}, bf16[2,128,384]{2,1,0:T(8,128)(2,1)S(1)}, u32[]{:S(2)}, u32[]{:S(2)}) collective-permute-start(bf16[2,128,384]{2,1,0:T(8,128)(2,1)S(1)} %copy-done.30), channel_id=1, source_target_pairs={{0,4},{4,0},{1,5},{5,1},{2,6},{6,2},{3,7},{7,3},{8,12},{12,8},{9,1... | collective-permute-start | bytes 589832 | tf_op jit(solution)/shard_map/ppermute | solution.py:466
  71.2 12.2 %collective-permute-start.9 = (bf16[2,128,384]{2,1,0:T(8,128)(2,1)S(1)}, bf16[2,128,384]{2,1,0:T(8,128)(2,1)S(1)}, u32[]{:S(2)}, u32[]{:S(2)}) collective-permute-start(bf16[2,128,384]{2,1,0:T(8,128)(2,1)S(1)} %copy-done.29), channel_id=1, source_target_pairs={{0,4},{4,0},{1,5},{5,1},{2,6},{6,2},{3,7},{7,3},{8,12},{12,8},{9,1... | collective-permute-start | bytes 589832 | tf_op jit(solution)/shard_map/ppermute | solution.py:466
  77.5 14.7 %collective-permute-start.10 = (bf16[4,96,384]{2,1,0:T(8,128)(2,1)}, bf16[4,96,384]{2,1,0:T(8,128)(2,1)S(1)}, u32[]{:S(2)}, u32[]{:S(2)}) collective-permute-start(bf16[4,96,384]{2,1,0:T(8,128)(2,1)} %get-tuple-element.97), channel_id=1, source_target_pairs={{0,1},{1,0},{4,5},{5,4},{2,3},{3,2},{6,7},{7,6},{8,9},{9,8},{12,13... | collective-permute-start | bytes 884744 | tf_op jit(solution)/shard_map/ppermute | solution.py:470
  80.2 16.0 %collective-permute-start.11 = (bf16[4,96,384]{2,1,0:T(8,128)(2,1)}, bf16[4,96,384]{2,1,0:T(8,128)(2,1)S(1)}, u32[]{:S(2)}, u32[]{:S(2)}) collective-permute-start(bf16[4,96,384]{2,1,0:T(8,128)(2,1)} %get-tuple-element.98), channel_id=1, source_target_pairs={{0,4},{1,5},{4,0},{5,1},{2,6},{3,7},{6,2},{7,3},{8,12},{9,13},{12,... | collective-permute-start | bytes 884744 | tf_op jit(solution)/shard_map/ppermute | solution.py:470
  80.9 15.8 %collective-permute-start.12 = (bf16[4,96,384]{2,1,0:T(8,128)(2,1)}, bf16[4,96,384]{2,1,0:T(8,128)(2,1)S(1)}, u32[]{:S(2)}, u32[]{:S(2)}) collective-permute-start(bf16[4,96,384]{2,1,0:T(8,128)(2,1)} %get-tuple-element.99), channel_id=1, source_target_pairs={{0,5},{1,4},{4,1},{5,0},{2,7},{3,6},{6,3},{7,2},{8,13},{9,12},{12,... | collective-permute-start | bytes 884744 | tf_op jit(solution)/shard_map/ppermute | solution.py:470
  81.3 2.2 %copy-start.15 = (bf16[2,128,384]{2,1,0:T(8,128)(2,1)}, bf16[2,128,384]{2,1,0:T(8,128)(2,1)S(1)}, u32[]{:S(2)}) copy-start(bf16[2,128,384]{2,1,0:T(8,128)(2,1)S(1)} %collective-permute-done.8.dwy) | copy-start | bytes 589828
  83.5 21.9 %copy-start.14 = (bf16[2,128,384]{2,1,0:T(8,128)(2,1)}, bf16[2,128,384]{2,1,0:T(8,128)(2,1)S(1)}, u32[]{:S(2)}) copy-start(bf16[2,128,384]{2,1,0:T(8,128)(2,1)S(1)} %collective-permute-done.9.dy) | copy-start | bytes 589828
  87.1 18.2 %all-to-all-start.3 = ((bf16[8,2,16,384]{3,2,1,0:T(8,128)(2,1)}), bf16[8,2,16,384]{3,2,1,0:T(8,128)(2,1)S(1)}, u32[]{:S(2)}, u32[]{:S(2)}) async-start(bf16[8,2,16,384]{3,2,1,0:T(8,128)(2,1)} %get-tuple-element.90), calls=%async_computation.3 | async-start | bytes 393216 | tf_op jit(solution)/shard_map/all_to_all | solution.py:506
  92.3 26.5 %copy-start.11 = (bf16[4,96,384]{2,1,0:T(8,128)(2,1)}, bf16[4,96,384]{2,1,0:T(8,128)(2,1)S(1)}, u32[]{:S(2)}) copy-start(bf16[4,96,384]{2,1,0:T(8,128)(2,1)S(1)} %collective-permute-done.10.t1) | copy-start | bytes 884740
  96.1 22.6 %copy-start.12 = (bf16[4,96,384]{2,1,0:T(8,128)(2,1)}, bf16[4,96,384]{2,1,0:T(8,128)(2,1)S(1)}, u32[]{:S(2)}) copy-start(bf16[4,96,384]{2,1,0:T(8,128)(2,1)S(1)} %collective-permute-done.11.t2) | copy-start | bytes 884740
  96.7 22.1 %copy-start.13 = (bf16[4,96,384]{2,1,0:T(8,128)(2,1)}, bf16[4,96,384]{2,1,0:T(8,128)(2,1)S(1)}, u32[]{:S(2)}) copy-start(bf16[4,96,384]{2,1,0:T(8,128)(2,1)S(1)} %collective-permute-done.12.t3) | copy-start | bytes 884740
  96.7 8.6 %collective-permute-start.13 = (bf16[2,64,384]{2,1,0:T(8,128)(2,1)}, bf16[2,64,384]{2,1,0:T(8,128)(2,1)S(1)}, u32[]{:S(2)}, u32[]{:S(2)}) collective-permute-start(bf16[2,64,384]{2,1,0:T(8,128)(2,1)} %get-tuple-element.100), channel_id=1, source_target_pairs={{0,8},{8,0},{16,24},{24,16},{1,9},{9,1},{17,25},{25,17},{2,10},{10... | collective-permute-start | bytes 294920 | tf_op jit(solution)/shard_map/ppermute | solution.py:470
  98.4 4.8 %collective-permute-start.14 = (bf16[2,32,384]{2,1,0:T(8,128)(2,1)}, bf16[2,32,384]{2,1,0:T(8,128)(2,1)S(1)}, u32[]{:S(2)}, u32[]{:S(2)}) collective-permute-start(bf16[2,32,384]{2,1,0:T(8,128)(2,1)} %get-tuple-element.101), channel_id=1, source_target_pairs={{0,16},{8,24},{16,0},{24,8},{1,17},{9,25},{17,1},{25,9},{2,18},{10... | collective-permute-start | bytes 147464 | tf_op jit(solution)/shard_map/ppermute | solution.py:470
  100.4 4.8 %collective-permute-start.15 = (bf16[2,32,384]{2,1,0:T(8,128)(2,1)}, bf16[2,32,384]{2,1,0:T(8,128)(2,1)S(1)}, u32[]{:S(2)}, u32[]{:S(2)}) collective-permute-start(bf16[2,32,384]{2,1,0:T(8,128)(2,1)} %get-tuple-element.102), channel_id=1, source_target_pairs={{0,24},{8,16},{16,8},{24,0},{1,25},{9,17},{17,9},{25,1},{2,26},{10... | collective-permute-start | bytes 147464 | tf_op jit(solution)/shard_map/ppermute | solution.py:470
  103.2 2.1 %copy-start.22 = (bf16[2,32,384]{2,1,0:T(8,128)(2,1)}, bf16[2,32,384]{2,1,0:T(8,128)(2,1)S(1)}, u32[]{:S(2)}) copy-start(bf16[2,32,384]{2,1,0:T(8,128)(2,1)S(1)} %collective-permute-done.14.g4_a) | copy-start | bytes 147460
  112.3 3.8 %copy-start.28 = (bf16[256,1152]{1,0:T(8,128)(2,1)S(1)}, bf16[256,1152]{1,0:T(8,128)(2,1)}, u32[]{:S(2)}) copy-start(bf16[256,1152]{1,0:T(8,128)(2,1)} %get-tuple-element.118) | copy-start | bytes 1769476
  112.3 19.3 %all-to-all-start.4 = ((bf16[16,96,384]{2,1,0:T(8,128)(2,1)}), bf16[16,96,384]{2,1,0:T(8,128)(2,1)S(1)}, u32[]{:S(2)}, u32[]{:S(2)}) async-start(bf16[16,96,384]{2,1,0:T(8,128)(2,1)} %bitcast.15), calls=%async_computation.4 | async-start | bytes 2359296 | tf_op jit(solution)/shard_map/all_to_all | solution.py:513
  116.2 9.5 %collective-permute-start.19 = (bf16[256,1152]{1,0:T(8,128)(2,1)S(1)}, bf16[256,1152]{1,0:T(8,128)(2,1)S(1)}, u32[]{:S(2)}, u32[]{:S(2)}) collective-permute-start(bf16[256,1152]{1,0:T(8,128)(2,1)S(1)} %copy-done.28), channel_id=1, source_target_pairs={{0,2},{2,0},{1,3},{3,1},{4,6},{6,4},{5,7},{7,5},{8,10},{10,8},{9,1... | collective-permute-start | bytes 1769480 | tf_op jit(solution)/shard_map/ppermute | solution.py:466
  121.6 10.1 %collective-permute-start.16 = (bf16[96,384]{1,0:T(8,128)(2,1)}, bf16[96,384]{1,0:T(8,128)(2,1)S(1)}, u32[]{:S(2)}, u32[]{:S(2)}) collective-permute-start(bf16[96,384]{1,0:T(8,128)(2,1)} %get-tuple-element.113), channel_id=1, source_target_pairs={{0,8},{8,0},{16,24},{24,16},{1,9},{9,1},{17,25},{25,17},{2,10},{10... | collective-permute-start | bytes 221192 | tf_op jit(solution)/shard_map/ppermute | solution.py:470
  123.2 10.0 %collective-permute-start.17 = (bf16[96,384]{1,0:T(8,128)(2,1)}, bf16[96,384]{1,0:T(8,128)(2,1)S(1)}, u32[]{:S(2)}, u32[]{:S(2)}) collective-permute-start(bf16[96,384]{1,0:T(8,128)(2,1)} %get-tuple-element.114), channel_id=1, source_target_pairs={{0,16},{8,24},{16,0},{24,8},{1,17},{9,25},{17,1},{25,9},{2,18},{10... | collective-permute-start | bytes 221192 | tf_op jit(solution)/shard_map/ppermute | solution.py:470
  125.6 7.6 %collective-permute-start.18 = (bf16[96,384]{1,0:T(8,128)(2,1)}, bf16[96,384]{1,0:T(8,128)(2,1)S(1)}, u32[]{:S(2)}, u32[]{:S(2)}) collective-permute-start(bf16[96,384]{1,0:T(8,128)(2,1)} %get-tuple-element.115), channel_id=1, source_target_pairs={{0,24},{8,16},{16,8},{24,0},{1,25},{9,17},{17,9},{25,1},{2,26},{10... | collective-permute-start | bytes 221192 | tf_op jit(solution)/shard_map/ppermute | solution.py:470
  131.7 1.6 copy-start
  131.7 1.6 copy-start.19
  137.1 14.1 %all-to-all-start.5 = ((bf16[8,2,16,384]{3,2,1,0:T(8,128)(2,1)}), bf16[8,2,16,384]{3,2,1,0:T(8,128)(2,1)S(1)}, u32[]{:S(2)}, u32[]{:S(2)}) async-start(bf16[8,2,16,384]{3,2,1,0:T(8,128)(2,1)} %shard_map.93), calls=%async_computation.5 | async-start | bytes 393216 | tf_op jit(solution)/shard_map/all_to_all | solution.py:517
  151.3 11.7 %copy-start.24 = (bf16[16,384]{1,0:T(8,128)(2,1)}, bf16[16,384]{1,0:T(8,128)(2,1)S(1)}, u32[]{:S(2)}) copy-start(bf16[16,384]{1,0:T(8,128)(2,1)S(1)} %get-tuple-element.129.own) | copy-start | bytes 36868
  151.3 9.0 %collective-permute-start.22 = (bf16[16,384]{1,0:T(8,128)(2,1)S(1)}, bf16[16,384]{1,0:T(8,128)(2,1)S(1)}, u32[]{:S(2)}, u32[]{:S(2)}) collective-permute-start(bf16[16,384]{1,0:T(8,128)(2,1)S(1)} %get-tuple-element.128), channel_id=1, source_target_pairs={{0,3},{1,2},{2,1},{3,0},{4,7},{5,6},{6,5},{7,4},{8,11},{9,10},{10,... | collective-permute-start | bytes 36872 | tf_op jit(solution)/shard_map/ppermute | solution.py:470
  158.8 1.4 collective-permute-start.21
  158.8 4.0 %collective-permute-start.20 = (bf16[16,384]{1,0:T(8,128)(2,1)S(1)}, bf16[16,384]{1,0:T(8,128)(2,1)S(1)}, u32[]{:S(2)}, u32[]{:S(2)}) collective-permute-start(bf16[16,384]{1,0:T(8,128)(2,1)S(1)} %get-tuple-element.129.own), channel_id=1, source_target_pairs={{0,1},{1,0},{2,3},{3,2},{4,5},{5,4},{6,7},{7,6},{8,9},{9,8},{10,11... | collective-permute-start | bytes 36872 | tf_op jit(solution)/shard_map/ppermute | solution.py:470
  160.2 2.7 %copy-start.25 = (bf16[16,384]{1,0:T(8,128)(2,1)}, bf16[16,384]{1,0:T(8,128)(2,1)S(1)}, u32[]{:S(2)}) copy-start(bf16[16,384]{1,0:T(8,128)(2,1)S(1)} %collective-permute-done.22.from_both) | copy-start | bytes 36868
  160.2 2.7 %copy-start.26 = (bf16[16,384]{1,0:T(8,128)(2,1)}, bf16[16,384]{1,0:T(8,128)(2,1)S(1)}, u32[]{:S(2)}) copy-start(bf16[16,384]{1,0:T(8,128)(2,1)S(1)} %collective-permute-done.21.from_core) | copy-start | bytes 36868
  (12 other events, 9.3 us)
